TPU v7x, 512 devices: a whole 4x8x8 slice. The times are simulated.
512 devices in a mesh: dom: 32 (over x, z), level: 16 (over y, core).
Axes of the slice: x: 4, y: 8, z: 8, core: 2. Of those that a mesh axis runs over, the one named last changes fastest.
Arguments:
- right_side: bfloat16 [2048, 64, 128], P(('dom', 'level')), may hold values from -6 to 6
- diag_inverse: bfloat16 [2048, 128, 128], P(('dom', 'level'))
- off_blocks: bfloat16 [2048, 3, 128, 128], P(('dom', 'level')), may hold values from -0.25 to 0.25
- columns: int32 [2048, 3], replicated, may hold values from -1 to 2047, as said below
- plan: int32 [16], replicated, may hold values from 0 to 15, as said below
Outputs:
- forward_solution: bfloat16 [2048, 64, 128], P(('dom', 'level'))
- preconditioned: bfloat16 [2048, 64, 128], P(('dom', 'level'))
Inputs may be any that keep to these rules, and one draw needn't show every extreme that they name: For block row g of partition d = g // 64 and level-axis index p = (g // 4) % 16: every entry is -1 where plan[p] // 2 == 0; otherwise columns[g, n] is a block row of partition (d + n - 1) mod 32 whose level-axis index q has plan[q] // 2 == plan[p] // 2 - 1. `plan`: A permutation of the level-axis indices; each level is held by exactly two of them.
All inputs are finite; a program needn't handle non-finite values.
Results may differ from a plain program's by a relative error of at most 0.03.
Values may be sent and summed in bfloat16 or wider, within the bound.
No kernel may reach another device: no remote copies, remote signals or barrier semaphores. Data moves between devices by JAX's collectives and lax.ppermute only.
A program may use at most 64 MiB of HBM per device.

v0:
```python
import jax
import jax.numpy as jnp
from jax import lax
from jax.sharding import PartitionSpec as P


def broadcast(block, axis, source):
    block = jnp.where(lax.axis_index(axis) == source, block, jnp.zeros_like(block))
    return lax.psum(block, axis)


def with_halo(block, sides, width):
    for axis, dim in sides:
        count = lax.axis_size(axis)
        forward = [(i, i + 1) for i in range(count - 1)]
        forward.append((count - 1, 0))
        backward = [(target, source) for source, target in forward]
        low = lax.ppermute(
            lax.slice_in_dim(block, block.shape[dim] - width, None, axis=dim), axis, forward
        )
        high = lax.ppermute(lax.slice_in_dim(block, 0, width, axis=dim), axis, backward)
        block = jnp.concatenate([low, block, high], axis=dim)
    return block


def local(right_side, diag_inverse, off_blocks, columns, plan):
    per_dev = right_side.shape[0]
    per_row = off_blocks.shape[1]
    dom_count = lax.axis_size("dom")
    lev_count = lax.axis_size("level")
    dom_index = lax.axis_index("dom")
    lev_index = lax.axis_index("level")
    levels = lev_count // 2
    level_ids = jnp.arange(lev_count, dtype=jnp.int32)
    inverse = jnp.sum(jnp.where(plan[None, :] == level_ids[:, None], level_ids[None, :], 0), axis=1)
    own_entry = jnp.sum(jnp.where(level_ids == lev_index, plan, 0))
    own_level = own_entry // 2
    first_row = (dom_index * lev_count + lev_index) * per_dev
    own_rows = first_row + jnp.arange(per_dev, dtype=jnp.int32)
    own_columns = lax.dynamic_slice_in_dim(columns, first_row, per_dev, 0)
    partitions = (dom_index + jnp.arange(3, dtype=jnp.int32) - 1) % dom_count

    def source_rows(level_now):
        owners = lax.dynamic_slice_in_dim(inverse, 2 * level_now, 2, 0)
        row_base = (partitions[:, None] * lev_count + owners[None, :]) * per_dev
        sources = (row_base[:, :, None] + jnp.arange(per_dev, dtype=jnp.int32)).reshape(-1)
        return (sources, owners)

    def level_rows(payload, owners):
        return jnp.stack([broadcast(payload, "level", owners[which]) for which in range(2)])

    def margin_rows(payload):
        return with_halo(payload[None], (("dom", 0),), 1)

    def spread_rows(payload, owners):
        return margin_rows(level_rows(payload, owners))

    def level_pushes(payload, owners):
        return jnp.stack([broadcast(payload, "level", owners[which]) for which in range(2)])

    def margin_pushes(payload):
        return with_halo(payload[None], (("dom", 0),), 1)

    def spread_pushes(payload, owners):
        return margin_pushes(level_pushes(payload, owners))

    def forward_step(level_now, carry):
        running, solved = carry
        shifted = (right_side.astype(jnp.float32) - running).astype(jnp.bfloat16)
        candidate = jnp.einsum(
            "rkb,rbc->rkc", shifted, diag_inverse, preferred_element_type=jnp.float32
        ).astype(jnp.bfloat16)
        active = own_level == level_now
        solved = jnp.where(active, candidate, solved)
        sources, owners = source_rows(level_now)
        arrived = spread_rows(solved, owners).reshape((-1,) + solved.shape[1:])
        selector = (own_columns[:, :, None] == sources[None, None, :]).astype(jnp.bfloat16)
        picked = jnp.einsum(
            "rnm,mkb->rnkb", selector, arrived, preferred_element_type=jnp.float32
        ).astype(jnp.bfloat16)
        running = running + jnp.einsum(
            "rnkb,rnbc->rkc", picked, off_blocks, preferred_element_type=jnp.float32
        )
        return (running, solved)

    start = (jnp.zeros(right_side.shape, jnp.float32), jnp.zeros(right_side.shape, jnp.bfloat16))
    running, solved = lax.fori_loop(0, levels, forward_step, start)

    def backward_step(sweep_turn, carry):
        running, result = carry
        level_now = levels - 1 - sweep_turn
        folded = running.astype(jnp.bfloat16)
        candidate = (
            solved.astype(jnp.float32)
            - jnp.einsum("rkb,rbc->rkc", folded, diag_inverse, preferred_element_type=jnp.float32)
        ).astype(jnp.bfloat16)
        active = own_level == level_now
        result = jnp.where(active, candidate, result)
        pushes = jnp.einsum(
            "rkc,rnbc->rnkb", result, off_blocks, preferred_element_type=jnp.float32
        ).astype(jnp.bfloat16)
        sources, owners = source_rows(level_now)
        arrived = spread_pushes(pushes, owners).reshape((-1, per_row) + pushes.shape[2:])
        targets = columns[sources]
        selector = (targets[:, :, None] == own_rows[None, None, :]).astype(jnp.bfloat16)
        running = running + jnp.einsum(
            "mnr,mnkb->rkb", selector, arrived, preferred_element_type=jnp.float32
        )
        return (running, result)

    start = (jnp.zeros(right_side.shape, jnp.float32), jnp.zeros(right_side.shape, jnp.bfloat16))
    running, result = lax.fori_loop(0, levels, backward_step, start)
    return (solved, result)


def solution(mesh):
    return jax.shard_map(
        local,
        mesh=mesh,
        in_specs=(
            P(("dom", "level"), None, None),
            P(("dom", "level"), None, None),
            P(("dom", "level"), None, None, None),
            P(),
            P(),
        ),
        out_specs=(P(("dom", "level"), None, None), P(("dom", "level"), None, None)),
        check_vma=False,
    )
```

profile of v0, /device:TPU:1, one launch (start us, length us, event | category | flops | bytes accessed | tf_op | source)
XLA Modules:
  0.0 2174.2 jit_solution(52740436006431408)
XLA Ops:
  13.0 1049.6 %while.32 = (s32[]{:T(128)}, f32[4,64,128]{2,1,0:T(8,128)S(1)}, bf16[4,64,128]{2,1,0:T(8,128)(2,1)S(1)}, s32[4,3]{1,0:T(4,128)S(1)}, s32[16]{0:T(128)S(1)}, /*in...) while((s32[]{:T(128)}, f32[4,64,128]{2,1,0:T(8,128)S(1)}, ...), condition=%wide.region_5.6_spmd.clone, body=%wide.region_2.5_spmd.clone.sunk | while | flops 39158136 | bytes 6554548 | solution.py:87
  17.0 118.5 %all-reduce.9.cloned.1.call-done = (bf16[1,4,64,128]{3,2,1,0:T(8,128)(2,1)}, bf16[1,4,64,128]{3,2,1,0:T(8,128)(2,1)}) async-done(((bf16[1,4,64,128]{3,2,1,0:T(8,128)(2,1)}, bf16[1,4,64,128]{3,2,1,0:T(8,128)(2,1)}), (bf16[1,4,64,128]{3,2,1,0:T(8,128)(2,1)}, bf16[1,4,64,128]{3,2,1,0:T(8,128)(2,1)})) %all-reduce.9.cloned.1.call-update) | async-done | bytes 131088 | tf_op jit(solution)/shard_map/while/body/eval_jaxpr/psum | solution.py:9
  136.4 7.7 collective-permute-start
  146.4 7.1 collective-permute-done.1
  158.2 107.1 %all-reduce.9.cloned.1.call-done = (bf16[1,4,64,128]{3,2,1,0:T(8,128)(2,1)}, bf16[1,4,64,128]{3,2,1,0:T(8,128)(2,1)}) async-done(((bf16[1,4,64,128]{3,2,1,0:T(8,128)(2,1)}, bf16[1,4,64,128]{3,2,1,0:T(8,128)(2,1)}), (bf16[1,4,64,128]{3,2,1,0:T(8,128)(2,1)}, bf16[1,4,64,128]{3,2,1,0:T(8,128)(2,1)})) %all-reduce.9.cloned.1.call-update) | async-done | bytes 131088 | tf_op jit(solution)/shard_map/while/body/eval_jaxpr/psum | solution.py:9
  266.2 7.7 collective-permute-start
  276.2 7.1 collective-permute-done.1
  288.0 107.1 %all-reduce.9.cloned.1.call-done = (bf16[1,4,64,128]{3,2,1,0:T(8,128)(2,1)}, bf16[1,4,64,128]{3,2,1,0:T(8,128)(2,1)}) async-done(((bf16[1,4,64,128]{3,2,1,0:T(8,128)(2,1)}, bf16[1,4,64,128]{3,2,1,0:T(8,128)(2,1)}), (bf16[1,4,64,128]{3,2,1,0:T(8,128)(2,1)}, bf16[1,4,64,128]{3,2,1,0:T(8,128)(2,1)})) %all-reduce.9.cloned.1.call-update) | async-done | bytes 131088 | tf_op jit(solution)/shard_map/while/body/eval_jaxpr/psum | solution.py:9
  395.9 7.7 collective-permute-start
  405.9 7.1 collective-permute-done.1
  417.8 107.1 %all-reduce.9.cloned.1.call-done = (bf16[1,4,64,128]{3,2,1,0:T(8,128)(2,1)}, bf16[1,4,64,128]{3,2,1,0:T(8,128)(2,1)}) async-done(((bf16[1,4,64,128]{3,2,1,0:T(8,128)(2,1)}, bf16[1,4,64,128]{3,2,1,0:T(8,128)(2,1)}), (bf16[1,4,64,128]{3,2,1,0:T(8,128)(2,1)}, bf16[1,4,64,128]{3,2,1,0:T(8,128)(2,1)})) %all-reduce.9.cloned.1.call-update) | async-done | bytes 131088 | tf_op jit(solution)/shard_map/while/body/eval_jaxpr/psum | solution.py:9
  525.7 7.7 collective-permute-start
  535.7 7.1 collective-permute-done.1
  547.5 107.1 %all-reduce.9.cloned.1.call-done = (bf16[1,4,64,128]{3,2,1,0:T(8,128)(2,1)}, bf16[1,4,64,128]{3,2,1,0:T(8,128)(2,1)}) async-done(((bf16[1,4,64,128]{3,2,1,0:T(8,128)(2,1)}, bf16[1,4,64,128]{3,2,1,0:T(8,128)(2,1)}), (bf16[1,4,64,128]{3,2,1,0:T(8,128)(2,1)}, bf16[1,4,64,128]{3,2,1,0:T(8,128)(2,1)})) %all-reduce.9.cloned.1.call-update) | async-done | bytes 131088 | tf_op jit(solution)/shard_map/while/body/eval_jaxpr/psum | solution.py:9
  655.5 7.7 collective-permute-start
  665.5 7.1 collective-permute-done.1
  677.3 107.1 %all-reduce.9.cloned.1.call-done = (bf16[1,4,64,128]{3,2,1,0:T(8,128)(2,1)}, bf16[1,4,64,128]{3,2,1,0:T(8,128)(2,1)}) async-done(((bf16[1,4,64,128]{3,2,1,0:T(8,128)(2,1)}, bf16[1,4,64,128]{3,2,1,0:T(8,128)(2,1)}), (bf16[1,4,64,128]{3,2,1,0:T(8,128)(2,1)}, bf16[1,4,64,128]{3,2,1,0:T(8,128)(2,1)})) %all-reduce.9.cloned.1.call-update) | async-done | bytes 131088 | tf_op jit(solution)/shard_map/while/body/eval_jaxpr/psum | solution.py:9
  785.3 7.7 collective-permute-start
  795.3 7.1 collective-permute-done.1
  807.1 107.1 %all-reduce.9.cloned.1.call-done = (bf16[1,4,64,128]{3,2,1,0:T(8,128)(2,1)}, bf16[1,4,64,128]{3,2,1,0:T(8,128)(2,1)}) async-done(((bf16[1,4,64,128]{3,2,1,0:T(8,128)(2,1)}, bf16[1,4,64,128]{3,2,1,0:T(8,128)(2,1)}), (bf16[1,4,64,128]{3,2,1,0:T(8,128)(2,1)}, bf16[1,4,64,128]{3,2,1,0:T(8,128)(2,1)})) %all-reduce.9.cloned.1.call-update) | async-done | bytes 131088 | tf_op jit(solution)/shard_map/while/body/eval_jaxpr/psum | solution.py:9
  915.1 7.7 collective-permute-start
  925.0 7.1 collective-permute-done.1
  936.9 107.1 %all-reduce.9.cloned.1.call-done = (bf16[1,4,64,128]{3,2,1,0:T(8,128)(2,1)}, bf16[1,4,64,128]{3,2,1,0:T(8,128)(2,1)}) async-done(((bf16[1,4,64,128]{3,2,1,0:T(8,128)(2,1)}, bf16[1,4,64,128]{3,2,1,0:T(8,128)(2,1)}), (bf16[1,4,64,128]{3,2,1,0:T(8,128)(2,1)}, bf16[1,4,64,128]{3,2,1,0:T(8,128)(2,1)})) %all-reduce.9.cloned.1.call-update) | async-done | bytes 131088 | tf_op jit(solution)/shard_map/while/body/eval_jaxpr/psum | solution.py:9
  1044.8 7.7 collective-permute-start
  1054.8 7.1 collective-permute-done.1
  1062.7 1104.4 %while.33 = (s32[]{:T(128)}, f32[4,64,128]{2,0,1:T(4,128)S(1)}, bf16[4,64,128]{2,1,0:T(8,128)(2,1)S(1)}, s32[16]{0:T(128)S(1)}, s32[2048,3]{1,0:T(8,128)S(1)}, /...) while((s32[]{:T(128)}, f32[4,64,128]{2,0,1:T(4,128)S(1)}, ...), condition=%wide.region_9.10_spmd.clone, body=%wide.region_6.9_spmd.clone.sunk | while | flops 40404424 | bytes 11541097 | solution.py:112
  1068.2 108.6 %all-reduce.11.cloned.1.call-done = (bf16[1,4,3,64,128]{4,3,2,1,0:T(8,128)(2,1)}, bf16[1,4,3,64,128]{4,3,2,1,0:T(8,128)(2,1)}) async-done(((bf16[1,4,3,64,128]{4,3,2,1,0:T(8,128)(2,1)}, bf16[1,4,3,64,128]{4,3,2,1,0:T(8,128)(2,1)}), (bf16[1,4,3,64,128]{4,3,2,1,0:T(8,128)(2,1)}, bf16[1,4,3,64,128]{4,3,2,1,0:T(8,128)(2,1)})) %all-reduce.11.cloned.1.call-update) | async-done | bytes 393232 | tf_op jit(solution)/shard_map/while/body/eval_jaxpr/psum | solution.py:9
  1177.9 7.7 collective-permute-start.2
  1193.4 7.1 collective-permute-done.3
  1207.1 107.7 %all-reduce.11.cloned.1.call-done = (bf16[1,4,3,64,128]{4,3,2,1,0:T(8,128)(2,1)}, bf16[1,4,3,64,128]{4,3,2,1,0:T(8,128)(2,1)}) async-done(((bf16[1,4,3,64,128]{4,3,2,1,0:T(8,128)(2,1)}, bf16[1,4,3,64,128]{4,3,2,1,0:T(8,128)(2,1)}), (bf16[1,4,3,64,128]{4,3,2,1,0:T(8,128)(2,1)}, bf16[1,4,3,64,128]{4,3,2,1,0:T(8,128)(2,1)})) %all-reduce.11.cloned.1.call-update) | async-done | bytes 393232 | tf_op jit(solution)/shard_map/while/body/eval_jaxpr/psum | solution.py:9
  1315.9 7.7 collective-permute-start.2
  1331.3 7.1 collective-permute-done.3
  1345.0 107.7 %all-reduce.11.cloned.1.call-done = (bf16[1,4,3,64,128]{4,3,2,1,0:T(8,128)(2,1)}, bf16[1,4,3,64,128]{4,3,2,1,0:T(8,128)(2,1)}) async-done(((bf16[1,4,3,64,128]{4,3,2,1,0:T(8,128)(2,1)}, bf16[1,4,3,64,128]{4,3,2,1,0:T(8,128)(2,1)}), (bf16[1,4,3,64,128]{4,3,2,1,0:T(8,128)(2,1)}, bf16[1,4,3,64,128]{4,3,2,1,0:T(8,128)(2,1)})) %all-reduce.11.cloned.1.call-update) | async-done | bytes 393232 | tf_op jit(solution)/shard_map/while/body/eval_jaxpr/psum | solution.py:9
  1453.8 7.7 collective-permute-start.2
  1469.2 7.1 collective-permute-done.3
  1482.9 107.7 %all-reduce.11.cloned.1.call-done = (bf16[1,4,3,64,128]{4,3,2,1,0:T(8,128)(2,1)}, bf16[1,4,3,64,128]{4,3,2,1,0:T(8,128)(2,1)}) async-done(((bf16[1,4,3,64,128]{4,3,2,1,0:T(8,128)(2,1)}, bf16[1,4,3,64,128]{4,3,2,1,0:T(8,128)(2,1)}), (bf16[1,4,3,64,128]{4,3,2,1,0:T(8,128)(2,1)}, bf16[1,4,3,64,128]{4,3,2,1,0:T(8,128)(2,1)})) %all-reduce.11.cloned.1.call-update) | async-done | bytes 393232 | tf_op jit(solution)/shard_map/while/body/eval_jaxpr/psum | solution.py:9
  1591.7 7.7 collective-permute-start.2
  1607.2 7.1 collective-permute-done.3
  1620.9 107.7 %all-reduce.11.cloned.1.call-done = (bf16[1,4,3,64,128]{4,3,2,1,0:T(8,128)(2,1)}, bf16[1,4,3,64,128]{4,3,2,1,0:T(8,128)(2,1)}) async-done(((bf16[1,4,3,64,128]{4,3,2,1,0:T(8,128)(2,1)}, bf16[1,4,3,64,128]{4,3,2,1,0:T(8,128)(2,1)}), (bf16[1,4,3,64,128]{4,3,2,1,0:T(8,128)(2,1)}, bf16[1,4,3,64,128]{4,3,2,1,0:T(8,128)(2,1)})) %all-reduce.11.cloned.1.call-update) | async-done | bytes 393232 | tf_op jit(solution)/shard_map/while/body/eval_jaxpr/psum | solution.py:9
  1729.6 7.7 collective-permute-start.2
  1745.1 7.1 collective-permute-done.3
  1758.8 107.7 %all-reduce.11.cloned.1.call-done = (bf16[1,4,3,64,128]{4,3,2,1,0:T(8,128)(2,1)}, bf16[1,4,3,64,128]{4,3,2,1,0:T(8,128)(2,1)}) async-done(((bf16[1,4,3,64,128]{4,3,2,1,0:T(8,128)(2,1)}, bf16[1,4,3,64,128]{4,3,2,1,0:T(8,128)(2,1)}), (bf16[1,4,3,64,128]{4,3,2,1,0:T(8,128)(2,1)}, bf16[1,4,3,64,128]{4,3,2,1,0:T(8,128)(2,1)})) %all-reduce.11.cloned.1.call-update) | async-done | bytes 393232 | tf_op jit(solution)/shard_map/while/body/eval_jaxpr/psum | solution.py:9
  1867.6 7.7 collective-permute-start.2
  1883.0 7.1 collective-permute-done.3
  1896.7 107.7 %all-reduce.11.cloned.1.call-done = (bf16[1,4,3,64,128]{4,3,2,1,0:T(8,128)(2,1)}, bf16[1,4,3,64,128]{4,3,2,1,0:T(8,128)(2,1)}) async-done(((bf16[1,4,3,64,128]{4,3,2,1,0:T(8,128)(2,1)}, bf16[1,4,3,64,128]{4,3,2,1,0:T(8,128)(2,1)}), (bf16[1,4,3,64,128]{4,3,2,1,0:T(8,128)(2,1)}, bf16[1,4,3,64,128]{4,3,2,1,0:T(8,128)(2,1)})) %all-reduce.11.cloned.1.call-update) | async-done | bytes 393232 | tf_op jit(solution)/shard_map/while/body/eval_jaxpr/psum | solution.py:9
  2005.5 7.7 collective-permute-start.2
  2034.6 107.7 %all-reduce.11.cloned.1.call-done = (bf16[1,4,3,64,128]{4,3,2,1,0:T(8,128)(2,1)}, bf16[1,4,3,64,128]{4,3,2,1,0:T(8,128)(2,1)}) async-done(((bf16[1,4,3,64,128]{4,3,2,1,0:T(8,128)(2,1)}, bf16[1,4,3,64,128]{4,3,2,1,0:T(8,128)(2,1)}), (bf16[1,4,3,64,128]{4,3,2,1,0:T(8,128)(2,1)}, bf16[1,4,3,64,128]{4,3,2,1,0:T(8,128)(2,1)})) %all-reduce.11.cloned.1.call-update) | async-done | bytes 393232 | tf_op jit(solution)/shard_map/while/body/eval_jaxpr/psum | solution.py:9
  2143.4 7.7 collective-permute-start.2
  (326 shorter events, 181.9 us)
Async XLA Ops:
  13.0 122.5 %all-reduce.9.cloned.1.call-start = ((), (), s32[]{:S(2)}) async-start(), calls=%async_computation | async-start | bytes 262144 | tf_op jit(solution)/shard_map/while/body/eval_jaxpr/psum | solution.py:9
  136.4 10.0 collective-permute-start
  144.1 9.4 collective-permute-start.1
  154.2 111.1 %all-reduce.9.cloned.1.call-start = ((), (), s32[]{:S(2)}) async-start(), calls=%async_computation | async-start | bytes 262144 | tf_op jit(solution)/shard_map/while/body/eval_jaxpr/psum | solution.py:9
  266.2 10.0 collective-permute-start
  273.9 9.4 collective-permute-start.1
  284.0 111.1 %all-reduce.9.cloned.1.call-start = ((), (), s32[]{:S(2)}) async-start(), calls=%async_computation | async-start | bytes 262144 | tf_op jit(solution)/shard_map/while/body/eval_jaxpr/psum | solution.py:9
  395.9 10.0 collective-permute-start
  403.7 9.4 collective-permute-start.1
  413.8 111.1 %all-reduce.9.cloned.1.call-start = ((), (), s32[]{:S(2)}) async-start(), calls=%async_computation | async-start | bytes 262144 | tf_op jit(solution)/shard_map/while/body/eval_jaxpr/psum | solution.py:9
  525.7 10.0 collective-permute-start
  533.4 9.4 collective-permute-start.1
  543.6 111.1 %all-reduce.9.cloned.1.call-start = ((), (), s32[]{:S(2)}) async-start(), calls=%async_computation | async-start | bytes 262144 | tf_op jit(solution)/shard_map/while/body/eval_jaxpr/psum | solution.py:9
  655.5 10.0 collective-permute-start
  663.2 9.4 collective-permute-start.1
  673.3 111.1 %all-reduce.9.cloned.1.call-start = ((), (), s32[]{:S(2)}) async-start(), calls=%async_computation | async-start | bytes 262144 | tf_op jit(solution)/shard_map/while/body/eval_jaxpr/psum | solution.py:9
  785.3 10.0 collective-permute-start
  793.0 9.4 collective-permute-start.1
  803.1 111.1 %all-reduce.9.cloned.1.call-start = ((), (), s32[]{:S(2)}) async-start(), calls=%async_computation | async-start | bytes 262144 | tf_op jit(solution)/shard_map/while/body/eval_jaxpr/psum | solution.py:9
  915.1 10.0 collective-permute-start
  922.8 9.4 collective-permute-start.1
  932.9 111.1 %all-reduce.9.cloned.1.call-start = ((), (), s32[]{:S(2)}) async-start(), calls=%async_computation | async-start | bytes 262144 | tf_op jit(solution)/shard_map/while/body/eval_jaxpr/psum | solution.py:9
  1044.8 10.0 collective-permute-start
  1052.5 9.4 collective-permute-start.1
  1062.7 114.2 %all-reduce.11.cloned.1.call-start = ((), (), s32[]{:S(2)}) async-start(), calls=%async_computation.1 | async-start | bytes 786432 | tf_op jit(solution)/shard_map/while/body/eval_jaxpr/psum | solution.py:9
  1177.9 15.5 collective-permute-start.2
  1185.6 14.9 collective-permute-start.3
  1201.5 113.3 %all-reduce.11.cloned.1.call-start = ((), (), s32[]{:S(2)}) async-start(), calls=%async_computation.1 | async-start | bytes 786432 | tf_op jit(solution)/shard_map/while/body/eval_jaxpr/psum | solution.py:9
  1315.9 15.5 collective-permute-start.2
  1323.6 14.9 collective-permute-start.3
  1339.5 113.3 %all-reduce.11.cloned.1.call-start = ((), (), s32[]{:S(2)}) async-start(), calls=%async_computation.1 | async-start | bytes 786432 | tf_op jit(solution)/shard_map/while/body/eval_jaxpr/psum | solution.py:9
  1453.8 15.5 collective-permute-start.2
  1461.5 14.9 collective-permute-start.3
  1477.4 113.3 %all-reduce.11.cloned.1.call-start = ((), (), s32[]{:S(2)}) async-start(), calls=%async_computation.1 | async-start | bytes 786432 | tf_op jit(solution)/shard_map/while/body/eval_jaxpr/psum | solution.py:9
  1591.7 15.5 collective-permute-start.2
  1599.4 14.9 collective-permute-start.3
  1615.3 113.3 %all-reduce.11.cloned.1.call-start = ((), (), s32[]{:S(2)}) async-start(), calls=%async_computation.1 | async-start | bytes 786432 | tf_op jit(solution)/shard_map/while/body/eval_jaxpr/psum | solution.py:9
  1729.6 15.5 collective-permute-start.2
  1737.4 14.9 collective-permute-start.3
  1753.3 113.3 %all-reduce.11.cloned.1.call-start = ((), (), s32[]{:S(2)}) async-start(), calls=%async_computation.1 | async-start | bytes 786432 | tf_op jit(solution)/shard_map/while/body/eval_jaxpr/psum | solution.py:9
  1867.6 15.5 collective-permute-start.2
  1875.3 14.9 collective-permute-start.3
  1891.2 113.3 %all-reduce.11.cloned.1.call-start = ((), (), s32[]{:S(2)}) async-start(), calls=%async_computation.1 | async-start | bytes 786432 | tf_op jit(solution)/shard_map/while/body/eval_jaxpr/psum | solution.py:9
  2005.5 15.5 collective-permute-start.2
  2013.2 14.9 collective-permute-start.3
  2029.1 113.3 %all-reduce.11.cloned.1.call-start = ((), (), s32[]{:S(2)}) async-start(), calls=%async_computation.1 | async-start | bytes 786432 | tf_op jit(solution)/shard_map/while/body/eval_jaxpr/psum | solution.py:9
  2143.4 15.5 collective-permute-start.2
  2151.1 14.9 collective-permute-start.3
  (10 other events, 1032.5 us)
Sparse Core Ops, SparseCore 0:
  17.0 118.4 all-reduce.8
  158.2 106.9 all-reduce.8
  288.0 106.9 all-reduce.8
  417.8 106.9 all-reduce.8
  547.6 106.9 all-reduce.8
  677.4 106.9 all-reduce.8
  807.1 106.9 all-reduce.8
  936.9 106.9 all-reduce.8
  1068.1 108.7 all-reduce.10
  1206.9 107.8 all-reduce.10
  1344.9 107.8 all-reduce.10
  1482.8 107.8 all-reduce.10
  1620.7 107.8 all-reduce.10
  1758.7 107.8 all-reduce.10
  1896.6 107.8 all-reduce.10
  2034.5 107.8 all-reduce.10
where the time goes:
time: 2180 us; the launch traced here: 2170 us
  waiting for transfers between devices  1890 us (87%)
  starting transfers between devices  155 us (7%)
  matrix products  46.9 us (2%)
  other arithmetic  27.3 us (1%)
  loops' own time  22.3 us (1%)
    psum x16, waiting for transfers between devices, broadcast(): return lax.psum(block, axis)  1730 us
    ppermute x16, starting transfers between devices, with_halo(): lax.ppermute(lax.slice_in_dim(block, 0, width, axis=dim), axis, backward)  123 us
    ppermute x16, waiting for transfers between devices, with_halo(): lax.ppermute(lax.slice_in_dim(block, block.shape[dim] - width, None, axis...  114 us
  transfers between devices with their start and end apart: 48, of which 48 were waited for; matrix products, arithmetic and copies ran while one was open for 0% of the time, Pallas kernels for 0%

commit v1 on v0

v1 whole, which is shorter than its diff:
```python
import functools

import jax
import jax.numpy as jnp
from jax import lax
from jax.experimental import pallas as pl
from jax.experimental.pallas import tpu as pltpu
from jax.sharding import PartitionSpec as P

BF16 = jnp.bfloat16
F32 = jnp.float32


def dot(a, b):
    return lax.dot_general(a, b, (((1,), (0,)), ((), ())), preferred_element_type=F32)


def dot_t(a, b):
    return lax.dot_general(a, b, (((1,), (1,)), ((), ())), preferred_element_type=F32)


def fetch(owners, weights, held, sems, level, half):
    return pltpu.make_async_copy(
        weights.at[owners[2 * level + half]], held.at[half], sems.at[half]
    )


def either(low, high, share):
    top = lax.broadcasted_iota(jnp.int32, low.shape, 0) < share
    return jnp.where(top, low, high)


def forward_kernel(level, share, owners, weights, pick, side, left, own, right, out, held, sems):
    copies = [fetch(owners, weights, held, sems, level, half) for half in range(2)]
    for copy in copies:
        copy.start()
    rows = held.shape[1]
    count = 2 * rows
    span = count * share
    near = jnp.concatenate([left[...], own[...], right[...]], axis=0)
    picked = dot(pick[level], near)
    copies[0].wait()
    for pair in range(count // 2):
        if pair == rows // 2:
            copies[1].wait()
        half, row = divmod(2 * pair, rows)
        at = 2 * share * pair
        terms = [picked[n * span + at : n * span + at + 2 * share] for n in range(3)]
        terms = jnp.concatenate(terms, axis=1).astype(BF16)
        total = either(
            *[dot(terms, held[half, row + one, 1:].reshape(-1, held.shape[-1])) for one in range(2)],
            share,
        )
        shifted = (side[level, at : at + 2 * share].astype(F32) - total).astype(BF16)
        solved = either(*[dot(shifted, held[half, row + one, 0]) for one in range(2)], share)
        out[at : at + 2 * share] = solved.astype(BF16)


def backward_kernel(
    level, share, last, owners, weights, spread, solved, from_left, own, from_right, result, *rest
):
    *outs, held, sems = rest
    copies = [fetch(owners, weights, held, sems, level, half) for half in range(2)]
    for copy in copies:
        copy.start()
    rows = held.shape[1]
    count = 2 * rows
    folded = (from_left[...] + own[...] + from_right[...]).astype(BF16)
    pushes = [[], [], []]
    copies[0].wait()
    for pair in range(count // 2):
        if pair == rows // 2:
            copies[1].wait()
        half, row = divmod(2 * pair, rows)
        at = 2 * share * pair
        part = folded[at : at + 2 * share]
        part = either(*[dot(part, held[half, row + one, 0]) for one in range(2)], share)
        done = (solved[at : at + 2 * share].astype(F32) - part).astype(BF16)
        result[at : at + 2 * share] = done
        if not last:
            for n in range(3):
                pushes[n].append(
                    either(*[dot_t(done, held[half, row + one, 1 + n]) for one in range(2)], share)
                )
    if not last:
        pushed = jnp.concatenate(pushes[0] + pushes[1] + pushes[2], axis=0).astype(BF16)
        total = dot(spread[level], pushed)
        span = count * share
        for n in range(3):
            outs[n][...] = total[n * span : (n + 1) * span]


def call(kernel, outs, owners, weights, *rest):
    vmem = pl.BlockSpec(memory_space=pltpu.VMEM)
    return pl.pallas_call(
        kernel,
        out_shape=outs,
        in_specs=[
            pl.BlockSpec(memory_space=pltpu.SMEM),
            pl.BlockSpec(memory_space=pl.ANY),
            *[vmem] * len(rest),
        ],
        out_specs=[vmem] * len(outs),
        scratch_shapes=[
            pltpu.VMEM((2,) + weights.shape[1:], weights.dtype),
            pltpu.SemaphoreType.DMA((2,)),
        ],
        compiler_params=pltpu.CompilerParams(vmem_limit_bytes=16 * 2**20),
    )(owners, weights, *rest)


def local(right_side, diag_inverse, off_blocks, columns, plan):
    rows, depth, width = right_side.shape
    doms = lax.axis_size("dom")
    levs = lax.axis_size("level")
    levels = levs // 2
    share = depth // levs
    count = 2 * rows
    dom = lax.axis_index("dom")
    lev = lax.axis_index("level")
    up = [(i, (i + 1) % doms) for i in range(doms)]
    down = [(target, source) for source, target in up]

    weights = jnp.concatenate([diag_inverse[:, None], off_blocks], axis=1)
    weights = lax.all_gather(weights, "level")

    ids = jnp.arange(levs, dtype=jnp.int32)
    own_level = jnp.sum(jnp.where(ids == lev, plan, 0)) // 2
    inverse = jnp.sum(jnp.where(plan[None, :] == ids[:, None], ids[None, :], 0), axis=1)

    first = jnp.einsum("rkb,rbc->rkc", right_side, diag_inverse, preferred_element_type=F32)
    side = jnp.where(own_level == 0, first.astype(BF16), right_side)
    side = side.reshape(rows, levs, share, width)
    side = lax.all_to_all(side, "level", 1, 0, tiled=False)
    side = side.reshape(levs, rows * share, width)[inverse].reshape(levels, count * share, width)

    part = lax.dynamic_slice_in_dim(columns, dom * levs * rows, levs * rows, 0)
    part = part.reshape(levs, rows * 3)[inverse].reshape(levels, count, 3)
    source = plan[(part // rows) % levs] % 2 * rows + part % rows
    j = jnp.arange(count, dtype=jnp.int32)
    meets = source[:, :, :, None] == j
    eye_n = jnp.eye(3, dtype=bool)
    eye_k = jnp.eye(share, dtype=bool)
    pick = (
        meets.transpose(0, 2, 1, 3)[:, :, :, None, None, :, None]
        & eye_n[None, :, None, None, :, None, None]
        & eye_k[None, None, None, :, None, None, :]
    )
    size = 3 * count * share
    pick = pick.reshape(levels, size, size).astype(BF16)
    spread = pick.transpose(0, 2, 1)

    vector = jax.ShapeDtypeStruct((count * share, width), BF16)
    summed = jax.ShapeDtypeStruct((count * share, width), F32)

    solved = [side[0]]
    for level in range(1, levels):
        own = solved[-1]
        left = lax.ppermute(own, "dom", up)
        right = lax.ppermute(own, "dom", down)
        kernel = functools.partial(forward_kernel, level, share)
        solved += call(kernel, [vector], inverse, weights, pick, side, left, own, right)

    zero = jnp.zeros(summed.shape, F32)
    left, own, right = zero, zero, zero
    results = []
    for level in range(levels - 1, -1, -1):
        last = level == 0
        kernel = functools.partial(backward_kernel, level, share, last)
        outs = [vector] if last else [vector, summed, summed, summed]
        result, *sums = call(
            kernel, outs, inverse, weights, spread, solved[level], left, own, right
        )
        results.append(result)
        if not last:
            right = lax.ppermute(sums[0], "dom", down)
            left = lax.ppermute(sums[2], "dom", up)
            own = sums[1]

    both = jnp.stack([jnp.stack(solved), jnp.stack(results[::-1])])
    both = both.reshape(2, levs, rows, share, width)[:, plan]
    both = lax.all_to_all(both, "level", 1, 0, tiled=False)
    both = both.transpose(1, 2, 0, 3, 4).reshape(2, rows, depth, width)
    return both[0], both[1]


def solution(mesh):
    return jax.shard_map(
        local,
        mesh=mesh,
        in_specs=(
            P(("dom", "level"), None, None),
            P(("dom", "level"), None, None),
            P(("dom", "level"), None, None, None),
            P(),
            P(),
        ),
        out_specs=(P(("dom", "level"), None, None), P(("dom", "level"), None, None)),
        check_vma=False,
    )
```

time: 2180 us -> 270 us (0.12)
  waiting for transfers between devices: 1890 us -> 37.6 us
  matrix products: 46.9 us -> 1.1 us
  blocking collectives: 0 us -> 28.2 us
  Pallas kernels: 0 us -> 24.9 us
  other arithmetic: 27.3 us -> 4.36 us
  loops' own time: 22.3 us -> 0 us
    psum x16 -> x0, waiting for transfers between devices: 1730 us -> none  [broadcast(): return lax.psum(block, axis)]
    ppermute x32 -> x28, waiting for transfers between devices: 156 us -> 10.9 us  [the longest x7 5.78 us: local(): right = lax.ppermute(sums[0], 'dom', down)]
    dot_general x48 -> x1, matrix products: 46.9 us -> 1.1 us  [local(): jnp.einsum('rkb,rbc->rkc', right_side, diag_inverse, preferred_element_ty...]
    all_to_all x0 -> x1, blocking collectives: none -> 28.2 us  [local(): both = lax.all_to_all(both, 'level', 1, 0, tiled=False)]
    all_gather x0 -> x1, waiting for transfers between devices: none -> 26.3 us  [local(): weights = lax.all_gather(weights, 'level')]
    pallas_call x0 -> x15, Pallas kernels: none -> 24.9 us  [call(): pl.pallas_call(kernel, out_shape=outs, in_specs=[pl.BlockSpec(memory_spac...]
    ppermute x32 -> x28, starting transfers between devices: 154 us -> 131 us  [the longest x7 53.6 us: local(): right = lax.ppermute(own, 'dom', down)]
    another operation x2 -> x0, loops' own time: 22.3 us -> none  [the longest x1 11.3 us: local(): running, solved = lax.fori_loop(0, levels, forward_step, start)]
  transfers between devices with their start and end apart: 48 -> 30, of which waited for: 48 -> 16; matrix products, arithmetic and copies ran while one was open for 0% -> 4% of each run, Pallas kernels for 0% -> 0%
where the time goes in v1:
time: 270 us; the launch traced here: 268 us
  starting transfers between devices  141 us (52%)
  waiting for transfers between devices  37.6 us (14%)
  blocking collectives  28.2 us (10%)
  Pallas kernels  24.9 us (9%)
  between operations  17.3 us (6%)
  local copies, waits for them, and re-layouts  13.3 us (5%)
  other arithmetic  4.36 us (2%)
    ppermute x7, starting transfers between devices, local(): right = lax.ppermute(own, 'dom', down)  53.6 us
    ppermute x7, starting transfers between devices, local(): right = lax.ppermute(sums[0], 'dom', down)  48.6 us
    all_to_all x1, blocking collectives, local(): both = lax.all_to_all(both, 'level', 1, 0, tiled=False)  28.2 us
    all_gather x1, waiting for transfers between devices, local(): weights = lax.all_gather(weights, 'level')  26.3 us
    pallas_call x15, Pallas kernels, call(): pl.pallas_call(kernel, out_shape=outs, in_specs=[pl.BlockSpec(memory_spac...  24.9 us
    ppermute x7, starting transfers between devices, local(): left = lax.ppermute(own, 'dom', up)  15.3 us
    ppermute x7, starting transfers between devices, local(): left = lax.ppermute(sums[2], 'dom', up)  13.4 us
    all_to_all x1, starting transfers between devices, local(): side = lax.all_to_all(side, 'level', 1, 0, tiled=False)  10.2 us
  transfers between devices with their start and end apart: 30, of which 16 were waited for; matrix products, arithmetic and copies ran while one was open for 4% of the time, Pallas kernels for 0%

profile of v1, /device:TPU:1, one launch (start us, length us, event | category | flops | bytes accessed | tf_op | source)
XLA Modules:
  0.0 267.9 jit_solution(12464986056787631362)
XLA Ops:
  7.2 1.9 pad_maximum_fusion
  14.8 10.2 %all-to-all-start = ((bf16[1,4,16,4,128]{4,3,1,0,2:T(4,128)(2,1)}), bf16[1,4,16,4,128]{4,3,1,0,2:T(4,128)(2,1)S(1)}, u32[]{:S(2)}, u32[]{:S(2)}) async-start(bf16[1,4,16,4,128]{4,3,1,0,2:T(4,128)(2,1)} %copy.80), calls=%async_computation | async-start | bytes 131072 | tf_op jit(solution)/shard_map/all_to_all | solution.py:134
  29.6 2.2 copy.86
  33.5 2.4 collective-permute-start
  35.9 11.4 %collective-permute-start.1 = (bf16[32,128]{1,0:T(8,128)(2,1)S(1)}, bf16[32,128]{1,0:T(8,128)(2,1)S(1)}, u32[]{:S(2)}, u32[]{:S(2)}) collective-permute-start(bf16[32,128]{1,0:T(8,128)(2,1)S(1)} %bitcast.97), channel_id=1, source_target_pairs={{16,0},{32,16},{48,32},{64,48},{80,64},{96,80},{112,96},{128,112},... | collective-permute-start | bytes 24584 | tf_op jit(solution)/shard_map/ppermute | solution.py:160
  48.1 26.3 %all-gather.3.cloned.1.call-done = bf16[64,4,128,128]{3,2,1,0:T(8,128)(2,1)} async-done(((bf16[4,4,128,128]{3,2,1,0:T(8,128)(2,1)}), bf16[64,4,128,128]{3,2,1,0:T(8,128)(2,1)}) %all-gather.3.cloned.1.call-update) | async-done | bytes 8388624 | tf_op jit(solution)/shard_map/all_gather | solution.py:125
  74.3 3.4 %copy-done.1 = bf16[64,4,128,128]{3,2,1,0:T(8,128)(2,1)S(1)} copy-done((bf16[64,4,128,128]{3,2,1,0:T(8,128)(2,1)S(1)}, bf16[64,4,128,128]{3,2,1,0:T(8,128)(2,1)}, u32[]{:S(2)}) %copy-start.1) | copy-done | bytes 8388632
  77.7 1.6 shard_map.68.own.solved
  79.3 3.2 %collective-permute-start.2 = (bf16[32,128]{1,0:T(8,128)(2,1)S(1)}, bf16[32,128]{1,0:T(8,128)(2,1)S(1)}, u32[]{:S(2)}, u32[]{:S(2)}) collective-permute-start(bf16[32,128]{1,0:T(8,128)(2,1)S(1)} %shard_map.68.own.solved), channel_id=1, source_target_pairs={{0,16},{16,32},{32,48},{48,64},{64,80},{80,96},{96,112},{112,128},... | collective-permute-start | bytes 24584 | tf_op jit(solution)/shard_map/ppermute | solution.py:159
  82.6 7.5 %collective-permute-start.3 = (bf16[32,128]{1,0:T(8,128)(2,1)S(1)}, bf16[32,128]{1,0:T(8,128)(2,1)S(1)}, u32[]{:S(2)}, u32[]{:S(2)}) collective-permute-start(bf16[32,128]{1,0:T(8,128)(2,1)S(1)} %shard_map.68.own.solved), channel_id=1, source_target_pairs={{16,0},{32,16},{48,32},{64,48},{80,64},{96,80},{112,96},{128,112},... | collective-permute-start | bytes 24584 | tf_op jit(solution)/shard_map/ppermute | solution.py:160
  90.9 1.6 shard_map.69.own.solved
  92.5 1.9 collective-permute-start.4
  94.4 6.9 %collective-permute-start.5 = (bf16[32,128]{1,0:T(8,128)(2,1)S(1)}, bf16[32,128]{1,0:T(8,128)(2,1)S(1)}, u32[]{:S(2)}, u32[]{:S(2)}) collective-permute-start(bf16[32,128]{1,0:T(8,128)(2,1)S(1)} %shard_map.69.own.solved), channel_id=1, source_target_pairs={{16,0},{32,16},{48,32},{64,48},{80,64},{96,80},{112,96},{128,112},... | collective-permute-start | bytes 24584 | tf_op jit(solution)/shard_map/ppermute | solution.py:160
  102.1 1.6 shard_map.70.own.solved
  103.8 1.9 collective-permute-start.6
  105.7 6.9 %collective-permute-start.7 = (bf16[32,128]{1,0:T(8,128)(2,1)S(1)}, bf16[32,128]{1,0:T(8,128)(2,1)S(1)}, u32[]{:S(2)}, u32[]{:S(2)}) collective-permute-start(bf16[32,128]{1,0:T(8,128)(2,1)S(1)} %shard_map.70.own.solved), channel_id=1, source_target_pairs={{16,0},{32,16},{48,32},{64,48},{80,64},{96,80},{112,96},{128,112},... | collective-permute-start | bytes 24584 | tf_op jit(solution)/shard_map/ppermute | solution.py:160
  113.4 1.6 shard_map.71.own.solved
  115.0 1.9 collective-permute-start.8
  116.9 6.9 %collective-permute-start.9 = (bf16[32,128]{1,0:T(8,128)(2,1)S(1)}, bf16[32,128]{1,0:T(8,128)(2,1)S(1)}, u32[]{:S(2)}, u32[]{:S(2)}) collective-permute-start(bf16[32,128]{1,0:T(8,128)(2,1)S(1)} %shard_map.71.own.solved), channel_id=1, source_target_pairs={{16,0},{32,16},{48,32},{64,48},{80,64},{96,80},{112,96},{128,112},... | collective-permute-start | bytes 24584 | tf_op jit(solution)/shard_map/ppermute | solution.py:160
  124.7 1.6 shard_map.72.own.solved
  126.3 1.9 collective-permute-start.10
  128.2 6.9 %collective-permute-start.11 = (bf16[32,128]{1,0:T(8,128)(2,1)S(1)}, bf16[32,128]{1,0:T(8,128)(2,1)S(1)}, u32[]{:S(2)}, u32[]{:S(2)}) collective-permute-start(bf16[32,128]{1,0:T(8,128)(2,1)S(1)} %shard_map.72.own.solved), channel_id=1, source_target_pairs={{16,0},{32,16},{48,32},{64,48},{80,64},{96,80},{112,96},{128,112},... | collective-permute-start | bytes 24584 | tf_op jit(solution)/shard_map/ppermute | solution.py:160
  135.9 1.6 shard_map.73.own.solved
  137.5 1.9 collective-permute-start.12
  139.5 6.9 %collective-permute-start.13 = (bf16[32,128]{1,0:T(8,128)(2,1)S(1)}, bf16[32,128]{1,0:T(8,128)(2,1)S(1)}, u32[]{:S(2)}, u32[]{:S(2)}) collective-permute-start(bf16[32,128]{1,0:T(8,128)(2,1)S(1)} %shard_map.73.own.solved), channel_id=1, source_target_pairs={{16,0},{32,16},{48,32},{64,48},{80,64},{96,80},{112,96},{128,112},... | collective-permute-start | bytes 24584 | tf_op jit(solution)/shard_map/ppermute | solution.py:160
  147.2 1.6 shard_map.74.solved
  148.8 1.8 shard_map.75
  150.7 1.9 collective-permute-start.14
  152.6 6.9 %collective-permute-start.15 = (f32[32,128]{1,0:T(8,128)S(1)}, f32[32,128]{1,0:T(8,128)S(1)}, u32[]{:S(2)}, u32[]{:S(2)}) collective-permute-start(f32[32,128]{1,0:T(8,128)S(1)} %get-tuple-element.32), channel_id=1, source_target_pairs={{16,0},{32,16},{48,32},{64,48},{80,64},{96,80},{112,96},{128,112},... | collective-permute-start | bytes 49160 | tf_op jit(solution)/shard_map/ppermute | solution.py:176
  160.4 1.8 shard_map.76
  162.2 1.9 collective-permute-start.16
  164.1 6.9 %collective-permute-start.17 = (f32[32,128]{1,0:T(8,128)S(1)}, f32[32,128]{1,0:T(8,128)S(1)}, u32[]{:S(2)}, u32[]{:S(2)}) collective-permute-start(f32[32,128]{1,0:T(8,128)S(1)} %get-tuple-element.35), channel_id=1, source_target_pairs={{16,0},{32,16},{48,32},{64,48},{80,64},{96,80},{112,96},{128,112},... | collective-permute-start | bytes 49160 | tf_op jit(solution)/shard_map/ppermute | solution.py:176
  171.9 1.8 shard_map.77
  173.7 1.9 collective-permute-start.18
  175.7 6.9 %collective-permute-start.19 = (f32[32,128]{1,0:T(8,128)S(1)}, f32[32,128]{1,0:T(8,128)S(1)}, u32[]{:S(2)}, u32[]{:S(2)}) collective-permute-start(f32[32,128]{1,0:T(8,128)S(1)} %get-tuple-element.38), channel_id=1, source_target_pairs={{16,0},{32,16},{48,32},{64,48},{80,64},{96,80},{112,96},{128,112},... | collective-permute-start | bytes 49160 | tf_op jit(solution)/shard_map/ppermute | solution.py:176
  183.5 1.8 shard_map.78
  185.3 1.9 collective-permute-start.20
  187.2 6.9 %collective-permute-start.21 = (f32[32,128]{1,0:T(8,128)S(1)}, f32[32,128]{1,0:T(8,128)S(1)}, u32[]{:S(2)}, u32[]{:S(2)}) collective-permute-start(f32[32,128]{1,0:T(8,128)S(1)} %get-tuple-element.41), channel_id=1, source_target_pairs={{16,0},{32,16},{48,32},{64,48},{80,64},{96,80},{112,96},{128,112},... | collective-permute-start | bytes 49160 | tf_op jit(solution)/shard_map/ppermute | solution.py:176
  195.0 1.8 shard_map.79
  196.9 1.9 collective-permute-start.22
  198.8 6.9 %collective-permute-start.23 = (f32[32,128]{1,0:T(8,128)S(1)}, f32[32,128]{1,0:T(8,128)S(1)}, u32[]{:S(2)}, u32[]{:S(2)}) collective-permute-start(f32[32,128]{1,0:T(8,128)S(1)} %get-tuple-element.44), channel_id=1, source_target_pairs={{16,0},{32,16},{48,32},{64,48},{80,64},{96,80},{112,96},{128,112},... | collective-permute-start | bytes 49160 | tf_op jit(solution)/shard_map/ppermute | solution.py:176
  206.6 1.8 shard_map.80
  208.4 1.9 collective-permute-start.24
  210.3 6.9 %collective-permute-start.25 = (f32[32,128]{1,0:T(8,128)S(1)}, f32[32,128]{1,0:T(8,128)S(1)}, u32[]{:S(2)}, u32[]{:S(2)}) collective-permute-start(f32[32,128]{1,0:T(8,128)S(1)} %get-tuple-element.47), channel_id=1, source_target_pairs={{16,0},{32,16},{48,32},{64,48},{80,64},{96,80},{112,96},{128,112},... | collective-permute-start | bytes 49160 | tf_op jit(solution)/shard_map/ppermute | solution.py:176
  218.1 1.8 shard_map.81
  220.0 1.9 collective-permute-start.26
  221.9 6.9 %collective-permute-start.27 = (f32[32,128]{1,0:T(8,128)S(1)}, f32[32,128]{1,0:T(8,128)S(1)}, u32[]{:S(2)}, u32[]{:S(2)}) collective-permute-start(f32[32,128]{1,0:T(8,128)S(1)} %get-tuple-element.50), channel_id=1, source_target_pairs={{16,0},{32,16},{48,32},{64,48},{80,64},{96,80},{112,96},{128,112},... | collective-permute-start | bytes 49160 | tf_op jit(solution)/shard_map/ppermute | solution.py:176
  231.5 28.2 %all_to_all.30 = bf16[1,2,16,4,4,128]{5,4,3,1,0,2:T(4,128)(2,1)S(1)} all-to-all(bf16[1,2,16,4,4,128]{5,4,3,1,0,2:T(4,128)(2,1)S(1)} %bitcast.103), channel_id=1, replica_groups=mesh['dom'=32,'level'=16] {'level'}, dimensions={2} | all-to-all | bytes 262144 | tf_op jit(solution)/shard_map/all_to_all | solution.py:182
  (92 shorter events, 23.5 us)
Async XLA Ops:
  7.2 17.8 %copy-start = (s32[2048,3]{0,1:T(4,128)S(1)}, s32[2048,3]{0,1:T(4,128)}, u32[]{:S(2)}) copy-start(s32[2048,3]{0,1:T(4,128)} %param.8) | copy-start | bytes 73732
  7.2 19.8 %copy-start.2 = (s32[16]{0:T(128)S(1)}, s32[16]{0:T(128)}, u32[]{:S(2)}) copy-start(s32[16]{0:T(128)} %param.9) | copy-start | bytes 196
  7.2 67.1 %all-gather.3.cloned.1.call-start = ((), (), s32[]{:S(2)}) async-start(), calls=%async_computation.2 | async-start | bytes 8912896 | tf_op jit(solution)/shard_map/all_gather | solution.py:125
  14.8 18.0 %all-to-all-start = ((bf16[1,4,16,4,128]{4,3,1,0,2:T(4,128)(2,1)}), bf16[1,4,16,4,128]{4,3,1,0,2:T(4,128)(2,1)S(1)}, u32[]{:S(2)}, u32[]{:S(2)}) async-start(bf16[1,4,16,4,128]{4,3,1,0,2:T(4,128)(2,1)} %copy.80), calls=%async_computation | async-start | bytes 131072 | tf_op jit(solution)/shard_map/all_to_all | solution.py:134
  33.5 14.1 %collective-permute-start = (bf16[32,128]{1,0:T(8,128)(2,1)S(1)}, bf16[32,128]{1,0:T(8,128)(2,1)S(1)}, u32[]{:S(2)}, u32[]{:S(2)}) collective-permute-start(bf16[32,128]{1,0:T(8,128)(2,1)S(1)} %bitcast.96), channel_id=1, source_target_pairs={{0,16},{16,32},{32,48},{48,64},{64,80},{80,96},{96,112},{112,128},... | collective-permute-start | bytes 24584 | tf_op jit(solution)/shard_map/ppermute | solution.py:159
  35.9 12.2 %collective-permute-start.1 = (bf16[32,128]{1,0:T(8,128)(2,1)S(1)}, bf16[32,128]{1,0:T(8,128)(2,1)S(1)}, u32[]{:S(2)}, u32[]{:S(2)}) collective-permute-start(bf16[32,128]{1,0:T(8,128)(2,1)S(1)} %bitcast.97), channel_id=1, source_target_pairs={{16,0},{32,16},{48,32},{64,48},{80,64},{96,80},{112,96},{128,112},... | collective-permute-start | bytes 24584 | tf_op jit(solution)/shard_map/ppermute | solution.py:160
  74.3 3.4 %copy-start.1 = (bf16[64,4,128,128]{3,2,1,0:T(8,128)(2,1)S(1)}, bf16[64,4,128,128]{3,2,1,0:T(8,128)(2,1)}, u32[]{:S(2)}) copy-start(bf16[64,4,128,128]{3,2,1,0:T(8,128)(2,1)} %all-gather.3.cloned.1.call-done) | copy-start | bytes 25165828
  79.3 10.8 %collective-permute-start.2 = (bf16[32,128]{1,0:T(8,128)(2,1)S(1)}, bf16[32,128]{1,0:T(8,128)(2,1)S(1)}, u32[]{:S(2)}, u32[]{:S(2)}) collective-permute-start(bf16[32,128]{1,0:T(8,128)(2,1)S(1)} %shard_map.68.own.solved), channel_id=1, source_target_pairs={{0,16},{16,32},{32,48},{48,64},{64,80},{80,96},{96,112},{112,128},... | collective-permute-start | bytes 24584 | tf_op jit(solution)/shard_map/ppermute | solution.py:159
  82.6 8.3 %collective-permute-start.3 = (bf16[32,128]{1,0:T(8,128)(2,1)S(1)}, bf16[32,128]{1,0:T(8,128)(2,1)S(1)}, u32[]{:S(2)}, u32[]{:S(2)}) collective-permute-start(bf16[32,128]{1,0:T(8,128)(2,1)S(1)} %shard_map.68.own.solved), channel_id=1, source_target_pairs={{16,0},{32,16},{48,32},{64,48},{80,64},{96,80},{112,96},{128,112},... | collective-permute-start | bytes 24584 | tf_op jit(solution)/shard_map/ppermute | solution.py:160
  92.5 8.9 %collective-permute-start.4 = (bf16[32,128]{1,0:T(8,128)(2,1)S(1)}, bf16[32,128]{1,0:T(8,128)(2,1)S(1)}, u32[]{:S(2)}, u32[]{:S(2)}) collective-permute-start(bf16[32,128]{1,0:T(8,128)(2,1)S(1)} %shard_map.69.own.solved), channel_id=1, source_target_pairs={{0,16},{16,32},{32,48},{48,64},{64,80},{80,96},{96,112},{112,128},... | collective-permute-start | bytes 24584 | tf_op jit(solution)/shard_map/ppermute | solution.py:159
  94.4 7.7 %collective-permute-start.5 = (bf16[32,128]{1,0:T(8,128)(2,1)S(1)}, bf16[32,128]{1,0:T(8,128)(2,1)S(1)}, u32[]{:S(2)}, u32[]{:S(2)}) collective-permute-start(bf16[32,128]{1,0:T(8,128)(2,1)S(1)} %shard_map.69.own.solved), channel_id=1, source_target_pairs={{16,0},{32,16},{48,32},{64,48},{80,64},{96,80},{112,96},{128,112},... | collective-permute-start | bytes 24584 | tf_op jit(solution)/shard_map/ppermute | solution.py:160
  103.8 8.9 %collective-permute-start.6 = (bf16[32,128]{1,0:T(8,128)(2,1)S(1)}, bf16[32,128]{1,0:T(8,128)(2,1)S(1)}, u32[]{:S(2)}, u32[]{:S(2)}) collective-permute-start(bf16[32,128]{1,0:T(8,128)(2,1)S(1)} %shard_map.70.own.solved), channel_id=1, source_target_pairs={{0,16},{16,32},{32,48},{48,64},{64,80},{80,96},{96,112},{112,128},... | collective-permute-start | bytes 24584 | tf_op jit(solution)/shard_map/ppermute | solution.py:159
  105.7 7.7 %collective-permute-start.7 = (bf16[32,128]{1,0:T(8,128)(2,1)S(1)}, bf16[32,128]{1,0:T(8,128)(2,1)S(1)}, u32[]{:S(2)}, u32[]{:S(2)}) collective-permute-start(bf16[32,128]{1,0:T(8,128)(2,1)S(1)} %shard_map.70.own.solved), channel_id=1, source_target_pairs={{16,0},{32,16},{48,32},{64,48},{80,64},{96,80},{112,96},{128,112},... | collective-permute-start | bytes 24584 | tf_op jit(solution)/shard_map/ppermute | solution.py:160
  115.0 8.9 %collective-permute-start.8 = (bf16[32,128]{1,0:T(8,128)(2,1)S(1)}, bf16[32,128]{1,0:T(8,128)(2,1)S(1)}, u32[]{:S(2)}, u32[]{:S(2)}) collective-permute-start(bf16[32,128]{1,0:T(8,128)(2,1)S(1)} %shard_map.71.own.solved), channel_id=1, source_target_pairs={{0,16},{16,32},{32,48},{48,64},{64,80},{80,96},{96,112},{112,128},... | collective-permute-start | bytes 24584 | tf_op jit(solution)/shard_map/ppermute | solution.py:159
  116.9 7.7 %collective-permute-start.9 = (bf16[32,128]{1,0:T(8,128)(2,1)S(1)}, bf16[32,128]{1,0:T(8,128)(2,1)S(1)}, u32[]{:S(2)}, u32[]{:S(2)}) collective-permute-start(bf16[32,128]{1,0:T(8,128)(2,1)S(1)} %shard_map.71.own.solved), channel_id=1, source_target_pairs={{16,0},{32,16},{48,32},{64,48},{80,64},{96,80},{112,96},{128,112},... | collective-permute-start | bytes 24584 | tf_op jit(solution)/shard_map/ppermute | solution.py:160
  126.3 8.9 %collective-permute-start.10 = (bf16[32,128]{1,0:T(8,128)(2,1)S(1)}, bf16[32,128]{1,0:T(8,128)(2,1)S(1)}, u32[]{:S(2)}, u32[]{:S(2)}) collective-permute-start(bf16[32,128]{1,0:T(8,128)(2,1)S(1)} %shard_map.72.own.solved), channel_id=1, source_target_pairs={{0,16},{16,32},{32,48},{48,64},{64,80},{80,96},{96,112},{112,128},... | collective-permute-start | bytes 24584 | tf_op jit(solution)/shard_map/ppermute | solution.py:159
  128.2 7.7 %collective-permute-start.11 = (bf16[32,128]{1,0:T(8,128)(2,1)S(1)}, bf16[32,128]{1,0:T(8,128)(2,1)S(1)}, u32[]{:S(2)}, u32[]{:S(2)}) collective-permute-start(bf16[32,128]{1,0:T(8,128)(2,1)S(1)} %shard_map.72.own.solved), channel_id=1, source_target_pairs={{16,0},{32,16},{48,32},{64,48},{80,64},{96,80},{112,96},{128,112},... | collective-permute-start | bytes 24584 | tf_op jit(solution)/shard_map/ppermute | solution.py:160
  137.5 8.9 %collective-permute-start.12 = (bf16[32,128]{1,0:T(8,128)(2,1)S(1)}, bf16[32,128]{1,0:T(8,128)(2,1)S(1)}, u32[]{:S(2)}, u32[]{:S(2)}) collective-permute-start(bf16[32,128]{1,0:T(8,128)(2,1)S(1)} %shard_map.73.own.solved), channel_id=1, source_target_pairs={{0,16},{16,32},{32,48},{48,64},{64,80},{80,96},{96,112},{112,128},... | collective-permute-start | bytes 24584 | tf_op jit(solution)/shard_map/ppermute | solution.py:159
  139.5 7.7 %collective-permute-start.13 = (bf16[32,128]{1,0:T(8,128)(2,1)S(1)}, bf16[32,128]{1,0:T(8,128)(2,1)S(1)}, u32[]{:S(2)}, u32[]{:S(2)}) collective-permute-start(bf16[32,128]{1,0:T(8,128)(2,1)S(1)} %shard_map.73.own.solved), channel_id=1, source_target_pairs={{16,0},{32,16},{48,32},{64,48},{80,64},{96,80},{112,96},{128,112},... | collective-permute-start | bytes 24584 | tf_op jit(solution)/shard_map/ppermute | solution.py:160
  150.7 8.9 %collective-permute-start.14 = (f32[32,128]{1,0:T(8,128)S(1)}, f32[32,128]{1,0:T(8,128)S(1)}, u32[]{:S(2)}, u32[]{:S(2)}) collective-permute-start(f32[32,128]{1,0:T(8,128)S(1)} %get-tuple-element.30), channel_id=1, source_target_pairs={{0,16},{16,32},{32,48},{48,64},{64,80},{80,96},{96,112},{112,128},... | collective-permute-start | bytes 49160 | tf_op jit(solution)/shard_map/ppermute | solution.py:177
  152.6 7.8 %collective-permute-start.15 = (f32[32,128]{1,0:T(8,128)S(1)}, f32[32,128]{1,0:T(8,128)S(1)}, u32[]{:S(2)}, u32[]{:S(2)}) collective-permute-start(f32[32,128]{1,0:T(8,128)S(1)} %get-tuple-element.32), channel_id=1, source_target_pairs={{16,0},{32,16},{48,32},{64,48},{80,64},{96,80},{112,96},{128,112},... | collective-permute-start | bytes 49160 | tf_op jit(solution)/shard_map/ppermute | solution.py:176
  162.2 8.9 %collective-permute-start.16 = (f32[32,128]{1,0:T(8,128)S(1)}, f32[32,128]{1,0:T(8,128)S(1)}, u32[]{:S(2)}, u32[]{:S(2)}) collective-permute-start(f32[32,128]{1,0:T(8,128)S(1)} %get-tuple-element.33), channel_id=1, source_target_pairs={{0,16},{16,32},{32,48},{48,64},{64,80},{80,96},{96,112},{112,128},... | collective-permute-start | bytes 49160 | tf_op jit(solution)/shard_map/ppermute | solution.py:177
  164.1 7.8 %collective-permute-start.17 = (f32[32,128]{1,0:T(8,128)S(1)}, f32[32,128]{1,0:T(8,128)S(1)}, u32[]{:S(2)}, u32[]{:S(2)}) collective-permute-start(f32[32,128]{1,0:T(8,128)S(1)} %get-tuple-element.35), channel_id=1, source_target_pairs={{16,0},{32,16},{48,32},{64,48},{80,64},{96,80},{112,96},{128,112},... | collective-permute-start | bytes 49160 | tf_op jit(solution)/shard_map/ppermute | solution.py:176
  173.7 8.9 %collective-permute-start.18 = (f32[32,128]{1,0:T(8,128)S(1)}, f32[32,128]{1,0:T(8,128)S(1)}, u32[]{:S(2)}, u32[]{:S(2)}) collective-permute-start(f32[32,128]{1,0:T(8,128)S(1)} %get-tuple-element.36), channel_id=1, source_target_pairs={{0,16},{16,32},{32,48},{48,64},{64,80},{80,96},{96,112},{112,128},... | collective-permute-start | bytes 49160 | tf_op jit(solution)/shard_map/ppermute | solution.py:177
  175.7 7.8 %collective-permute-start.19 = (f32[32,128]{1,0:T(8,128)S(1)}, f32[32,128]{1,0:T(8,128)S(1)}, u32[]{:S(2)}, u32[]{:S(2)}) collective-permute-start(f32[32,128]{1,0:T(8,128)S(1)} %get-tuple-element.38), channel_id=1, source_target_pairs={{16,0},{32,16},{48,32},{64,48},{80,64},{96,80},{112,96},{128,112},... | collective-permute-start | bytes 49160 | tf_op jit(solution)/shard_map/ppermute | solution.py:176
  185.3 8.9 %collective-permute-start.20 = (f32[32,128]{1,0:T(8,128)S(1)}, f32[32,128]{1,0:T(8,128)S(1)}, u32[]{:S(2)}, u32[]{:S(2)}) collective-permute-start(f32[32,128]{1,0:T(8,128)S(1)} %get-tuple-element.39), channel_id=1, source_target_pairs={{0,16},{16,32},{32,48},{48,64},{64,80},{80,96},{96,112},{112,128},... | collective-permute-start | bytes 49160 | tf_op jit(solution)/shard_map/ppermute | solution.py:177
  187.2 7.8 %collective-permute-start.21 = (f32[32,128]{1,0:T(8,128)S(1)}, f32[32,128]{1,0:T(8,128)S(1)}, u32[]{:S(2)}, u32[]{:S(2)}) collective-permute-start(f32[32,128]{1,0:T(8,128)S(1)} %get-tuple-element.41), channel_id=1, source_target_pairs={{16,0},{32,16},{48,32},{64,48},{80,64},{96,80},{112,96},{128,112},... | collective-permute-start | bytes 49160 | tf_op jit(solution)/shard_map/ppermute | solution.py:176
  196.9 8.9 %collective-permute-start.22 = (f32[32,128]{1,0:T(8,128)S(1)}, f32[32,128]{1,0:T(8,128)S(1)}, u32[]{:S(2)}, u32[]{:S(2)}) collective-permute-start(f32[32,128]{1,0:T(8,128)S(1)} %get-tuple-element.42), channel_id=1, source_target_pairs={{0,16},{16,32},{32,48},{48,64},{64,80},{80,96},{96,112},{112,128},... | collective-permute-start | bytes 49160 | tf_op jit(solution)/shard_map/ppermute | solution.py:177
  198.8 7.8 %collective-permute-start.23 = (f32[32,128]{1,0:T(8,128)S(1)}, f32[32,128]{1,0:T(8,128)S(1)}, u32[]{:S(2)}, u32[]{:S(2)}) collective-permute-start(f32[32,128]{1,0:T(8,128)S(1)} %get-tuple-element.44), channel_id=1, source_target_pairs={{16,0},{32,16},{48,32},{64,48},{80,64},{96,80},{112,96},{128,112},... | collective-permute-start | bytes 49160 | tf_op jit(solution)/shard_map/ppermute | solution.py:176
  208.4 8.9 %collective-permute-start.24 = (f32[32,128]{1,0:T(8,128)S(1)}, f32[32,128]{1,0:T(8,128)S(1)}, u32[]{:S(2)}, u32[]{:S(2)}) collective-permute-start(f32[32,128]{1,0:T(8,128)S(1)} %get-tuple-element.45), channel_id=1, source_target_pairs={{0,16},{16,32},{32,48},{48,64},{64,80},{80,96},{96,112},{112,128},... | collective-permute-start | bytes 49160 | tf_op jit(solution)/shard_map/ppermute | solution.py:177
  210.3 7.8 %collective-permute-start.25 = (f32[32,128]{1,0:T(8,128)S(1)}, f32[32,128]{1,0:T(8,128)S(1)}, u32[]{:S(2)}, u32[]{:S(2)}) collective-permute-start(f32[32,128]{1,0:T(8,128)S(1)} %get-tuple-element.47), channel_id=1, source_target_pairs={{16,0},{32,16},{48,32},{64,48},{80,64},{96,80},{112,96},{128,112},... | collective-permute-start | bytes 49160 | tf_op jit(solution)/shard_map/ppermute | solution.py:176
  220.0 8.9 %collective-permute-start.26 = (f32[32,128]{1,0:T(8,128)S(1)}, f32[32,128]{1,0:T(8,128)S(1)}, u32[]{:S(2)}, u32[]{:S(2)}) collective-permute-start(f32[32,128]{1,0:T(8,128)S(1)} %get-tuple-element.48), channel_id=1, source_target_pairs={{0,16},{16,32},{32,48},{48,64},{64,80},{80,96},{96,112},{112,128},... | collective-permute-start | bytes 49160 | tf_op jit(solution)/shard_map/ppermute | solution.py:177
  221.9 7.8 %collective-permute-start.27 = (f32[32,128]{1,0:T(8,128)S(1)}, f32[32,128]{1,0:T(8,128)S(1)}, u32[]{:S(2)}, u32[]{:S(2)}) collective-permute-start(f32[32,128]{1,0:T(8,128)S(1)} %get-tuple-element.50), channel_id=1, source_target_pairs={{16,0},{32,16},{48,32},{64,48},{80,64},{96,80},{112,96},{128,112},... | collective-permute-start | bytes 49160 | tf_op jit(solution)/shard_map/ppermute | solution.py:176
Sparse Core Ops, SparseCore 0:
  10.1 64.1 all-gather.2

commit v2 on v1

v2 whole, which is shorter than its diff:
```python
import functools

import jax
import jax.numpy as jnp
from jax import lax
from jax.experimental import pallas as pl
from jax.experimental.pallas import tpu as pltpu
from jax.sharding import PartitionSpec as P

BF16 = jnp.bfloat16
F32 = jnp.float32


def dot(a, b):
    return lax.dot_general(a, b, (((1,), (0,)), ((), ())), preferred_element_type=F32)


def dot_t(a, b):
    return lax.dot_general(a, b, (((1,), (1,)), ((), ())), preferred_element_type=F32)


def either(low, high, share):
    top = lax.broadcasted_iota(jnp.int32, low.shape, 0) < share
    return jnp.where(top, low, high)


def forward_kernel(level, share, owners, weights, pick, side, far, own, near, out):
    rows = weights.shape[1]
    count = 2 * rows
    span = count * share
    around = jnp.concatenate([far[...], own[...], near[...]], axis=0)
    picked = dot(pick[level], around)
    for pair in range(count // 2):
        half, row = divmod(2 * pair, rows)
        owner = owners[2 * level + half]
        at = 2 * share * pair
        terms = [picked[n * span + at : n * span + at + 2 * share] for n in range(3)]
        terms = jnp.concatenate(terms, axis=1).astype(BF16)
        blocks = [weights[owner, row + one, 1:].reshape(-1, terms.shape[1] // 3) for one in range(2)]
        total = either(*[dot(terms, block) for block in blocks], share)
        shifted = (side[level, at : at + 2 * share].astype(F32) - total).astype(BF16)
        solved = either(*[dot(shifted, weights[owner, row + one, 0]) for one in range(2)], share)
        out[at : at + 2 * share] = solved.astype(BF16)


def backward_kernel(
    level, share, last, owners, weights, spread, solved, far, own, near, result, *outs
):
    rows = weights.shape[1]
    count = 2 * rows
    folded = (far[...] + own[...] + near[...]).astype(BF16)
    pushes = [[], [], []]
    for pair in range(count // 2):
        half, row = divmod(2 * pair, rows)
        owner = owners[2 * level + half]
        at = 2 * share * pair
        part = folded[at : at + 2 * share]
        part = either(*[dot(part, weights[owner, row + one, 0]) for one in range(2)], share)
        done = (solved[at : at + 2 * share].astype(F32) - part).astype(BF16)
        result[at : at + 2 * share] = done
        if not last:
            for n in range(3):
                pushes[n].append(
                    either(*[dot_t(done, weights[owner, row + one, 1 + n]) for one in range(2)], share)
                )
    if not last:
        pushed = jnp.concatenate(pushes[0] + pushes[1] + pushes[2], axis=0).astype(BF16)
        total = dot(spread[level], pushed)
        span = count * share
        for n in range(3):
            outs[n][...] = total[n * span : (n + 1) * span]


def call(kernel, outs, owners, *rest):
    vmem = pl.BlockSpec(memory_space=pltpu.VMEM)
    return pl.pallas_call(
        kernel,
        out_shape=outs,
        in_specs=[pl.BlockSpec(memory_space=pltpu.SMEM)] + [vmem] * len(rest),
        out_specs=[vmem] * len(outs),
        compiler_params=pltpu.CompilerParams(vmem_limit_bytes=32 * 2**20),
    )(owners, *rest)


def local(right_side, diag_inverse, off_blocks, columns, plan):
    rows, depth, width = right_side.shape
    doms = lax.axis_size("dom")
    levs = lax.axis_size("level")
    levels = levs // 2
    share = depth // levs
    count = 2 * rows
    dom = lax.axis_index("dom")
    lev = lax.axis_index("level")
    near_pairs = [(i, i ^ 1) for i in range(doms)]
    far_pairs = [(i, ((i + 1) ^ 1) - 1) for i in range(1, doms - 1)] + [(0, doms - 1), (doms - 1, 0)]

    weights = jnp.concatenate([diag_inverse[:, None], off_blocks], axis=1)
    weights = lax.all_gather(weights, "level")

    ids = jnp.arange(levs, dtype=jnp.int32)
    own_level = jnp.sum(jnp.where(ids == lev, plan, 0)) // 2
    inverse = jnp.sum(jnp.where(plan[None, :] == ids[:, None], ids[None, :], 0), axis=1)

    first = jnp.einsum("rkb,rbc->rkc", right_side, diag_inverse, preferred_element_type=F32)
    side = jnp.where(own_level == 0, first.astype(BF16), right_side)
    side = side.reshape(rows, levs, share, width)
    side = lax.all_to_all(side, "level", 1, 0, tiled=False)
    side = side.reshape(levs, rows * share, width)[inverse].reshape(levels, count * share, width)

    part = lax.dynamic_slice_in_dim(columns, dom * levs * rows, levs * rows, 0)
    part = part.reshape(levs, rows * 3)[inverse].reshape(levels, count, 3)
    source = plan[(part // rows) % levs] % 2 * rows + part % rows
    j = jnp.arange(count, dtype=jnp.int32)
    meets = source[:, :, :, None] == j
    eye_n = jnp.eye(3, dtype=bool)
    eye_n = jnp.where(dom % 2 == 0, eye_n, eye_n[::-1])
    eye_k = jnp.eye(share, dtype=bool)
    pick = (
        meets.transpose(0, 2, 1, 3)[:, :, :, None, None, :, None]
        & eye_n[None, :, None, None, :, None, None]
        & eye_k[None, None, None, :, None, None, :]
    )
    size = 3 * count * share
    pick = pick.reshape(levels, size, size).astype(BF16)
    spread = pick.transpose(0, 2, 1)

    vector = jax.ShapeDtypeStruct((count * share, width), BF16)
    summed = jax.ShapeDtypeStruct((count * share, width), F32)

    solved = [side[0]]
    for level in range(1, levels):
        own = solved[-1]
        far = lax.ppermute(own, "dom", far_pairs)
        near = lax.ppermute(own, "dom", near_pairs)
        kernel = functools.partial(forward_kernel, level, share)
        solved += call(kernel, [vector], inverse, weights, pick, side, far, own, near)

    zero = jnp.zeros(summed.shape, F32)
    far, own, near = zero, zero, zero
    results = []
    for level in range(levels - 1, -1, -1):
        last = level == 0
        kernel = functools.partial(backward_kernel, level, share, last)
        outs = [vector] if last else [vector, summed, summed, summed]
        result, *sums = call(
            kernel, outs, inverse, weights, spread, solved[level], far, own, near
        )
        results.append(result)
        if not last:
            far = lax.ppermute(sums[0], "dom", far_pairs)
            near = lax.ppermute(sums[2], "dom", near_pairs)
            own = sums[1]

    both = jnp.stack([jnp.stack(solved), jnp.stack(results[::-1])])
    both = both.reshape(2, levs, rows, share, width)[:, plan]
    both = lax.all_to_all(both, "level", 1, 0, tiled=False)
    both = both.transpose(1, 2, 0, 3, 4).reshape(2, rows, depth, width)
    return both[0], both[1]


def solution(mesh):
    return jax.shard_map(
        local,
        mesh=mesh,
        in_specs=(
            P(("dom", "level"), None, None),
            P(("dom", "level"), None, None),
            P(("dom", "level"), None, None, None),
            P(),
            P(),
        ),
        out_specs=(P(("dom", "level"), None, None), P(("dom", "level"), None, None)),
        check_vma=False,
    )
```

time: 270 us -> 260 us (0.963)
  starting transfers between devices: 141 us -> 109 us
  waiting for transfers between devices: 37.6 us -> 61.1 us
  Pallas kernels: 24.9 us -> 21.3 us
  blocking collectives: 28.2 us -> 31.1 us
    ppermute x28, starting transfers between devices: 131 us -> 99.1 us  [the longest x7 41.1 us: local(): far = lax.ppermute(own, 'dom', far_pairs)]
    ppermute x28, waiting for transfers between devices: 10.9 us -> 36.5 us  [the longest x7 10.5 us: local(): far = lax.ppermute(sums[0], 'dom', far_pairs)]
    pallas_call x15, Pallas kernels: 24.9 us -> 21.3 us  [call(): pl.pallas_call(kernel, out_shape=outs, in_specs=[pl.BlockSpec(memory_spac...]
    all_to_all x1, blocking collectives: 28.2 us -> 31.1 us  [local(): both = lax.all_to_all(both, 'level', 1, 0, tiled=False)]
  transfers between devices with their start and end apart: 30 -> 30, of which waited for: 16 -> 23; matrix products, arithmetic and copies ran while one was open for 4% -> 4% of each run, Pallas kernels for 0% -> 0%
where the time goes in v2:
time: 260 us; the launch traced here: 259 us
  starting transfers between devices  109 us (42%)
  waiting for transfers between devices  61.1 us (24%)
  blocking collectives  31.1 us (12%)
  Pallas kernels  21.3 us (8%)
  between operations  17.1 us (7%)
  local copies, waits for them, and re-layouts  13.3 us (5%)
  other arithmetic  4.36 us (2%)
    ppermute x7, starting transfers between devices, local(): far = lax.ppermute(own, 'dom', far_pairs)  41.1 us
    ppermute x7, starting transfers between devices, local(): far = lax.ppermute(sums[0], 'dom', far_pairs)  31.1 us
    all_to_all x1, blocking collectives, local(): both = lax.all_to_all(both, 'level', 1, 0, tiled=False)  31.1 us
    all_gather x1, waiting for transfers between devices, local(): weights = lax.all_gather(weights, 'level')  24.2 us
    pallas_call x15, Pallas kernels, call(): pl.pallas_call(kernel, out_shape=outs, in_specs=[pl.BlockSpec(memory_spac...  21.3 us
    ppermute x7, starting transfers between devices, local(): near = lax.ppermute(own, 'dom', near_pairs)  13.4 us
    ppermute x7, starting transfers between devices, local(): near = lax.ppermute(sums[2], 'dom', near_pairs)  13.4 us
    ppermute x7, waiting for transfers between devices, local(): far = lax.ppermute(sums[0], 'dom', far_pairs)  10.5 us
  transfers between devices with their start and end apart: 30, of which 23 were waited for; matrix products, arithmetic and copies ran while one was open for 4% of the time, Pallas kernels for 0%

profile of v2, /device:TPU:1, one launch (start us, length us, event | category | flops | bytes accessed | tf_op | source)
XLA Modules:
  0.0 258.7 jit_solution(10604256477036136090)
XLA Ops:
  7.2 1.9 pad_maximum_fusion
  14.8 10.2 %all-to-all-start = ((bf16[1,4,16,4,128]{4,3,1,0,2:T(4,128)(2,1)}), bf16[1,4,16,4,128]{4,3,1,0,2:T(4,128)(2,1)S(1)}, u32[]{:S(2)}, u32[]{:S(2)}) async-start(bf16[1,4,16,4,128]{4,3,1,0,2:T(4,128)(2,1)} %copy.80), calls=%async_computation | async-start | bytes 131072 | tf_op jit(solution)/shard_map/all_to_all | solution.py:107
  29.6 2.2 copy.86
  33.5 11.9 %collective-permute-start = (bf16[32,128]{1,0:T(8,128)(2,1)S(1)}, bf16[32,128]{1,0:T(8,128)(2,1)S(1)}, u32[]{:S(2)}, u32[]{:S(2)}) collective-permute-start(bf16[32,128]{1,0:T(8,128)(2,1)S(1)} %bitcast.96), channel_id=1, source_target_pairs={{16,32},{32,16},{48,64},{64,48},{80,96},{96,80},{112,128},{128,112... | collective-permute-start | bytes 24584 | tf_op jit(solution)/shard_map/ppermute | solution.py:133
  45.4 1.9 collective-permute-start.1
  47.5 2.6 %collective-permute-done.1.near = bf16[32,128]{1,0:T(8,128)(2,1)S(1)} collective-permute-done((bf16[32,128]{1,0:T(8,128)(2,1)S(1)}, bf16[32,128]{1,0:T(8,128)(2,1)S(1)}, u32[]{:S(2)}, u32[]{:S(2)}) %collective-permute-start.1) | collective-permute-done | bytes 8224 | tf_op jit(solution)/shard_map/ppermute | solution.py:134
  50.2 24.2 %all-gather.3.cloned.1.call-done = bf16[64,4,128,128]{3,2,1,0:T(8,128)(2,1)} async-done(((bf16[4,4,128,128]{3,2,1,0:T(8,128)(2,1)}), bf16[64,4,128,128]{3,2,1,0:T(8,128)(2,1)}) %all-gather.3.cloned.1.call-update) | async-done | bytes 8388624 | tf_op jit(solution)/shard_map/all_gather | solution.py:98
  74.4 3.4 %copy-done.1 = bf16[64,4,128,128]{3,2,1,0:T(8,128)(2,1)S(1)} copy-done((bf16[64,4,128,128]{3,2,1,0:T(8,128)(2,1)S(1)}, bf16[64,4,128,128]{3,2,1,0:T(8,128)(2,1)}, u32[]{:S(2)}) %copy-start.1) | copy-done | bytes 8388632
  79.1 8.8 %collective-permute-start.2 = (bf16[32,128]{1,0:T(8,128)(2,1)S(1)}, bf16[32,128]{1,0:T(8,128)(2,1)S(1)}, u32[]{:S(2)}, u32[]{:S(2)}) collective-permute-start(bf16[32,128]{1,0:T(8,128)(2,1)S(1)} %shard_map.68.own.solved), channel_id=1, source_target_pairs={{16,32},{32,16},{48,64},{64,48},{80,96},{96,80},{112,128},{128,112... | collective-permute-start | bytes 24584 | tf_op jit(solution)/shard_map/ppermute | solution.py:133
  87.9 1.9 collective-permute-start.3
  89.9 2.5 collective-permute-done.3.near
  93.7 3.3 %collective-permute-start.4 = (bf16[32,128]{1,0:T(8,128)(2,1)S(1)}, bf16[32,128]{1,0:T(8,128)(2,1)S(1)}, u32[]{:S(2)}, u32[]{:S(2)}) collective-permute-start(bf16[32,128]{1,0:T(8,128)(2,1)S(1)} %shard_map.69.own.solved), channel_id=1, source_target_pairs={{16,32},{32,16},{48,64},{64,48},{80,96},{96,80},{112,128},{128,112... | collective-permute-start | bytes 24584 | tf_op jit(solution)/shard_map/ppermute | solution.py:133
  97.0 1.9 collective-permute-start.5
  98.9 2.5 collective-permute-done.4.far
  102.8 5.5 %collective-permute-start.6 = (bf16[32,128]{1,0:T(8,128)(2,1)S(1)}, bf16[32,128]{1,0:T(8,128)(2,1)S(1)}, u32[]{:S(2)}, u32[]{:S(2)}) collective-permute-start(bf16[32,128]{1,0:T(8,128)(2,1)S(1)} %shard_map.70.own.solved), channel_id=1, source_target_pairs={{16,32},{32,16},{48,64},{64,48},{80,96},{96,80},{112,128},{128,112... | collective-permute-start | bytes 24584 | tf_op jit(solution)/shard_map/ppermute | solution.py:133
  108.3 1.9 collective-permute-start.7
  110.5 2.5 collective-permute-done.7.near
  114.3 3.0 %collective-permute-start.8 = (bf16[32,128]{1,0:T(8,128)(2,1)S(1)}, bf16[32,128]{1,0:T(8,128)(2,1)S(1)}, u32[]{:S(2)}, u32[]{:S(2)}) collective-permute-start(bf16[32,128]{1,0:T(8,128)(2,1)S(1)} %shard_map.71.own.solved), channel_id=1, source_target_pairs={{16,32},{32,16},{48,64},{64,48},{80,96},{96,80},{112,128},{128,112... | collective-permute-start | bytes 24584 | tf_op jit(solution)/shard_map/ppermute | solution.py:133
  117.4 1.9 collective-permute-start.9
  119.3 2.8 %collective-permute-done.8.far = bf16[32,128]{1,0:T(8,128)(2,1)S(1)} collective-permute-done((bf16[32,128]{1,0:T(8,128)(2,1)S(1)}, bf16[32,128]{1,0:T(8,128)(2,1)S(1)}, u32[]{:S(2)}, u32[]{:S(2)}) %collective-permute-start.8) | collective-permute-done | bytes 8224 | tf_op jit(solution)/shard_map/ppermute | solution.py:133
  123.4 5.3 %collective-permute-start.10 = (bf16[32,128]{1,0:T(8,128)(2,1)S(1)}, bf16[32,128]{1,0:T(8,128)(2,1)S(1)}, u32[]{:S(2)}, u32[]{:S(2)}) collective-permute-start(bf16[32,128]{1,0:T(8,128)(2,1)S(1)} %shard_map.72.own.solved), channel_id=1, source_target_pairs={{16,32},{32,16},{48,64},{64,48},{80,96},{96,80},{112,128},{128,112... | collective-permute-start | bytes 24584 | tf_op jit(solution)/shard_map/ppermute | solution.py:133
  128.7 1.9 collective-permute-start.11
  131.1 2.0 collective-permute-done.11.near
  134.5 3.3 %collective-permute-start.12 = (bf16[32,128]{1,0:T(8,128)(2,1)S(1)}, bf16[32,128]{1,0:T(8,128)(2,1)S(1)}, u32[]{:S(2)}, u32[]{:S(2)}) collective-permute-start(bf16[32,128]{1,0:T(8,128)(2,1)S(1)} %shard_map.73.own.solved), channel_id=1, source_target_pairs={{16,32},{32,16},{48,64},{64,48},{80,96},{96,80},{112,128},{128,112... | collective-permute-start | bytes 24584 | tf_op jit(solution)/shard_map/ppermute | solution.py:133
  137.8 1.9 collective-permute-start.13
  139.7 2.5 collective-permute-done.12.far
  145.1 5.3 %collective-permute-start.14 = (f32[32,128]{1,0:T(8,128)S(1)}, f32[32,128]{1,0:T(8,128)S(1)}, u32[]{:S(2)}, u32[]{:S(2)}) collective-permute-start(f32[32,128]{1,0:T(8,128)S(1)} %get-tuple-element.30), channel_id=1, source_target_pairs={{16,32},{32,16},{48,64},{64,48},{80,96},{96,80},{112,128},{128,112... | collective-permute-start | bytes 49160 | tf_op jit(solution)/shard_map/ppermute | solution.py:150
  150.5 1.9 collective-permute-start.15
  153.0 2.0 collective-permute-done.15.near
  156.5 3.3 %collective-permute-start.16 = (f32[32,128]{1,0:T(8,128)S(1)}, f32[32,128]{1,0:T(8,128)S(1)}, u32[]{:S(2)}, u32[]{:S(2)}) collective-permute-start(f32[32,128]{1,0:T(8,128)S(1)} %get-tuple-element.33), channel_id=1, source_target_pairs={{16,32},{32,16},{48,64},{64,48},{80,96},{96,80},{112,128},{128,112... | collective-permute-start | bytes 49160 | tf_op jit(solution)/shard_map/ppermute | solution.py:150
  159.9 1.9 collective-permute-start.17
  161.8 2.5 collective-permute-done.16.far
  165.9 5.3 %collective-permute-start.18 = (f32[32,128]{1,0:T(8,128)S(1)}, f32[32,128]{1,0:T(8,128)S(1)}, u32[]{:S(2)}, u32[]{:S(2)}) collective-permute-start(f32[32,128]{1,0:T(8,128)S(1)} %get-tuple-element.36), channel_id=1, source_target_pairs={{16,32},{32,16},{48,64},{64,48},{80,96},{96,80},{112,128},{128,112... | collective-permute-start | bytes 49160 | tf_op jit(solution)/shard_map/ppermute | solution.py:150
  171.2 1.9 collective-permute-start.19
  173.7 2.0 collective-permute-done.19.near
  177.3 3.3 %collective-permute-start.20 = (f32[32,128]{1,0:T(8,128)S(1)}, f32[32,128]{1,0:T(8,128)S(1)}, u32[]{:S(2)}, u32[]{:S(2)}) collective-permute-start(f32[32,128]{1,0:T(8,128)S(1)} %get-tuple-element.39), channel_id=1, source_target_pairs={{16,32},{32,16},{48,64},{64,48},{80,96},{96,80},{112,128},{128,112... | collective-permute-start | bytes 49160 | tf_op jit(solution)/shard_map/ppermute | solution.py:150
  180.6 1.9 collective-permute-start.21
  182.6 3.0 %collective-permute-done.20.far = f32[32,128]{1,0:T(8,128)S(1)} collective-permute-done((f32[32,128]{1,0:T(8,128)S(1)}, f32[32,128]{1,0:T(8,128)S(1)}, u32[]{:S(2)}, u32[]{:S(2)}) %collective-permute-start.20) | collective-permute-done | bytes 16416 | tf_op jit(solution)/shard_map/ppermute | solution.py:150
  187.1 5.2 %collective-permute-start.22 = (f32[32,128]{1,0:T(8,128)S(1)}, f32[32,128]{1,0:T(8,128)S(1)}, u32[]{:S(2)}, u32[]{:S(2)}) collective-permute-start(f32[32,128]{1,0:T(8,128)S(1)} %get-tuple-element.42), channel_id=1, source_target_pairs={{16,32},{32,16},{48,64},{64,48},{80,96},{96,80},{112,128},{128,112... | collective-permute-start | bytes 49160 | tf_op jit(solution)/shard_map/ppermute | solution.py:150
  192.3 1.9 collective-permute-start.23
  194.9 2.1 collective-permute-done.23.near
  198.6 3.5 %collective-permute-start.24 = (f32[32,128]{1,0:T(8,128)S(1)}, f32[32,128]{1,0:T(8,128)S(1)}, u32[]{:S(2)}, u32[]{:S(2)}) collective-permute-start(f32[32,128]{1,0:T(8,128)S(1)} %get-tuple-element.45), channel_id=1, source_target_pairs={{16,32},{32,16},{48,64},{64,48},{80,96},{96,80},{112,128},{128,112... | collective-permute-start | bytes 49160 | tf_op jit(solution)/shard_map/ppermute | solution.py:150
  202.1 1.9 collective-permute-start.25
  204.1 2.4 collective-permute-done.24.far
  208.2 5.2 %collective-permute-start.26 = (f32[32,128]{1,0:T(8,128)S(1)}, f32[32,128]{1,0:T(8,128)S(1)}, u32[]{:S(2)}, u32[]{:S(2)}) collective-permute-start(f32[32,128]{1,0:T(8,128)S(1)} %get-tuple-element.48), channel_id=1, source_target_pairs={{16,32},{32,16},{48,64},{64,48},{80,96},{96,80},{112,128},{128,112... | collective-permute-start | bytes 49160 | tf_op jit(solution)/shard_map/ppermute | solution.py:150
  213.4 1.9 collective-permute-start.27
  216.0 1.8 collective-permute-done.27.near
  219.4 31.1 %all_to_all.30 = bf16[1,2,16,4,4,128]{5,4,3,1,0,2:T(4,128)(2,1)S(1)} all-to-all(bf16[1,2,16,4,4,128]{5,4,3,1,0,2:T(4,128)(2,1)S(1)} %bitcast.103), channel_id=1, replica_groups=mesh['dom'=32,'level'=16] {'level'}, dimensions={2} | all-to-all | bytes 262144 | tf_op jit(solution)/shard_map/all_to_all | solution.py:156
  (94 shorter events, 36.5 us)
Async XLA Ops:
  7.2 17.8 %copy-start = (s32[2048,3]{0,1:T(4,128)S(1)}, s32[2048,3]{0,1:T(4,128)}, u32[]{:S(2)}) copy-start(s32[2048,3]{0,1:T(4,128)} %param.8) | copy-start | bytes 73732
  7.2 19.8 %copy-start.2 = (s32[16]{0:T(128)S(1)}, s32[16]{0:T(128)}, u32[]{:S(2)}) copy-start(s32[16]{0:T(128)} %param.9) | copy-start | bytes 196
  7.2 67.2 %all-gather.3.cloned.1.call-start = ((), (), s32[]{:S(2)}) async-start(), calls=%async_computation.2 | async-start | bytes 8912896 | tf_op jit(solution)/shard_map/all_gather | solution.py:98
  14.8 18.0 %all-to-all-start = ((bf16[1,4,16,4,128]{4,3,1,0,2:T(4,128)(2,1)}), bf16[1,4,16,4,128]{4,3,1,0,2:T(4,128)(2,1)S(1)}, u32[]{:S(2)}, u32[]{:S(2)}) async-start(bf16[1,4,16,4,128]{4,3,1,0,2:T(4,128)(2,1)} %copy.80), calls=%async_computation | async-start | bytes 131072 | tf_op jit(solution)/shard_map/all_to_all | solution.py:107
  33.5 14.1 %collective-permute-start = (bf16[32,128]{1,0:T(8,128)(2,1)S(1)}, bf16[32,128]{1,0:T(8,128)(2,1)S(1)}, u32[]{:S(2)}, u32[]{:S(2)}) collective-permute-start(bf16[32,128]{1,0:T(8,128)(2,1)S(1)} %bitcast.96), channel_id=1, source_target_pairs={{16,32},{32,16},{48,64},{64,48},{80,96},{96,80},{112,128},{128,112... | collective-permute-start | bytes 24584 | tf_op jit(solution)/shard_map/ppermute | solution.py:133
  45.4 4.8 %collective-permute-start.1 = (bf16[32,128]{1,0:T(8,128)(2,1)S(1)}, bf16[32,128]{1,0:T(8,128)(2,1)S(1)}, u32[]{:S(2)}, u32[]{:S(2)}) collective-permute-start(bf16[32,128]{1,0:T(8,128)(2,1)S(1)} %bitcast.97), channel_id=1, source_target_pairs={{0,16},{16,0},{32,48},{48,32},{64,80},{80,64},{96,112},{112,96},{1... | collective-permute-start | bytes 24584 | tf_op jit(solution)/shard_map/ppermute | solution.py:134
  74.4 3.4 %copy-start.1 = (bf16[64,4,128,128]{3,2,1,0:T(8,128)(2,1)S(1)}, bf16[64,4,128,128]{3,2,1,0:T(8,128)(2,1)}, u32[]{:S(2)}) copy-start(bf16[64,4,128,128]{3,2,1,0:T(8,128)(2,1)} %all-gather.3.cloned.1.call-done) | copy-start | bytes 25165828
  79.1 10.7 %collective-permute-start.2 = (bf16[32,128]{1,0:T(8,128)(2,1)S(1)}, bf16[32,128]{1,0:T(8,128)(2,1)S(1)}, u32[]{:S(2)}, u32[]{:S(2)}) collective-permute-start(bf16[32,128]{1,0:T(8,128)(2,1)S(1)} %shard_map.68.own.solved), channel_id=1, source_target_pairs={{16,32},{32,16},{48,64},{64,48},{80,96},{96,80},{112,128},{128,112... | collective-permute-start | bytes 24584 | tf_op jit(solution)/shard_map/ppermute | solution.py:133
  87.9 4.4 %collective-permute-start.3 = (bf16[32,128]{1,0:T(8,128)(2,1)S(1)}, bf16[32,128]{1,0:T(8,128)(2,1)S(1)}, u32[]{:S(2)}, u32[]{:S(2)}) collective-permute-start(bf16[32,128]{1,0:T(8,128)(2,1)S(1)} %shard_map.68.own.solved), channel_id=1, source_target_pairs={{0,16},{16,0},{32,48},{48,32},{64,80},{80,64},{96,112},{112,96},{1... | collective-permute-start | bytes 24584 | tf_op jit(solution)/shard_map/ppermute | solution.py:134
  93.7 7.7 %collective-permute-start.4 = (bf16[32,128]{1,0:T(8,128)(2,1)S(1)}, bf16[32,128]{1,0:T(8,128)(2,1)S(1)}, u32[]{:S(2)}, u32[]{:S(2)}) collective-permute-start(bf16[32,128]{1,0:T(8,128)(2,1)S(1)} %shard_map.69.own.solved), channel_id=1, source_target_pairs={{16,32},{32,16},{48,64},{64,48},{80,96},{96,80},{112,128},{128,112... | collective-permute-start | bytes 24584 | tf_op jit(solution)/shard_map/ppermute | solution.py:133
  97.0 4.4 %collective-permute-start.5 = (bf16[32,128]{1,0:T(8,128)(2,1)S(1)}, bf16[32,128]{1,0:T(8,128)(2,1)S(1)}, u32[]{:S(2)}, u32[]{:S(2)}) collective-permute-start(bf16[32,128]{1,0:T(8,128)(2,1)S(1)} %shard_map.69.own.solved), channel_id=1, source_target_pairs={{0,16},{16,0},{32,48},{48,32},{64,80},{80,64},{96,112},{112,96},{1... | collective-permute-start | bytes 24584 | tf_op jit(solution)/shard_map/ppermute | solution.py:134
  102.8 7.7 %collective-permute-start.6 = (bf16[32,128]{1,0:T(8,128)(2,1)S(1)}, bf16[32,128]{1,0:T(8,128)(2,1)S(1)}, u32[]{:S(2)}, u32[]{:S(2)}) collective-permute-start(bf16[32,128]{1,0:T(8,128)(2,1)S(1)} %shard_map.70.own.solved), channel_id=1, source_target_pairs={{16,32},{32,16},{48,64},{64,48},{80,96},{96,80},{112,128},{128,112... | collective-permute-start | bytes 24584 | tf_op jit(solution)/shard_map/ppermute | solution.py:133
  108.3 4.7 %collective-permute-start.7 = (bf16[32,128]{1,0:T(8,128)(2,1)S(1)}, bf16[32,128]{1,0:T(8,128)(2,1)S(1)}, u32[]{:S(2)}, u32[]{:S(2)}) collective-permute-start(bf16[32,128]{1,0:T(8,128)(2,1)S(1)} %shard_map.70.own.solved), channel_id=1, source_target_pairs={{0,16},{16,0},{32,48},{48,32},{64,80},{80,64},{96,112},{112,96},{1... | collective-permute-start | bytes 24584 | tf_op jit(solution)/shard_map/ppermute | solution.py:134
  114.3 7.7 %collective-permute-start.8 = (bf16[32,128]{1,0:T(8,128)(2,1)S(1)}, bf16[32,128]{1,0:T(8,128)(2,1)S(1)}, u32[]{:S(2)}, u32[]{:S(2)}) collective-permute-start(bf16[32,128]{1,0:T(8,128)(2,1)S(1)} %shard_map.71.own.solved), channel_id=1, source_target_pairs={{16,32},{32,16},{48,64},{64,48},{80,96},{96,80},{112,128},{128,112... | collective-permute-start | bytes 24584 | tf_op jit(solution)/shard_map/ppermute | solution.py:133
  117.4 4.7 %collective-permute-start.9 = (bf16[32,128]{1,0:T(8,128)(2,1)S(1)}, bf16[32,128]{1,0:T(8,128)(2,1)S(1)}, u32[]{:S(2)}, u32[]{:S(2)}) collective-permute-start(bf16[32,128]{1,0:T(8,128)(2,1)S(1)} %shard_map.71.own.solved), channel_id=1, source_target_pairs={{0,16},{16,0},{32,48},{48,32},{64,80},{80,64},{96,112},{112,96},{1... | collective-permute-start | bytes 24584 | tf_op jit(solution)/shard_map/ppermute | solution.py:134
  123.4 7.7 %collective-permute-start.10 = (bf16[32,128]{1,0:T(8,128)(2,1)S(1)}, bf16[32,128]{1,0:T(8,128)(2,1)S(1)}, u32[]{:S(2)}, u32[]{:S(2)}) collective-permute-start(bf16[32,128]{1,0:T(8,128)(2,1)S(1)} %shard_map.72.own.solved), channel_id=1, source_target_pairs={{16,32},{32,16},{48,64},{64,48},{80,96},{96,80},{112,128},{128,112... | collective-permute-start | bytes 24584 | tf_op jit(solution)/shard_map/ppermute | solution.py:133
  128.7 4.4 %collective-permute-start.11 = (bf16[32,128]{1,0:T(8,128)(2,1)S(1)}, bf16[32,128]{1,0:T(8,128)(2,1)S(1)}, u32[]{:S(2)}, u32[]{:S(2)}) collective-permute-start(bf16[32,128]{1,0:T(8,128)(2,1)S(1)} %shard_map.72.own.solved), channel_id=1, source_target_pairs={{0,16},{16,0},{32,48},{48,32},{64,80},{80,64},{96,112},{112,96},{1... | collective-permute-start | bytes 24584 | tf_op jit(solution)/shard_map/ppermute | solution.py:134
  134.5 7.7 %collective-permute-start.12 = (bf16[32,128]{1,0:T(8,128)(2,1)S(1)}, bf16[32,128]{1,0:T(8,128)(2,1)S(1)}, u32[]{:S(2)}, u32[]{:S(2)}) collective-permute-start(bf16[32,128]{1,0:T(8,128)(2,1)S(1)} %shard_map.73.own.solved), channel_id=1, source_target_pairs={{16,32},{32,16},{48,64},{64,48},{80,96},{96,80},{112,128},{128,112... | collective-permute-start | bytes 24584 | tf_op jit(solution)/shard_map/ppermute | solution.py:133
  137.8 4.4 %collective-permute-start.13 = (bf16[32,128]{1,0:T(8,128)(2,1)S(1)}, bf16[32,128]{1,0:T(8,128)(2,1)S(1)}, u32[]{:S(2)}, u32[]{:S(2)}) collective-permute-start(bf16[32,128]{1,0:T(8,128)(2,1)S(1)} %shard_map.73.own.solved), channel_id=1, source_target_pairs={{0,16},{16,0},{32,48},{48,32},{64,80},{80,64},{96,112},{112,96},{1... | collective-permute-start | bytes 24584 | tf_op jit(solution)/shard_map/ppermute | solution.py:134
  145.1 7.8 %collective-permute-start.14 = (f32[32,128]{1,0:T(8,128)S(1)}, f32[32,128]{1,0:T(8,128)S(1)}, u32[]{:S(2)}, u32[]{:S(2)}) collective-permute-start(f32[32,128]{1,0:T(8,128)S(1)} %get-tuple-element.30), channel_id=1, source_target_pairs={{16,32},{32,16},{48,64},{64,48},{80,96},{96,80},{112,128},{128,112... | collective-permute-start | bytes 49160 | tf_op jit(solution)/shard_map/ppermute | solution.py:150
  150.5 4.5 %collective-permute-start.15 = (f32[32,128]{1,0:T(8,128)S(1)}, f32[32,128]{1,0:T(8,128)S(1)}, u32[]{:S(2)}, u32[]{:S(2)}) collective-permute-start(f32[32,128]{1,0:T(8,128)S(1)} %get-tuple-element.32), channel_id=1, source_target_pairs={{0,16},{16,0},{32,48},{48,32},{64,80},{80,64},{96,112},{112,96},{1... | collective-permute-start | bytes 49160 | tf_op jit(solution)/shard_map/ppermute | solution.py:151
  156.5 7.8 %collective-permute-start.16 = (f32[32,128]{1,0:T(8,128)S(1)}, f32[32,128]{1,0:T(8,128)S(1)}, u32[]{:S(2)}, u32[]{:S(2)}) collective-permute-start(f32[32,128]{1,0:T(8,128)S(1)} %get-tuple-element.33), channel_id=1, source_target_pairs={{16,32},{32,16},{48,64},{64,48},{80,96},{96,80},{112,128},{128,112... | collective-permute-start | bytes 49160 | tf_op jit(solution)/shard_map/ppermute | solution.py:150
  159.9 4.5 %collective-permute-start.17 = (f32[32,128]{1,0:T(8,128)S(1)}, f32[32,128]{1,0:T(8,128)S(1)}, u32[]{:S(2)}, u32[]{:S(2)}) collective-permute-start(f32[32,128]{1,0:T(8,128)S(1)} %get-tuple-element.35), channel_id=1, source_target_pairs={{0,16},{16,0},{32,48},{48,32},{64,80},{80,64},{96,112},{112,96},{1... | collective-permute-start | bytes 49160 | tf_op jit(solution)/shard_map/ppermute | solution.py:151
  165.9 7.8 %collective-permute-start.18 = (f32[32,128]{1,0:T(8,128)S(1)}, f32[32,128]{1,0:T(8,128)S(1)}, u32[]{:S(2)}, u32[]{:S(2)}) collective-permute-start(f32[32,128]{1,0:T(8,128)S(1)} %get-tuple-element.36), channel_id=1, source_target_pairs={{16,32},{32,16},{48,64},{64,48},{80,96},{96,80},{112,128},{128,112... | collective-permute-start | bytes 49160 | tf_op jit(solution)/shard_map/ppermute | solution.py:150
  171.2 4.5 %collective-permute-start.19 = (f32[32,128]{1,0:T(8,128)S(1)}, f32[32,128]{1,0:T(8,128)S(1)}, u32[]{:S(2)}, u32[]{:S(2)}) collective-permute-start(f32[32,128]{1,0:T(8,128)S(1)} %get-tuple-element.38), channel_id=1, source_target_pairs={{0,16},{16,0},{32,48},{48,32},{64,80},{80,64},{96,112},{112,96},{1... | collective-permute-start | bytes 49160 | tf_op jit(solution)/shard_map/ppermute | solution.py:151
  177.3 8.3 %collective-permute-start.20 = (f32[32,128]{1,0:T(8,128)S(1)}, f32[32,128]{1,0:T(8,128)S(1)}, u32[]{:S(2)}, u32[]{:S(2)}) collective-permute-start(f32[32,128]{1,0:T(8,128)S(1)} %get-tuple-element.39), channel_id=1, source_target_pairs={{16,32},{32,16},{48,64},{64,48},{80,96},{96,80},{112,128},{128,112... | collective-permute-start | bytes 49160 | tf_op jit(solution)/shard_map/ppermute | solution.py:150
  180.6 4.9 %collective-permute-start.21 = (f32[32,128]{1,0:T(8,128)S(1)}, f32[32,128]{1,0:T(8,128)S(1)}, u32[]{:S(2)}, u32[]{:S(2)}) collective-permute-start(f32[32,128]{1,0:T(8,128)S(1)} %get-tuple-element.41), channel_id=1, source_target_pairs={{0,16},{16,0},{32,48},{48,32},{64,80},{80,64},{96,112},{112,96},{1... | collective-permute-start | bytes 49160 | tf_op jit(solution)/shard_map/ppermute | solution.py:151
  187.1 7.8 %collective-permute-start.22 = (f32[32,128]{1,0:T(8,128)S(1)}, f32[32,128]{1,0:T(8,128)S(1)}, u32[]{:S(2)}, u32[]{:S(2)}) collective-permute-start(f32[32,128]{1,0:T(8,128)S(1)} %get-tuple-element.42), channel_id=1, source_target_pairs={{16,32},{32,16},{48,64},{64,48},{80,96},{96,80},{112,128},{128,112... | collective-permute-start | bytes 49160 | tf_op jit(solution)/shard_map/ppermute | solution.py:150
  192.3 4.8 %collective-permute-start.23 = (f32[32,128]{1,0:T(8,128)S(1)}, f32[32,128]{1,0:T(8,128)S(1)}, u32[]{:S(2)}, u32[]{:S(2)}) collective-permute-start(f32[32,128]{1,0:T(8,128)S(1)} %get-tuple-element.44), channel_id=1, source_target_pairs={{0,16},{16,0},{32,48},{48,32},{64,80},{80,64},{96,112},{112,96},{1... | collective-permute-start | bytes 49160 | tf_op jit(solution)/shard_map/ppermute | solution.py:151
  198.6 7.8 %collective-permute-start.24 = (f32[32,128]{1,0:T(8,128)S(1)}, f32[32,128]{1,0:T(8,128)S(1)}, u32[]{:S(2)}, u32[]{:S(2)}) collective-permute-start(f32[32,128]{1,0:T(8,128)S(1)} %get-tuple-element.45), channel_id=1, source_target_pairs={{16,32},{32,16},{48,64},{64,48},{80,96},{96,80},{112,128},{128,112... | collective-permute-start | bytes 49160 | tf_op jit(solution)/shard_map/ppermute | solution.py:150
  202.1 4.5 %collective-permute-start.25 = (f32[32,128]{1,0:T(8,128)S(1)}, f32[32,128]{1,0:T(8,128)S(1)}, u32[]{:S(2)}, u32[]{:S(2)}) collective-permute-start(f32[32,128]{1,0:T(8,128)S(1)} %get-tuple-element.47), channel_id=1, source_target_pairs={{0,16},{16,0},{32,48},{48,32},{64,80},{80,64},{96,112},{112,96},{1... | collective-permute-start | bytes 49160 | tf_op jit(solution)/shard_map/ppermute | solution.py:151
  208.2 7.8 %collective-permute-start.26 = (f32[32,128]{1,0:T(8,128)S(1)}, f32[32,128]{1,0:T(8,128)S(1)}, u32[]{:S(2)}, u32[]{:S(2)}) collective-permute-start(f32[32,128]{1,0:T(8,128)S(1)} %get-tuple-element.48), channel_id=1, source_target_pairs={{16,32},{32,16},{48,64},{64,48},{80,96},{96,80},{112,128},{128,112... | collective-permute-start | bytes 49160 | tf_op jit(solution)/shard_map/ppermute | solution.py:150
  213.4 4.5 %collective-permute-start.27 = (f32[32,128]{1,0:T(8,128)S(1)}, f32[32,128]{1,0:T(8,128)S(1)}, u32[]{:S(2)}, u32[]{:S(2)}) collective-permute-start(f32[32,128]{1,0:T(8,128)S(1)} %get-tuple-element.50), channel_id=1, source_target_pairs={{0,16},{16,0},{32,48},{48,32},{64,80},{80,64},{96,112},{112,96},{1... | collective-permute-start | bytes 49160 | tf_op jit(solution)/shard_map/ppermute | solution.py:151
Sparse Core Ops, SparseCore 0:
  10.1 64.1 all-gather.2

commit v3 on v2

--- a/solution.py
+++ b/solution.py
@@ -44,31 +44,39 @@
 
 
 def backward_kernel(
-    level, share, last, owners, weights, spread, solved, far, own, near, result, *outs
+    level, share, top, owners, weights, mates, spread, solved, solved_mate, held, came, result, *outs
 ):
     rows = weights.shape[1]
     count = 2 * rows
-    folded = (far[...] + own[...] + near[...]).astype(BF16)
+    span = count * share
+    side = 2 * owners[owners.shape[0] - 1]
+    side = side if level % 2 else 2 - side
+    if not top:
+        folded = (held[:span] + came[span:]).astype(BF16)
+        folded_mate = (held[span:] + came[:span]).astype(BF16)
     pushes = [[], [], []]
     for pair in range(count // 2):
         half, row = divmod(2 * pair, rows)
         owner = owners[2 * level + half]
-        at = 2 * share * pair
-        part = folded[at : at + 2 * share]
-        part = either(*[dot(part, weights[owner, row + one, 0]) for one in range(2)], share)
-        done = (solved[at : at + 2 * share].astype(F32) - part).astype(BF16)
-        result[at : at + 2 * share] = done
-        if not last:
-            for n in range(3):
-                pushes[n].append(
-                    either(*[dot_t(done, weights[owner, row + one, 1 + n]) for one in range(2)], share)
-                )
-    if not last:
+        at = slice(2 * share * pair, 2 * share * (pair + 1))
+
+        def both(product, vector, blocks, kind):
+            return either(*[product(vector, blocks[owner, row + one, kind]) for one in range(2)], share)
+
+        done, done_mate = solved[at], solved_mate[at]
+        if not top:
+            done = (done.astype(F32) - both(dot, folded[at], weights, 0)).astype(BF16)
+        result[at] = done
+        if outs:
+            if not top:
+                done_mate = done_mate.astype(F32) - both(dot, folded_mate[at], mates, 0)
+                done_mate = done_mate.astype(BF16)
+            pushes[0].append(both(dot_t, done, weights, 2))
+            pushes[1].append(both(dot_t, done_mate, mates, 1))
+            pushes[2].append(both(dot_t, done, weights, 1 + side))
+    if outs:
         pushed = jnp.concatenate(pushes[0] + pushes[1] + pushes[2], axis=0).astype(BF16)
-        total = dot(spread[level], pushed)
-        span = count * share
-        for n in range(3):
-            outs[n][...] = total[n * span : (n + 1) * span]
+        outs[0][...] = dot(spread[level], pushed)
 
 
 def call(kernel, outs, owners, *rest):
@@ -97,9 +105,19 @@
     weights = jnp.concatenate([diag_inverse[:, None], off_blocks], axis=1)
     weights = lax.all_gather(weights, "level")
 
+    turn = dom % 2
     ids = jnp.arange(levs, dtype=jnp.int32)
     own_level = jnp.sum(jnp.where(ids == lev, plan, 0)) // 2
     inverse = jnp.sum(jnp.where(plan[None, :] == ids[:, None], ids[None, :], 0), axis=1)
+    owners = jnp.concatenate([inverse, turn[None]])
+
+    here = jnp.where(own_level % 2 == turn, off_blocks[:, 0], off_blocks[:, 2])
+    mates = jnp.stack([diag_inverse, here], axis=1)
+    by_near = lax.ppermute(mates, "dom", near_pairs)
+    by_far = lax.ppermute(mates, "dom", far_pairs)
+    mates = jnp.where(own_level % 2 == 1, by_near, by_far)
+    mates, weights = lax.optimization_barrier((mates, weights))
+    mates = lax.all_gather(mates, "level")
 
     first = jnp.einsum("rkb,rbc->rkc", right_side, diag_inverse, preferred_element_type=F32)
     side = jnp.where(own_level == 0, first.astype(BF16), right_side)
@@ -107,13 +125,16 @@
     side = lax.all_to_all(side, "level", 1, 0, tiled=False)
     side = side.reshape(levs, rows * share, width)[inverse].reshape(levels, count * share, width)
 
-    part = lax.dynamic_slice_in_dim(columns, dom * levs * rows, levs * rows, 0)
-    part = part.reshape(levs, rows * 3)[inverse].reshape(levels, count, 3)
-    source = plan[(part // rows) % levs] % 2 * rows + part % rows
+    def sources(partition):
+        part = lax.dynamic_slice_in_dim(columns, partition * levs * rows, levs * rows, 0)
+        part = part.reshape(levs, rows * 3)[inverse].reshape(levels, count, 3)
+        return plan[(part // rows) % levs] % 2 * rows + part % rows
+
+    source = sources(dom)
     j = jnp.arange(count, dtype=jnp.int32)
     meets = source[:, :, :, None] == j
     eye_n = jnp.eye(3, dtype=bool)
-    eye_n = jnp.where(dom % 2 == 0, eye_n, eye_n[::-1])
+    eye_n = jnp.where(turn == 0, eye_n, eye_n[::-1])
     eye_k = jnp.eye(share, dtype=bool)
     pick = (
         meets.transpose(0, 2, 1, 3)[:, :, :, None, None, :, None]
@@ -122,34 +143,56 @@
     )
     size = 3 * count * share
     pick = pick.reshape(levels, size, size).astype(BF16)
-    spread = pick.transpose(0, 2, 1)
+
+    odd = (jnp.arange(levels) % 2 == 1)[:, None]
+    near_dom = dom + 1 - 2 * turn
+    far_dom = (dom - 1 + 2 * turn) % doms
+    ahead = jnp.where(odd == (turn == 0), 0, 2)
+
+    def target(which):
+        rises = (which[:, None, :] == j[None, :, None])[:, :, None, :, None]
+        rises = rises & eye_k[None, None, :, None, :]
+        return rises.reshape(levels, count * share, count * share).astype(BF16)
+
+    source_mate = jnp.where(odd[..., None], sources(near_dom), sources(far_dom))
+    own_own = target(source[..., 1])
+    own_mate = target(jnp.where(ahead == 0, source[..., 0], source[..., 2]))
+    mate_own = target(jnp.where(ahead == 0, source_mate[..., 0], source_mate[..., 2]))
+    none = jnp.zeros_like(own_own)
+    spread = jnp.concatenate(
+        [
+            jnp.concatenate([own_own, mate_own, none], axis=2),
+            jnp.concatenate([none, none, own_mate], axis=2),
+        ],
+        axis=1,
+    )
 
     vector = jax.ShapeDtypeStruct((count * share, width), BF16)
-    summed = jax.ShapeDtypeStruct((count * share, width), F32)
+    summed = jax.ShapeDtypeStruct((2 * count * share, width), F32)
 
     solved = [side[0]]
+    around = []
     for level in range(1, levels):
         own = solved[-1]
         far = lax.ppermute(own, "dom", far_pairs)
         near = lax.ppermute(own, "dom", near_pairs)
+        around.append(near if level % 2 == 0 else far)
         kernel = functools.partial(forward_kernel, level, share)
-        solved += call(kernel, [vector], inverse, weights, pick, side, far, own, near)
-
-    zero = jnp.zeros(summed.shape, F32)
-    far, own, near = zero, zero, zero
+        solved += call(kernel, [vector], owners, weights, pick, side, far, own, near)
+    around.append(lax.ppermute(solved[-1], "dom", near_pairs))
+
+    held = came = jnp.zeros(summed.shape, F32)
     results = []
     for level in range(levels - 1, -1, -1):
-        last = level == 0
-        kernel = functools.partial(backward_kernel, level, share, last)
-        outs = [vector] if last else [vector, summed, summed, summed]
-        result, *sums = call(
-            kernel, outs, inverse, weights, spread, solved[level], far, own, near
+        kernel = functools.partial(backward_kernel, level, share, level == levels - 1)
+        outs = [vector, summed] if level else [vector]
+        result, *rest = call(
+            kernel, outs, owners, weights, mates, spread, solved[level], around[level], held, came
         )
         results.append(result)
-        if not last:
-            far = lax.ppermute(sums[0], "dom", far_pairs)
-            near = lax.ppermute(sums[2], "dom", near_pairs)
-            own = sums[1]
+        if level:
+            held = rest[0]
+            came = lax.ppermute(held, "dom", far_pairs if level % 2 else near_pairs)
 
     both = jnp.stack([jnp.stack(solved), jnp.stack(results[::-1])])
     both = both.reshape(2, levs, rows, share, width)[:, plan]

time: 260 us -> 296 us (1.14)
  waiting for transfers between devices: 61.1 us -> 88.7 us
  local copies, waits for them, and re-layouts: 13.3 us -> 36.5 us
  starting transfers between devices: 109 us -> 88.8 us
  blocking collectives: 31.1 us -> 34.2 us
    ppermute x14 -> x10, waiting for transfers between devices: 18.5 us -> 34.9 us  [the longest x7 26.8 us: local(): came = lax.ppermute(held, 'dom', far_pairs if level % 2 else near_pairs)]
    unnamed x20 -> x30, local copies, waits for them, and re-layouts: 3.51 us -> 19.4 us
    all_gather x1, waiting for transfers between devices: 24.2 us -> 36.9 us  [local(): weights = lax.all_gather(weights, 'level')]
    ppermute x7, starting transfers between devices: 41.1 us -> 33.5 us  [local(): far = lax.ppermute(own, 'dom', far_pairs)]
    ppermute x14 -> x10, starting transfers between devices: 44.6 us -> 37.1 us  [the longest x7 19.3 us: local(): came = lax.ppermute(held, 'dom', far_pairs if level % 2 else near_pairs)]
    all_to_all x1, starting transfers between devices: 10.2 us -> 4.74 us  [local(): side = lax.all_to_all(side, 'level', 1, 0, tiled=False)]
    gather x3 -> x9, local copies, waits for them, and re-layouts: 2.24 us -> 6.74 us  [the longest x6 5.04 us: sources(): return plan[part // rows % levs] % 2 * rows + part % rows]
    all_to_all x1, blocking collectives: 31.1 us -> 34.2 us  [local(): both = lax.all_to_all(both, 'level', 1, 0, tiled=False)]
  transfers between devices with their start and end apart: 30 -> 27, of which waited for: 23 -> 19; matrix products, arithmetic and copies ran while one was open for 4% -> 7% of each run, Pallas kernels for 0% -> 3%
where the time goes in v3:
time: 296 us; the launch traced here: 294 us
  starting transfers between devices  88.8 us (30%)
  waiting for transfers between devices  88.7 us (30%)
  local copies, waits for them, and re-layouts  36.5 us (12%)
  blocking collectives  34.2 us (12%)
  Pallas kernels  20.7 us (7%)
  between operations  17.3 us (6%)
  other arithmetic  7 us (2%)
    all_gather x1, waiting for transfers between devices, local(): weights = lax.all_gather(weights, 'level')  36.9 us
    all_to_all x1, blocking collectives, local(): both = lax.all_to_all(both, 'level', 1, 0, tiled=False)  34.2 us
    ppermute x7, starting transfers between devices, local(): far = lax.ppermute(own, 'dom', far_pairs)  33.5 us
    ppermute x7, waiting for transfers between devices, local(): came = lax.ppermute(held, 'dom', far_pairs if level % 2 else near_pairs)  26.8 us
    pallas_call x15, Pallas kernels, call(): pl.pallas_call(kernel, out_shape=outs, in_specs=[pl.BlockSpec(memory_spac...  20.7 us
    unnamed x30, local copies, waits for them, and re-layouts  19.4 us
    ppermute x7, starting transfers between devices, local(): came = lax.ppermute(held, 'dom', far_pairs if level % 2 else near_pairs)  19.3 us
    ppermute x7, starting transfers between devices, local(): near = lax.ppermute(own, 'dom', near_pairs)  13.4 us
  transfers between devices with their start and end apart: 27, of which 19 were waited for; matrix products, arithmetic and copies ran while one was open for 7% of the time, Pallas kernels for 3%

profile of v3, /device:TPU:1, one launch (start us, length us, event | category | flops | bytes accessed | tf_op | source)
XLA Modules:
  0.0 294.4 jit_solution(16527666884701335521)
XLA Ops:
  15.1 4.8 %collective-permute-start = (bf16[4,2,128,128]{3,2,1,0:T(8,128)(2,1)S(1)}, bf16[4,2,128,128]{3,2,1,0:T(8,128)(2,1)S(1)}, u32[]{:S(2)}, u32[]{:S(2)}) collective-permute-start(bf16[4,2,128,128]{3,2,1,0:T(8,128)(2,1)S(1)} %pad_maximum_fusion.1), channel_id=1, source_target_pairs={{0,16},{16,0},{32,48},{48,32},{64,80},{80,64},{96,112},{112,96},{1... | collective-permute-start | bytes 786440 | tf_op jit(solution)/shard_map/ppermute | solution.py:116
  19.9 11.0 %collective-permute-start.1 = (bf16[4,2,128,128]{3,2,1,0:T(8,128)(2,1)S(1)}, bf16[4,2,128,128]{3,2,1,0:T(8,128)(2,1)S(1)}, u32[]{:S(2)}, u32[]{:S(2)}) collective-permute-start(bf16[4,2,128,128]{3,2,1,0:T(8,128)(2,1)S(1)} %pad_maximum_fusion.1), channel_id=1, source_target_pairs={{16,32},{32,16},{48,64},{64,48},{80,96},{96,80},{112,128},{128,112... | collective-permute-start | bytes 786440 | tf_op jit(solution)/shard_map/ppermute | solution.py:117
  31.0 5.7 %collective-permute-done.1 = bf16[4,2,128,128]{3,2,1,0:T(8,128)(2,1)S(1)} collective-permute-done((bf16[4,2,128,128]{3,2,1,0:T(8,128)(2,1)S(1)}, bf16[4,2,128,128]{3,2,1,0:T(8,128)(2,1)S(1)}, u32[]{:S(2)}, u32[]{:S(2)}) %collective-permute-start.1) | collective-permute-done | bytes 262176 | tf_op jit(solution)/shard_map/ppermute | solution.py:117
  37.4 36.9 %all-gather.5.cloned.1.call-done = bf16[64,4,128,128]{3,2,1,0:T(8,128)(2,1)} async-done(((bf16[4,4,128,128]{3,2,1,0:T(8,128)(2,1)}), bf16[64,4,128,128]{3,2,1,0:T(8,128)(2,1)}) %all-gather.5.cloned.1.call-update) | async-done | bytes 8388624 | tf_op jit(solution)/shard_map/all_gather | solution.py:106
  76.1 4.7 %all-to-all-start = ((bf16[1,4,16,4,128]{4,3,1,0,2:T(4,128)(2,1)}), bf16[1,4,16,4,128]{4,3,1,0,2:T(4,128)(2,1)S(1)}, u32[]{:S(2)}, u32[]{:S(2)}) async-start(bf16[1,4,16,4,128]{4,3,1,0,2:T(4,128)(2,1)} %copy.84), calls=%async_computation | async-start | bytes 131072 | tf_op jit(solution)/shard_map/all_to_all | solution.py:125
  94.8 7.7 %collective-permute-start.2 = (bf16[32,128]{1,0:T(8,128)(2,1)S(1)}, bf16[32,128]{1,0:T(8,128)(2,1)S(1)}, u32[]{:S(2)}, u32[]{:S(2)}) collective-permute-start(bf16[32,128]{1,0:T(8,128)(2,1)S(1)} %bitcast.117), channel_id=1, source_target_pairs={{16,32},{32,16},{48,64},{64,48},{80,96},{96,80},{112,128},{128,112... | collective-permute-start | bytes 24584 | tf_op jit(solution)/shard_map/ppermute | solution.py:177
  102.5 1.9 collective-permute-start.3
  104.6 2.7 collective-permute-done.3.near
  107.3 3.5 %copy-done = bf16[64,4,128,128]{3,2,1,0:T(8,128)(2,1)S(1)} copy-done((bf16[64,4,128,128]{3,2,1,0:T(8,128)(2,1)S(1)}, bf16[64,4,128,128]{3,2,1,0:T(8,128)(2,1)}, u32[]{:S(2)}) %copy-start) | copy-done | bytes 8388632
  112.2 2.9 collective-permute-start.4
  115.1 1.9 collective-permute-start.5
  117.2 2.8 collective-permute-done.4.far
  120.0 3.4 %copy-done.1 = bf16[64,4,128,128]{3,2,1,0:T(8,128)(2,1)S(1)} copy-done((bf16[64,4,128,128]{3,2,1,0:T(8,128)(2,1)S(1)}, bf16[64,4,128,128]{3,2,1,0:T(8,128)(2,1)}, u32[]{:S(2)}) %copy-start.1) | copy-done | bytes 8388632
  124.7 5.7 %collective-permute-start.6 = (bf16[32,128]{1,0:T(8,128)(2,1)S(1)}, bf16[32,128]{1,0:T(8,128)(2,1)S(1)}, u32[]{:S(2)}, u32[]{:S(2)}) collective-permute-start(bf16[32,128]{1,0:T(8,128)(2,1)S(1)} %shard_map.69.own.solved), channel_id=1, source_target_pairs={{16,32},{32,16},{48,64},{64,48},{80,96},{96,80},{112,128},{128,112... | collective-permute-start | bytes 24584 | tf_op jit(solution)/shard_map/ppermute | solution.py:177
  130.4 1.9 collective-permute-start.7
  132.5 2.6 collective-permute-done.7.near
  135.1 3.4 %copy-done.2 = bf16[64,4,128,128]{3,2,1,0:T(8,128)(2,1)S(1)} copy-done((bf16[64,4,128,128]{3,2,1,0:T(8,128)(2,1)S(1)}, bf16[64,4,128,128]{3,2,1,0:T(8,128)(2,1)}, u32[]{:S(2)}) %copy-start.2) | copy-done | bytes 8388632
  139.8 3.0 %collective-permute-start.8 = (bf16[32,128]{1,0:T(8,128)(2,1)S(1)}, bf16[32,128]{1,0:T(8,128)(2,1)S(1)}, u32[]{:S(2)}, u32[]{:S(2)}) collective-permute-start(bf16[32,128]{1,0:T(8,128)(2,1)S(1)} %shard_map.70.own.solved), channel_id=1, source_target_pairs={{16,32},{32,16},{48,64},{64,48},{80,96},{96,80},{112,128},{128,112... | collective-permute-start | bytes 24584 | tf_op jit(solution)/shard_map/ppermute | solution.py:177
  142.9 1.9 collective-permute-start.9
  147.6 3.4 %copy-done.3 = bf16[64,4,128,128]{3,2,1,0:T(8,128)(2,1)S(1)} copy-done((bf16[64,4,128,128]{3,2,1,0:T(8,128)(2,1)S(1)}, bf16[64,4,128,128]{3,2,1,0:T(8,128)(2,1)}, u32[]{:S(2)}) %copy-start.3) | copy-done | bytes 8388632
  152.3 5.6 %collective-permute-start.10 = (bf16[32,128]{1,0:T(8,128)(2,1)S(1)}, bf16[32,128]{1,0:T(8,128)(2,1)S(1)}, u32[]{:S(2)}, u32[]{:S(2)}) collective-permute-start(bf16[32,128]{1,0:T(8,128)(2,1)S(1)} %shard_map.71.own.solved), channel_id=1, source_target_pairs={{16,32},{32,16},{48,64},{64,48},{80,96},{96,80},{112,128},{128,112... | collective-permute-start | bytes 24584 | tf_op jit(solution)/shard_map/ppermute | solution.py:177
  157.9 1.9 collective-permute-start.11
  160.0 2.3 collective-permute-done.11.near
  163.7 3.3 %collective-permute-start.12 = (bf16[32,128]{1,0:T(8,128)(2,1)S(1)}, bf16[32,128]{1,0:T(8,128)(2,1)S(1)}, u32[]{:S(2)}, u32[]{:S(2)}) collective-permute-start(bf16[32,128]{1,0:T(8,128)(2,1)S(1)} %shard_map.72.own.solved), channel_id=1, source_target_pairs={{16,32},{32,16},{48,64},{64,48},{80,96},{96,80},{112,128},{128,112... | collective-permute-start | bytes 24584 | tf_op jit(solution)/shard_map/ppermute | solution.py:177
  167.0 1.9 collective-permute-start.13
  169.1 2.3 collective-permute-done.12.far
  172.8 5.3 %collective-permute-start.14 = (bf16[32,128]{1,0:T(8,128)(2,1)S(1)}, bf16[32,128]{1,0:T(8,128)(2,1)S(1)}, u32[]{:S(2)}, u32[]{:S(2)}) collective-permute-start(bf16[32,128]{1,0:T(8,128)(2,1)S(1)} %shard_map.73.own.solved), channel_id=1, source_target_pairs={{16,32},{32,16},{48,64},{64,48},{80,96},{96,80},{112,128},{128,112... | collective-permute-start | bytes 24584 | tf_op jit(solution)/shard_map/ppermute | solution.py:177
  178.1 1.9 collective-permute-start.15
  180.5 2.0 collective-permute-done.15.near
  183.8 1.9 collective-permute-start.16
  185.8 2.5 collective-permute-done.16.solved_mate
  188.2 3.4 %copy-done.4 = bf16[64,4,128,128]{3,2,1,0:T(8,128)(2,1)S(1)} copy-done((bf16[64,4,128,128]{3,2,1,0:T(8,128)(2,1)S(1)}, bf16[64,4,128,128]{3,2,1,0:T(8,128)(2,1)}, u32[]{:S(2)}) %copy-start.4) | copy-done | bytes 8388632
  191.6 2.2 copy-done.5
  195.0 3.5 %collective-permute-start.17 = (f32[64,128]{1,0:T(8,128)S(1)}, f32[64,128]{1,0:T(8,128)S(1)}, u32[]{:S(2)}, u32[]{:S(2)}) collective-permute-start(f32[64,128]{1,0:T(8,128)S(1)} %get-tuple-element.20.held), channel_id=1, source_target_pairs={{16,32},{32,16},{48,64},{64,48},{80,96},{96,80},{112,128},{128,112... | collective-permute-start | bytes 98312 | tf_op jit(solution)/shard_map/ppermute | solution.py:195
  198.4 4.7 %collective-permute-done.17.came = f32[64,128]{1,0:T(8,128)S(1)} collective-permute-done((f32[64,128]{1,0:T(8,128)S(1)}, f32[64,128]{1,0:T(8,128)S(1)}, u32[]{:S(2)}, u32[]{:S(2)}) %collective-permute-start.17) | collective-permute-done | bytes 32800 | tf_op jit(solution)/shard_map/ppermute | solution.py:195
  204.6 1.9 collective-permute-start.18
  206.6 2.7 collective-permute-done.18.came
  210.9 3.3 %collective-permute-start.19 = (f32[64,128]{1,0:T(8,128)S(1)}, f32[64,128]{1,0:T(8,128)S(1)}, u32[]{:S(2)}, u32[]{:S(2)}) collective-permute-start(f32[64,128]{1,0:T(8,128)S(1)} %get-tuple-element.22.held), channel_id=1, source_target_pairs={{16,32},{32,16},{48,64},{64,48},{80,96},{96,80},{112,128},{128,112... | collective-permute-start | bytes 98312 | tf_op jit(solution)/shard_map/ppermute | solution.py:195
  214.2 4.7 %collective-permute-done.19.came = f32[64,128]{1,0:T(8,128)S(1)} collective-permute-done((f32[64,128]{1,0:T(8,128)S(1)}, f32[64,128]{1,0:T(8,128)S(1)}, u32[]{:S(2)}, u32[]{:S(2)}) %collective-permute-start.19) | collective-permute-done | bytes 32800 | tf_op jit(solution)/shard_map/ppermute | solution.py:195
  220.4 1.9 collective-permute-start.20
  222.4 2.7 collective-permute-done.20.came
  226.6 3.3 %collective-permute-start.21 = (f32[64,128]{1,0:T(8,128)S(1)}, f32[64,128]{1,0:T(8,128)S(1)}, u32[]{:S(2)}, u32[]{:S(2)}) collective-permute-start(f32[64,128]{1,0:T(8,128)S(1)} %get-tuple-element.24.held), channel_id=1, source_target_pairs={{16,32},{32,16},{48,64},{64,48},{80,96},{96,80},{112,128},{128,112... | collective-permute-start | bytes 98312 | tf_op jit(solution)/shard_map/ppermute | solution.py:195
  230.0 4.7 %collective-permute-done.21.came = f32[64,128]{1,0:T(8,128)S(1)} collective-permute-done((f32[64,128]{1,0:T(8,128)S(1)}, f32[64,128]{1,0:T(8,128)S(1)}, u32[]{:S(2)}, u32[]{:S(2)}) %collective-permute-start.21) | collective-permute-done | bytes 32800 | tf_op jit(solution)/shard_map/ppermute | solution.py:195
  236.2 1.9 collective-permute-start.22
  238.2 2.7 collective-permute-done.22.came
  242.4 3.3 %collective-permute-start.23 = (f32[64,128]{1,0:T(8,128)S(1)}, f32[64,128]{1,0:T(8,128)S(1)}, u32[]{:S(2)}, u32[]{:S(2)}) collective-permute-start(f32[64,128]{1,0:T(8,128)S(1)} %get-tuple-element.26.held), channel_id=1, source_target_pairs={{16,32},{32,16},{48,64},{64,48},{80,96},{96,80},{112,128},{128,112... | collective-permute-start | bytes 98312 | tf_op jit(solution)/shard_map/ppermute | solution.py:195
  245.8 4.7 %collective-permute-done.23.came = f32[64,128]{1,0:T(8,128)S(1)} collective-permute-done((f32[64,128]{1,0:T(8,128)S(1)}, f32[64,128]{1,0:T(8,128)S(1)}, u32[]{:S(2)}, u32[]{:S(2)}) %collective-permute-start.23) | collective-permute-done | bytes 32800 | tf_op jit(solution)/shard_map/ppermute | solution.py:195
  252.0 34.2 %all_to_all.30 = bf16[1,2,16,4,4,128]{5,4,3,1,0,2:T(4,128)(2,1)S(1)} all-to-all(bf16[1,2,16,4,4,128]{5,4,3,1,0,2:T(4,128)(2,1)S(1)} %bitcast.130), channel_id=1, replica_groups=mesh['dom'=32,'level'=16] {'level'}, dimensions={2} | all-to-all | bytes 262144 | tf_op jit(solution)/shard_map/all_to_all | solution.py:199
  (145 shorter events, 48.5 us)
Async XLA Ops:
  7.2 74.7 %copy-start.7 = (s32[16]{0:T(128)S(1)}, s32[16]{0:T(128)}, u32[]{:S(2)}) copy-start(s32[16]{0:T(128)} %param.9) | copy-start | bytes 196
  7.2 67.1 %all-gather.5.cloned.1.call-start = ((), (), s32[]{:S(2)}) async-start(), calls=%async_computation.2 | async-start | bytes 8912896 | tf_op jit(solution)/shard_map/all_gather | solution.py:106
  9.2 179.1 %all-gather.7.cloned.1.call-start = ((), (), s32[]{:S(2)}) async-start(), calls=%async_computation.3 | async-start | bytes 4456448 | tf_op jit(solution)/shard_map/all_gather | solution.py:120
  15.1 15.9 %collective-permute-start = (bf16[4,2,128,128]{3,2,1,0:T(8,128)(2,1)S(1)}, bf16[4,2,128,128]{3,2,1,0:T(8,128)(2,1)S(1)}, u32[]{:S(2)}, u32[]{:S(2)}) collective-permute-start(bf16[4,2,128,128]{3,2,1,0:T(8,128)(2,1)S(1)} %pad_maximum_fusion.1), channel_id=1, source_target_pairs={{0,16},{16,0},{32,48},{48,32},{64,80},{80,64},{96,112},{112,96},{1... | collective-permute-start | bytes 786440 | tf_op jit(solution)/shard_map/ppermute | solution.py:116
  19.9 16.7 %collective-permute-start.1 = (bf16[4,2,128,128]{3,2,1,0:T(8,128)(2,1)S(1)}, bf16[4,2,128,128]{3,2,1,0:T(8,128)(2,1)S(1)}, u32[]{:S(2)}, u32[]{:S(2)}) collective-permute-start(bf16[4,2,128,128]{3,2,1,0:T(8,128)(2,1)S(1)} %pad_maximum_fusion.1), channel_id=1, source_target_pairs={{16,32},{32,16},{48,64},{64,48},{80,96},{96,80},{112,128},{128,112... | collective-permute-start | bytes 786440 | tf_op jit(solution)/shard_map/ppermute | solution.py:117
  76.1 18.1 %all-to-all-start = ((bf16[1,4,16,4,128]{4,3,1,0,2:T(4,128)(2,1)}), bf16[1,4,16,4,128]{4,3,1,0,2:T(4,128)(2,1)S(1)}, u32[]{:S(2)}, u32[]{:S(2)}) async-start(bf16[1,4,16,4,128]{4,3,1,0,2:T(4,128)(2,1)} %copy.84), calls=%async_computation | async-start | bytes 131072 | tf_op jit(solution)/shard_map/all_to_all | solution.py:125
  94.8 9.8 %collective-permute-start.2 = (bf16[32,128]{1,0:T(8,128)(2,1)S(1)}, bf16[32,128]{1,0:T(8,128)(2,1)S(1)}, u32[]{:S(2)}, u32[]{:S(2)}) collective-permute-start(bf16[32,128]{1,0:T(8,128)(2,1)S(1)} %bitcast.117), channel_id=1, source_target_pairs={{16,32},{32,16},{48,64},{64,48},{80,96},{96,80},{112,128},{128,112... | collective-permute-start | bytes 24584 | tf_op jit(solution)/shard_map/ppermute | solution.py:177
  102.5 4.8 %collective-permute-start.3 = (bf16[32,128]{1,0:T(8,128)(2,1)S(1)}, bf16[32,128]{1,0:T(8,128)(2,1)S(1)}, u32[]{:S(2)}, u32[]{:S(2)}) collective-permute-start(bf16[32,128]{1,0:T(8,128)(2,1)S(1)} %bitcast.118), channel_id=1, source_target_pairs={{0,16},{16,0},{32,48},{48,32},{64,80},{80,64},{96,112},{112,96},{1... | collective-permute-start | bytes 24584 | tf_op jit(solution)/shard_map/ppermute | solution.py:178
  107.3 3.5 %copy-start = (bf16[64,4,128,128]{3,2,1,0:T(8,128)(2,1)S(1)}, bf16[64,4,128,128]{3,2,1,0:T(8,128)(2,1)}, u32[]{:S(2)}) copy-start(bf16[64,4,128,128]{3,2,1,0:T(8,128)(2,1)} %all-gather.5.cloned.1.call-done) | copy-start | bytes 25165828
  112.2 7.7 %collective-permute-start.4 = (bf16[32,128]{1,0:T(8,128)(2,1)S(1)}, bf16[32,128]{1,0:T(8,128)(2,1)S(1)}, u32[]{:S(2)}, u32[]{:S(2)}) collective-permute-start(bf16[32,128]{1,0:T(8,128)(2,1)S(1)} %shard_map.68.own.solved), channel_id=1, source_target_pairs={{16,32},{32,16},{48,64},{64,48},{80,96},{96,80},{112,128},{128,112... | collective-permute-start | bytes 24584 | tf_op jit(solution)/shard_map/ppermute | solution.py:177
  115.1 4.8 %collective-permute-start.5 = (bf16[32,128]{1,0:T(8,128)(2,1)S(1)}, bf16[32,128]{1,0:T(8,128)(2,1)S(1)}, u32[]{:S(2)}, u32[]{:S(2)}) collective-permute-start(bf16[32,128]{1,0:T(8,128)(2,1)S(1)} %shard_map.68.own.solved), channel_id=1, source_target_pairs={{0,16},{16,0},{32,48},{48,32},{64,80},{80,64},{96,112},{112,96},{1... | collective-permute-start | bytes 24584 | tf_op jit(solution)/shard_map/ppermute | solution.py:178
  120.0 3.4 %copy-start.1 = (bf16[64,4,128,128]{3,2,1,0:T(8,128)(2,1)S(1)}, bf16[64,4,128,128]{3,2,1,0:T(8,128)(2,1)}, u32[]{:S(2)}) copy-start(bf16[64,4,128,128]{3,2,1,0:T(8,128)(2,1)} %all-gather.5.cloned.1.call-done) | copy-start | bytes 25165828
  124.7 7.8 %collective-permute-start.6 = (bf16[32,128]{1,0:T(8,128)(2,1)S(1)}, bf16[32,128]{1,0:T(8,128)(2,1)S(1)}, u32[]{:S(2)}, u32[]{:S(2)}) collective-permute-start(bf16[32,128]{1,0:T(8,128)(2,1)S(1)} %shard_map.69.own.solved), channel_id=1, source_target_pairs={{16,32},{32,16},{48,64},{64,48},{80,96},{96,80},{112,128},{128,112... | collective-permute-start | bytes 24584 | tf_op jit(solution)/shard_map/ppermute | solution.py:177
  130.4 4.7 %collective-permute-start.7 = (bf16[32,128]{1,0:T(8,128)(2,1)S(1)}, bf16[32,128]{1,0:T(8,128)(2,1)S(1)}, u32[]{:S(2)}, u32[]{:S(2)}) collective-permute-start(bf16[32,128]{1,0:T(8,128)(2,1)S(1)} %shard_map.69.own.solved), channel_id=1, source_target_pairs={{0,16},{16,0},{32,48},{48,32},{64,80},{80,64},{96,112},{112,96},{1... | collective-permute-start | bytes 24584 | tf_op jit(solution)/shard_map/ppermute | solution.py:178
  135.1 3.4 %copy-start.2 = (bf16[64,4,128,128]{3,2,1,0:T(8,128)(2,1)S(1)}, bf16[64,4,128,128]{3,2,1,0:T(8,128)(2,1)}, u32[]{:S(2)}) copy-start(bf16[64,4,128,128]{3,2,1,0:T(8,128)(2,1)} %all-gather.5.cloned.1.call-done) | copy-start | bytes 25165828
  139.8 7.7 %collective-permute-start.8 = (bf16[32,128]{1,0:T(8,128)(2,1)S(1)}, bf16[32,128]{1,0:T(8,128)(2,1)S(1)}, u32[]{:S(2)}, u32[]{:S(2)}) collective-permute-start(bf16[32,128]{1,0:T(8,128)(2,1)S(1)} %shard_map.70.own.solved), channel_id=1, source_target_pairs={{16,32},{32,16},{48,64},{64,48},{80,96},{96,80},{112,128},{128,112... | collective-permute-start | bytes 24584 | tf_op jit(solution)/shard_map/ppermute | solution.py:177
  142.9 4.7 %collective-permute-start.9 = (bf16[32,128]{1,0:T(8,128)(2,1)S(1)}, bf16[32,128]{1,0:T(8,128)(2,1)S(1)}, u32[]{:S(2)}, u32[]{:S(2)}) collective-permute-start(bf16[32,128]{1,0:T(8,128)(2,1)S(1)} %shard_map.70.own.solved), channel_id=1, source_target_pairs={{0,16},{16,0},{32,48},{48,32},{64,80},{80,64},{96,112},{112,96},{1... | collective-permute-start | bytes 24584 | tf_op jit(solution)/shard_map/ppermute | solution.py:178
  147.6 3.4 %copy-start.3 = (bf16[64,4,128,128]{3,2,1,0:T(8,128)(2,1)S(1)}, bf16[64,4,128,128]{3,2,1,0:T(8,128)(2,1)}, u32[]{:S(2)}) copy-start(bf16[64,4,128,128]{3,2,1,0:T(8,128)(2,1)} %all-gather.5.cloned.1.call-done) | copy-start | bytes 25165828
  152.3 7.7 %collective-permute-start.10 = (bf16[32,128]{1,0:T(8,128)(2,1)S(1)}, bf16[32,128]{1,0:T(8,128)(2,1)S(1)}, u32[]{:S(2)}, u32[]{:S(2)}) collective-permute-start(bf16[32,128]{1,0:T(8,128)(2,1)S(1)} %shard_map.71.own.solved), channel_id=1, source_target_pairs={{16,32},{32,16},{48,64},{64,48},{80,96},{96,80},{112,128},{128,112... | collective-permute-start | bytes 24584 | tf_op jit(solution)/shard_map/ppermute | solution.py:177
  157.9 4.4 %collective-permute-start.11 = (bf16[32,128]{1,0:T(8,128)(2,1)S(1)}, bf16[32,128]{1,0:T(8,128)(2,1)S(1)}, u32[]{:S(2)}, u32[]{:S(2)}) collective-permute-start(bf16[32,128]{1,0:T(8,128)(2,1)S(1)} %shard_map.71.own.solved), channel_id=1, source_target_pairs={{0,16},{16,0},{32,48},{48,32},{64,80},{80,64},{96,112},{112,96},{1... | collective-permute-start | bytes 24584 | tf_op jit(solution)/shard_map/ppermute | solution.py:178
  163.7 7.7 %collective-permute-start.12 = (bf16[32,128]{1,0:T(8,128)(2,1)S(1)}, bf16[32,128]{1,0:T(8,128)(2,1)S(1)}, u32[]{:S(2)}, u32[]{:S(2)}) collective-permute-start(bf16[32,128]{1,0:T(8,128)(2,1)S(1)} %shard_map.72.own.solved), channel_id=1, source_target_pairs={{16,32},{32,16},{48,64},{64,48},{80,96},{96,80},{112,128},{128,112... | collective-permute-start | bytes 24584 | tf_op jit(solution)/shard_map/ppermute | solution.py:177
  167.0 4.4 %collective-permute-start.13 = (bf16[32,128]{1,0:T(8,128)(2,1)S(1)}, bf16[32,128]{1,0:T(8,128)(2,1)S(1)}, u32[]{:S(2)}, u32[]{:S(2)}) collective-permute-start(bf16[32,128]{1,0:T(8,128)(2,1)S(1)} %shard_map.72.own.solved), channel_id=1, source_target_pairs={{0,16},{16,0},{32,48},{48,32},{64,80},{80,64},{96,112},{112,96},{1... | collective-permute-start | bytes 24584 | tf_op jit(solution)/shard_map/ppermute | solution.py:178
  172.8 7.7 %collective-permute-start.14 = (bf16[32,128]{1,0:T(8,128)(2,1)S(1)}, bf16[32,128]{1,0:T(8,128)(2,1)S(1)}, u32[]{:S(2)}, u32[]{:S(2)}) collective-permute-start(bf16[32,128]{1,0:T(8,128)(2,1)S(1)} %shard_map.73.own.solved), channel_id=1, source_target_pairs={{16,32},{32,16},{48,64},{64,48},{80,96},{96,80},{112,128},{128,112... | collective-permute-start | bytes 24584 | tf_op jit(solution)/shard_map/ppermute | solution.py:177
  178.1 4.4 %collective-permute-start.15 = (bf16[32,128]{1,0:T(8,128)(2,1)S(1)}, bf16[32,128]{1,0:T(8,128)(2,1)S(1)}, u32[]{:S(2)}, u32[]{:S(2)}) collective-permute-start(bf16[32,128]{1,0:T(8,128)(2,1)S(1)} %shard_map.73.own.solved), channel_id=1, source_target_pairs={{0,16},{16,0},{32,48},{48,32},{64,80},{80,64},{96,112},{112,96},{1... | collective-permute-start | bytes 24584 | tf_op jit(solution)/shard_map/ppermute | solution.py:178
  183.8 4.4 %collective-permute-start.16 = (bf16[32,128]{1,0:T(8,128)(2,1)S(1)}, bf16[32,128]{1,0:T(8,128)(2,1)S(1)}, u32[]{:S(2)}, u32[]{:S(2)}) collective-permute-start(bf16[32,128]{1,0:T(8,128)(2,1)S(1)} %shard_map.74.solved), channel_id=1, source_target_pairs={{0,16},{16,0},{32,48},{48,32},{64,80},{80,64},{96,112},{112,96},{1... | collective-permute-start | bytes 24584 | tf_op jit(solution)/shard_map/ppermute | solution.py:182
  188.2 3.4 %copy-start.4 = (bf16[64,4,128,128]{3,2,1,0:T(8,128)(2,1)S(1)}, bf16[64,4,128,128]{3,2,1,0:T(8,128)(2,1)}, u32[]{:S(2)}) copy-start(bf16[64,4,128,128]{3,2,1,0:T(8,128)(2,1)} %all-gather.5.cloned.1.call-done) | copy-start | bytes 25165828
  191.6 2.2 copy-start.5
  193.8 9.3 %copy-start.6 = (bf16[64,2,128,128]{3,2,1,0:T(8,128)(2,1)S(1)}, bf16[64,2,128,128]{3,2,1,0:T(8,128)(2,1)}, u32[]{:S(2)}) copy-start(bf16[64,2,128,128]{3,2,1,0:T(8,128)(2,1)} %all-gather.7.cloned.1.call-done) | copy-start | bytes 12582916
  195.0 8.1 %collective-permute-start.17 = (f32[64,128]{1,0:T(8,128)S(1)}, f32[64,128]{1,0:T(8,128)S(1)}, u32[]{:S(2)}, u32[]{:S(2)}) collective-permute-start(f32[64,128]{1,0:T(8,128)S(1)} %get-tuple-element.20.held), channel_id=1, source_target_pairs={{16,32},{32,16},{48,64},{64,48},{80,96},{96,80},{112,128},{128,112... | collective-permute-start | bytes 98312 | tf_op jit(solution)/shard_map/ppermute | solution.py:195
  204.6 4.7 %collective-permute-start.18 = (f32[64,128]{1,0:T(8,128)S(1)}, f32[64,128]{1,0:T(8,128)S(1)}, u32[]{:S(2)}, u32[]{:S(2)}) collective-permute-start(f32[64,128]{1,0:T(8,128)S(1)} %get-tuple-element.21.held), channel_id=1, source_target_pairs={{0,16},{16,0},{32,48},{48,32},{64,80},{80,64},{96,112},{112,96},{1... | collective-permute-start | bytes 98312 | tf_op jit(solution)/shard_map/ppermute | solution.py:195
  210.9 8.0 %collective-permute-start.19 = (f32[64,128]{1,0:T(8,128)S(1)}, f32[64,128]{1,0:T(8,128)S(1)}, u32[]{:S(2)}, u32[]{:S(2)}) collective-permute-start(f32[64,128]{1,0:T(8,128)S(1)} %get-tuple-element.22.held), channel_id=1, source_target_pairs={{16,32},{32,16},{48,64},{64,48},{80,96},{96,80},{112,128},{128,112... | collective-permute-start | bytes 98312 | tf_op jit(solution)/shard_map/ppermute | solution.py:195
  220.4 4.7 %collective-permute-start.20 = (f32[64,128]{1,0:T(8,128)S(1)}, f32[64,128]{1,0:T(8,128)S(1)}, u32[]{:S(2)}, u32[]{:S(2)}) collective-permute-start(f32[64,128]{1,0:T(8,128)S(1)} %get-tuple-element.23.held), channel_id=1, source_target_pairs={{0,16},{16,0},{32,48},{48,32},{64,80},{80,64},{96,112},{112,96},{1... | collective-permute-start | bytes 98312 | tf_op jit(solution)/shard_map/ppermute | solution.py:195
  226.6 8.0 %collective-permute-start.21 = (f32[64,128]{1,0:T(8,128)S(1)}, f32[64,128]{1,0:T(8,128)S(1)}, u32[]{:S(2)}, u32[]{:S(2)}) collective-permute-start(f32[64,128]{1,0:T(8,128)S(1)} %get-tuple-element.24.held), channel_id=1, source_target_pairs={{16,32},{32,16},{48,64},{64,48},{80,96},{96,80},{112,128},{128,112... | collective-permute-start | bytes 98312 | tf_op jit(solution)/shard_map/ppermute | solution.py:195
  236.2 4.7 %collective-permute-start.22 = (f32[64,128]{1,0:T(8,128)S(1)}, f32[64,128]{1,0:T(8,128)S(1)}, u32[]{:S(2)}, u32[]{:S(2)}) collective-permute-start(f32[64,128]{1,0:T(8,128)S(1)} %get-tuple-element.25.held), channel_id=1, source_target_pairs={{0,16},{16,0},{32,48},{48,32},{64,80},{80,64},{96,112},{112,96},{1... | collective-permute-start | bytes 98312 | tf_op jit(solution)/shard_map/ppermute | solution.py:195
  242.4 8.0 %collective-permute-start.23 = (f32[64,128]{1,0:T(8,128)S(1)}, f32[64,128]{1,0:T(8,128)S(1)}, u32[]{:S(2)}, u32[]{:S(2)}) collective-permute-start(f32[64,128]{1,0:T(8,128)S(1)} %get-tuple-element.26.held), channel_id=1, source_target_pairs={{16,32},{32,16},{48,64},{64,48},{80,96},{96,80},{112,128},{128,112... | collective-permute-start | bytes 98312 | tf_op jit(solution)/shard_map/ppermute | solution.py:195
Sparse Core Ops, SparseCore 0:
  10.1 64.1 all-gather.4
  76.4 43.9 all-gather.6

commit v4 on v3

--- a/solution.py
+++ b/solution.py
@@ -24,70 +24,87 @@
     return jnp.where(top, low, high)
 
 
-def forward_kernel(level, share, owners, weights, pick, side, far, own, near, out):
-    rows = weights.shape[1]
-    count = 2 * rows
-    span = count * share
+def fetches(level, owners, source, held, sems):
+    copies = []
+    for pair in range(held.shape[0]):
+        half, part = divmod(2 * pair, source.shape[1])
+        rows = source.at[owners[2 * level + half], part : part + 2]
+        copies.append(pltpu.make_async_copy(rows, held.at[pair], sems.at[pair]))
+    for copy in copies:
+        copy.start()
+    return copies
+
+
+def forward_kernel(level, share, owners, weights, pick, side, far, own, near, out, blocks, sems):
+    copies = fetches(level, owners, weights, blocks, sems)
+    span = out.shape[0]
     around = jnp.concatenate([far[...], own[...], near[...]], axis=0)
     picked = dot(pick[level], around)
-    for pair in range(count // 2):
-        half, row = divmod(2 * pair, rows)
-        owner = owners[2 * level + half]
+    for pair in range(blocks.shape[0]):
         at = 2 * share * pair
         terms = [picked[n * span + at : n * span + at + 2 * share] for n in range(3)]
         terms = jnp.concatenate(terms, axis=1).astype(BF16)
-        blocks = [weights[owner, row + one, 1:].reshape(-1, terms.shape[1] // 3) for one in range(2)]
-        total = either(*[dot(terms, block) for block in blocks], share)
+        copies[pair].wait()
+        wide = [blocks[pair, one, 1:].reshape(-1, out.shape[1]) for one in range(2)]
+        total = either(*[dot(terms, block) for block in wide], share)
         shifted = (side[level, at : at + 2 * share].astype(F32) - total).astype(BF16)
-        solved = either(*[dot(shifted, weights[owner, row + one, 0]) for one in range(2)], share)
+        solved = either(*[dot(shifted, blocks[pair, one, 0]) for one in range(2)], share)
         out[at : at + 2 * share] = solved.astype(BF16)
 
 
 def backward_kernel(
-    level, share, top, owners, weights, mates, spread, solved, solved_mate, held, came, result, *outs
+    level, share, top, owners, weights, mates, spread, solved, solved_mate, held, came, result, *rest
 ):
-    rows = weights.shape[1]
-    count = 2 * rows
-    span = count * share
+    *outs, blocks, blocks_mate, sems, sems_mate = rest
+    copies = fetches(level, owners, weights, blocks, sems)
+    if outs:
+        copies_mate = fetches(level, owners, mates, blocks_mate, sems_mate)
+    span = result.shape[0]
     side = 2 * owners[owners.shape[0] - 1]
     side = side if level % 2 else 2 - side
     if not top:
         folded = (held[:span] + came[span:]).astype(BF16)
         folded_mate = (held[span:] + came[:span]).astype(BF16)
     pushes = [[], [], []]
-    for pair in range(count // 2):
-        half, row = divmod(2 * pair, rows)
-        owner = owners[2 * level + half]
+    for pair in range(blocks.shape[0]):
         at = slice(2 * share * pair, 2 * share * (pair + 1))
 
-        def both(product, vector, blocks, kind):
-            return either(*[product(vector, blocks[owner, row + one, kind]) for one in range(2)], share)
+        def both(product, vector, source, kind):
+            return either(*[product(vector, source[pair, one, kind]) for one in range(2)], share)
 
         done, done_mate = solved[at], solved_mate[at]
+        copies[pair].wait()
         if not top:
-            done = (done.astype(F32) - both(dot, folded[at], weights, 0)).astype(BF16)
+            done = (done.astype(F32) - both(dot, folded[at], blocks, 0)).astype(BF16)
         result[at] = done
         if outs:
+            pushes[0].append(both(dot_t, done, blocks, 2))
+            pushes[2].append(both(dot_t, done, blocks, 1 + side))
+            copies_mate[pair].wait()
             if not top:
-                done_mate = done_mate.astype(F32) - both(dot, folded_mate[at], mates, 0)
+                done_mate = done_mate.astype(F32) - both(dot, folded_mate[at], blocks_mate, 0)
                 done_mate = done_mate.astype(BF16)
-            pushes[0].append(both(dot_t, done, weights, 2))
-            pushes[1].append(both(dot_t, done_mate, mates, 1))
-            pushes[2].append(both(dot_t, done, weights, 1 + side))
+            pushes[1].append(both(dot_t, done_mate, blocks_mate, 1))
     if outs:
         pushed = jnp.concatenate(pushes[0] + pushes[1] + pushes[2], axis=0).astype(BF16)
         outs[0][...] = dot(spread[level], pushed)
 
 
-def call(kernel, outs, owners, *rest):
+def call(kernel, outs, owners, blocks, *rest):
     vmem = pl.BlockSpec(memory_space=pltpu.VMEM)
+    hbm = pl.BlockSpec(memory_space=pltpu.HBM)
+    pairs = blocks[0].shape[1]
     return pl.pallas_call(
         kernel,
         out_shape=outs,
-        in_specs=[pl.BlockSpec(memory_space=pltpu.SMEM)] + [vmem] * len(rest),
+        in_specs=[pl.BlockSpec(memory_space=pltpu.SMEM)] + [hbm] * len(blocks) + [vmem] * len(rest),
         out_specs=[vmem] * len(outs),
-        compiler_params=pltpu.CompilerParams(vmem_limit_bytes=32 * 2**20),
-    )(owners, *rest)
+        scratch_shapes=[
+            *[pltpu.VMEM((pairs, 2) + block.shape[2:], block.dtype) for block in blocks],
+            *[pltpu.SemaphoreType.DMA((pairs,)) for _ in blocks],
+        ],
+        compiler_params=pltpu.CompilerParams(vmem_limit_bytes=8 * 2**20),
+    )(owners, *[pltpu.with_memory_space_constraint(block, pltpu.HBM) for block in blocks], *rest)
 
 
 def local(right_side, diag_inverse, off_blocks, columns, plan):
@@ -116,8 +133,6 @@
     by_near = lax.ppermute(mates, "dom", near_pairs)
     by_far = lax.ppermute(mates, "dom", far_pairs)
     mates = jnp.where(own_level % 2 == 1, by_near, by_far)
-    mates, weights = lax.optimization_barrier((mates, weights))
-    mates = lax.all_gather(mates, "level")
 
     first = jnp.einsum("rkb,rbc->rkc", right_side, diag_inverse, preferred_element_type=F32)
     side = jnp.where(own_level == 0, first.astype(BF16), right_side)
@@ -176,9 +191,12 @@
         own = solved[-1]
         far = lax.ppermute(own, "dom", far_pairs)
         near = lax.ppermute(own, "dom", near_pairs)
+        if level == 1:
+            mates, far, near = lax.optimization_barrier((mates, far, near))
+            mates = lax.all_gather(mates, "level")
         around.append(near if level % 2 == 0 else far)
         kernel = functools.partial(forward_kernel, level, share)
-        solved += call(kernel, [vector], owners, weights, pick, side, far, own, near)
+        solved += call(kernel, [vector], owners, [weights], pick, side, far, own, near)
     around.append(lax.ppermute(solved[-1], "dom", near_pairs))
 
     held = came = jnp.zeros(summed.shape, F32)
@@ -187,7 +205,7 @@
         kernel = functools.partial(backward_kernel, level, share, level == levels - 1)
         outs = [vector, summed] if level else [vector]
         result, *rest = call(
-            kernel, outs, owners, weights, mates, spread, solved[level], around[level], held, came
+            kernel, outs, owners, [weights, mates], spread, solved[level], around[level], held, came
         )
         results.append(result)
         if level:

time: 296 us -> 269 us (0.909)
  waiting for transfers between devices: 88.7 us -> 52.2 us
  Pallas kernels: 20.7 us -> 46.2 us
  local copies, waits for them, and re-layouts: 36.5 us -> 17.3 us
  starting transfers between devices: 88.8 us -> 95.5 us
  blocking collectives: 34.2 us -> 29.8 us
    all_gather x1, waiting for transfers between devices: 36.9 us -> 4.22 us  [local(): weights = lax.all_gather(weights, 'level')]
    pallas_call x15, Pallas kernels: 20.7 us -> 46.2 us  [call(): pl.pallas_call(kernel, out_shape=outs, in_specs=[pl.BlockSpec(memory_spac...]
    unnamed x30 -> x16, local copies, waits for them, and re-layouts: 19.4 us -> 0.12 us
    all_to_all x1, waiting for transfers between devices: 0.01 us -> 7.81 us  [local(): side = lax.all_to_all(side, 'level', 1, 0, tiled=False)]
    ppermute x7, starting transfers between devices: 19.3 us -> 25.7 us  [local(): came = lax.ppermute(held, 'dom', far_pairs if level % 2 else near_pairs)]
    ppermute x7, waiting for transfers between devices: 26.8 us -> 20.3 us  [local(): came = lax.ppermute(held, 'dom', far_pairs if level % 2 else near_pairs)]
    ppermute x1, waiting for transfers between devices: 5.68 us -> 0.01 us  [local(): by_far = lax.ppermute(mates, 'dom', far_pairs)]
    all_to_all x1, blocking collectives: 34.2 us -> 29.8 us  [local(): both = lax.all_to_all(both, 'level', 1, 0, tiled=False)]
  transfers between devices with their start and end apart: 27 -> 27, of which waited for: 19 -> 19; matrix products, arithmetic and copies ran while one was open for 7% -> 8% of each run, Pallas kernels for 3% -> 7%
where the time goes in v4:
time: 269 us; the launch traced here: 267 us
  starting transfers between devices  95.5 us (36%)
  waiting for transfers between devices  52.2 us (19%)
  Pallas kernels  46.2 us (17%)
  blocking collectives  29.8 us (11%)
  between operations  17.5 us (7%)
  local copies, waits for them, and re-layouts  17.3 us (6%)
  other arithmetic  7.64 us (3%)
    pallas_call x15, Pallas kernels, call(): pl.pallas_call(kernel, out_shape=outs, in_specs=[pl.BlockSpec(memory_spac...  46.2 us
    ppermute x7, starting transfers between devices, local(): far = lax.ppermute(own, 'dom', far_pairs)  30.2 us
    all_to_all x1, blocking collectives, local(): both = lax.all_to_all(both, 'level', 1, 0, tiled=False)  29.8 us
    ppermute x7, starting transfers between devices, local(): came = lax.ppermute(held, 'dom', far_pairs if level % 2 else near_pairs)  25.7 us
    ppermute x7, waiting for transfers between devices, local(): came = lax.ppermute(held, 'dom', far_pairs if level % 2 else near_pairs)  20.3 us
    ppermute x7, starting transfers between devices, local(): near = lax.ppermute(own, 'dom', near_pairs)  13.4 us
    ppermute x1, starting transfers between devices, local(): by_far = lax.ppermute(mates, 'dom', far_pairs)  11 us
    ppermute x7, waiting for transfers between devices, local(): far = lax.ppermute(own, 'dom', far_pairs)  10.7 us
  transfers between devices with their start and end apart: 27, of which 19 were waited for; matrix products, arithmetic and copies ran while one was open for 8% of the time, Pallas kernels for 7%

profile of v4, /device:TPU:1, one launch (start us, length us, event | category | flops | bytes accessed | tf_op | source)
XLA Modules:
  0.0 267.3 jit_solution(10064944376890771694)
XLA Ops:
  7.2 1.9 pad_maximum_fusion
  15.0 4.8 %collective-permute-start = (bf16[4,2,128,128]{3,2,1,0:T(8,128)(2,1)S(1)}, bf16[4,2,128,128]{3,2,1,0:T(8,128)(2,1)S(1)}, u32[]{:S(2)}, u32[]{:S(2)}) collective-permute-start(bf16[4,2,128,128]{3,2,1,0:T(8,128)(2,1)S(1)} %pad_maximum_fusion.1), channel_id=1, source_target_pairs={{0,16},{16,0},{32,48},{48,32},{64,80},{80,64},{96,112},{112,96},{1... | collective-permute-start | bytes 786440 | tf_op jit(solution)/shard_map/ppermute | solution.py:133
  19.9 11.0 %collective-permute-start.1 = (bf16[4,2,128,128]{3,2,1,0:T(8,128)(2,1)S(1)}, bf16[4,2,128,128]{3,2,1,0:T(8,128)(2,1)S(1)}, u32[]{:S(2)}, u32[]{:S(2)}) collective-permute-start(bf16[4,2,128,128]{3,2,1,0:T(8,128)(2,1)S(1)} %pad_maximum_fusion.1), channel_id=1, source_target_pairs={{16,32},{32,16},{48,64},{64,48},{80,96},{96,80},{112,128},{128,112... | collective-permute-start | bytes 786440 | tf_op jit(solution)/shard_map/ppermute | solution.py:134
  32.7 8.3 %all-to-all-start = ((bf16[1,4,16,4,128]{4,3,1,0,2:T(4,128)(2,1)}), bf16[1,4,16,4,128]{4,3,1,0,2:T(4,128)(2,1)S(1)}, u32[]{:S(2)}, u32[]{:S(2)}) async-start(bf16[1,4,16,4,128]{4,3,1,0,2:T(4,128)(2,1)} %copy.84), calls=%async_computation | async-start | bytes 131072 | tf_op jit(solution)/shard_map/all_to_all | solution.py:140
  41.9 7.8 %all-to-all-done = bf16[1,4,16,4,128]{4,3,1,0,2:T(4,128)(2,1)S(1)} async-done(((bf16[1,4,16,4,128]{4,3,1,0,2:T(4,128)(2,1)}), bf16[1,4,16,4,128]{4,3,1,0,2:T(4,128)(2,1)S(1)}, u32[]{:S(2)}, u32[]{:S(2)}) %all-to-all-start) | async-done | bytes 65568 | tf_op jit(solution)/shard_map/all_to_all | solution.py:140
  50.3 1.9 collective-permute-start.2
  52.2 1.9 collective-permute-start.3
  54.9 3.1 %collective-permute-done.2.far.solved_mate = bf16[32,128]{1,0:T(8,128)(2,1)S(1)} collective-permute-done((bf16[32,128]{1,0:T(8,128)(2,1)S(1)}, bf16[32,128]{1,0:T(8,128)(2,1)S(1)}, u32[]{:S(2)}, u32[]{:S(2)}) %collective-permute-start.2) | collective-permute-done | bytes 8224 | tf_op jit(solution)/shard_map/ppermute | solution.py:192
  71.5 4.2 %all-gather.5.cloned.1.call-done = bf16[64,4,128,128]{3,2,1,0:T(8,128)(2,1)} async-done(((bf16[4,4,128,128]{3,2,1,0:T(8,128)(2,1)}), bf16[64,4,128,128]{3,2,1,0:T(8,128)(2,1)}) %all-gather.5.cloned.1.call-update) | async-done | bytes 8388624 | tf_op jit(solution)/shard_map/all_gather | solution.py:123
  75.7 2.6 shard_map.68.own.solved
  78.3 7.7 %collective-permute-start.4 = (bf16[32,128]{1,0:T(8,128)(2,1)S(1)}, bf16[32,128]{1,0:T(8,128)(2,1)S(1)}, u32[]{:S(2)}, u32[]{:S(2)}) collective-permute-start(bf16[32,128]{1,0:T(8,128)(2,1)S(1)} %shard_map.68.own.solved), channel_id=1, source_target_pairs={{16,32},{32,16},{48,64},{64,48},{80,96},{96,80},{112,128},{128,112... | collective-permute-start | bytes 24584 | tf_op jit(solution)/shard_map/ppermute | solution.py:192
  88.0 2.4 collective-permute-done.5.near.solved_mate
  90.4 2.6 shard_map.69.own.solved
  93.0 3.3 %collective-permute-start.6 = (bf16[32,128]{1,0:T(8,128)(2,1)S(1)}, bf16[32,128]{1,0:T(8,128)(2,1)S(1)}, u32[]{:S(2)}, u32[]{:S(2)}) collective-permute-start(bf16[32,128]{1,0:T(8,128)(2,1)S(1)} %shard_map.69.own.solved), channel_id=1, source_target_pairs={{16,32},{32,16},{48,64},{64,48},{80,96},{96,80},{112,128},{128,112... | collective-permute-start | bytes 24584 | tf_op jit(solution)/shard_map/ppermute | solution.py:192
  98.4 2.3 collective-permute-done.6.far.solved_mate
  100.9 2.6 shard_map.70.own.solved
  103.5 5.5 %collective-permute-start.8 = (bf16[32,128]{1,0:T(8,128)(2,1)S(1)}, bf16[32,128]{1,0:T(8,128)(2,1)S(1)}, u32[]{:S(2)}, u32[]{:S(2)}) collective-permute-start(bf16[32,128]{1,0:T(8,128)(2,1)S(1)} %shard_map.70.own.solved), channel_id=1, source_target_pairs={{16,32},{32,16},{48,64},{64,48},{80,96},{96,80},{112,128},{128,112... | collective-permute-start | bytes 24584 | tf_op jit(solution)/shard_map/ppermute | solution.py:192
  113.9 2.6 shard_map.71.own.solved
  116.5 3.1 %collective-permute-start.10 = (bf16[32,128]{1,0:T(8,128)(2,1)S(1)}, bf16[32,128]{1,0:T(8,128)(2,1)S(1)}, u32[]{:S(2)}, u32[]{:S(2)}) collective-permute-start(bf16[32,128]{1,0:T(8,128)(2,1)S(1)} %shard_map.71.own.solved), channel_id=1, source_target_pairs={{16,32},{32,16},{48,64},{64,48},{80,96},{96,80},{112,128},{128,112... | collective-permute-start | bytes 24584 | tf_op jit(solution)/shard_map/ppermute | solution.py:192
  121.5 2.6 collective-permute-done.10.far.solved_mate
  124.2 2.6 shard_map.72.own.solved
  126.8 5.3 %collective-permute-start.12 = (bf16[32,128]{1,0:T(8,128)(2,1)S(1)}, bf16[32,128]{1,0:T(8,128)(2,1)S(1)}, u32[]{:S(2)}, u32[]{:S(2)}) collective-permute-start(bf16[32,128]{1,0:T(8,128)(2,1)S(1)} %shard_map.72.own.solved), channel_id=1, source_target_pairs={{16,32},{32,16},{48,64},{64,48},{80,96},{96,80},{112,128},{128,112... | collective-permute-start | bytes 24584 | tf_op jit(solution)/shard_map/ppermute | solution.py:192
  134.5 2.0 collective-permute-done.13.near.solved_mate
  136.5 2.6 shard_map.73.own.solved
  139.1 3.3 %collective-permute-start.14 = (bf16[32,128]{1,0:T(8,128)(2,1)S(1)}, bf16[32,128]{1,0:T(8,128)(2,1)S(1)}, u32[]{:S(2)}, u32[]{:S(2)}) collective-permute-start(bf16[32,128]{1,0:T(8,128)(2,1)S(1)} %shard_map.73.own.solved), channel_id=1, source_target_pairs={{16,32},{32,16},{48,64},{64,48},{80,96},{96,80},{112,128},{128,112... | collective-permute-start | bytes 24584 | tf_op jit(solution)/shard_map/ppermute | solution.py:192
  144.5 2.4 collective-permute-done.14.far.solved_mate
  146.8 2.6 shard_map.74.solved
  151.4 2.7 %collective-permute-done.16.solved_mate = bf16[32,128]{1,0:T(8,128)(2,1)S(1)} collective-permute-done((bf16[32,128]{1,0:T(8,128)(2,1)S(1)}, bf16[32,128]{1,0:T(8,128)(2,1)S(1)}, u32[]{:S(2)}, u32[]{:S(2)}) %collective-permute-start.16) | collective-permute-done | bytes 8224 | tf_op jit(solution)/shard_map/ppermute | solution.py:200
  154.1 3.0 %shard_map.75 = (bf16[32,128]{1,0:T(8,128)(2,1)S(1)}, f32[64,128]{1,0:T(8,128)S(1)}) custom-call(s32[17]{0:T(128)S(1)} %pad_add_fusion.owners, bf16[16,4,4,128,128]{4,3,2,1,0:T(8,128)(2,1)} %bitcast.106, bf16[16,4,2,128,128]{4,3,2,1,0:T(8,128)(2,1)} %bitcast.114, bf16[8,64,96]{2,1,0:T(8,128)(2,1)S(1)} %pad_maximum_fusion.2.spread, ...), custom_call_target="tpu_custom_call" | custom-call | tf_op jit(solution)/shard_map/pallas_call | solution.py:97
  157.2 5.0 %collective-permute-start.17 = (f32[64,128]{1,0:T(8,128)S(1)}, f32[64,128]{1,0:T(8,128)S(1)}, u32[]{:S(2)}, u32[]{:S(2)}) collective-permute-start(f32[64,128]{1,0:T(8,128)S(1)} %get-tuple-element.22.held), channel_id=1, source_target_pairs={{16,32},{32,16},{48,64},{64,48},{80,96},{96,80},{112,128},{128,112... | collective-permute-start | bytes 98312 | tf_op jit(solution)/shard_map/ppermute | solution.py:213
  162.2 3.0 %collective-permute-done.17.came = f32[64,128]{1,0:T(8,128)S(1)} collective-permute-done((f32[64,128]{1,0:T(8,128)S(1)}, f32[64,128]{1,0:T(8,128)S(1)}, u32[]{:S(2)}, u32[]{:S(2)}) %collective-permute-start.17) | collective-permute-done | bytes 32800 | tf_op jit(solution)/shard_map/ppermute | solution.py:213
  165.1 3.8 %shard_map.76 = (bf16[32,128]{1,0:T(8,128)(2,1)S(1)}, f32[64,128]{1,0:T(8,128)S(1)}) custom-call(s32[17]{0:T(128)S(1)} %pad_add_fusion.owners, bf16[16,4,4,128,128]{4,3,2,1,0:T(8,128)(2,1)} %bitcast.107, bf16[16,4,2,128,128]{4,3,2,1,0:T(8,128)(2,1)} %bitcast.115, bf16[8,64,96]{2,1,0:T(8,128)(2,1)S(1)} %pad_maximum_fusion.2.spread, ...), custom_call_target="tpu_custom_call" | custom-call | tf_op jit(solution)/shard_map/pallas_call | solution.py:97
  170.9 3.0 %collective-permute-done.18.came = f32[64,128]{1,0:T(8,128)S(1)} collective-permute-done((f32[64,128]{1,0:T(8,128)S(1)}, f32[64,128]{1,0:T(8,128)S(1)}, u32[]{:S(2)}, u32[]{:S(2)}) %collective-permute-start.18) | collective-permute-done | bytes 32800 | tf_op jit(solution)/shard_map/ppermute | solution.py:213
  173.9 3.8 %shard_map.77 = (bf16[32,128]{1,0:T(8,128)(2,1)S(1)}, f32[64,128]{1,0:T(8,128)S(1)}) custom-call(s32[17]{0:T(128)S(1)} %pad_add_fusion.owners, bf16[16,4,4,128,128]{4,3,2,1,0:T(8,128)(2,1)} %bitcast.108, bf16[16,4,2,128,128]{4,3,2,1,0:T(8,128)(2,1)} %bitcast.116, bf16[8,64,96]{2,1,0:T(8,128)(2,1)S(1)} %pad_maximum_fusion.2.spread, ...), custom_call_target="tpu_custom_call" | custom-call | tf_op jit(solution)/shard_map/pallas_call | solution.py:97
  177.7 5.0 %collective-permute-start.19 = (f32[64,128]{1,0:T(8,128)S(1)}, f32[64,128]{1,0:T(8,128)S(1)}, u32[]{:S(2)}, u32[]{:S(2)}) collective-permute-start(f32[64,128]{1,0:T(8,128)S(1)} %get-tuple-element.24.held), channel_id=1, source_target_pairs={{16,32},{32,16},{48,64},{64,48},{80,96},{96,80},{112,128},{128,112... | collective-permute-start | bytes 98312 | tf_op jit(solution)/shard_map/ppermute | solution.py:213
  182.7 3.0 %collective-permute-done.19.came = f32[64,128]{1,0:T(8,128)S(1)} collective-permute-done((f32[64,128]{1,0:T(8,128)S(1)}, f32[64,128]{1,0:T(8,128)S(1)}, u32[]{:S(2)}, u32[]{:S(2)}) %collective-permute-start.19) | collective-permute-done | bytes 32800 | tf_op jit(solution)/shard_map/ppermute | solution.py:213
  185.7 3.8 %shard_map.78 = (bf16[32,128]{1,0:T(8,128)(2,1)S(1)}, f32[64,128]{1,0:T(8,128)S(1)}) custom-call(s32[17]{0:T(128)S(1)} %pad_add_fusion.owners, bf16[16,4,4,128,128]{4,3,2,1,0:T(8,128)(2,1)} %bitcast.109, bf16[16,4,2,128,128]{4,3,2,1,0:T(8,128)(2,1)} %bitcast.117, bf16[8,64,96]{2,1,0:T(8,128)(2,1)S(1)} %pad_maximum_fusion.2.spread, ...), custom_call_target="tpu_custom_call" | custom-call | tf_op jit(solution)/shard_map/pallas_call | solution.py:97
  191.5 2.7 %collective-permute-done.20.came = f32[64,128]{1,0:T(8,128)S(1)} collective-permute-done((f32[64,128]{1,0:T(8,128)S(1)}, f32[64,128]{1,0:T(8,128)S(1)}, u32[]{:S(2)}, u32[]{:S(2)}) %collective-permute-start.20) | collective-permute-done | bytes 32800 | tf_op jit(solution)/shard_map/ppermute | solution.py:213
  194.2 3.8 %shard_map.79 = (bf16[32,128]{1,0:T(8,128)(2,1)S(1)}, f32[64,128]{1,0:T(8,128)S(1)}) custom-call(s32[17]{0:T(128)S(1)} %pad_add_fusion.owners, bf16[16,4,4,128,128]{4,3,2,1,0:T(8,128)(2,1)} %bitcast.110, bf16[16,4,2,128,128]{4,3,2,1,0:T(8,128)(2,1)} %bitcast.118, bf16[8,64,96]{2,1,0:T(8,128)(2,1)S(1)} %pad_maximum_fusion.2.spread, ...), custom_call_target="tpu_custom_call" | custom-call | tf_op jit(solution)/shard_map/pallas_call | solution.py:97
  198.0 5.0 %collective-permute-start.21 = (f32[64,128]{1,0:T(8,128)S(1)}, f32[64,128]{1,0:T(8,128)S(1)}, u32[]{:S(2)}, u32[]{:S(2)}) collective-permute-start(f32[64,128]{1,0:T(8,128)S(1)} %get-tuple-element.26.held), channel_id=1, source_target_pairs={{16,32},{32,16},{48,64},{64,48},{80,96},{96,80},{112,128},{128,112... | collective-permute-start | bytes 98312 | tf_op jit(solution)/shard_map/ppermute | solution.py:213
  203.0 3.0 %collective-permute-done.21.came = f32[64,128]{1,0:T(8,128)S(1)} collective-permute-done((f32[64,128]{1,0:T(8,128)S(1)}, f32[64,128]{1,0:T(8,128)S(1)}, u32[]{:S(2)}, u32[]{:S(2)}) %collective-permute-start.21) | collective-permute-done | bytes 32800 | tf_op jit(solution)/shard_map/ppermute | solution.py:213
  206.0 3.8 %shard_map.80 = (bf16[32,128]{1,0:T(8,128)(2,1)S(1)}, f32[64,128]{1,0:T(8,128)S(1)}) custom-call(s32[17]{0:T(128)S(1)} %pad_add_fusion.owners, bf16[16,4,4,128,128]{4,3,2,1,0:T(8,128)(2,1)} %bitcast.111, bf16[16,4,2,128,128]{4,3,2,1,0:T(8,128)(2,1)} %bitcast.119, bf16[8,64,96]{2,1,0:T(8,128)(2,1)S(1)} %pad_maximum_fusion.2.spread, ...), custom_call_target="tpu_custom_call" | custom-call | tf_op jit(solution)/shard_map/pallas_call | solution.py:97
  211.8 2.7 %collective-permute-done.22.came = f32[64,128]{1,0:T(8,128)S(1)} collective-permute-done((f32[64,128]{1,0:T(8,128)S(1)}, f32[64,128]{1,0:T(8,128)S(1)}, u32[]{:S(2)}, u32[]{:S(2)}) %collective-permute-start.22) | collective-permute-done | bytes 32800 | tf_op jit(solution)/shard_map/ppermute | solution.py:213
  214.5 3.8 %shard_map.81 = (bf16[32,128]{1,0:T(8,128)(2,1)S(1)}, f32[64,128]{1,0:T(8,128)S(1)}) custom-call(s32[17]{0:T(128)S(1)} %pad_add_fusion.owners, bf16[16,4,4,128,128]{4,3,2,1,0:T(8,128)(2,1)} %bitcast.112, bf16[16,4,2,128,128]{4,3,2,1,0:T(8,128)(2,1)} %bitcast.120, bf16[8,64,96]{2,1,0:T(8,128)(2,1)S(1)} %pad_maximum_fusion.2.spread, ...), custom_call_target="tpu_custom_call" | custom-call | tf_op jit(solution)/shard_map/pallas_call | solution.py:97
  218.3 5.0 %collective-permute-start.23 = (f32[64,128]{1,0:T(8,128)S(1)}, f32[64,128]{1,0:T(8,128)S(1)}, u32[]{:S(2)}, u32[]{:S(2)}) collective-permute-start(f32[64,128]{1,0:T(8,128)S(1)} %get-tuple-element.28.held), channel_id=1, source_target_pairs={{16,32},{32,16},{48,64},{64,48},{80,96},{96,80},{112,128},{128,112... | collective-permute-start | bytes 98312 | tf_op jit(solution)/shard_map/ppermute | solution.py:213
  223.3 3.0 %collective-permute-done.23.came = f32[64,128]{1,0:T(8,128)S(1)} collective-permute-done((f32[64,128]{1,0:T(8,128)S(1)}, f32[64,128]{1,0:T(8,128)S(1)}, u32[]{:S(2)}, u32[]{:S(2)}) %collective-permute-start.23) | collective-permute-done | bytes 32800 | tf_op jit(solution)/shard_map/ppermute | solution.py:213
  226.3 2.1 shard_map.82
  229.2 29.8 %all_to_all.30 = bf16[1,2,16,4,4,128]{5,4,3,1,0,2:T(4,128)(2,1)S(1)} all-to-all(bf16[1,2,16,4,4,128]{5,4,3,1,0,2:T(4,128)(2,1)S(1)} %bitcast.130), channel_id=1, replica_groups=mesh['dom'=32,'level'=16] {'level'}, dimensions={2} | all-to-all | bytes 262144 | tf_op jit(solution)/shard_map/all_to_all | solution.py:217
  (131 shorter events, 45.7 us)
Async XLA Ops:
  7.2 54.8 %copy-start = (s32[16]{0:T(128)S(1)}, s32[16]{0:T(128)}, u32[]{:S(2)}) copy-start(s32[16]{0:T(128)} %param.9) | copy-start | bytes 196
  7.2 68.5 %all-gather.5.cloned.1.call-start = ((), (), s32[]{:S(2)}) async-start(), calls=%async_computation.2 | async-start | bytes 8912896 | tf_op jit(solution)/shard_map/all_gather | solution.py:123
  15.0 39.1 %collective-permute-start = (bf16[4,2,128,128]{3,2,1,0:T(8,128)(2,1)S(1)}, bf16[4,2,128,128]{3,2,1,0:T(8,128)(2,1)S(1)}, u32[]{:S(2)}, u32[]{:S(2)}) collective-permute-start(bf16[4,2,128,128]{3,2,1,0:T(8,128)(2,1)S(1)} %pad_maximum_fusion.1), channel_id=1, source_target_pairs={{0,16},{16,0},{32,48},{48,32},{64,80},{80,64},{96,112},{112,96},{1... | collective-permute-start | bytes 786440 | tf_op jit(solution)/shard_map/ppermute | solution.py:133
  19.9 34.3 %collective-permute-start.1 = (bf16[4,2,128,128]{3,2,1,0:T(8,128)(2,1)S(1)}, bf16[4,2,128,128]{3,2,1,0:T(8,128)(2,1)S(1)}, u32[]{:S(2)}, u32[]{:S(2)}) collective-permute-start(bf16[4,2,128,128]{3,2,1,0:T(8,128)(2,1)S(1)} %pad_maximum_fusion.1), channel_id=1, source_target_pairs={{16,32},{32,16},{48,64},{64,48},{80,96},{96,80},{112,128},{128,112... | collective-permute-start | bytes 786440 | tf_op jit(solution)/shard_map/ppermute | solution.py:134
  32.7 17.0 %all-to-all-start = ((bf16[1,4,16,4,128]{4,3,1,0,2:T(4,128)(2,1)}), bf16[1,4,16,4,128]{4,3,1,0,2:T(4,128)(2,1)S(1)}, u32[]{:S(2)}, u32[]{:S(2)}) async-start(bf16[1,4,16,4,128]{4,3,1,0,2:T(4,128)(2,1)} %copy.84), calls=%async_computation | async-start | bytes 131072 | tf_op jit(solution)/shard_map/all_to_all | solution.py:140
  41.0 110.3 %all-gather.7.cloned.1.call-start = ((), (), s32[]{:S(2)}) async-start(), calls=%async_computation.3 | async-start | bytes 4456448 | tf_op jit(solution)/shard_map/all_gather | solution.py:196
  50.3 7.7 %collective-permute-start.2 = (bf16[32,128]{1,0:T(8,128)(2,1)S(1)}, bf16[32,128]{1,0:T(8,128)(2,1)S(1)}, u32[]{:S(2)}, u32[]{:S(2)}) collective-permute-start(bf16[32,128]{1,0:T(8,128)(2,1)S(1)} %bitcast.94), channel_id=1, source_target_pairs={{16,32},{32,16},{48,64},{64,48},{80,96},{96,80},{112,128},{128,112... | collective-permute-start | bytes 24584 | tf_op jit(solution)/shard_map/ppermute | solution.py:192
  52.2 5.8 %collective-permute-start.3 = (bf16[32,128]{1,0:T(8,128)(2,1)S(1)}, bf16[32,128]{1,0:T(8,128)(2,1)S(1)}, u32[]{:S(2)}, u32[]{:S(2)}) collective-permute-start(bf16[32,128]{1,0:T(8,128)(2,1)S(1)} %bitcast.95), channel_id=1, source_target_pairs={{0,16},{16,0},{32,48},{48,32},{64,80},{80,64},{96,112},{112,96},{1... | collective-permute-start | bytes 24584 | tf_op jit(solution)/shard_map/ppermute | solution.py:193
  78.3 9.7 %collective-permute-start.4 = (bf16[32,128]{1,0:T(8,128)(2,1)S(1)}, bf16[32,128]{1,0:T(8,128)(2,1)S(1)}, u32[]{:S(2)}, u32[]{:S(2)}) collective-permute-start(bf16[32,128]{1,0:T(8,128)(2,1)S(1)} %shard_map.68.own.solved), channel_id=1, source_target_pairs={{16,32},{32,16},{48,64},{64,48},{80,96},{96,80},{112,128},{128,112... | collective-permute-start | bytes 24584 | tf_op jit(solution)/shard_map/ppermute | solution.py:192
  86.0 4.4 %collective-permute-start.5 = (bf16[32,128]{1,0:T(8,128)(2,1)S(1)}, bf16[32,128]{1,0:T(8,128)(2,1)S(1)}, u32[]{:S(2)}, u32[]{:S(2)}) collective-permute-start(bf16[32,128]{1,0:T(8,128)(2,1)S(1)} %shard_map.68.own.solved), channel_id=1, source_target_pairs={{0,16},{16,0},{32,48},{48,32},{64,80},{80,64},{96,112},{112,96},{1... | collective-permute-start | bytes 24584 | tf_op jit(solution)/shard_map/ppermute | solution.py:193
  93.0 7.7 %collective-permute-start.6 = (bf16[32,128]{1,0:T(8,128)(2,1)S(1)}, bf16[32,128]{1,0:T(8,128)(2,1)S(1)}, u32[]{:S(2)}, u32[]{:S(2)}) collective-permute-start(bf16[32,128]{1,0:T(8,128)(2,1)S(1)} %shard_map.69.own.solved), channel_id=1, source_target_pairs={{16,32},{32,16},{48,64},{64,48},{80,96},{96,80},{112,128},{128,112... | collective-permute-start | bytes 24584 | tf_op jit(solution)/shard_map/ppermute | solution.py:192
  96.4 4.6 %collective-permute-start.7 = (bf16[32,128]{1,0:T(8,128)(2,1)S(1)}, bf16[32,128]{1,0:T(8,128)(2,1)S(1)}, u32[]{:S(2)}, u32[]{:S(2)}) collective-permute-start(bf16[32,128]{1,0:T(8,128)(2,1)S(1)} %shard_map.69.own.solved), channel_id=1, source_target_pairs={{0,16},{16,0},{32,48},{48,32},{64,80},{80,64},{96,112},{112,96},{1... | collective-permute-start | bytes 24584 | tf_op jit(solution)/shard_map/ppermute | solution.py:193
  103.5 8.6 %collective-permute-start.8 = (bf16[32,128]{1,0:T(8,128)(2,1)S(1)}, bf16[32,128]{1,0:T(8,128)(2,1)S(1)}, u32[]{:S(2)}, u32[]{:S(2)}) collective-permute-start(bf16[32,128]{1,0:T(8,128)(2,1)S(1)} %shard_map.70.own.solved), channel_id=1, source_target_pairs={{16,32},{32,16},{48,64},{64,48},{80,96},{96,80},{112,128},{128,112... | collective-permute-start | bytes 24584 | tf_op jit(solution)/shard_map/ppermute | solution.py:192
  109.1 4.8 %collective-permute-start.9 = (bf16[32,128]{1,0:T(8,128)(2,1)S(1)}, bf16[32,128]{1,0:T(8,128)(2,1)S(1)}, u32[]{:S(2)}, u32[]{:S(2)}) collective-permute-start(bf16[32,128]{1,0:T(8,128)(2,1)S(1)} %shard_map.70.own.solved), channel_id=1, source_target_pairs={{0,16},{16,0},{32,48},{48,32},{64,80},{80,64},{96,112},{112,96},{1... | collective-permute-start | bytes 24584 | tf_op jit(solution)/shard_map/ppermute | solution.py:193
  116.5 7.7 %collective-permute-start.10 = (bf16[32,128]{1,0:T(8,128)(2,1)S(1)}, bf16[32,128]{1,0:T(8,128)(2,1)S(1)}, u32[]{:S(2)}, u32[]{:S(2)}) collective-permute-start(bf16[32,128]{1,0:T(8,128)(2,1)S(1)} %shard_map.71.own.solved), channel_id=1, source_target_pairs={{16,32},{32,16},{48,64},{64,48},{80,96},{96,80},{112,128},{128,112... | collective-permute-start | bytes 24584 | tf_op jit(solution)/shard_map/ppermute | solution.py:192
  119.5 4.6 %collective-permute-start.11 = (bf16[32,128]{1,0:T(8,128)(2,1)S(1)}, bf16[32,128]{1,0:T(8,128)(2,1)S(1)}, u32[]{:S(2)}, u32[]{:S(2)}) collective-permute-start(bf16[32,128]{1,0:T(8,128)(2,1)S(1)} %shard_map.71.own.solved), channel_id=1, source_target_pairs={{0,16},{16,0},{32,48},{48,32},{64,80},{80,64},{96,112},{112,96},{1... | collective-permute-start | bytes 24584 | tf_op jit(solution)/shard_map/ppermute | solution.py:193
  126.8 7.7 %collective-permute-start.12 = (bf16[32,128]{1,0:T(8,128)(2,1)S(1)}, bf16[32,128]{1,0:T(8,128)(2,1)S(1)}, u32[]{:S(2)}, u32[]{:S(2)}) collective-permute-start(bf16[32,128]{1,0:T(8,128)(2,1)S(1)} %shard_map.72.own.solved), channel_id=1, source_target_pairs={{16,32},{32,16},{48,64},{64,48},{80,96},{96,80},{112,128},{128,112... | collective-permute-start | bytes 24584 | tf_op jit(solution)/shard_map/ppermute | solution.py:192
  132.1 4.4 %collective-permute-start.13 = (bf16[32,128]{1,0:T(8,128)(2,1)S(1)}, bf16[32,128]{1,0:T(8,128)(2,1)S(1)}, u32[]{:S(2)}, u32[]{:S(2)}) collective-permute-start(bf16[32,128]{1,0:T(8,128)(2,1)S(1)} %shard_map.72.own.solved), channel_id=1, source_target_pairs={{0,16},{16,0},{32,48},{48,32},{64,80},{80,64},{96,112},{112,96},{1... | collective-permute-start | bytes 24584 | tf_op jit(solution)/shard_map/ppermute | solution.py:193
  139.1 7.7 %collective-permute-start.14 = (bf16[32,128]{1,0:T(8,128)(2,1)S(1)}, bf16[32,128]{1,0:T(8,128)(2,1)S(1)}, u32[]{:S(2)}, u32[]{:S(2)}) collective-permute-start(bf16[32,128]{1,0:T(8,128)(2,1)S(1)} %shard_map.73.own.solved), channel_id=1, source_target_pairs={{16,32},{32,16},{48,64},{64,48},{80,96},{96,80},{112,128},{128,112... | collective-permute-start | bytes 24584 | tf_op jit(solution)/shard_map/ppermute | solution.py:192
  142.4 4.4 %collective-permute-start.15 = (bf16[32,128]{1,0:T(8,128)(2,1)S(1)}, bf16[32,128]{1,0:T(8,128)(2,1)S(1)}, u32[]{:S(2)}, u32[]{:S(2)}) collective-permute-start(bf16[32,128]{1,0:T(8,128)(2,1)S(1)} %shard_map.73.own.solved), channel_id=1, source_target_pairs={{0,16},{16,0},{32,48},{48,32},{64,80},{80,64},{96,112},{112,96},{1... | collective-permute-start | bytes 24584 | tf_op jit(solution)/shard_map/ppermute | solution.py:193
  149.4 4.7 %collective-permute-start.16 = (bf16[32,128]{1,0:T(8,128)(2,1)S(1)}, bf16[32,128]{1,0:T(8,128)(2,1)S(1)}, u32[]{:S(2)}, u32[]{:S(2)}) collective-permute-start(bf16[32,128]{1,0:T(8,128)(2,1)S(1)} %shard_map.74.solved), channel_id=1, source_target_pairs={{0,16},{16,0},{32,48},{48,32},{64,80},{80,64},{96,112},{112,96},{1... | collective-permute-start | bytes 24584 | tf_op jit(solution)/shard_map/ppermute | solution.py:200
  157.2 8.0 %collective-permute-start.17 = (f32[64,128]{1,0:T(8,128)S(1)}, f32[64,128]{1,0:T(8,128)S(1)}, u32[]{:S(2)}, u32[]{:S(2)}) collective-permute-start(f32[64,128]{1,0:T(8,128)S(1)} %get-tuple-element.22.held), channel_id=1, source_target_pairs={{16,32},{32,16},{48,64},{64,48},{80,96},{96,80},{112,128},{128,112... | collective-permute-start | bytes 98312 | tf_op jit(solution)/shard_map/ppermute | solution.py:213
  169.0 5.0 %collective-permute-start.18 = (f32[64,128]{1,0:T(8,128)S(1)}, f32[64,128]{1,0:T(8,128)S(1)}, u32[]{:S(2)}, u32[]{:S(2)}) collective-permute-start(f32[64,128]{1,0:T(8,128)S(1)} %get-tuple-element.23.held), channel_id=1, source_target_pairs={{0,16},{16,0},{32,48},{48,32},{64,80},{80,64},{96,112},{112,96},{1... | collective-permute-start | bytes 98312 | tf_op jit(solution)/shard_map/ppermute | solution.py:213
  177.7 8.0 %collective-permute-start.19 = (f32[64,128]{1,0:T(8,128)S(1)}, f32[64,128]{1,0:T(8,128)S(1)}, u32[]{:S(2)}, u32[]{:S(2)}) collective-permute-start(f32[64,128]{1,0:T(8,128)S(1)} %get-tuple-element.24.held), channel_id=1, source_target_pairs={{16,32},{32,16},{48,64},{64,48},{80,96},{96,80},{112,128},{128,112... | collective-permute-start | bytes 98312 | tf_op jit(solution)/shard_map/ppermute | solution.py:213
  189.5 4.7 %collective-permute-start.20 = (f32[64,128]{1,0:T(8,128)S(1)}, f32[64,128]{1,0:T(8,128)S(1)}, u32[]{:S(2)}, u32[]{:S(2)}) collective-permute-start(f32[64,128]{1,0:T(8,128)S(1)} %get-tuple-element.25.held), channel_id=1, source_target_pairs={{0,16},{16,0},{32,48},{48,32},{64,80},{80,64},{96,112},{112,96},{1... | collective-permute-start | bytes 98312 | tf_op jit(solution)/shard_map/ppermute | solution.py:213
  198.0 8.0 %collective-permute-start.21 = (f32[64,128]{1,0:T(8,128)S(1)}, f32[64,128]{1,0:T(8,128)S(1)}, u32[]{:S(2)}, u32[]{:S(2)}) collective-permute-start(f32[64,128]{1,0:T(8,128)S(1)} %get-tuple-element.26.held), channel_id=1, source_target_pairs={{16,32},{32,16},{48,64},{64,48},{80,96},{96,80},{112,128},{128,112... | collective-permute-start | bytes 98312 | tf_op jit(solution)/shard_map/ppermute | solution.py:213
  209.8 4.7 %collective-permute-start.22 = (f32[64,128]{1,0:T(8,128)S(1)}, f32[64,128]{1,0:T(8,128)S(1)}, u32[]{:S(2)}, u32[]{:S(2)}) collective-permute-start(f32[64,128]{1,0:T(8,128)S(1)} %get-tuple-element.27.held), channel_id=1, source_target_pairs={{0,16},{16,0},{32,48},{48,32},{64,80},{80,64},{96,112},{112,96},{1... | collective-permute-start | bytes 98312 | tf_op jit(solution)/shard_map/ppermute | solution.py:213
  218.3 8.0 %collective-permute-start.23 = (f32[64,128]{1,0:T(8,128)S(1)}, f32[64,128]{1,0:T(8,128)S(1)}, u32[]{:S(2)}, u32[]{:S(2)}) collective-permute-start(f32[64,128]{1,0:T(8,128)S(1)} %get-tuple-element.28.held), channel_id=1, source_target_pairs={{16,32},{32,16},{48,64},{64,48},{80,96},{96,80},{112,128},{128,112... | collective-permute-start | bytes 98312 | tf_op jit(solution)/shard_map/ppermute | solution.py:213
Sparse Core Ops, SparseCore 0:
  10.1 65.5 all-gather.4
  77.8 43.4 all-gather.6

commit v5 on v3

v5 whole, which is shorter than its diff:
```python
import functools

import jax
import jax.numpy as jnp
from jax import lax
from jax.experimental import pallas as pl
from jax.experimental.pallas import tpu as pltpu
from jax.sharding import PartitionSpec as P

BF16 = jnp.bfloat16
F32 = jnp.float32


def dot(a, b):
    return lax.dot_general(a, b, (((1,), (0,)), ((), ())), preferred_element_type=F32)


def dot_t(a, b):
    return lax.dot_general(a, b, (((1,), (1,)), ((), ())), preferred_element_type=F32)


def either(low, high, share):
    top = lax.broadcasted_iota(jnp.int32, low.shape, 0) < share
    return jnp.where(top, low, high)


def ones_where(condition):
    return jnp.where(condition, 1.0, 0.0).astype(BF16)


def forward_kernel(level, share, owners, weights, places, side, far, own, near, out):
    rows = weights.shape[1]
    span = out.shape[0]
    around = jnp.concatenate([far[...], own[...], near[...]], axis=0)
    at = lax.broadcasted_iota(jnp.int32, (3 * span, 3 * span), 1)
    picked = dot(ones_where(at == places[level]), around)
    for pair in range(rows):
        half, row = divmod(2 * pair, rows)
        owner = owners[2 * level + half]
        at = 2 * share * pair
        terms = [picked[n * span + at : n * span + at + 2 * share] for n in range(3)]
        terms = jnp.concatenate(terms, axis=1).astype(BF16)
        wide = [weights[owner, row + one, 1:].reshape(-1, out.shape[1]) for one in range(2)]
        total = either(*[dot(terms, block) for block in wide], share)
        shifted = (side[level, at : at + 2 * share].astype(F32) - total).astype(BF16)
        solved = either(*[dot(shifted, weights[owner, row + one, 0]) for one in range(2)], share)
        out[at : at + 2 * share] = solved.astype(BF16)


def backward_kernel(level, share, top, owners, weights, mates, targets, solved, solved_mate, *rest):
    if top:
        result, *outs = rest
    else:
        held, came, result, *outs = rest
    rows = weights.shape[1]
    span = result.shape[0]
    side = 2 * owners[owners.shape[0] - 1]
    side = side if level % 2 else 2 - side
    if not top:
        folded = (held[:span] + came[span:]).astype(BF16)
        folded_mate = (held[span:] + came[:span]).astype(BF16)
    pushes = [[], [], []]
    for pair in range(rows):
        half, row = divmod(2 * pair, rows)
        owner = owners[2 * level + half]
        at = slice(2 * share * pair, 2 * share * (pair + 1))

        def both(product, vector, blocks, kind):
            return either(*[product(vector, blocks[owner, row + one, kind]) for one in range(2)], share)

        done, done_mate = solved[at], solved_mate[at]
        if not top:
            done = (done.astype(F32) - both(dot, folded[at], weights, 0)).astype(BF16)
        result[at] = done
        if outs:
            if not top:
                done_mate = done_mate.astype(F32) - both(dot, folded_mate[at], mates, 0)
                done_mate = done_mate.astype(BF16)
            pushes[0].append(both(dot_t, done, weights, 2))
            pushes[1].append(both(dot_t, done_mate, mates, 1))
            pushes[2].append(both(dot_t, done, weights, 1 + side))
    if outs:
        pushed = jnp.concatenate(pushes[0] + pushes[1] + pushes[2], axis=0).astype(BF16)
        to = lax.broadcasted_iota(jnp.int32, (2 * span, 3 * span), 0)
        outs[0][...] = dot(ones_where(to == targets[level]), pushed)


def call(kernel, outs, owners, *rest):
    vmem = pl.BlockSpec(memory_space=pltpu.VMEM)
    return pl.pallas_call(
        kernel,
        out_shape=outs,
        in_specs=[pl.BlockSpec(memory_space=pltpu.SMEM)] + [vmem] * len(rest),
        out_specs=[vmem] * len(outs),
        compiler_params=pltpu.CompilerParams(vmem_limit_bytes=16 * 2**20),
    )(owners, *rest)


def local(right_side, diag_inverse, off_blocks, columns, plan):
    rows, depth, width = right_side.shape
    doms = lax.axis_size("dom")
    levs = lax.axis_size("level")
    levels = levs // 2
    share = depth // levs
    count = 2 * rows
    dom = lax.axis_index("dom")
    lev = lax.axis_index("level")
    near_pairs = [(i, i ^ 1) for i in range(doms)]
    far_pairs = [(i, ((i + 1) ^ 1) - 1) for i in range(1, doms - 1)] + [(0, doms - 1), (doms - 1, 0)]

    weights = jnp.concatenate([diag_inverse[:, None], off_blocks], axis=1)
    weights = lax.all_gather(weights, "level")

    turn = dom % 2
    ids = jnp.arange(levs, dtype=jnp.int32)
    own_level = jnp.sum(jnp.where(ids == lev, plan, 0)) // 2
    inverse = jnp.sum(jnp.where(plan[None, :] == ids[:, None], ids[None, :], 0), axis=1)
    owners = jnp.concatenate([inverse, turn[None]])

    here = jnp.where(own_level % 2 == turn, off_blocks[:, 0], off_blocks[:, 2])
    mates = jnp.stack([diag_inverse, here], axis=1)
    by_near = lax.ppermute(mates, "dom", near_pairs)
    by_far = lax.ppermute(mates, "dom", far_pairs)
    mates = jnp.where(own_level % 2 == 1, by_near, by_far)
    first = jnp.einsum("rkb,rbc->rkc", right_side, diag_inverse, preferred_element_type=F32)
    side = jnp.where(own_level == 0, first.astype(BF16), right_side)
    side = side.reshape(rows, levs, share, width)
    side = lax.all_to_all(side, "level", 1, 0, tiled=False)
    side = side.reshape(levs, rows * share, width)[inverse].reshape(levels, count * share, width)

    near_dom = dom + 1 - 2 * turn
    far_dom = (dom - 1 + 2 * turn) % doms
    part = jnp.stack(
        [
            lax.dynamic_slice_in_dim(columns, which * levs * rows, levs * rows, 0)
            for which in (dom, near_dom, far_dom)
        ]
    )
    part = part.reshape(3, levs, rows * 3)[:, inverse].reshape(3, levels, count, 3)
    second = jnp.roll(inverse[1::2], 1)[None, :, None, None]
    meets = jnp.where(part // rows % levs == second, rows, 0) + part % rows
    odd = (jnp.arange(levels) % 2 == 1)[:, None]
    meets_own = meets[0]
    meets_mate = jnp.where(odd[..., None], meets[1], meets[2])
    ahead = odd == (turn == 0)
    own_mate = jnp.where(ahead, meets_own[..., 0], meets_own[..., 2])
    mate_own = jnp.where(ahead, meets_mate[..., 0], meets_mate[..., 2])
    k = jnp.arange(share, dtype=jnp.int32)
    span = count * share
    slot = jnp.where(turn == 0, 1, -1) * (jnp.arange(3, dtype=jnp.int32) - 1) + 1
    places = meets_own.transpose(0, 2, 1) * share + slot[None, :, None] * span
    places = (places[..., None] + k).reshape(levels, 3 * span, 1)
    targets = jnp.stack([meets_own[..., 1], mate_own, own_mate + count], axis=1) * share
    targets = (targets[..., None] + k).reshape(levels, 1, 3 * span)

    vector = jax.ShapeDtypeStruct((count * share, width), BF16)
    summed = jax.ShapeDtypeStruct((2 * count * share, width), F32)

    own = side[0]
    far = lax.ppermute(own, "dom", far_pairs)
    near = lax.ppermute(own, "dom", near_pairs)
    mates, owners, side, places, targets, own, far, near = lax.optimization_barrier(
        (mates, owners, side, places, targets, own, far, near)
    )
    mates = lax.all_gather(mates, "level")

    solved = [own]
    around = []
    for level in range(1, levels):
        if level > 1:
            own = solved[-1]
            if level == levels - 1:
                own, mates = lax.optimization_barrier((own, mates))
                solved[-1] = own
            far = lax.ppermute(own, "dom", far_pairs)
            near = lax.ppermute(own, "dom", near_pairs)
        around.append(near if level % 2 == 0 else far)
        kernel = functools.partial(forward_kernel, level, share)
        solved += call(kernel, [vector], owners, weights, places, side, far, own, near)
    around.append(lax.ppermute(solved[-1], "dom", near_pairs))

    flow = []
    results = []
    for level in range(levels - 1, -1, -1):
        kernel = functools.partial(backward_kernel, level, share, level == levels - 1)
        outs = [vector, summed] if level else [vector]
        result, *rest = call(
            kernel, outs, owners, weights, mates, targets, solved[level], around[level], *flow
        )
        results.append(result)
        if level:
            held = rest[0]
            flow = [held, lax.ppermute(held, "dom", far_pairs if level % 2 else near_pairs)]

    both = jnp.stack([jnp.stack(solved), jnp.stack(results[::-1])])
    both = both.reshape(2, levs, rows, share, width)[:, plan]
    both = lax.all_to_all(both, "level", 1, 0, tiled=False)
    both = both.transpose(1, 2, 0, 3, 4).reshape(2, rows, depth, width)
    return both[0], both[1]


def solution(mesh):
    return jax.shard_map(
        local,
        mesh=mesh,
        in_specs=(
            P(("dom", "level"), None, None),
            P(("dom", "level"), None, None),
            P(("dom", "level"), None, None, None),
            P(),
            P(),
        ),
        out_specs=(P(("dom", "level"), None, None), P(("dom", "level"), None, None)),
        check_vma=False,
    )
```

time: 296 us -> 250 us (0.84)
  waiting for transfers between devices: 88.7 us -> 59.3 us
  local copies, waits for them, and re-layouts: 36.5 us -> 14.9 us
  starting transfers between devices: 88.8 us -> 96.8 us
  blocking collectives: 34.2 us -> 30.4 us
    all_gather x1, waiting for transfers between devices: 36.9 us -> 17.6 us  [local(): weights = lax.all_gather(weights, 'level')]
    unnamed x30 -> x20, local copies, waits for them, and re-layouts: 19.4 us -> 6.88 us
    ppermute x7, waiting for transfers between devices: 26.8 us -> 18.8 us  [local(): lax.ppermute(held, 'dom', far_pairs if level % 2 else near_pairs)]
    ppermute x7, starting transfers between devices: 19.3 us -> 27 us  [local(): lax.ppermute(held, 'dom', far_pairs if level % 2 else near_pairs)]
    gather x9 -> x2, local copies, waits for them, and re-layouts: 6.74 us -> 0.59 us  [local(): part.reshape(3, levs, rows * 3)[:, inverse].reshape(3, levels, count, 3)]
    ppermute x1, waiting for transfers between devices: 5.68 us -> 0.01 us  [local(): by_far = lax.ppermute(mates, 'dom', far_pairs)]
    ppermute x7, waiting for transfers between devices: 7.27 us -> 11.5 us  [local(): far = lax.ppermute(own, 'dom', far_pairs)]
    all_to_all x1, blocking collectives: 34.2 us -> 30.4 us  [local(): both = lax.all_to_all(both, 'level', 1, 0, tiled=False)]
  transfers between devices with their start and end apart: 27 -> 27, of which waited for: 19 -> 20; matrix products, arithmetic and copies ran while one was open for 7% -> 5% of each run, Pallas kernels for 3% -> 3%
where the time goes in v5:
time: 250 us; the launch traced here: 249 us
  starting transfers between devices  96.8 us (39%)
  waiting for transfers between devices  59.3 us (24%)
  blocking collectives  30.4 us (12%)
  Pallas kernels  21.2 us (8%)
  between operations  17.1 us (7%)
  local copies, waits for them, and re-layouts  14.9 us (6%)
  other arithmetic  8.06 us (3%)
    all_to_all x1, blocking collectives, local(): both = lax.all_to_all(both, 'level', 1, 0, tiled=False)  30.4 us
    ppermute x7, starting transfers between devices, local(): far = lax.ppermute(own, 'dom', far_pairs)  30.2 us
    ppermute x7, starting transfers between devices, local(): lax.ppermute(held, 'dom', far_pairs if level % 2 else near_pairs)  27 us
    pallas_call x15, Pallas kernels, call(): pl.pallas_call(kernel, out_shape=outs, in_specs=[pl.BlockSpec(memory_spac...  21.2 us
    ppermute x7, waiting for transfers between devices, local(): lax.ppermute(held, 'dom', far_pairs if level % 2 else near_pairs)  18.8 us
    all_gather x1, waiting for transfers between devices, local(): weights = lax.all_gather(weights, 'level')  17.6 us
    ppermute x7, starting transfers between devices, local(): near = lax.ppermute(own, 'dom', near_pairs)  13.4 us
    ppermute x7, waiting for transfers between devices, local(): far = lax.ppermute(own, 'dom', far_pairs)  11.5 us
  transfers between devices with their start and end apart: 27, of which 20 were waited for; matrix products, arithmetic and copies ran while one was open for 5% of the time, Pallas kernels for 3%

profile of v5, /device:TPU:1, one launch (start us, length us, event | category | flops | bytes accessed | tf_op | source)
XLA Modules:
  0.0 249.0 jit_solution(3304974910031393818)
XLA Ops:
  7.2 1.9 pad_maximum_fusion
  15.0 4.8 %collective-permute-start = (bf16[4,2,128,128]{3,2,1,0:T(8,128)(2,1)S(1)}, bf16[4,2,128,128]{3,2,1,0:T(8,128)(2,1)S(1)}, u32[]{:S(2)}, u32[]{:S(2)}) collective-permute-start(bf16[4,2,128,128]{3,2,1,0:T(8,128)(2,1)S(1)} %pad_maximum_fusion.1), channel_id=1, source_target_pairs={{0,16},{16,0},{32,48},{48,32},{64,80},{80,64},{96,112},{112,96},{1... | collective-permute-start | bytes 786440 | tf_op jit(solution)/shard_map/ppermute | solution.py:122
  19.9 11.0 %collective-permute-start.1 = (bf16[4,2,128,128]{3,2,1,0:T(8,128)(2,1)S(1)}, bf16[4,2,128,128]{3,2,1,0:T(8,128)(2,1)S(1)}, u32[]{:S(2)}, u32[]{:S(2)}) collective-permute-start(bf16[4,2,128,128]{3,2,1,0:T(8,128)(2,1)S(1)} %pad_maximum_fusion.1), channel_id=1, source_target_pairs={{16,32},{32,16},{48,64},{64,48},{80,96},{96,80},{112,128},{128,112... | collective-permute-start | bytes 786440 | tf_op jit(solution)/shard_map/ppermute | solution.py:123
  32.7 8.3 %all-to-all-start = ((bf16[1,4,16,4,128]{4,3,1,0,2:T(4,128)(2,1)}), bf16[1,4,16,4,128]{4,3,1,0,2:T(4,128)(2,1)S(1)}, u32[]{:S(2)}, u32[]{:S(2)}) async-start(bf16[1,4,16,4,128]{4,3,1,0,2:T(4,128)(2,1)} %copy.72), calls=%async_computation | async-start | bytes 131072 | tf_op jit(solution)/shard_map/all_to_all | solution.py:128
  48.0 1.6 all-to-all-done
  50.3 1.9 collective-permute-start.2
  52.2 1.9 collective-permute-start.3
  54.9 3.1 %collective-permute-done.2.far.solved_mate = bf16[32,128]{1,0:T(8,128)(2,1)S(1)} collective-permute-done((bf16[32,128]{1,0:T(8,128)(2,1)S(1)}, bf16[32,128]{1,0:T(8,128)(2,1)S(1)}, u32[]{:S(2)}, u32[]{:S(2)}) %collective-permute-start.2) | collective-permute-done | bytes 8224 | tf_op jit(solution)/shard_map/ppermute | solution.py:160
  58.1 17.6 %all-gather.5.cloned.1.call-done = bf16[64,4,128,128]{3,2,1,0:T(8,128)(2,1)} async-done(((bf16[4,4,128,128]{3,2,1,0:T(8,128)(2,1)}), bf16[64,4,128,128]{3,2,1,0:T(8,128)(2,1)}) %all-gather.5.cloned.1.call-update) | async-done | bytes 8388624 | tf_op jit(solution)/shard_map/all_gather | solution.py:112
  75.7 3.4 %copy-done = bf16[64,4,128,128]{3,2,1,0:T(8,128)(2,1)S(1)} copy-done((bf16[64,4,128,128]{3,2,1,0:T(8,128)(2,1)S(1)}, bf16[64,4,128,128]{3,2,1,0:T(8,128)(2,1)}, u32[]{:S(2)}) %copy-start) | copy-done | bytes 8388632
  80.5 7.7 %collective-permute-start.4 = (bf16[32,128]{1,0:T(8,128)(2,1)S(1)}, bf16[32,128]{1,0:T(8,128)(2,1)S(1)}, u32[]{:S(2)}, u32[]{:S(2)}) collective-permute-start(bf16[32,128]{1,0:T(8,128)(2,1)S(1)} %shard_map.68.own.solved), channel_id=1, source_target_pairs={{16,32},{32,16},{48,64},{64,48},{80,96},{96,80},{112,128},{128,112... | collective-permute-start | bytes 24584 | tf_op jit(solution)/shard_map/ppermute | solution.py:175
  88.2 1.9 collective-permute-start.5
  90.2 2.5 collective-permute-done.5.near.solved_mate
  94.0 3.3 %collective-permute-start.6 = (bf16[32,128]{1,0:T(8,128)(2,1)S(1)}, bf16[32,128]{1,0:T(8,128)(2,1)S(1)}, u32[]{:S(2)}, u32[]{:S(2)}) collective-permute-start(bf16[32,128]{1,0:T(8,128)(2,1)S(1)} %shard_map.69.own.solved), channel_id=1, source_target_pairs={{16,32},{32,16},{48,64},{64,48},{80,96},{96,80},{112,128},{128,112... | collective-permute-start | bytes 24584 | tf_op jit(solution)/shard_map/ppermute | solution.py:175
  97.4 1.9 collective-permute-start.7
  99.3 2.5 collective-permute-done.6.far.solved_mate
  103.6 5.3 %collective-permute-start.8 = (bf16[32,128]{1,0:T(8,128)(2,1)S(1)}, bf16[32,128]{1,0:T(8,128)(2,1)S(1)}, u32[]{:S(2)}, u32[]{:S(2)}) collective-permute-start(bf16[32,128]{1,0:T(8,128)(2,1)S(1)} %shard_map.70.own.solved), channel_id=1, source_target_pairs={{16,32},{32,16},{48,64},{64,48},{80,96},{96,80},{112,128},{128,112... | collective-permute-start | bytes 24584 | tf_op jit(solution)/shard_map/ppermute | solution.py:175
  108.9 1.9 collective-permute-start.9
  111.3 2.4 collective-permute-done.9.near.solved_mate
  115.1 3.3 %collective-permute-start.10 = (bf16[32,128]{1,0:T(8,128)(2,1)S(1)}, bf16[32,128]{1,0:T(8,128)(2,1)S(1)}, u32[]{:S(2)}, u32[]{:S(2)}) collective-permute-start(bf16[32,128]{1,0:T(8,128)(2,1)S(1)} %shard_map.71.own.solved), channel_id=1, source_target_pairs={{16,32},{32,16},{48,64},{64,48},{80,96},{96,80},{112,128},{128,112... | collective-permute-start | bytes 24584 | tf_op jit(solution)/shard_map/ppermute | solution.py:175
  118.4 1.9 collective-permute-start.11
  120.4 2.5 collective-permute-done.10.far.solved_mate
  124.3 5.3 %collective-permute-start.12 = (bf16[32,128]{1,0:T(8,128)(2,1)S(1)}, bf16[32,128]{1,0:T(8,128)(2,1)S(1)}, u32[]{:S(2)}, u32[]{:S(2)}) collective-permute-start(bf16[32,128]{1,0:T(8,128)(2,1)S(1)} %shard_map.72.own.solved), channel_id=1, source_target_pairs={{16,32},{32,16},{48,64},{64,48},{80,96},{96,80},{112,128},{128,112... | collective-permute-start | bytes 24584 | tf_op jit(solution)/shard_map/ppermute | solution.py:175
  129.6 1.9 collective-permute-start.13
  132.0 2.0 collective-permute-done.13.near.solved_mate
  135.4 3.3 %collective-permute-start.14 = (bf16[32,128]{1,0:T(8,128)(2,1)S(1)}, bf16[32,128]{1,0:T(8,128)(2,1)S(1)}, u32[]{:S(2)}, u32[]{:S(2)}) collective-permute-start(bf16[32,128]{1,0:T(8,128)(2,1)S(1)} %shard_map.73.own.solved), channel_id=1, source_target_pairs={{16,32},{32,16},{48,64},{64,48},{80,96},{96,80},{112,128},{128,112... | collective-permute-start | bytes 24584 | tf_op jit(solution)/shard_map/ppermute | solution.py:175
  138.7 1.9 collective-permute-start.15
  140.6 2.5 collective-permute-done.14.far.solved_mate
  143.1 3.4 %copy-done.1 = bf16[64,4,128,128]{3,2,1,0:T(8,128)(2,1)S(1)} copy-done((bf16[64,4,128,128]{3,2,1,0:T(8,128)(2,1)S(1)}, bf16[64,4,128,128]{3,2,1,0:T(8,128)(2,1)}, u32[]{:S(2)}) %copy-start.1) | copy-done | bytes 8388632
  147.9 1.9 collective-permute-start.16
  149.9 2.5 collective-permute-done.16.solved_mate
  153.5 5.3 %collective-permute-start.17 = (f32[64,128]{1,0:T(8,128)S(1)}, f32[64,128]{1,0:T(8,128)S(1)}, u32[]{:S(2)}, u32[]{:S(2)}) collective-permute-start(f32[64,128]{1,0:T(8,128)S(1)} %get-tuple-element.36.rest_0_), channel_id=1, source_target_pairs={{16,32},{32,16},{48,64},{64,48},{80,96},{96,80},{112,128},{128,112... | collective-permute-start | bytes 98312 | tf_op jit(solution)/shard_map/ppermute | solution.py:193
  158.8 2.7 %collective-permute-done.17.rest_1_ = f32[64,128]{1,0:T(8,128)S(1)} collective-permute-done((f32[64,128]{1,0:T(8,128)S(1)}, f32[64,128]{1,0:T(8,128)S(1)}, u32[]{:S(2)}, u32[]{:S(2)}) %collective-permute-start.17) | collective-permute-done | bytes 32800 | tf_op jit(solution)/shard_map/ppermute | solution.py:193
  163.0 1.9 collective-permute-start.18
  165.0 2.7 %collective-permute-done.18.rest_1_ = f32[64,128]{1,0:T(8,128)S(1)} collective-permute-done((f32[64,128]{1,0:T(8,128)S(1)}, f32[64,128]{1,0:T(8,128)S(1)}, u32[]{:S(2)}, u32[]{:S(2)}) %collective-permute-start.18) | collective-permute-done | bytes 32800 | tf_op jit(solution)/shard_map/ppermute | solution.py:193
  167.7 1.6 shard_map.77
  169.3 5.3 %collective-permute-start.19 = (f32[64,128]{1,0:T(8,128)S(1)}, f32[64,128]{1,0:T(8,128)S(1)}, u32[]{:S(2)}, u32[]{:S(2)}) collective-permute-start(f32[64,128]{1,0:T(8,128)S(1)} %get-tuple-element.38.rest_0_), channel_id=1, source_target_pairs={{16,32},{32,16},{48,64},{64,48},{80,96},{96,80},{112,128},{128,112... | collective-permute-start | bytes 98312 | tf_op jit(solution)/shard_map/ppermute | solution.py:193
  174.6 2.7 %collective-permute-done.19.rest_1_ = f32[64,128]{1,0:T(8,128)S(1)} collective-permute-done((f32[64,128]{1,0:T(8,128)S(1)}, f32[64,128]{1,0:T(8,128)S(1)}, u32[]{:S(2)}, u32[]{:S(2)}) %collective-permute-start.19) | collective-permute-done | bytes 32800 | tf_op jit(solution)/shard_map/ppermute | solution.py:193
  178.8 1.9 collective-permute-start.20
  180.8 2.7 %collective-permute-done.20.rest_1_ = f32[64,128]{1,0:T(8,128)S(1)} collective-permute-done((f32[64,128]{1,0:T(8,128)S(1)}, f32[64,128]{1,0:T(8,128)S(1)}, u32[]{:S(2)}, u32[]{:S(2)}) %collective-permute-start.20) | collective-permute-done | bytes 32800 | tf_op jit(solution)/shard_map/ppermute | solution.py:193
  183.5 1.6 shard_map.79
  185.0 5.3 %collective-permute-start.21 = (f32[64,128]{1,0:T(8,128)S(1)}, f32[64,128]{1,0:T(8,128)S(1)}, u32[]{:S(2)}, u32[]{:S(2)}) collective-permute-start(f32[64,128]{1,0:T(8,128)S(1)} %get-tuple-element.40.rest_0_), channel_id=1, source_target_pairs={{16,32},{32,16},{48,64},{64,48},{80,96},{96,80},{112,128},{128,112... | collective-permute-start | bytes 98312 | tf_op jit(solution)/shard_map/ppermute | solution.py:193
  190.4 2.7 %collective-permute-done.21.rest_1_ = f32[64,128]{1,0:T(8,128)S(1)} collective-permute-done((f32[64,128]{1,0:T(8,128)S(1)}, f32[64,128]{1,0:T(8,128)S(1)}, u32[]{:S(2)}, u32[]{:S(2)}) %collective-permute-start.21) | collective-permute-done | bytes 32800 | tf_op jit(solution)/shard_map/ppermute | solution.py:193
  194.6 1.9 collective-permute-start.22
  196.5 2.7 %collective-permute-done.22.rest_1_ = f32[64,128]{1,0:T(8,128)S(1)} collective-permute-done((f32[64,128]{1,0:T(8,128)S(1)}, f32[64,128]{1,0:T(8,128)S(1)}, u32[]{:S(2)}, u32[]{:S(2)}) %collective-permute-start.22) | collective-permute-done | bytes 32800 | tf_op jit(solution)/shard_map/ppermute | solution.py:193
  200.8 5.3 %collective-permute-start.23 = (f32[64,128]{1,0:T(8,128)S(1)}, f32[64,128]{1,0:T(8,128)S(1)}, u32[]{:S(2)}, u32[]{:S(2)}) collective-permute-start(f32[64,128]{1,0:T(8,128)S(1)} %get-tuple-element.42.rest_0_), channel_id=1, source_target_pairs={{16,32},{32,16},{48,64},{64,48},{80,96},{96,80},{112,128},{128,112... | collective-permute-start | bytes 98312 | tf_op jit(solution)/shard_map/ppermute | solution.py:193
  206.1 2.7 %collective-permute-done.23.rest_1_ = f32[64,128]{1,0:T(8,128)S(1)} collective-permute-done((f32[64,128]{1,0:T(8,128)S(1)}, f32[64,128]{1,0:T(8,128)S(1)}, u32[]{:S(2)}, u32[]{:S(2)}) %collective-permute-start.23) | collective-permute-done | bytes 32800 | tf_op jit(solution)/shard_map/ppermute | solution.py:193
  210.4 30.4 %all_to_all.30 = bf16[1,2,16,4,4,128]{5,4,3,1,0,2:T(4,128)(2,1)S(1)} all-to-all(bf16[1,2,16,4,4,128]{5,4,3,1,0,2:T(4,128)(2,1)S(1)} %bitcast.134), channel_id=1, replica_groups=mesh['dom'=32,'level'=16] {'level'}, dimensions={2} | all-to-all | bytes 262144 | tf_op jit(solution)/shard_map/all_to_all | solution.py:197
  (100 shorter events, 35.0 us)
Async XLA Ops:
  7.2 68.5 %all-gather.5.cloned.1.call-start = ((), (), s32[]{:S(2)}) async-start(), calls=%async_computation.2 | async-start | bytes 8912896 | tf_op jit(solution)/shard_map/all_gather | solution.py:112
  15.0 39.1 %collective-permute-start = (bf16[4,2,128,128]{3,2,1,0:T(8,128)(2,1)S(1)}, bf16[4,2,128,128]{3,2,1,0:T(8,128)(2,1)S(1)}, u32[]{:S(2)}, u32[]{:S(2)}) collective-permute-start(bf16[4,2,128,128]{3,2,1,0:T(8,128)(2,1)S(1)} %pad_maximum_fusion.1), channel_id=1, source_target_pairs={{0,16},{16,0},{32,48},{48,32},{64,80},{80,64},{96,112},{112,96},{1... | collective-permute-start | bytes 786440 | tf_op jit(solution)/shard_map/ppermute | solution.py:122
  19.9 34.3 %collective-permute-start.1 = (bf16[4,2,128,128]{3,2,1,0:T(8,128)(2,1)S(1)}, bf16[4,2,128,128]{3,2,1,0:T(8,128)(2,1)S(1)}, u32[]{:S(2)}, u32[]{:S(2)}) collective-permute-start(bf16[4,2,128,128]{3,2,1,0:T(8,128)(2,1)S(1)} %pad_maximum_fusion.1), channel_id=1, source_target_pairs={{16,32},{32,16},{48,64},{64,48},{80,96},{96,80},{112,128},{128,112... | collective-permute-start | bytes 786440 | tf_op jit(solution)/shard_map/ppermute | solution.py:123
  32.7 17.0 %all-to-all-start = ((bf16[1,4,16,4,128]{4,3,1,0,2:T(4,128)(2,1)}), bf16[1,4,16,4,128]{4,3,1,0,2:T(4,128)(2,1)S(1)}, u32[]{:S(2)}, u32[]{:S(2)}) async-start(bf16[1,4,16,4,128]{4,3,1,0,2:T(4,128)(2,1)} %copy.72), calls=%async_computation | async-start | bytes 131072 | tf_op jit(solution)/shard_map/all_to_all | solution.py:128
  41.0 94.4 %all-gather.7.cloned.1.call-start = ((), (), s32[]{:S(2)}) async-start(), calls=%async_computation.3 | async-start | bytes 4456448 | tf_op jit(solution)/shard_map/all_gather | solution.py:165
  50.3 7.7 %collective-permute-start.2 = (bf16[32,128]{1,0:T(8,128)(2,1)S(1)}, bf16[32,128]{1,0:T(8,128)(2,1)S(1)}, u32[]{:S(2)}, u32[]{:S(2)}) collective-permute-start(bf16[32,128]{1,0:T(8,128)(2,1)S(1)} %bitcast.126), channel_id=1, source_target_pairs={{16,32},{32,16},{48,64},{64,48},{80,96},{96,80},{112,128},{128,112... | collective-permute-start | bytes 24584 | tf_op jit(solution)/shard_map/ppermute | solution.py:160
  52.2 5.8 %collective-permute-start.3 = (bf16[32,128]{1,0:T(8,128)(2,1)S(1)}, bf16[32,128]{1,0:T(8,128)(2,1)S(1)}, u32[]{:S(2)}, u32[]{:S(2)}) collective-permute-start(bf16[32,128]{1,0:T(8,128)(2,1)S(1)} %bitcast.127), channel_id=1, source_target_pairs={{0,16},{16,0},{32,48},{48,32},{64,80},{80,64},{96,112},{112,96},{1... | collective-permute-start | bytes 24584 | tf_op jit(solution)/shard_map/ppermute | solution.py:161
  75.7 3.4 %copy-start = (bf16[64,4,128,128]{3,2,1,0:T(8,128)(2,1)S(1)}, bf16[64,4,128,128]{3,2,1,0:T(8,128)(2,1)}, u32[]{:S(2)}) copy-start(bf16[64,4,128,128]{3,2,1,0:T(8,128)(2,1)} %all-gather.5.cloned.1.call-done) | copy-start | bytes 25165828
  80.5 9.6 %collective-permute-start.4 = (bf16[32,128]{1,0:T(8,128)(2,1)S(1)}, bf16[32,128]{1,0:T(8,128)(2,1)S(1)}, u32[]{:S(2)}, u32[]{:S(2)}) collective-permute-start(bf16[32,128]{1,0:T(8,128)(2,1)S(1)} %shard_map.68.own.solved), channel_id=1, source_target_pairs={{16,32},{32,16},{48,64},{64,48},{80,96},{96,80},{112,128},{128,112... | collective-permute-start | bytes 24584 | tf_op jit(solution)/shard_map/ppermute | solution.py:175
  88.2 4.4 %collective-permute-start.5 = (bf16[32,128]{1,0:T(8,128)(2,1)S(1)}, bf16[32,128]{1,0:T(8,128)(2,1)S(1)}, u32[]{:S(2)}, u32[]{:S(2)}) collective-permute-start(bf16[32,128]{1,0:T(8,128)(2,1)S(1)} %shard_map.68.own.solved), channel_id=1, source_target_pairs={{0,16},{16,0},{32,48},{48,32},{64,80},{80,64},{96,112},{112,96},{1... | collective-permute-start | bytes 24584 | tf_op jit(solution)/shard_map/ppermute | solution.py:176
  94.0 7.7 %collective-permute-start.6 = (bf16[32,128]{1,0:T(8,128)(2,1)S(1)}, bf16[32,128]{1,0:T(8,128)(2,1)S(1)}, u32[]{:S(2)}, u32[]{:S(2)}) collective-permute-start(bf16[32,128]{1,0:T(8,128)(2,1)S(1)} %shard_map.69.own.solved), channel_id=1, source_target_pairs={{16,32},{32,16},{48,64},{64,48},{80,96},{96,80},{112,128},{128,112... | collective-permute-start | bytes 24584 | tf_op jit(solution)/shard_map/ppermute | solution.py:175
  97.4 4.8 %collective-permute-start.7 = (bf16[32,128]{1,0:T(8,128)(2,1)S(1)}, bf16[32,128]{1,0:T(8,128)(2,1)S(1)}, u32[]{:S(2)}, u32[]{:S(2)}) collective-permute-start(bf16[32,128]{1,0:T(8,128)(2,1)S(1)} %shard_map.69.own.solved), channel_id=1, source_target_pairs={{0,16},{16,0},{32,48},{48,32},{64,80},{80,64},{96,112},{112,96},{1... | collective-permute-start | bytes 24584 | tf_op jit(solution)/shard_map/ppermute | solution.py:176
  103.6 7.7 %collective-permute-start.8 = (bf16[32,128]{1,0:T(8,128)(2,1)S(1)}, bf16[32,128]{1,0:T(8,128)(2,1)S(1)}, u32[]{:S(2)}, u32[]{:S(2)}) collective-permute-start(bf16[32,128]{1,0:T(8,128)(2,1)S(1)} %shard_map.70.own.solved), channel_id=1, source_target_pairs={{16,32},{32,16},{48,64},{64,48},{80,96},{96,80},{112,128},{128,112... | collective-permute-start | bytes 24584 | tf_op jit(solution)/shard_map/ppermute | solution.py:175
  108.9 4.8 %collective-permute-start.9 = (bf16[32,128]{1,0:T(8,128)(2,1)S(1)}, bf16[32,128]{1,0:T(8,128)(2,1)S(1)}, u32[]{:S(2)}, u32[]{:S(2)}) collective-permute-start(bf16[32,128]{1,0:T(8,128)(2,1)S(1)} %shard_map.70.own.solved), channel_id=1, source_target_pairs={{0,16},{16,0},{32,48},{48,32},{64,80},{80,64},{96,112},{112,96},{1... | collective-permute-start | bytes 24584 | tf_op jit(solution)/shard_map/ppermute | solution.py:176
  115.1 7.7 %collective-permute-start.10 = (bf16[32,128]{1,0:T(8,128)(2,1)S(1)}, bf16[32,128]{1,0:T(8,128)(2,1)S(1)}, u32[]{:S(2)}, u32[]{:S(2)}) collective-permute-start(bf16[32,128]{1,0:T(8,128)(2,1)S(1)} %shard_map.71.own.solved), channel_id=1, source_target_pairs={{16,32},{32,16},{48,64},{64,48},{80,96},{96,80},{112,128},{128,112... | collective-permute-start | bytes 24584 | tf_op jit(solution)/shard_map/ppermute | solution.py:175
  118.4 4.4 %collective-permute-start.11 = (bf16[32,128]{1,0:T(8,128)(2,1)S(1)}, bf16[32,128]{1,0:T(8,128)(2,1)S(1)}, u32[]{:S(2)}, u32[]{:S(2)}) collective-permute-start(bf16[32,128]{1,0:T(8,128)(2,1)S(1)} %shard_map.71.own.solved), channel_id=1, source_target_pairs={{0,16},{16,0},{32,48},{48,32},{64,80},{80,64},{96,112},{112,96},{1... | collective-permute-start | bytes 24584 | tf_op jit(solution)/shard_map/ppermute | solution.py:176
  124.3 7.7 %collective-permute-start.12 = (bf16[32,128]{1,0:T(8,128)(2,1)S(1)}, bf16[32,128]{1,0:T(8,128)(2,1)S(1)}, u32[]{:S(2)}, u32[]{:S(2)}) collective-permute-start(bf16[32,128]{1,0:T(8,128)(2,1)S(1)} %shard_map.72.own.solved), channel_id=1, source_target_pairs={{16,32},{32,16},{48,64},{64,48},{80,96},{96,80},{112,128},{128,112... | collective-permute-start | bytes 24584 | tf_op jit(solution)/shard_map/ppermute | solution.py:175
  129.6 4.4 %collective-permute-start.13 = (bf16[32,128]{1,0:T(8,128)(2,1)S(1)}, bf16[32,128]{1,0:T(8,128)(2,1)S(1)}, u32[]{:S(2)}, u32[]{:S(2)}) collective-permute-start(bf16[32,128]{1,0:T(8,128)(2,1)S(1)} %shard_map.72.own.solved), channel_id=1, source_target_pairs={{0,16},{16,0},{32,48},{48,32},{64,80},{80,64},{96,112},{112,96},{1... | collective-permute-start | bytes 24584 | tf_op jit(solution)/shard_map/ppermute | solution.py:176
  135.4 7.7 %collective-permute-start.14 = (bf16[32,128]{1,0:T(8,128)(2,1)S(1)}, bf16[32,128]{1,0:T(8,128)(2,1)S(1)}, u32[]{:S(2)}, u32[]{:S(2)}) collective-permute-start(bf16[32,128]{1,0:T(8,128)(2,1)S(1)} %shard_map.73.own.solved), channel_id=1, source_target_pairs={{16,32},{32,16},{48,64},{64,48},{80,96},{96,80},{112,128},{128,112... | collective-permute-start | bytes 24584 | tf_op jit(solution)/shard_map/ppermute | solution.py:175
  138.7 4.4 %collective-permute-start.15 = (bf16[32,128]{1,0:T(8,128)(2,1)S(1)}, bf16[32,128]{1,0:T(8,128)(2,1)S(1)}, u32[]{:S(2)}, u32[]{:S(2)}) collective-permute-start(bf16[32,128]{1,0:T(8,128)(2,1)S(1)} %shard_map.73.own.solved), channel_id=1, source_target_pairs={{0,16},{16,0},{32,48},{48,32},{64,80},{80,64},{96,112},{112,96},{1... | collective-permute-start | bytes 24584 | tf_op jit(solution)/shard_map/ppermute | solution.py:176
  143.1 3.4 %copy-start.1 = (bf16[64,4,128,128]{3,2,1,0:T(8,128)(2,1)S(1)}, bf16[64,4,128,128]{3,2,1,0:T(8,128)(2,1)}, u32[]{:S(2)}) copy-start(bf16[64,4,128,128]{3,2,1,0:T(8,128)(2,1)} %all-gather.5.cloned.1.call-done) | copy-start | bytes 25165828
  146.5 5.8 %copy-start.2 = (bf16[64,2,128,128]{3,2,1,0:T(8,128)(2,1)S(1)}, bf16[64,2,128,128]{3,2,1,0:T(8,128)(2,1)}, u32[]{:S(2)}) copy-start(bf16[64,2,128,128]{3,2,1,0:T(8,128)(2,1)} %all-gather.7.cloned.1.call-done) | copy-start | bytes 12582916
  147.9 4.4 %collective-permute-start.16 = (bf16[32,128]{1,0:T(8,128)(2,1)S(1)}, bf16[32,128]{1,0:T(8,128)(2,1)S(1)}, u32[]{:S(2)}, u32[]{:S(2)}) collective-permute-start(bf16[32,128]{1,0:T(8,128)(2,1)S(1)} %shard_map.74.solved), channel_id=1, source_target_pairs={{0,16},{16,0},{32,48},{48,32},{64,80},{80,64},{96,112},{112,96},{1... | collective-permute-start | bytes 24584 | tf_op jit(solution)/shard_map/ppermute | solution.py:180
  153.5 8.0 %collective-permute-start.17 = (f32[64,128]{1,0:T(8,128)S(1)}, f32[64,128]{1,0:T(8,128)S(1)}, u32[]{:S(2)}, u32[]{:S(2)}) collective-permute-start(f32[64,128]{1,0:T(8,128)S(1)} %get-tuple-element.36.rest_0_), channel_id=1, source_target_pairs={{16,32},{32,16},{48,64},{64,48},{80,96},{96,80},{112,128},{128,112... | collective-permute-start | bytes 98312 | tf_op jit(solution)/shard_map/ppermute | solution.py:193
  163.0 4.7 %collective-permute-start.18 = (f32[64,128]{1,0:T(8,128)S(1)}, f32[64,128]{1,0:T(8,128)S(1)}, u32[]{:S(2)}, u32[]{:S(2)}) collective-permute-start(f32[64,128]{1,0:T(8,128)S(1)} %get-tuple-element.37.rest_0_), channel_id=1, source_target_pairs={{0,16},{16,0},{32,48},{48,32},{64,80},{80,64},{96,112},{112,96},{1... | collective-permute-start | bytes 98312 | tf_op jit(solution)/shard_map/ppermute | solution.py:193
  169.3 8.0 %collective-permute-start.19 = (f32[64,128]{1,0:T(8,128)S(1)}, f32[64,128]{1,0:T(8,128)S(1)}, u32[]{:S(2)}, u32[]{:S(2)}) collective-permute-start(f32[64,128]{1,0:T(8,128)S(1)} %get-tuple-element.38.rest_0_), channel_id=1, source_target_pairs={{16,32},{32,16},{48,64},{64,48},{80,96},{96,80},{112,128},{128,112... | collective-permute-start | bytes 98312 | tf_op jit(solution)/shard_map/ppermute | solution.py:193
  178.8 4.7 %collective-permute-start.20 = (f32[64,128]{1,0:T(8,128)S(1)}, f32[64,128]{1,0:T(8,128)S(1)}, u32[]{:S(2)}, u32[]{:S(2)}) collective-permute-start(f32[64,128]{1,0:T(8,128)S(1)} %get-tuple-element.39.rest_0_), channel_id=1, source_target_pairs={{0,16},{16,0},{32,48},{48,32},{64,80},{80,64},{96,112},{112,96},{1... | collective-permute-start | bytes 98312 | tf_op jit(solution)/shard_map/ppermute | solution.py:193
  185.0 8.0 %collective-permute-start.21 = (f32[64,128]{1,0:T(8,128)S(1)}, f32[64,128]{1,0:T(8,128)S(1)}, u32[]{:S(2)}, u32[]{:S(2)}) collective-permute-start(f32[64,128]{1,0:T(8,128)S(1)} %get-tuple-element.40.rest_0_), channel_id=1, source_target_pairs={{16,32},{32,16},{48,64},{64,48},{80,96},{96,80},{112,128},{128,112... | collective-permute-start | bytes 98312 | tf_op jit(solution)/shard_map/ppermute | solution.py:193
  194.6 4.7 %collective-permute-start.22 = (f32[64,128]{1,0:T(8,128)S(1)}, f32[64,128]{1,0:T(8,128)S(1)}, u32[]{:S(2)}, u32[]{:S(2)}) collective-permute-start(f32[64,128]{1,0:T(8,128)S(1)} %get-tuple-element.41.rest_0_), channel_id=1, source_target_pairs={{0,16},{16,0},{32,48},{48,32},{64,80},{80,64},{96,112},{112,96},{1... | collective-permute-start | bytes 98312 | tf_op jit(solution)/shard_map/ppermute | solution.py:193
  200.8 8.0 %collective-permute-start.23 = (f32[64,128]{1,0:T(8,128)S(1)}, f32[64,128]{1,0:T(8,128)S(1)}, u32[]{:S(2)}, u32[]{:S(2)}) collective-permute-start(f32[64,128]{1,0:T(8,128)S(1)} %get-tuple-element.42.rest_0_), channel_id=1, source_target_pairs={{16,32},{32,16},{48,64},{64,48},{80,96},{96,80},{112,128},{128,112... | collective-permute-start | bytes 98312 | tf_op jit(solution)/shard_map/ppermute | solution.py:193
Sparse Core Ops, SparseCore 0:
  10.1 65.5 all-gather.4
  77.8 43.3 all-gather.6

commit v6 on v5

--- a/solution.py
+++ b/solution.py
@@ -28,72 +28,78 @@
     return jnp.where(condition, 1.0, 0.0).astype(BF16)
 
 
-def forward_kernel(level, share, owners, weights, places, side, far, own, near, out):
-    rows = weights.shape[1]
+BITS = 8
+
+
+def unpack(packed, level):
+    value = jnp.max(packed[level : level + 1])
+    mask = (1 << BITS) - 1
+    return value & mask, (value >> BITS) & mask, value >> (2 * BITS)
+
+
+def products(product, share, owners, vectors, blocks, kind):
+    rows = blocks.shape[1]
+    totals = []
+    for pair in range(rows):
+        half, row = divmod(2 * pair, rows)
+        part = vectors[2 * share * pair : 2 * share * (pair + 1)]
+        wide = [blocks[owners[half], row + one, kind] for one in range(2)]
+        if isinstance(kind, slice):
+            wide = [block.reshape(-1, block.shape[-1]) for block in wide]
+        totals.append(either(*[product(part, block) for block in wide], share))
+    return jnp.concatenate(totals, axis=0)
+
+
+def forward_kernel(level, share, packed, weights, places, side, far, own, near, out):
+    *owners, _ = unpack(packed, level)
     span = out.shape[0]
     around = jnp.concatenate([far[...], own[...], near[...]], axis=0)
     at = lax.broadcasted_iota(jnp.int32, (3 * span, 3 * span), 1)
     picked = dot(ones_where(at == places[level]), around)
-    for pair in range(rows):
-        half, row = divmod(2 * pair, rows)
-        owner = owners[2 * level + half]
-        at = 2 * share * pair
-        terms = [picked[n * span + at : n * span + at + 2 * share] for n in range(3)]
-        terms = jnp.concatenate(terms, axis=1).astype(BF16)
-        wide = [weights[owner, row + one, 1:].reshape(-1, out.shape[1]) for one in range(2)]
-        total = either(*[dot(terms, block) for block in wide], share)
-        shifted = (side[level, at : at + 2 * share].astype(F32) - total).astype(BF16)
-        solved = either(*[dot(shifted, weights[owner, row + one, 0]) for one in range(2)], share)
-        out[at : at + 2 * share] = solved.astype(BF16)
-
-
-def backward_kernel(level, share, top, owners, weights, mates, targets, solved, solved_mate, *rest):
+    picked = jnp.concatenate([picked[n * span : (n + 1) * span] for n in range(3)], axis=1)
+    total = products(dot, share, owners, picked.astype(BF16), weights, slice(1, None))
+    shifted = (side[level].astype(F32) - total).astype(BF16)
+    out[...] = products(dot, share, owners, shifted, weights, 0).astype(BF16)
+
+
+def backward_kernel(level, share, top, packed, weights, mates, targets, solved, solved_mate, *rest):
     if top:
         result, *outs = rest
     else:
         held, came, result, *outs = rest
-    rows = weights.shape[1]
+    *owners, side = unpack(packed, level)
     span = result.shape[0]
-    side = 2 * owners[owners.shape[0] - 1]
-    side = side if level % 2 else 2 - side
+    done, done_mate = solved[...], solved_mate[...]
     if not top:
         folded = (held[:span] + came[span:]).astype(BF16)
-        folded_mate = (held[span:] + came[:span]).astype(BF16)
-    pushes = [[], [], []]
-    for pair in range(rows):
-        half, row = divmod(2 * pair, rows)
-        owner = owners[2 * level + half]
-        at = slice(2 * share * pair, 2 * share * (pair + 1))
-
-        def both(product, vector, blocks, kind):
-            return either(*[product(vector, blocks[owner, row + one, kind]) for one in range(2)], share)
-
-        done, done_mate = solved[at], solved_mate[at]
-        if not top:
-            done = (done.astype(F32) - both(dot, folded[at], weights, 0)).astype(BF16)
-        result[at] = done
-        if outs:
-            if not top:
-                done_mate = done_mate.astype(F32) - both(dot, folded_mate[at], mates, 0)
-                done_mate = done_mate.astype(BF16)
-            pushes[0].append(both(dot_t, done, weights, 2))
-            pushes[1].append(both(dot_t, done_mate, mates, 1))
-            pushes[2].append(both(dot_t, done, weights, 1 + side))
-    if outs:
-        pushed = jnp.concatenate(pushes[0] + pushes[1] + pushes[2], axis=0).astype(BF16)
-        to = lax.broadcasted_iota(jnp.int32, (2 * span, 3 * span), 0)
-        outs[0][...] = dot(ones_where(to == targets[level]), pushed)
-
-
-def call(kernel, outs, owners, *rest):
+        done = done.astype(F32) - products(dot, share, owners, folded, weights, 0)
+        done = done.astype(BF16)
+    result[...] = done
+    if not outs:
+        return
+    if not top:
+        folded = (held[span:] + came[:span]).astype(BF16)
+        done_mate = done_mate.astype(F32) - products(dot, share, owners, folded, mates, 0)
+        done_mate = done_mate.astype(BF16)
+    pushed = [
+        products(dot_t, share, owners, done, weights, 2),
+        products(dot_t, share, owners, done_mate, mates, 1),
+        products(dot_t, share, owners, done, weights, 1 + side),
+    ]
+    pushed = jnp.concatenate(pushed, axis=0).astype(BF16)
+    to = lax.broadcasted_iota(jnp.int32, (2 * span, 3 * span), 0)
+    outs[0][...] = dot(ones_where(to == targets[level]), pushed)
+
+
+def call(kernel, outs, *args):
     vmem = pl.BlockSpec(memory_space=pltpu.VMEM)
     return pl.pallas_call(
         kernel,
         out_shape=outs,
-        in_specs=[pl.BlockSpec(memory_space=pltpu.SMEM)] + [vmem] * len(rest),
+        in_specs=[vmem] * len(args),
         out_specs=[vmem] * len(outs),
         compiler_params=pltpu.CompilerParams(vmem_limit_bytes=16 * 2**20),
-    )(owners, *rest)
+    )(*args)
 
 
 def local(right_side, diag_inverse, off_blocks, columns, plan):
@@ -115,7 +121,9 @@
     ids = jnp.arange(levs, dtype=jnp.int32)
     own_level = jnp.sum(jnp.where(ids == lev, plan, 0)) // 2
     inverse = jnp.sum(jnp.where(plan[None, :] == ids[:, None], ids[None, :], 0), axis=1)
-    owners = jnp.concatenate([inverse, turn[None]])
+    side_of = jnp.where(jnp.arange(levels) % 2 == 1, 2 * turn, 2 - 2 * turn)
+    packed = inverse[0::2] + (inverse[1::2] << BITS) + (side_of << (2 * BITS))
+    packed = jnp.broadcast_to(packed[:, None], (levels, 128)).astype(jnp.int32)
 
     here = jnp.where(own_level % 2 == turn, off_blocks[:, 0], off_blocks[:, 2])
     mates = jnp.stack([diag_inverse, here], axis=1)
@@ -159,8 +167,8 @@
     own = side[0]
     far = lax.ppermute(own, "dom", far_pairs)
     near = lax.ppermute(own, "dom", near_pairs)
-    mates, owners, side, places, targets, own, far, near = lax.optimization_barrier(
-        (mates, owners, side, places, targets, own, far, near)
+    mates, packed, side, places, targets, own, far, near = lax.optimization_barrier(
+        (mates, packed, side, places, targets, own, far, near)
     )
     mates = lax.all_gather(mates, "level")
 
@@ -169,14 +177,12 @@
     for level in range(1, levels):
         if level > 1:
             own = solved[-1]
-            if level == levels - 1:
-                own, mates = lax.optimization_barrier((own, mates))
-                solved[-1] = own
             far = lax.ppermute(own, "dom", far_pairs)
             near = lax.ppermute(own, "dom", near_pairs)
         around.append(near if level % 2 == 0 else far)
         kernel = functools.partial(forward_kernel, level, share)
-        solved += call(kernel, [vector], owners, weights, places, side, far, own, near)
+        solved += call(kernel, [vector], packed, weights, places, side, far, own, near)
+    solved[-1], mates = lax.optimization_barrier((solved[-1], mates))
     around.append(lax.ppermute(solved[-1], "dom", near_pairs))
 
     flow = []
@@ -185,7 +191,7 @@
         kernel = functools.partial(backward_kernel, level, share, level == levels - 1)
         outs = [vector, summed] if level else [vector]
         result, *rest = call(
-            kernel, outs, owners, weights, mates, targets, solved[level], around[level], *flow
+            kernel, outs, packed, weights, mates, targets, solved[level], around[level], *flow
         )
         results.append(result)
         if level:

time: 250 us -> 242 us (0.968)
  Pallas kernels: 21.2 us -> 11.1 us
    pallas_call x15, Pallas kernels: 21.2 us -> 11.1 us  [call(): pl.pallas_call(kernel, out_shape=outs, in_specs=[vmem] * len(args), out_s...]
    unnamed x20 -> x22, local copies, waits for them, and re-layouts: 6.88 us -> 9.07 us
  transfers between devices with their start and end apart: 27 -> 27, of which waited for: 20 -> 21; matrix products, arithmetic and copies ran while one was open for 5% -> 5% of each run, Pallas kernels for 3% -> 2%
where the time goes in v6:
time: 242 us; the launch traced here: 241 us
  starting transfers between devices  96.9 us (40%)
  waiting for transfers between devices  59.7 us (25%)
  blocking collectives  30 us (12%)
  local copies, waits for them, and re-layouts  17.2 us (7%)
  between operations  17.2 us (7%)
  Pallas kernels  11.1 us (5%)
  other arithmetic  7.96 us (3%)
    ppermute x7, starting transfers between devices, local(): far = lax.ppermute(own, 'dom', far_pairs)  30.2 us
    all_to_all x1, blocking collectives, local(): both = lax.all_to_all(both, 'level', 1, 0, tiled=False)  30 us
    ppermute x7, starting transfers between devices, local(): lax.ppermute(held, 'dom', far_pairs if level % 2 else near_pairs)  27.1 us
    ppermute x7, waiting for transfers between devices, local(): lax.ppermute(held, 'dom', far_pairs if level % 2 else near_pairs)  18.8 us
    all_gather x1, waiting for transfers between devices, local(): weights = lax.all_gather(weights, 'level')  17.5 us
    ppermute x7, starting transfers between devices, local(): near = lax.ppermute(own, 'dom', near_pairs)  13.4 us
    ppermute x7, waiting for transfers between devices, local(): far = lax.ppermute(own, 'dom', far_pairs)  11.5 us
    pallas_call x15, Pallas kernels, call(): pl.pallas_call(kernel, out_shape=outs, in_specs=[vmem] * len(args), out_s...  11.1 us
  transfers between devices with their start and end apart: 27, of which 21 were waited for; matrix products, arithmetic and copies ran while one was open for 5% of the time, Pallas kernels for 2%

profile of v6, /device:TPU:1, one launch (start us, length us, event | category | flops | bytes accessed | tf_op | source)
XLA Modules:
  0.0 241.2 jit_solution(7699370017126545407)
XLA Ops:
  7.2 1.9 pad_maximum_fusion
  9.2 1.3 compare_select_fusion
  15.0 4.8 %collective-permute-start = (bf16[4,2,128,128]{3,2,1,0:T(8,128)(2,1)S(1)}, bf16[4,2,128,128]{3,2,1,0:T(8,128)(2,1)S(1)}, u32[]{:S(2)}, u32[]{:S(2)}) collective-permute-start(bf16[4,2,128,128]{3,2,1,0:T(8,128)(2,1)S(1)} %pad_maximum_fusion.1), channel_id=1, source_target_pairs={{0,16},{16,0},{32,48},{48,32},{64,80},{80,64},{96,112},{112,96},{1... | collective-permute-start | bytes 786440 | tf_op jit(solution)/shard_map/ppermute | solution.py:130
  19.9 11.0 %collective-permute-start.1 = (bf16[4,2,128,128]{3,2,1,0:T(8,128)(2,1)S(1)}, bf16[4,2,128,128]{3,2,1,0:T(8,128)(2,1)S(1)}, u32[]{:S(2)}, u32[]{:S(2)}) collective-permute-start(bf16[4,2,128,128]{3,2,1,0:T(8,128)(2,1)S(1)} %pad_maximum_fusion.1), channel_id=1, source_target_pairs={{16,32},{32,16},{48,64},{64,48},{80,96},{96,80},{112,128},{128,112... | collective-permute-start | bytes 786440 | tf_op jit(solution)/shard_map/ppermute | solution.py:131
  32.7 8.3 %all-to-all-start = ((bf16[1,4,16,4,128]{4,3,1,0,2:T(4,128)(2,1)}), bf16[1,4,16,4,128]{4,3,1,0,2:T(4,128)(2,1)S(1)}, u32[]{:S(2)}, u32[]{:S(2)}) async-start(bf16[1,4,16,4,128]{4,3,1,0,2:T(4,128)(2,1)} %copy.72), calls=%async_computation | async-start | bytes 131072 | tf_op jit(solution)/shard_map/all_to_all | solution.py:136
  48.0 1.7 all-to-all-done
  50.3 1.9 collective-permute-start.2
  52.3 1.9 collective-permute-start.3
  54.9 3.1 %collective-permute-done.2.far.solved_mate = bf16[32,128]{1,0:T(8,128)(2,1)S(1)} collective-permute-done((bf16[32,128]{1,0:T(8,128)(2,1)S(1)}, bf16[32,128]{1,0:T(8,128)(2,1)S(1)}, u32[]{:S(2)}, u32[]{:S(2)}) %collective-permute-start.2) | collective-permute-done | bytes 8224 | tf_op jit(solution)/shard_map/ppermute | solution.py:168
  58.1 17.5 %all-gather.5.cloned.1.call-done = bf16[64,4,128,128]{3,2,1,0:T(8,128)(2,1)} async-done(((bf16[4,4,128,128]{3,2,1,0:T(8,128)(2,1)}), bf16[64,4,128,128]{3,2,1,0:T(8,128)(2,1)}) %all-gather.5.cloned.1.call-update) | async-done | bytes 8388624 | tf_op jit(solution)/shard_map/all_gather | solution.py:118
  75.7 3.4 %copy-done = bf16[64,4,128,128]{3,2,1,0:T(8,128)(2,1)S(1)} copy-done((bf16[64,4,128,128]{3,2,1,0:T(8,128)(2,1)S(1)}, bf16[64,4,128,128]{3,2,1,0:T(8,128)(2,1)}, u32[]{:S(2)}) %copy-start) | copy-done | bytes 8388632
  79.7 7.7 %collective-permute-start.4 = (bf16[32,128]{1,0:T(8,128)(2,1)S(1)}, bf16[32,128]{1,0:T(8,128)(2,1)S(1)}, u32[]{:S(2)}, u32[]{:S(2)}) collective-permute-start(bf16[32,128]{1,0:T(8,128)(2,1)S(1)} %shard_map.68.own.solved), channel_id=1, source_target_pairs={{16,32},{32,16},{48,64},{64,48},{80,96},{96,80},{112,128},{128,112... | collective-permute-start | bytes 24584 | tf_op jit(solution)/shard_map/ppermute | solution.py:180
  87.4 1.9 collective-permute-start.5
  89.3 2.5 %collective-permute-done.5.near.solved_mate = bf16[32,128]{1,0:T(8,128)(2,1)S(1)} collective-permute-done((bf16[32,128]{1,0:T(8,128)(2,1)S(1)}, bf16[32,128]{1,0:T(8,128)(2,1)S(1)}, u32[]{:S(2)}, u32[]{:S(2)}) %collective-permute-start.5) | collective-permute-done | bytes 8224 | tf_op jit(solution)/shard_map/ppermute | solution.py:181
  92.4 3.3 %collective-permute-start.6 = (bf16[32,128]{1,0:T(8,128)(2,1)S(1)}, bf16[32,128]{1,0:T(8,128)(2,1)S(1)}, u32[]{:S(2)}, u32[]{:S(2)}) collective-permute-start(bf16[32,128]{1,0:T(8,128)(2,1)S(1)} %shard_map.69.own.solved), channel_id=1, source_target_pairs={{16,32},{32,16},{48,64},{64,48},{80,96},{96,80},{112,128},{128,112... | collective-permute-start | bytes 24584 | tf_op jit(solution)/shard_map/ppermute | solution.py:180
  95.7 1.9 collective-permute-start.7
  97.6 2.5 %collective-permute-done.6.far.solved_mate = bf16[32,128]{1,0:T(8,128)(2,1)S(1)} collective-permute-done((bf16[32,128]{1,0:T(8,128)(2,1)S(1)}, bf16[32,128]{1,0:T(8,128)(2,1)S(1)}, u32[]{:S(2)}, u32[]{:S(2)}) %collective-permute-start.6) | collective-permute-done | bytes 8224 | tf_op jit(solution)/shard_map/ppermute | solution.py:180
  101.1 5.3 %collective-permute-start.8 = (bf16[32,128]{1,0:T(8,128)(2,1)S(1)}, bf16[32,128]{1,0:T(8,128)(2,1)S(1)}, u32[]{:S(2)}, u32[]{:S(2)}) collective-permute-start(bf16[32,128]{1,0:T(8,128)(2,1)S(1)} %shard_map.70.own.solved), channel_id=1, source_target_pairs={{16,32},{32,16},{48,64},{64,48},{80,96},{96,80},{112,128},{128,112... | collective-permute-start | bytes 24584 | tf_op jit(solution)/shard_map/ppermute | solution.py:180
  106.4 1.9 collective-permute-start.9
  108.8 2.4 collective-permute-done.9.near.solved_mate
  111.8 3.3 %collective-permute-start.10 = (bf16[32,128]{1,0:T(8,128)(2,1)S(1)}, bf16[32,128]{1,0:T(8,128)(2,1)S(1)}, u32[]{:S(2)}, u32[]{:S(2)}) collective-permute-start(bf16[32,128]{1,0:T(8,128)(2,1)S(1)} %shard_map.71.own.solved), channel_id=1, source_target_pairs={{16,32},{32,16},{48,64},{64,48},{80,96},{96,80},{112,128},{128,112... | collective-permute-start | bytes 24584 | tf_op jit(solution)/shard_map/ppermute | solution.py:180
  115.1 1.9 collective-permute-start.11
  117.0 2.5 %collective-permute-done.10.far.solved_mate = bf16[32,128]{1,0:T(8,128)(2,1)S(1)} collective-permute-done((bf16[32,128]{1,0:T(8,128)(2,1)S(1)}, bf16[32,128]{1,0:T(8,128)(2,1)S(1)}, u32[]{:S(2)}, u32[]{:S(2)}) %collective-permute-start.10) | collective-permute-done | bytes 8224 | tf_op jit(solution)/shard_map/ppermute | solution.py:180
  120.5 5.3 %collective-permute-start.12 = (bf16[32,128]{1,0:T(8,128)(2,1)S(1)}, bf16[32,128]{1,0:T(8,128)(2,1)S(1)}, u32[]{:S(2)}, u32[]{:S(2)}) collective-permute-start(bf16[32,128]{1,0:T(8,128)(2,1)S(1)} %shard_map.72.own.solved), channel_id=1, source_target_pairs={{16,32},{32,16},{48,64},{64,48},{80,96},{96,80},{112,128},{128,112... | collective-permute-start | bytes 24584 | tf_op jit(solution)/shard_map/ppermute | solution.py:180
  125.8 1.9 collective-permute-start.13
  128.2 2.0 collective-permute-done.13.near.solved_mate
  130.8 3.3 %collective-permute-start.14 = (bf16[32,128]{1,0:T(8,128)(2,1)S(1)}, bf16[32,128]{1,0:T(8,128)(2,1)S(1)}, u32[]{:S(2)}, u32[]{:S(2)}) collective-permute-start(bf16[32,128]{1,0:T(8,128)(2,1)S(1)} %shard_map.73.own.solved), channel_id=1, source_target_pairs={{16,32},{32,16},{48,64},{64,48},{80,96},{96,80},{112,128},{128,112... | collective-permute-start | bytes 24584 | tf_op jit(solution)/shard_map/ppermute | solution.py:180
  134.1 1.9 collective-permute-start.15
  136.1 2.5 %collective-permute-done.14.far.solved_mate = bf16[32,128]{1,0:T(8,128)(2,1)S(1)} collective-permute-done((bf16[32,128]{1,0:T(8,128)(2,1)S(1)}, bf16[32,128]{1,0:T(8,128)(2,1)S(1)}, u32[]{:S(2)}, u32[]{:S(2)}) %collective-permute-start.14) | collective-permute-done | bytes 8224 | tf_op jit(solution)/shard_map/ppermute | solution.py:180
  139.1 1.9 collective-permute-start.16
  141.1 2.5 %collective-permute-done.16.solved_mate = bf16[32,128]{1,0:T(8,128)(2,1)S(1)} collective-permute-done((bf16[32,128]{1,0:T(8,128)(2,1)S(1)}, bf16[32,128]{1,0:T(8,128)(2,1)S(1)}, u32[]{:S(2)}, u32[]{:S(2)}) %collective-permute-start.16) | collective-permute-done | bytes 8224 | tf_op jit(solution)/shard_map/ppermute | solution.py:186
  143.5 3.4 %copy-done.1 = bf16[64,4,128,128]{3,2,1,0:T(8,128)(2,1)S(1)} copy-done((bf16[64,4,128,128]{3,2,1,0:T(8,128)(2,1)S(1)}, bf16[64,4,128,128]{3,2,1,0:T(8,128)(2,1)}, u32[]{:S(2)}) %copy-start.1) | copy-done | bytes 8388632
  146.9 2.2 copy-done.2
  149.9 5.4 %collective-permute-start.17 = (f32[64,128]{1,0:T(8,128)S(1)}, f32[64,128]{1,0:T(8,128)S(1)}, u32[]{:S(2)}, u32[]{:S(2)}) collective-permute-start(f32[64,128]{1,0:T(8,128)S(1)} %get-tuple-element.36.rest_0_), channel_id=1, source_target_pairs={{16,32},{32,16},{48,64},{64,48},{80,96},{96,80},{112,128},{128,112... | collective-permute-start | bytes 98312 | tf_op jit(solution)/shard_map/ppermute | solution.py:199
  155.4 2.7 %collective-permute-done.17.rest_1_ = f32[64,128]{1,0:T(8,128)S(1)} collective-permute-done((f32[64,128]{1,0:T(8,128)S(1)}, f32[64,128]{1,0:T(8,128)S(1)}, u32[]{:S(2)}, u32[]{:S(2)}) %collective-permute-start.17) | collective-permute-done | bytes 32800 | tf_op jit(solution)/shard_map/ppermute | solution.py:199
  159.0 1.9 collective-permute-start.18
  160.9 2.7 %collective-permute-done.18.rest_1_ = f32[64,128]{1,0:T(8,128)S(1)} collective-permute-done((f32[64,128]{1,0:T(8,128)S(1)}, f32[64,128]{1,0:T(8,128)S(1)}, u32[]{:S(2)}, u32[]{:S(2)}) %collective-permute-start.18) | collective-permute-done | bytes 32800 | tf_op jit(solution)/shard_map/ppermute | solution.py:199
  164.6 5.3 %collective-permute-start.19 = (f32[64,128]{1,0:T(8,128)S(1)}, f32[64,128]{1,0:T(8,128)S(1)}, u32[]{:S(2)}, u32[]{:S(2)}) collective-permute-start(f32[64,128]{1,0:T(8,128)S(1)} %get-tuple-element.38.rest_0_), channel_id=1, source_target_pairs={{16,32},{32,16},{48,64},{64,48},{80,96},{96,80},{112,128},{128,112... | collective-permute-start | bytes 98312 | tf_op jit(solution)/shard_map/ppermute | solution.py:199
  169.9 2.7 %collective-permute-done.19.rest_1_ = f32[64,128]{1,0:T(8,128)S(1)} collective-permute-done((f32[64,128]{1,0:T(8,128)S(1)}, f32[64,128]{1,0:T(8,128)S(1)}, u32[]{:S(2)}, u32[]{:S(2)}) %collective-permute-start.19) | collective-permute-done | bytes 32800 | tf_op jit(solution)/shard_map/ppermute | solution.py:199
  173.6 1.9 collective-permute-start.20
  175.5 2.7 %collective-permute-done.20.rest_1_ = f32[64,128]{1,0:T(8,128)S(1)} collective-permute-done((f32[64,128]{1,0:T(8,128)S(1)}, f32[64,128]{1,0:T(8,128)S(1)}, u32[]{:S(2)}, u32[]{:S(2)}) %collective-permute-start.20) | collective-permute-done | bytes 32800 | tf_op jit(solution)/shard_map/ppermute | solution.py:199
  179.2 5.3 %collective-permute-start.21 = (f32[64,128]{1,0:T(8,128)S(1)}, f32[64,128]{1,0:T(8,128)S(1)}, u32[]{:S(2)}, u32[]{:S(2)}) collective-permute-start(f32[64,128]{1,0:T(8,128)S(1)} %get-tuple-element.40.rest_0_), channel_id=1, source_target_pairs={{16,32},{32,16},{48,64},{64,48},{80,96},{96,80},{112,128},{128,112... | collective-permute-start | bytes 98312 | tf_op jit(solution)/shard_map/ppermute | solution.py:199
  184.5 2.7 %collective-permute-done.21.rest_1_ = f32[64,128]{1,0:T(8,128)S(1)} collective-permute-done((f32[64,128]{1,0:T(8,128)S(1)}, f32[64,128]{1,0:T(8,128)S(1)}, u32[]{:S(2)}, u32[]{:S(2)}) %collective-permute-start.21) | collective-permute-done | bytes 32800 | tf_op jit(solution)/shard_map/ppermute | solution.py:199
  188.2 1.9 collective-permute-start.22
  190.1 2.7 %collective-permute-done.22.rest_1_ = f32[64,128]{1,0:T(8,128)S(1)} collective-permute-done((f32[64,128]{1,0:T(8,128)S(1)}, f32[64,128]{1,0:T(8,128)S(1)}, u32[]{:S(2)}, u32[]{:S(2)}) %collective-permute-start.22) | collective-permute-done | bytes 32800 | tf_op jit(solution)/shard_map/ppermute | solution.py:199
  193.8 5.3 %collective-permute-start.23 = (f32[64,128]{1,0:T(8,128)S(1)}, f32[64,128]{1,0:T(8,128)S(1)}, u32[]{:S(2)}, u32[]{:S(2)}) collective-permute-start(f32[64,128]{1,0:T(8,128)S(1)} %get-tuple-element.42.rest_0_), channel_id=1, source_target_pairs={{16,32},{32,16},{48,64},{64,48},{80,96},{96,80},{112,128},{128,112... | collective-permute-start | bytes 98312 | tf_op jit(solution)/shard_map/ppermute | solution.py:199
  199.1 2.7 %collective-permute-done.23.rest_1_ = f32[64,128]{1,0:T(8,128)S(1)} collective-permute-done((f32[64,128]{1,0:T(8,128)S(1)}, f32[64,128]{1,0:T(8,128)S(1)}, u32[]{:S(2)}, u32[]{:S(2)}) %collective-permute-start.23) | collective-permute-done | bytes 32800 | tf_op jit(solution)/shard_map/ppermute | solution.py:199
  203.0 30.0 %all_to_all.30 = bf16[1,2,16,4,4,128]{5,4,3,1,0,2:T(4,128)(2,1)S(1)} all-to-all(bf16[1,2,16,4,4,128]{5,4,3,1,0,2:T(4,128)(2,1)S(1)} %bitcast.133), channel_id=1, replica_groups=mesh['dom'=32,'level'=16] {'level'}, dimensions={2} | all-to-all | bytes 262144 | tf_op jit(solution)/shard_map/all_to_all | solution.py:203
  (104 shorter events, 27.1 us)
Async XLA Ops:
  7.2 68.5 %all-gather.5.cloned.1.call-start = ((), (), s32[]{:S(2)}) async-start(), calls=%async_computation.2 | async-start | bytes 8912896 | tf_op jit(solution)/shard_map/all_gather | solution.py:118
  15.0 39.1 %collective-permute-start = (bf16[4,2,128,128]{3,2,1,0:T(8,128)(2,1)S(1)}, bf16[4,2,128,128]{3,2,1,0:T(8,128)(2,1)S(1)}, u32[]{:S(2)}, u32[]{:S(2)}) collective-permute-start(bf16[4,2,128,128]{3,2,1,0:T(8,128)(2,1)S(1)} %pad_maximum_fusion.1), channel_id=1, source_target_pairs={{0,16},{16,0},{32,48},{48,32},{64,80},{80,64},{96,112},{112,96},{1... | collective-permute-start | bytes 786440 | tf_op jit(solution)/shard_map/ppermute | solution.py:130
  19.9 34.3 %collective-permute-start.1 = (bf16[4,2,128,128]{3,2,1,0:T(8,128)(2,1)S(1)}, bf16[4,2,128,128]{3,2,1,0:T(8,128)(2,1)S(1)}, u32[]{:S(2)}, u32[]{:S(2)}) collective-permute-start(bf16[4,2,128,128]{3,2,1,0:T(8,128)(2,1)S(1)} %pad_maximum_fusion.1), channel_id=1, source_target_pairs={{16,32},{32,16},{48,64},{64,48},{80,96},{96,80},{112,128},{128,112... | collective-permute-start | bytes 786440 | tf_op jit(solution)/shard_map/ppermute | solution.py:131
  32.7 17.0 %all-to-all-start = ((bf16[1,4,16,4,128]{4,3,1,0,2:T(4,128)(2,1)}), bf16[1,4,16,4,128]{4,3,1,0,2:T(4,128)(2,1)S(1)}, u32[]{:S(2)}, u32[]{:S(2)}) async-start(bf16[1,4,16,4,128]{4,3,1,0,2:T(4,128)(2,1)} %copy.72), calls=%async_computation | async-start | bytes 131072 | tf_op jit(solution)/shard_map/all_to_all | solution.py:136
  41.0 98.1 %all-gather.7.cloned.1.call-start = ((), (), s32[]{:S(2)}) async-start(), calls=%async_computation.3 | async-start | bytes 4456448 | tf_op jit(solution)/shard_map/all_gather | solution.py:173
  50.3 7.7 %collective-permute-start.2 = (bf16[32,128]{1,0:T(8,128)(2,1)S(1)}, bf16[32,128]{1,0:T(8,128)(2,1)S(1)}, u32[]{:S(2)}, u32[]{:S(2)}) collective-permute-start(bf16[32,128]{1,0:T(8,128)(2,1)S(1)} %bitcast.125), channel_id=1, source_target_pairs={{16,32},{32,16},{48,64},{64,48},{80,96},{96,80},{112,128},{128,112... | collective-permute-start | bytes 24584 | tf_op jit(solution)/shard_map/ppermute | solution.py:168
  52.3 5.8 %collective-permute-start.3 = (bf16[32,128]{1,0:T(8,128)(2,1)S(1)}, bf16[32,128]{1,0:T(8,128)(2,1)S(1)}, u32[]{:S(2)}, u32[]{:S(2)}) collective-permute-start(bf16[32,128]{1,0:T(8,128)(2,1)S(1)} %bitcast.126), channel_id=1, source_target_pairs={{0,16},{16,0},{32,48},{48,32},{64,80},{80,64},{96,112},{112,96},{1... | collective-permute-start | bytes 24584 | tf_op jit(solution)/shard_map/ppermute | solution.py:169
  75.7 3.4 %copy-start = (bf16[64,4,128,128]{3,2,1,0:T(8,128)(2,1)S(1)}, bf16[64,4,128,128]{3,2,1,0:T(8,128)(2,1)}, u32[]{:S(2)}) copy-start(bf16[64,4,128,128]{3,2,1,0:T(8,128)(2,1)} %all-gather.5.cloned.1.call-done) | copy-start | bytes 25165828
  79.7 9.7 %collective-permute-start.4 = (bf16[32,128]{1,0:T(8,128)(2,1)S(1)}, bf16[32,128]{1,0:T(8,128)(2,1)S(1)}, u32[]{:S(2)}, u32[]{:S(2)}) collective-permute-start(bf16[32,128]{1,0:T(8,128)(2,1)S(1)} %shard_map.68.own.solved), channel_id=1, source_target_pairs={{16,32},{32,16},{48,64},{64,48},{80,96},{96,80},{112,128},{128,112... | collective-permute-start | bytes 24584 | tf_op jit(solution)/shard_map/ppermute | solution.py:180
  87.4 4.4 %collective-permute-start.5 = (bf16[32,128]{1,0:T(8,128)(2,1)S(1)}, bf16[32,128]{1,0:T(8,128)(2,1)S(1)}, u32[]{:S(2)}, u32[]{:S(2)}) collective-permute-start(bf16[32,128]{1,0:T(8,128)(2,1)S(1)} %shard_map.68.own.solved), channel_id=1, source_target_pairs={{0,16},{16,0},{32,48},{48,32},{64,80},{80,64},{96,112},{112,96},{1... | collective-permute-start | bytes 24584 | tf_op jit(solution)/shard_map/ppermute | solution.py:181
  92.4 7.7 %collective-permute-start.6 = (bf16[32,128]{1,0:T(8,128)(2,1)S(1)}, bf16[32,128]{1,0:T(8,128)(2,1)S(1)}, u32[]{:S(2)}, u32[]{:S(2)}) collective-permute-start(bf16[32,128]{1,0:T(8,128)(2,1)S(1)} %shard_map.69.own.solved), channel_id=1, source_target_pairs={{16,32},{32,16},{48,64},{64,48},{80,96},{96,80},{112,128},{128,112... | collective-permute-start | bytes 24584 | tf_op jit(solution)/shard_map/ppermute | solution.py:180
  95.7 4.8 %collective-permute-start.7 = (bf16[32,128]{1,0:T(8,128)(2,1)S(1)}, bf16[32,128]{1,0:T(8,128)(2,1)S(1)}, u32[]{:S(2)}, u32[]{:S(2)}) collective-permute-start(bf16[32,128]{1,0:T(8,128)(2,1)S(1)} %shard_map.69.own.solved), channel_id=1, source_target_pairs={{0,16},{16,0},{32,48},{48,32},{64,80},{80,64},{96,112},{112,96},{1... | collective-permute-start | bytes 24584 | tf_op jit(solution)/shard_map/ppermute | solution.py:181
  101.1 7.7 %collective-permute-start.8 = (bf16[32,128]{1,0:T(8,128)(2,1)S(1)}, bf16[32,128]{1,0:T(8,128)(2,1)S(1)}, u32[]{:S(2)}, u32[]{:S(2)}) collective-permute-start(bf16[32,128]{1,0:T(8,128)(2,1)S(1)} %shard_map.70.own.solved), channel_id=1, source_target_pairs={{16,32},{32,16},{48,64},{64,48},{80,96},{96,80},{112,128},{128,112... | collective-permute-start | bytes 24584 | tf_op jit(solution)/shard_map/ppermute | solution.py:180
  106.4 4.8 %collective-permute-start.9 = (bf16[32,128]{1,0:T(8,128)(2,1)S(1)}, bf16[32,128]{1,0:T(8,128)(2,1)S(1)}, u32[]{:S(2)}, u32[]{:S(2)}) collective-permute-start(bf16[32,128]{1,0:T(8,128)(2,1)S(1)} %shard_map.70.own.solved), channel_id=1, source_target_pairs={{0,16},{16,0},{32,48},{48,32},{64,80},{80,64},{96,112},{112,96},{1... | collective-permute-start | bytes 24584 | tf_op jit(solution)/shard_map/ppermute | solution.py:181
  111.8 7.7 %collective-permute-start.10 = (bf16[32,128]{1,0:T(8,128)(2,1)S(1)}, bf16[32,128]{1,0:T(8,128)(2,1)S(1)}, u32[]{:S(2)}, u32[]{:S(2)}) collective-permute-start(bf16[32,128]{1,0:T(8,128)(2,1)S(1)} %shard_map.71.own.solved), channel_id=1, source_target_pairs={{16,32},{32,16},{48,64},{64,48},{80,96},{96,80},{112,128},{128,112... | collective-permute-start | bytes 24584 | tf_op jit(solution)/shard_map/ppermute | solution.py:180
  115.1 4.8 %collective-permute-start.11 = (bf16[32,128]{1,0:T(8,128)(2,1)S(1)}, bf16[32,128]{1,0:T(8,128)(2,1)S(1)}, u32[]{:S(2)}, u32[]{:S(2)}) collective-permute-start(bf16[32,128]{1,0:T(8,128)(2,1)S(1)} %shard_map.71.own.solved), channel_id=1, source_target_pairs={{0,16},{16,0},{32,48},{48,32},{64,80},{80,64},{96,112},{112,96},{1... | collective-permute-start | bytes 24584 | tf_op jit(solution)/shard_map/ppermute | solution.py:181
  120.5 7.7 %collective-permute-start.12 = (bf16[32,128]{1,0:T(8,128)(2,1)S(1)}, bf16[32,128]{1,0:T(8,128)(2,1)S(1)}, u32[]{:S(2)}, u32[]{:S(2)}) collective-permute-start(bf16[32,128]{1,0:T(8,128)(2,1)S(1)} %shard_map.72.own.solved), channel_id=1, source_target_pairs={{16,32},{32,16},{48,64},{64,48},{80,96},{96,80},{112,128},{128,112... | collective-permute-start | bytes 24584 | tf_op jit(solution)/shard_map/ppermute | solution.py:180
  125.8 4.4 %collective-permute-start.13 = (bf16[32,128]{1,0:T(8,128)(2,1)S(1)}, bf16[32,128]{1,0:T(8,128)(2,1)S(1)}, u32[]{:S(2)}, u32[]{:S(2)}) collective-permute-start(bf16[32,128]{1,0:T(8,128)(2,1)S(1)} %shard_map.72.own.solved), channel_id=1, source_target_pairs={{0,16},{16,0},{32,48},{48,32},{64,80},{80,64},{96,112},{112,96},{1... | collective-permute-start | bytes 24584 | tf_op jit(solution)/shard_map/ppermute | solution.py:181
  130.8 7.7 %collective-permute-start.14 = (bf16[32,128]{1,0:T(8,128)(2,1)S(1)}, bf16[32,128]{1,0:T(8,128)(2,1)S(1)}, u32[]{:S(2)}, u32[]{:S(2)}) collective-permute-start(bf16[32,128]{1,0:T(8,128)(2,1)S(1)} %shard_map.73.own.solved), channel_id=1, source_target_pairs={{16,32},{32,16},{48,64},{64,48},{80,96},{96,80},{112,128},{128,112... | collective-permute-start | bytes 24584 | tf_op jit(solution)/shard_map/ppermute | solution.py:180
  134.1 4.4 %collective-permute-start.15 = (bf16[32,128]{1,0:T(8,128)(2,1)S(1)}, bf16[32,128]{1,0:T(8,128)(2,1)S(1)}, u32[]{:S(2)}, u32[]{:S(2)}) collective-permute-start(bf16[32,128]{1,0:T(8,128)(2,1)S(1)} %shard_map.73.own.solved), channel_id=1, source_target_pairs={{0,16},{16,0},{32,48},{48,32},{64,80},{80,64},{96,112},{112,96},{1... | collective-permute-start | bytes 24584 | tf_op jit(solution)/shard_map/ppermute | solution.py:181
  139.1 4.4 %collective-permute-start.16 = (bf16[32,128]{1,0:T(8,128)(2,1)S(1)}, bf16[32,128]{1,0:T(8,128)(2,1)S(1)}, u32[]{:S(2)}, u32[]{:S(2)}) collective-permute-start(bf16[32,128]{1,0:T(8,128)(2,1)S(1)} %shard_map.74.solved), channel_id=1, source_target_pairs={{0,16},{16,0},{32,48},{48,32},{64,80},{80,64},{96,112},{112,96},{1... | collective-permute-start | bytes 24584 | tf_op jit(solution)/shard_map/ppermute | solution.py:186
  143.5 3.4 %copy-start.1 = (bf16[64,4,128,128]{3,2,1,0:T(8,128)(2,1)S(1)}, bf16[64,4,128,128]{3,2,1,0:T(8,128)(2,1)}, u32[]{:S(2)}) copy-start(bf16[64,4,128,128]{3,2,1,0:T(8,128)(2,1)} %all-gather.5.cloned.1.call-done) | copy-start | bytes 25165828
  146.9 2.2 copy-start.2
  149.1 8.9 %copy-start.3 = (bf16[64,2,128,128]{3,2,1,0:T(8,128)(2,1)S(1)}, bf16[64,2,128,128]{3,2,1,0:T(8,128)(2,1)}, u32[]{:S(2)}) copy-start(bf16[64,2,128,128]{3,2,1,0:T(8,128)(2,1)} %all-gather.7.cloned.1.call-done) | copy-start | bytes 12582916
  149.9 8.1 %collective-permute-start.17 = (f32[64,128]{1,0:T(8,128)S(1)}, f32[64,128]{1,0:T(8,128)S(1)}, u32[]{:S(2)}, u32[]{:S(2)}) collective-permute-start(f32[64,128]{1,0:T(8,128)S(1)} %get-tuple-element.36.rest_0_), channel_id=1, source_target_pairs={{16,32},{32,16},{48,64},{64,48},{80,96},{96,80},{112,128},{128,112... | collective-permute-start | bytes 98312 | tf_op jit(solution)/shard_map/ppermute | solution.py:199
  159.0 4.7 %collective-permute-start.18 = (f32[64,128]{1,0:T(8,128)S(1)}, f32[64,128]{1,0:T(8,128)S(1)}, u32[]{:S(2)}, u32[]{:S(2)}) collective-permute-start(f32[64,128]{1,0:T(8,128)S(1)} %get-tuple-element.37.rest_0_), channel_id=1, source_target_pairs={{0,16},{16,0},{32,48},{48,32},{64,80},{80,64},{96,112},{112,96},{1... | collective-permute-start | bytes 98312 | tf_op jit(solution)/shard_map/ppermute | solution.py:199
  164.6 8.0 %collective-permute-start.19 = (f32[64,128]{1,0:T(8,128)S(1)}, f32[64,128]{1,0:T(8,128)S(1)}, u32[]{:S(2)}, u32[]{:S(2)}) collective-permute-start(f32[64,128]{1,0:T(8,128)S(1)} %get-tuple-element.38.rest_0_), channel_id=1, source_target_pairs={{16,32},{32,16},{48,64},{64,48},{80,96},{96,80},{112,128},{128,112... | collective-permute-start | bytes 98312 | tf_op jit(solution)/shard_map/ppermute | solution.py:199
  173.6 4.7 %collective-permute-start.20 = (f32[64,128]{1,0:T(8,128)S(1)}, f32[64,128]{1,0:T(8,128)S(1)}, u32[]{:S(2)}, u32[]{:S(2)}) collective-permute-start(f32[64,128]{1,0:T(8,128)S(1)} %get-tuple-element.39.rest_0_), channel_id=1, source_target_pairs={{0,16},{16,0},{32,48},{48,32},{64,80},{80,64},{96,112},{112,96},{1... | collective-permute-start | bytes 98312 | tf_op jit(solution)/shard_map/ppermute | solution.py:199
  179.2 8.0 %collective-permute-start.21 = (f32[64,128]{1,0:T(8,128)S(1)}, f32[64,128]{1,0:T(8,128)S(1)}, u32[]{:S(2)}, u32[]{:S(2)}) collective-permute-start(f32[64,128]{1,0:T(8,128)S(1)} %get-tuple-element.40.rest_0_), channel_id=1, source_target_pairs={{16,32},{32,16},{48,64},{64,48},{80,96},{96,80},{112,128},{128,112... | collective-permute-start | bytes 98312 | tf_op jit(solution)/shard_map/ppermute | solution.py:199
  188.2 4.7 %collective-permute-start.22 = (f32[64,128]{1,0:T(8,128)S(1)}, f32[64,128]{1,0:T(8,128)S(1)}, u32[]{:S(2)}, u32[]{:S(2)}) collective-permute-start(f32[64,128]{1,0:T(8,128)S(1)} %get-tuple-element.41.rest_0_), channel_id=1, source_target_pairs={{0,16},{16,0},{32,48},{48,32},{64,80},{80,64},{96,112},{112,96},{1... | collective-permute-start | bytes 98312 | tf_op jit(solution)/shard_map/ppermute | solution.py:199
  193.8 8.0 %collective-permute-start.23 = (f32[64,128]{1,0:T(8,128)S(1)}, f32[64,128]{1,0:T(8,128)S(1)}, u32[]{:S(2)}, u32[]{:S(2)}) collective-permute-start(f32[64,128]{1,0:T(8,128)S(1)} %get-tuple-element.42.rest_0_), channel_id=1, source_target_pairs={{16,32},{32,16},{48,64},{64,48},{80,96},{96,80},{112,128},{128,112... | collective-permute-start | bytes 98312 | tf_op jit(solution)/shard_map/ppermute | solution.py:199
Sparse Core Ops, SparseCore 0:
  10.1 65.5 all-gather.4
  77.8 43.6 all-gather.6

commit v7 on v6

--- a/solution.py
+++ b/solution.py
@@ -50,56 +50,120 @@
     return jnp.concatenate(totals, axis=0)
 
 
-def forward_kernel(level, share, packed, weights, places, side, far, own, near, out):
+def picked_from(places, around):
+    at = lax.broadcasted_iota(jnp.int32, (places.shape[0], around.shape[0]), 1)
+    return dot(ones_where(at == places), around)
+
+
+def forward_kernel(level, share, fetched, packed, weights, places, side, far, own, near, out, *held):
     *owners, _ = unpack(packed, level)
+    if fetched:
+        held, sems = held
+        copies = [
+            pltpu.make_async_copy(weights.at[owners[half]], held.at[half], sems.at[half])
+            for half in range(2)
+        ]
+        for copy in copies:
+            copy.start()
     span = out.shape[0]
-    around = jnp.concatenate([far[...], own[...], near[...]], axis=0)
-    at = lax.broadcasted_iota(jnp.int32, (3 * span, 3 * span), 1)
-    picked = dot(ones_where(at == places[level]), around)
+    picked = picked_from(places[level], jnp.concatenate([far[...], own[...], near[...]], axis=0))
     picked = jnp.concatenate([picked[n * span : (n + 1) * span] for n in range(3)], axis=1)
+    if fetched:
+        for copy in copies:
+            copy.wait()
+        owners, weights = range(2), held
     total = products(dot, share, owners, picked.astype(BF16), weights, slice(1, None))
     shifted = (side[level].astype(F32) - total).astype(BF16)
     out[...] = products(dot, share, owners, shifted, weights, 0).astype(BF16)
 
 
-def backward_kernel(level, share, top, packed, weights, mates, targets, solved, solved_mate, *rest):
-    if top:
-        result, *outs = rest
-    else:
-        held, came, result, *outs = rest
+def gathered_sums(level, share, packed, weights, mates, places, own, mate):
     *owners, side = unpack(packed, level)
-    span = result.shape[0]
-    done, done_mate = solved[...], solved_mate[...]
-    if not top:
-        folded = (held[:span] + came[span:]).astype(BF16)
-        done = done.astype(F32) - products(dot, share, owners, folded, weights, 0)
-        done = done.astype(BF16)
-    result[...] = done
-    if not outs:
-        return
-    if not top:
-        folded = (held[span:] + came[:span]).astype(BF16)
-        done_mate = done_mate.astype(F32) - products(dot, share, owners, folded, mates, 0)
-        done_mate = done_mate.astype(BF16)
+    span = own.shape[0]
+    picked = picked_from(places[level], jnp.concatenate([own, mate], axis=0)).astype(BF16)
+    sums = products(dot, share, owners, picked[:span], weights, 2)
+    sums += products(dot, share, owners, picked[2 * span :], weights, 1 + side)
+    sums_mate = products(dot, share, owners, picked[span : 2 * span], mates, 1)
+    return jnp.concatenate([sums, sums_mate], axis=0)
+
+
+def pushed_sums(level, share, packed, weights, mates, targets, own, mate):
+    *owners, side = unpack(packed, level)
+    span = own.shape[0]
     pushed = [
-        products(dot_t, share, owners, done, weights, 2),
-        products(dot_t, share, owners, done_mate, mates, 1),
-        products(dot_t, share, owners, done, weights, 1 + side),
+        products(dot_t, share, owners, own, weights, 2),
+        products(dot_t, share, owners, mate, mates, 1),
+        products(dot_t, share, owners, own, weights, 1 + side),
     ]
     pushed = jnp.concatenate(pushed, axis=0).astype(BF16)
     to = lax.broadcasted_iota(jnp.int32, (2 * span, 3 * span), 0)
-    outs[0][...] = dot(ones_where(to == targets[level]), pushed)
-
-
-def call(kernel, outs, *args):
+    return dot(ones_where(to == targets[level]), pushed)
+
+
+def pass_on(sums, held, sent):
+    held[...] = sums
+    sent[...] = sums.astype(BF16)
+
+
+def joined(held, came):
+    span = held.shape[0] // 2
+    came = came[...].astype(F32)
+    return held[:span] + came[span:], held[span:] + came[:span]
+
+
+def entry_kernel(level, share, packed, weights, mates, meets, own, mate, held, sent):
+    sums = gathered_sums(level, share, packed, weights, mates, meets, own[...], mate[...])
+    pass_on(sums, held, sent)
+
+
+def forward_pair_kernel(
+    level, share, last, packed, weights, mates, meets, targets, side, side_mate, held, came,
+    solved, solved_mate, to_hold, to_send,
+):
+    *owners, _ = unpack(packed, level)
+    pair = []
+    for total, right, blocks in zip(joined(held, came), (side[level], side_mate[...]), (weights, mates)):
+        shifted = (right.astype(F32) - total).astype(BF16)
+        pair.append(products(dot, share, owners, shifted, blocks, 0).astype(BF16))
+    solved[...], solved_mate[...] = pair
+    if last:
+        sums = pushed_sums(level, share, packed, weights, mates, targets, *pair)
+    else:
+        sums = gathered_sums(level + 1, share, packed, weights, mates, meets, *pair)
+    pass_on(sums, to_hold, to_send)
+
+
+def backward_kernel(
+    level, share, packed, weights, mates, targets, solved, solved_mate, held, came, result, *outs
+):
+    *owners, _ = unpack(packed, level)
+    pair = []
+    for total, vector, blocks in zip(joined(held, came), (solved, solved_mate), (weights, mates)):
+        part = products(dot, share, owners, total.astype(BF16), blocks, 0)
+        pair.append((vector[...].astype(F32) - part).astype(BF16))
+        if not outs:
+            break
+    result[...] = pair[0]
+    if outs:
+        pass_on(pushed_sums(level, share, packed, weights, mates, targets, *pair), *outs)
+
+
+def call(kernel, outs, packed, weights, *rest, fetched=False):
     vmem = pl.BlockSpec(memory_space=pltpu.VMEM)
+    specs = [vmem] * (2 + len(rest))
+    scratch = []
+    if fetched:
+        specs[1] = pl.BlockSpec(memory_space=pltpu.HBM)
+        weights = pltpu.with_memory_space_constraint(weights, pltpu.HBM)
+        scratch = [pltpu.VMEM((2,) + weights.shape[1:], weights.dtype), pltpu.SemaphoreType.DMA((2,))]
     return pl.pallas_call(
         kernel,
         out_shape=outs,
-        in_specs=[vmem] * len(args),
+        in_specs=specs,
         out_specs=[vmem] * len(outs),
+        scratch_shapes=scratch,
         compiler_params=pltpu.CompilerParams(vmem_limit_bytes=16 * 2**20),
-    )(*args)
+    )(packed, weights, *rest)
 
 
 def local(right_side, diag_inverse, off_blocks, columns, plan):
@@ -146,10 +210,10 @@
     )
     part = part.reshape(3, levs, rows * 3)[:, inverse].reshape(3, levels, count, 3)
     second = jnp.roll(inverse[1::2], 1)[None, :, None, None]
-    meets = jnp.where(part // rows % levs == second, rows, 0) + part % rows
+    met = jnp.where(part // rows % levs == second, rows, 0) + part % rows
     odd = (jnp.arange(levels) % 2 == 1)[:, None]
-    meets_own = meets[0]
-    meets_mate = jnp.where(odd[..., None], meets[1], meets[2])
+    meets_own = met[0]
+    meets_mate = jnp.where(odd[..., None], met[1], met[2])
     ahead = odd == (turn == 0)
     own_mate = jnp.where(ahead, meets_own[..., 0], meets_own[..., 2])
     mate_own = jnp.where(ahead, meets_mate[..., 0], meets_mate[..., 2])
@@ -159,44 +223,57 @@
     places = meets_own.transpose(0, 2, 1) * share + slot[None, :, None] * span
     places = (places[..., None] + k).reshape(levels, 3 * span, 1)
     targets = jnp.stack([meets_own[..., 1], mate_own, own_mate + count], axis=1) * share
-    targets = (targets[..., None] + k).reshape(levels, 1, 3 * span)
+    targets = (targets[..., None] + k).reshape(levels, 3 * span)
+    targets, meets = targets[:, None, :], targets[:, :, None]
 
     vector = jax.ShapeDtypeStruct((count * share, width), BF16)
-    summed = jax.ShapeDtypeStruct((2 * count * share, width), F32)
+    sums = [jax.ShapeDtypeStruct((2 * span, width), kind) for kind in (F32, BF16)]
+    paired = levels - 2
 
     own = side[0]
-    far = lax.ppermute(own, "dom", far_pairs)
-    near = lax.ppermute(own, "dom", near_pairs)
-    mates, packed, side, places, targets, own, far, near = lax.optimization_barrier(
-        (mates, packed, side, places, targets, own, far, near)
+    far = lax.ppermute(jnp.stack([own, side[paired]]), "dom", far_pairs)
+    near = lax.ppermute(jnp.stack([own, side[paired + 1]]), "dom", near_pairs)
+    mates, packed, side, places, targets, meets, own, far, near = lax.optimization_barrier(
+        (mates, packed, side, places, targets, meets, own, far, near)
     )
+    side_mates = [far[1], near[1]]
+    far, near = far[0], near[0]
     mates = lax.all_gather(mates, "level")
 
+    def swap(vector, level):
+        return lax.ppermute(vector, "dom", far_pairs if level % 2 == 0 else near_pairs)
+
     solved = [own]
-    around = []
-    for level in range(1, levels):
+    solved_mate = []
+    for level in range(1, paired):
         if level > 1:
             own = solved[-1]
-            far = lax.ppermute(own, "dom", far_pairs)
-            near = lax.ppermute(own, "dom", near_pairs)
-        around.append(near if level % 2 == 0 else far)
-        kernel = functools.partial(forward_kernel, level, share)
-        solved += call(kernel, [vector], packed, weights, places, side, far, own, near)
-    solved[-1], mates = lax.optimization_barrier((solved[-1], mates))
-    around.append(lax.ppermute(solved[-1], "dom", near_pairs))
-
-    flow = []
-    results = []
-    for level in range(levels - 1, -1, -1):
-        kernel = functools.partial(backward_kernel, level, share, level == levels - 1)
-        outs = [vector, summed] if level else [vector]
-        result, *rest = call(
-            kernel, outs, packed, weights, mates, targets, solved[level], around[level], *flow
-        )
+            far, near = swap(own, 0), swap(own, 1)
+        fetched = level == paired - 1
+        if fetched:
+            far, near, mates = lax.optimization_barrier((far, near, mates))
+        solved_mate.append(near if level % 2 == 0 else far)
+        kernel = functools.partial(forward_kernel, level, share, fetched)
+        args = packed, weights, places, side, far, own, near
+        solved += call(kernel, [vector], *args, fetched=fetched)
+
+    solved_mate.append(swap(solved[-1], paired - 1))
+    kernel = functools.partial(entry_kernel, paired, share)
+    held, sent = call(kernel, sums, packed, weights, mates, meets, solved[-1], solved_mate[-1])
+    for level in range(paired, levels):
+        kernel = functools.partial(forward_pair_kernel, level, share, level == levels - 1)
+        args = packed, weights, mates, meets, targets, side, side_mates[level - paired]
+        own, mate, held, sent = call(kernel, [vector] * 2 + sums, *args, held, swap(sent, level))
+        solved.append(own)
+        solved_mate.append(mate)
+
+    results = [own]
+    for level in range(levels - 2, -1, -1):
+        kernel = functools.partial(backward_kernel, level, share)
+        args = packed, weights, mates, targets, solved[level], solved_mate[level], held, swap(sent, level)
+        result, *rest = call(kernel, [vector] + (sums if level else []), *args)
         results.append(result)
-        if level:
-            held = rest[0]
-            flow = [held, lax.ppermute(held, "dom", far_pairs if level % 2 else near_pairs)]
+        held, sent = rest or (held, sent)
 
     both = jnp.stack([jnp.stack(solved), jnp.stack(results[::-1])])
     both = both.reshape(2, levs, rows, share, width)[:, plan]

time: 242 us -> 235 us (0.971)
  waiting for transfers between devices: 59.7 us -> 51.7 us
  starting transfers between devices: 96.9 us -> 101 us
  blocking collectives: 30 us -> 26.2 us
    ppermute x22 -> x20, waiting for transfers between devices: 40.4 us -> 28.8 us  [the longest x18 25.6 us: swap(): lax.ppermute(vector, 'dom', far_pairs if level % 2 == 0 else near_pairs)]
    all_gather x1, waiting for transfers between devices: 0.01 us -> 4.43 us  [local(): mates = lax.all_gather(mates, 'level')]
    ppermute x22 -> x20, starting transfers between devices: 72.6 us -> 76.5 us  [the longest x18 72.7 us: swap(): lax.ppermute(vector, 'dom', far_pairs if level % 2 == 0 else near_pairs)]
    all_to_all x1, blocking collectives: 30 us -> 26.2 us  [local(): both = lax.all_to_all(both, 'level', 1, 0, tiled=False)]
    unnamed x22 -> x20, local copies, waits for them, and re-layouts: 9.07 us -> 6.88 us
  transfers between devices with their start and end apart: 27 -> 25, of which waited for: 21 -> 19; matrix products, arithmetic and copies ran while one was open for 5% -> 6% of each run, Pallas kernels for 2% -> 1%
where the time goes in v7:
time: 235 us; the launch traced here: 234 us
  starting transfers between devices  101 us (43%)
  waiting for transfers between devices  51.7 us (22%)
  blocking collectives  26.2 us (11%)
  between operations  17.2 us (7%)
  local copies, waits for them, and re-layouts  15.7 us (7%)
  Pallas kernels  13.2 us (6%)
  other arithmetic  8 us (3%)
    ppermute x18, starting transfers between devices, swap(): lax.ppermute(vector, 'dom', far_pairs if level % 2 == 0 else near_pairs)  72.7 us
    all_to_all x1, blocking collectives, local(): both = lax.all_to_all(both, 'level', 1, 0, tiled=False)  26.2 us
    ppermute x18, waiting for transfers between devices, swap(): lax.ppermute(vector, 'dom', far_pairs if level % 2 == 0 else near_pairs)  25.6 us
    all_gather x1, waiting for transfers between devices, local(): weights = lax.all_gather(weights, 'level')  17.4 us
    pallas_call x15, Pallas kernels, call(): pl.pallas_call(kernel, out_shape=outs, in_specs=specs, out_specs=[vmem] *...  13.2 us
    ppermute x1, starting transfers between devices, local(): by_far = lax.ppermute(mates, 'dom', far_pairs)  11 us
    all_to_all x1, starting transfers between devices, local(): side = lax.all_to_all(side, 'level', 1, 0, tiled=False)  8.35 us
    unnamed x20, local copies, waits for them, and re-layouts  6.88 us
  transfers between devices with their start and end apart: 25, of which 19 were waited for; matrix products, arithmetic and copies ran while one was open for 6% of the time, Pallas kernels for 1%

profile of v7, /device:TPU:1, one launch (start us, length us, event | category | flops | bytes accessed | tf_op | source)
XLA Modules:
  0.0 233.8 jit_solution(1397817278736539915)
XLA Ops:
  7.2 1.9 pad_maximum_fusion
  9.2 1.3 compare_select_fusion
  13.1 1.0 slice_select_fusion
  15.0 4.8 %collective-permute-start = (bf16[4,2,128,128]{3,2,1,0:T(8,128)(2,1)S(1)}, bf16[4,2,128,128]{3,2,1,0:T(8,128)(2,1)S(1)}, u32[]{:S(2)}, u32[]{:S(2)}) collective-permute-start(bf16[4,2,128,128]{3,2,1,0:T(8,128)(2,1)S(1)} %pad_maximum_fusion.1), channel_id=1, source_target_pairs={{0,16},{16,0},{32,48},{48,32},{64,80},{80,64},{96,112},{112,96},{1... | collective-permute-start | bytes 786440 | tf_op jit(solution)/shard_map/ppermute | solution.py:194
  19.8 11.0 %collective-permute-start.1 = (bf16[4,2,128,128]{3,2,1,0:T(8,128)(2,1)S(1)}, bf16[4,2,128,128]{3,2,1,0:T(8,128)(2,1)S(1)}, u32[]{:S(2)}, u32[]{:S(2)}) collective-permute-start(bf16[4,2,128,128]{3,2,1,0:T(8,128)(2,1)S(1)} %pad_maximum_fusion.1), channel_id=1, source_target_pairs={{16,32},{32,16},{48,64},{64,48},{80,96},{96,80},{112,128},{128,112... | collective-permute-start | bytes 786440 | tf_op jit(solution)/shard_map/ppermute | solution.py:195
  30.9 1.1 fusion
  32.7 8.3 %all-to-all-start = ((bf16[1,4,16,4,128]{4,3,1,0,2:T(4,128)(2,1)}), bf16[1,4,16,4,128]{4,3,1,0,2:T(4,128)(2,1)S(1)}, u32[]{:S(2)}, u32[]{:S(2)}) async-start(bf16[1,4,16,4,128]{4,3,1,0,2:T(4,128)(2,1)} %copy.79), calls=%async_computation | async-start | bytes 131072 | tf_op jit(solution)/shard_map/all_to_all | solution.py:200
  50.3 1.9 collective-permute-start.2
  52.2 1.9 collective-permute-start.3
  54.9 3.2 %collective-permute-done.2 = bf16[2,32,128]{2,1,0:T(8,128)(2,1)S(1)} collective-permute-done((bf16[2,32,128]{2,1,0:T(8,128)(2,1)S(1)}, bf16[2,32,128]{2,1,0:T(8,128)(2,1)S(1)}, u32[]{:S(2)}, u32[]{:S(2)}) %collective-permute-start.2) | collective-permute-done | bytes 16416 | tf_op jit(solution)/shard_map/ppermute | solution.py:234
  58.2 17.4 %all-gather.5.cloned.1.call-done = bf16[64,4,128,128]{3,2,1,0:T(8,128)(2,1)} async-done(((bf16[4,4,128,128]{3,2,1,0:T(8,128)(2,1)}), bf16[64,4,128,128]{3,2,1,0:T(8,128)(2,1)}) %all-gather.5.cloned.1.call-update) | async-done | bytes 8388624 | tf_op jit(solution)/shard_map/all_gather | solution.py:182
  75.7 3.4 %copy-done = bf16[64,4,128,128]{3,2,1,0:T(8,128)(2,1)S(1)} copy-done((bf16[64,4,128,128]{3,2,1,0:T(8,128)(2,1)S(1)}, bf16[64,4,128,128]{3,2,1,0:T(8,128)(2,1)}, u32[]{:S(2)}) %copy-start) | copy-done | bytes 8388632
  79.7 7.7 %collective-permute-start.4 = (bf16[32,128]{1,0:T(8,128)(2,1)S(1)}, bf16[32,128]{1,0:T(8,128)(2,1)S(1)}, u32[]{:S(2)}, u32[]{:S(2)}) collective-permute-start(bf16[32,128]{1,0:T(8,128)(2,1)S(1)} %shard_map.68.own.solved), channel_id=1, source_target_pairs={{16,32},{32,16},{48,64},{64,48},{80,96},{96,80},{112,128},{128,112... | collective-permute-start | bytes 24584 | tf_op jit(solution)/shard_map/ppermute | solution.py:244
  87.4 1.9 collective-permute-start.5
  89.3 2.5 %collective-permute-done.5.near.solved_mate = bf16[32,128]{1,0:T(8,128)(2,1)S(1)} collective-permute-done((bf16[32,128]{1,0:T(8,128)(2,1)S(1)}, bf16[32,128]{1,0:T(8,128)(2,1)S(1)}, u32[]{:S(2)}, u32[]{:S(2)}) %collective-permute-start.5) | collective-permute-done | bytes 8224 | tf_op jit(solution)/shard_map/ppermute | solution.py:244
  92.4 3.3 %collective-permute-start.6 = (bf16[32,128]{1,0:T(8,128)(2,1)S(1)}, bf16[32,128]{1,0:T(8,128)(2,1)S(1)}, u32[]{:S(2)}, u32[]{:S(2)}) collective-permute-start(bf16[32,128]{1,0:T(8,128)(2,1)S(1)} %shard_map.69.own.solved), channel_id=1, source_target_pairs={{16,32},{32,16},{48,64},{64,48},{80,96},{96,80},{112,128},{128,112... | collective-permute-start | bytes 24584 | tf_op jit(solution)/shard_map/ppermute | solution.py:244
  95.7 1.9 collective-permute-start.7
  97.6 2.5 %collective-permute-done.6.far.solved_mate = bf16[32,128]{1,0:T(8,128)(2,1)S(1)} collective-permute-done((bf16[32,128]{1,0:T(8,128)(2,1)S(1)}, bf16[32,128]{1,0:T(8,128)(2,1)S(1)}, u32[]{:S(2)}, u32[]{:S(2)}) %collective-permute-start.6) | collective-permute-done | bytes 8224 | tf_op jit(solution)/shard_map/ppermute | solution.py:244
  101.1 5.3 %collective-permute-start.8 = (bf16[32,128]{1,0:T(8,128)(2,1)S(1)}, bf16[32,128]{1,0:T(8,128)(2,1)S(1)}, u32[]{:S(2)}, u32[]{:S(2)}) collective-permute-start(bf16[32,128]{1,0:T(8,128)(2,1)S(1)} %shard_map.70.own.solved), channel_id=1, source_target_pairs={{16,32},{32,16},{48,64},{64,48},{80,96},{96,80},{112,128},{128,112... | collective-permute-start | bytes 24584 | tf_op jit(solution)/shard_map/ppermute | solution.py:244
  106.4 1.9 collective-permute-start.9
  108.8 2.4 %collective-permute-done.9.near.solved_mate = bf16[32,128]{1,0:T(8,128)(2,1)S(1)} collective-permute-done((bf16[32,128]{1,0:T(8,128)(2,1)S(1)}, bf16[32,128]{1,0:T(8,128)(2,1)S(1)}, u32[]{:S(2)}, u32[]{:S(2)}) %collective-permute-start.9) | collective-permute-done | bytes 8224 | tf_op jit(solution)/shard_map/ppermute | solution.py:244
  111.8 3.3 %collective-permute-start.10 = (bf16[32,128]{1,0:T(8,128)(2,1)S(1)}, bf16[32,128]{1,0:T(8,128)(2,1)S(1)}, u32[]{:S(2)}, u32[]{:S(2)}) collective-permute-start(bf16[32,128]{1,0:T(8,128)(2,1)S(1)} %shard_map.71.own.solved), channel_id=1, source_target_pairs={{16,32},{32,16},{48,64},{64,48},{80,96},{96,80},{112,128},{128,112... | collective-permute-start | bytes 24584 | tf_op jit(solution)/shard_map/ppermute | solution.py:244
  115.1 1.9 collective-permute-start.11
  117.0 4.4 %all-gather.7.cloned.1.call-done = bf16[64,2,128,128]{3,2,1,0:T(8,128)(2,1)} async-done(((bf16[4,2,128,128]{3,2,1,0:T(8,128)(2,1)}), bf16[64,2,128,128]{3,2,1,0:T(8,128)(2,1)}) %all-gather.7.cloned.1.call-update) | async-done | bytes 4194320 | tf_op jit(solution)/shard_map/all_gather | solution.py:241
  121.5 2.0 shard_map.72.own.solved
  123.5 3.3 %collective-permute-start.12 = (bf16[32,128]{1,0:T(8,128)(2,1)S(1)}, bf16[32,128]{1,0:T(8,128)(2,1)S(1)}, u32[]{:S(2)}, u32[]{:S(2)}) collective-permute-start(bf16[32,128]{1,0:T(8,128)(2,1)S(1)} %shard_map.72.own.solved), channel_id=1, source_target_pairs={{0,16},{16,0},{32,48},{48,32},{64,80},{80,64},{96,112},{112,96},{1... | collective-permute-start | bytes 24584 | tf_op jit(solution)/shard_map/ppermute | solution.py:244
  126.7 1.1 collective-permute-done.12.mate.solved_mate
  127.9 3.4 %copy-done.1 = bf16[64,4,128,128]{3,2,1,0:T(8,128)(2,1)S(1)} copy-done((bf16[64,4,128,128]{3,2,1,0:T(8,128)(2,1)S(1)}, bf16[64,4,128,128]{3,2,1,0:T(8,128)(2,1)}, u32[]{:S(2)}) %copy-start.1) | copy-done | bytes 8388632
  131.8 7.9 %collective-permute-start.13 = (bf16[64,128]{1,0:T(8,128)(2,1)S(1)}, bf16[64,128]{1,0:T(8,128)(2,1)S(1)}, u32[]{:S(2)}, u32[]{:S(2)}) collective-permute-start(bf16[64,128]{1,0:T(8,128)(2,1)S(1)} %get-tuple-element.54), channel_id=1, source_target_pairs={{16,32},{32,16},{48,64},{64,48},{80,96},{96,80},{112,128},{128,112... | collective-permute-start | bytes 49160 | tf_op jit(solution)/shard_map/ppermute | solution.py:244
  139.7 1.1 collective-permute-done.13.came
  141.7 1.9 collective-permute-start.14
  143.6 2.6 %collective-permute-done.14.came = bf16[64,128]{1,0:T(8,128)(2,1)S(1)} collective-permute-done((bf16[64,128]{1,0:T(8,128)(2,1)S(1)}, bf16[64,128]{1,0:T(8,128)(2,1)S(1)}, u32[]{:S(2)}, u32[]{:S(2)}) %collective-permute-start.14) | collective-permute-done | bytes 16416 | tf_op jit(solution)/shard_map/ppermute | solution.py:244
  146.2 1.3 shard_map.75
  147.5 6.7 %collective-permute-start.15 = (bf16[64,128]{1,0:T(8,128)(2,1)S(1)}, bf16[64,128]{1,0:T(8,128)(2,1)S(1)}, u32[]{:S(2)}, u32[]{:S(2)}) collective-permute-start(bf16[64,128]{1,0:T(8,128)(2,1)S(1)} %get-tuple-element.61), channel_id=1, source_target_pairs={{16,32},{32,16},{48,64},{64,48},{80,96},{96,80},{112,128},{128,112... | collective-permute-start | bytes 49160 | tf_op jit(solution)/shard_map/ppermute | solution.py:244
  154.2 1.1 collective-permute-done.15.came
  156.2 1.9 collective-permute-start.16
  158.2 2.8 %collective-permute-done.16.came = bf16[64,128]{1,0:T(8,128)(2,1)S(1)} collective-permute-done((bf16[64,128]{1,0:T(8,128)(2,1)S(1)}, bf16[64,128]{1,0:T(8,128)(2,1)S(1)}, u32[]{:S(2)}, u32[]{:S(2)}) %collective-permute-start.16) | collective-permute-done | bytes 16416 | tf_op jit(solution)/shard_map/ppermute | solution.py:244
  162.0 6.4 %collective-permute-start.17 = (bf16[64,128]{1,0:T(8,128)(2,1)S(1)}, bf16[64,128]{1,0:T(8,128)(2,1)S(1)}, u32[]{:S(2)}, u32[]{:S(2)}) collective-permute-start(bf16[64,128]{1,0:T(8,128)(2,1)S(1)} %get-tuple-element.65), channel_id=1, source_target_pairs={{16,32},{32,16},{48,64},{64,48},{80,96},{96,80},{112,128},{128,112... | collective-permute-start | bytes 49160 | tf_op jit(solution)/shard_map/ppermute | solution.py:244
  168.4 1.4 collective-permute-done.17.came
  170.7 1.9 collective-permute-start.18
  172.7 2.5 %collective-permute-done.18.came = bf16[64,128]{1,0:T(8,128)(2,1)S(1)} collective-permute-done((bf16[64,128]{1,0:T(8,128)(2,1)S(1)}, bf16[64,128]{1,0:T(8,128)(2,1)S(1)}, u32[]{:S(2)}, u32[]{:S(2)}) %collective-permute-start.18) | collective-permute-done | bytes 16416 | tf_op jit(solution)/shard_map/ppermute | solution.py:244
  176.2 6.7 %collective-permute-start.19 = (bf16[64,128]{1,0:T(8,128)(2,1)S(1)}, bf16[64,128]{1,0:T(8,128)(2,1)S(1)}, u32[]{:S(2)}, u32[]{:S(2)}) collective-permute-start(bf16[64,128]{1,0:T(8,128)(2,1)S(1)} %get-tuple-element.69), channel_id=1, source_target_pairs={{16,32},{32,16},{48,64},{64,48},{80,96},{96,80},{112,128},{128,112... | collective-permute-start | bytes 49160 | tf_op jit(solution)/shard_map/ppermute | solution.py:244
  182.9 1.1 collective-permute-done.19.came
  185.0 1.9 collective-permute-start.20
  186.9 2.5 %collective-permute-done.20.came = bf16[64,128]{1,0:T(8,128)(2,1)S(1)} collective-permute-done((bf16[64,128]{1,0:T(8,128)(2,1)S(1)}, bf16[64,128]{1,0:T(8,128)(2,1)S(1)}, u32[]{:S(2)}, u32[]{:S(2)}) %collective-permute-start.20) | collective-permute-done | bytes 16416 | tf_op jit(solution)/shard_map/ppermute | solution.py:244
  190.4 6.7 %collective-permute-start.21 = (bf16[64,128]{1,0:T(8,128)(2,1)S(1)}, bf16[64,128]{1,0:T(8,128)(2,1)S(1)}, u32[]{:S(2)}, u32[]{:S(2)}) collective-permute-start(bf16[64,128]{1,0:T(8,128)(2,1)S(1)} %get-tuple-element.73), channel_id=1, source_target_pairs={{16,32},{32,16},{48,64},{64,48},{80,96},{96,80},{112,128},{128,112... | collective-permute-start | bytes 49160 | tf_op jit(solution)/shard_map/ppermute | solution.py:244
  197.1 1.1 collective-permute-done.21.came
  199.5 26.2 %all_to_all.30 = bf16[1,2,16,4,4,128]{5,4,3,1,0,2:T(4,128)(2,1)S(1)} all-to-all(bf16[1,2,16,4,4,128]{5,4,3,1,0,2:T(4,128)(2,1)S(1)} %bitcast.145), channel_id=1, replica_groups=mesh['dom'=32,'level'=16] {'level'}, dimensions={2} | all-to-all | bytes 262144 | tf_op jit(solution)/shard_map/all_to_all | solution.py:280
  (101 shorter events, 24.7 us)
Async XLA Ops:
  7.2 68.5 %all-gather.5.cloned.1.call-start = ((), (), s32[]{:S(2)}) async-start(), calls=%async_computation.2 | async-start | bytes 8912896 | tf_op jit(solution)/shard_map/all_gather | solution.py:182
  15.0 39.1 %collective-permute-start = (bf16[4,2,128,128]{3,2,1,0:T(8,128)(2,1)S(1)}, bf16[4,2,128,128]{3,2,1,0:T(8,128)(2,1)S(1)}, u32[]{:S(2)}, u32[]{:S(2)}) collective-permute-start(bf16[4,2,128,128]{3,2,1,0:T(8,128)(2,1)S(1)} %pad_maximum_fusion.1), channel_id=1, source_target_pairs={{0,16},{16,0},{32,48},{48,32},{64,80},{80,64},{96,112},{112,96},{1... | collective-permute-start | bytes 786440 | tf_op jit(solution)/shard_map/ppermute | solution.py:194
  19.8 34.3 %collective-permute-start.1 = (bf16[4,2,128,128]{3,2,1,0:T(8,128)(2,1)S(1)}, bf16[4,2,128,128]{3,2,1,0:T(8,128)(2,1)S(1)}, u32[]{:S(2)}, u32[]{:S(2)}) collective-permute-start(bf16[4,2,128,128]{3,2,1,0:T(8,128)(2,1)S(1)} %pad_maximum_fusion.1), channel_id=1, source_target_pairs={{16,32},{32,16},{48,64},{64,48},{80,96},{96,80},{112,128},{128,112... | collective-permute-start | bytes 786440 | tf_op jit(solution)/shard_map/ppermute | solution.py:195
  32.7 17.0 %all-to-all-start = ((bf16[1,4,16,4,128]{4,3,1,0,2:T(4,128)(2,1)}), bf16[1,4,16,4,128]{4,3,1,0,2:T(4,128)(2,1)S(1)}, u32[]{:S(2)}, u32[]{:S(2)}) async-start(bf16[1,4,16,4,128]{4,3,1,0,2:T(4,128)(2,1)} %copy.79), calls=%async_computation | async-start | bytes 131072 | tf_op jit(solution)/shard_map/all_to_all | solution.py:200
  41.0 80.5 %all-gather.7.cloned.1.call-start = ((), (), s32[]{:S(2)}) async-start(), calls=%async_computation.3 | async-start | bytes 4456448 | tf_op jit(solution)/shard_map/all_gather | solution.py:241
  50.3 7.8 %collective-permute-start.2 = (bf16[2,32,128]{2,1,0:T(8,128)(2,1)S(1)}, bf16[2,32,128]{2,1,0:T(8,128)(2,1)S(1)}, u32[]{:S(2)}, u32[]{:S(2)}) collective-permute-start(bf16[2,32,128]{2,1,0:T(8,128)(2,1)S(1)} %get-tuple-element.102), channel_id=1, source_target_pairs={{16,32},{32,16},{48,64},{64,48},{80,96},{96,80},{112,128},{128,112... | collective-permute-start | bytes 49160 | tf_op jit(solution)/shard_map/ppermute | solution.py:234
  52.2 5.9 %collective-permute-start.3 = (bf16[2,32,128]{2,1,0:T(8,128)(2,1)S(1)}, bf16[2,32,128]{2,1,0:T(8,128)(2,1)S(1)}, u32[]{:S(2)}, u32[]{:S(2)}) collective-permute-start(bf16[2,32,128]{2,1,0:T(8,128)(2,1)S(1)} %get-tuple-element.101), channel_id=1, source_target_pairs={{0,16},{16,0},{32,48},{48,32},{64,80},{80,64},{96,112},{112,96},{1... | collective-permute-start | bytes 49160 | tf_op jit(solution)/shard_map/ppermute | solution.py:235
  75.7 3.4 %copy-start = (bf16[64,4,128,128]{3,2,1,0:T(8,128)(2,1)S(1)}, bf16[64,4,128,128]{3,2,1,0:T(8,128)(2,1)}, u32[]{:S(2)}) copy-start(bf16[64,4,128,128]{3,2,1,0:T(8,128)(2,1)} %all-gather.5.cloned.1.call-done) | copy-start | bytes 25165828
  79.7 9.7 %collective-permute-start.4 = (bf16[32,128]{1,0:T(8,128)(2,1)S(1)}, bf16[32,128]{1,0:T(8,128)(2,1)S(1)}, u32[]{:S(2)}, u32[]{:S(2)}) collective-permute-start(bf16[32,128]{1,0:T(8,128)(2,1)S(1)} %shard_map.68.own.solved), channel_id=1, source_target_pairs={{16,32},{32,16},{48,64},{64,48},{80,96},{96,80},{112,128},{128,112... | collective-permute-start | bytes 24584 | tf_op jit(solution)/shard_map/ppermute | solution.py:244
  87.4 4.4 %collective-permute-start.5 = (bf16[32,128]{1,0:T(8,128)(2,1)S(1)}, bf16[32,128]{1,0:T(8,128)(2,1)S(1)}, u32[]{:S(2)}, u32[]{:S(2)}) collective-permute-start(bf16[32,128]{1,0:T(8,128)(2,1)S(1)} %shard_map.68.own.solved), channel_id=1, source_target_pairs={{0,16},{16,0},{32,48},{48,32},{64,80},{80,64},{96,112},{112,96},{1... | collective-permute-start | bytes 24584 | tf_op jit(solution)/shard_map/ppermute | solution.py:244
  92.4 7.7 %collective-permute-start.6 = (bf16[32,128]{1,0:T(8,128)(2,1)S(1)}, bf16[32,128]{1,0:T(8,128)(2,1)S(1)}, u32[]{:S(2)}, u32[]{:S(2)}) collective-permute-start(bf16[32,128]{1,0:T(8,128)(2,1)S(1)} %shard_map.69.own.solved), channel_id=1, source_target_pairs={{16,32},{32,16},{48,64},{64,48},{80,96},{96,80},{112,128},{128,112... | collective-permute-start | bytes 24584 | tf_op jit(solution)/shard_map/ppermute | solution.py:244
  95.7 4.8 %collective-permute-start.7 = (bf16[32,128]{1,0:T(8,128)(2,1)S(1)}, bf16[32,128]{1,0:T(8,128)(2,1)S(1)}, u32[]{:S(2)}, u32[]{:S(2)}) collective-permute-start(bf16[32,128]{1,0:T(8,128)(2,1)S(1)} %shard_map.69.own.solved), channel_id=1, source_target_pairs={{0,16},{16,0},{32,48},{48,32},{64,80},{80,64},{96,112},{112,96},{1... | collective-permute-start | bytes 24584 | tf_op jit(solution)/shard_map/ppermute | solution.py:244
  101.1 7.7 %collective-permute-start.8 = (bf16[32,128]{1,0:T(8,128)(2,1)S(1)}, bf16[32,128]{1,0:T(8,128)(2,1)S(1)}, u32[]{:S(2)}, u32[]{:S(2)}) collective-permute-start(bf16[32,128]{1,0:T(8,128)(2,1)S(1)} %shard_map.70.own.solved), channel_id=1, source_target_pairs={{16,32},{32,16},{48,64},{64,48},{80,96},{96,80},{112,128},{128,112... | collective-permute-start | bytes 24584 | tf_op jit(solution)/shard_map/ppermute | solution.py:244
  106.4 4.8 %collective-permute-start.9 = (bf16[32,128]{1,0:T(8,128)(2,1)S(1)}, bf16[32,128]{1,0:T(8,128)(2,1)S(1)}, u32[]{:S(2)}, u32[]{:S(2)}) collective-permute-start(bf16[32,128]{1,0:T(8,128)(2,1)S(1)} %shard_map.70.own.solved), channel_id=1, source_target_pairs={{0,16},{16,0},{32,48},{48,32},{64,80},{80,64},{96,112},{112,96},{1... | collective-permute-start | bytes 24584 | tf_op jit(solution)/shard_map/ppermute | solution.py:244
  111.8 9.7 %collective-permute-start.10 = (bf16[32,128]{1,0:T(8,128)(2,1)S(1)}, bf16[32,128]{1,0:T(8,128)(2,1)S(1)}, u32[]{:S(2)}, u32[]{:S(2)}) collective-permute-start(bf16[32,128]{1,0:T(8,128)(2,1)S(1)} %shard_map.71.own.solved), channel_id=1, source_target_pairs={{16,32},{32,16},{48,64},{64,48},{80,96},{96,80},{112,128},{128,112... | collective-permute-start | bytes 24584 | tf_op jit(solution)/shard_map/ppermute | solution.py:244
  115.1 6.4 %collective-permute-start.11 = (bf16[32,128]{1,0:T(8,128)(2,1)S(1)}, bf16[32,128]{1,0:T(8,128)(2,1)S(1)}, u32[]{:S(2)}, u32[]{:S(2)}) collective-permute-start(bf16[32,128]{1,0:T(8,128)(2,1)S(1)} %shard_map.71.own.solved), channel_id=1, source_target_pairs={{0,16},{16,0},{32,48},{48,32},{64,80},{80,64},{96,112},{112,96},{1... | collective-permute-start | bytes 24584 | tf_op jit(solution)/shard_map/ppermute | solution.py:244
  121.5 6.4 %copy-start.2 = (bf16[64,2,128,128]{3,2,1,0:T(8,128)(2,1)S(1)}, bf16[64,2,128,128]{3,2,1,0:T(8,128)(2,1)}, u32[]{:S(2)}) copy-start(bf16[64,2,128,128]{3,2,1,0:T(8,128)(2,1)} %all-gather.7.cloned.1.call-done) | copy-start | bytes 12582916
  123.5 4.4 %collective-permute-start.12 = (bf16[32,128]{1,0:T(8,128)(2,1)S(1)}, bf16[32,128]{1,0:T(8,128)(2,1)S(1)}, u32[]{:S(2)}, u32[]{:S(2)}) collective-permute-start(bf16[32,128]{1,0:T(8,128)(2,1)S(1)} %shard_map.72.own.solved), channel_id=1, source_target_pairs={{0,16},{16,0},{32,48},{48,32},{64,80},{80,64},{96,112},{112,96},{1... | collective-permute-start | bytes 24584 | tf_op jit(solution)/shard_map/ppermute | solution.py:244
  127.9 3.4 %copy-start.1 = (bf16[64,4,128,128]{3,2,1,0:T(8,128)(2,1)S(1)}, bf16[64,4,128,128]{3,2,1,0:T(8,128)(2,1)}, u32[]{:S(2)}) copy-start(bf16[64,4,128,128]{3,2,1,0:T(8,128)(2,1)} %all-gather.5.cloned.1.call-done) | copy-start | bytes 25165828
  131.8 9.1 %collective-permute-start.13 = (bf16[64,128]{1,0:T(8,128)(2,1)S(1)}, bf16[64,128]{1,0:T(8,128)(2,1)S(1)}, u32[]{:S(2)}, u32[]{:S(2)}) collective-permute-start(bf16[64,128]{1,0:T(8,128)(2,1)S(1)} %get-tuple-element.54), channel_id=1, source_target_pairs={{16,32},{32,16},{48,64},{64,48},{80,96},{96,80},{112,128},{128,112... | collective-permute-start | bytes 49160 | tf_op jit(solution)/shard_map/ppermute | solution.py:244
  141.7 4.5 %collective-permute-start.14 = (bf16[64,128]{1,0:T(8,128)(2,1)S(1)}, bf16[64,128]{1,0:T(8,128)(2,1)S(1)}, u32[]{:S(2)}, u32[]{:S(2)}) collective-permute-start(bf16[64,128]{1,0:T(8,128)(2,1)S(1)} %get-tuple-element.57), channel_id=1, source_target_pairs={{0,16},{16,0},{32,48},{48,32},{64,80},{80,64},{96,112},{112,96},{1... | collective-permute-start | bytes 49160 | tf_op jit(solution)/shard_map/ppermute | solution.py:244
  147.5 7.8 %collective-permute-start.15 = (bf16[64,128]{1,0:T(8,128)(2,1)S(1)}, bf16[64,128]{1,0:T(8,128)(2,1)S(1)}, u32[]{:S(2)}, u32[]{:S(2)}) collective-permute-start(bf16[64,128]{1,0:T(8,128)(2,1)S(1)} %get-tuple-element.61), channel_id=1, source_target_pairs={{16,32},{32,16},{48,64},{64,48},{80,96},{96,80},{112,128},{128,112... | collective-permute-start | bytes 49160 | tf_op jit(solution)/shard_map/ppermute | solution.py:244
  156.2 4.8 %collective-permute-start.16 = (bf16[64,128]{1,0:T(8,128)(2,1)S(1)}, bf16[64,128]{1,0:T(8,128)(2,1)S(1)}, u32[]{:S(2)}, u32[]{:S(2)}) collective-permute-start(bf16[64,128]{1,0:T(8,128)(2,1)S(1)} %get-tuple-element.63), channel_id=1, source_target_pairs={{0,16},{16,0},{32,48},{48,32},{64,80},{80,64},{96,112},{112,96},{1... | collective-permute-start | bytes 49160 | tf_op jit(solution)/shard_map/ppermute | solution.py:244
  162.0 7.8 %collective-permute-start.17 = (bf16[64,128]{1,0:T(8,128)(2,1)S(1)}, bf16[64,128]{1,0:T(8,128)(2,1)S(1)}, u32[]{:S(2)}, u32[]{:S(2)}) collective-permute-start(bf16[64,128]{1,0:T(8,128)(2,1)S(1)} %get-tuple-element.65), channel_id=1, source_target_pairs={{16,32},{32,16},{48,64},{64,48},{80,96},{96,80},{112,128},{128,112... | collective-permute-start | bytes 49160 | tf_op jit(solution)/shard_map/ppermute | solution.py:244
  170.7 4.5 %collective-permute-start.18 = (bf16[64,128]{1,0:T(8,128)(2,1)S(1)}, bf16[64,128]{1,0:T(8,128)(2,1)S(1)}, u32[]{:S(2)}, u32[]{:S(2)}) collective-permute-start(bf16[64,128]{1,0:T(8,128)(2,1)S(1)} %get-tuple-element.67), channel_id=1, source_target_pairs={{0,16},{16,0},{32,48},{48,32},{64,80},{80,64},{96,112},{112,96},{1... | collective-permute-start | bytes 49160 | tf_op jit(solution)/shard_map/ppermute | solution.py:244
  176.2 7.8 %collective-permute-start.19 = (bf16[64,128]{1,0:T(8,128)(2,1)S(1)}, bf16[64,128]{1,0:T(8,128)(2,1)S(1)}, u32[]{:S(2)}, u32[]{:S(2)}) collective-permute-start(bf16[64,128]{1,0:T(8,128)(2,1)S(1)} %get-tuple-element.69), channel_id=1, source_target_pairs={{16,32},{32,16},{48,64},{64,48},{80,96},{96,80},{112,128},{128,112... | collective-permute-start | bytes 49160 | tf_op jit(solution)/shard_map/ppermute | solution.py:244
  185.0 4.5 %collective-permute-start.20 = (bf16[64,128]{1,0:T(8,128)(2,1)S(1)}, bf16[64,128]{1,0:T(8,128)(2,1)S(1)}, u32[]{:S(2)}, u32[]{:S(2)}) collective-permute-start(bf16[64,128]{1,0:T(8,128)(2,1)S(1)} %get-tuple-element.71), channel_id=1, source_target_pairs={{0,16},{16,0},{32,48},{48,32},{64,80},{80,64},{96,112},{112,96},{1... | collective-permute-start | bytes 49160 | tf_op jit(solution)/shard_map/ppermute | solution.py:244
  190.4 7.8 %collective-permute-start.21 = (bf16[64,128]{1,0:T(8,128)(2,1)S(1)}, bf16[64,128]{1,0:T(8,128)(2,1)S(1)}, u32[]{:S(2)}, u32[]{:S(2)}) collective-permute-start(bf16[64,128]{1,0:T(8,128)(2,1)S(1)} %get-tuple-element.73), channel_id=1, source_target_pairs={{16,32},{32,16},{48,64},{64,48},{80,96},{96,80},{112,128},{128,112... | collective-permute-start | bytes 49160 | tf_op jit(solution)/shard_map/ppermute | solution.py:244
Sparse Core Ops, SparseCore 0:
  10.1 65.5 all-gather.4
  77.8 43.6 all-gather.6

commit v8 on v7

--- a/solution.py
+++ b/solution.py
@@ -83,7 +83,11 @@
     picked = picked_from(places[level], jnp.concatenate([own, mate], axis=0)).astype(BF16)
     sums = products(dot, share, owners, picked[:span], weights, 2)
     sums += products(dot, share, owners, picked[2 * span :], weights, 1 + side)
-    sums_mate = products(dot, share, owners, picked[span : 2 * span], mates, 1)
+    if callable(mates):
+        owners, mates, kind = mates()
+    else:
+        kind = 1
+    sums_mate = products(dot, share, owners, picked[span : 2 * span], mates, kind)
     return jnp.concatenate([sums, sums_mate], axis=0)
 
 
@@ -111,8 +115,21 @@
     return held[:span] + came[span:], held[span:] + came[:span]
 
 
-def entry_kernel(level, share, packed, weights, mates, meets, own, mate, held, sent):
-    sums = gathered_sums(level, share, packed, weights, mates, meets, own[...], mate[...])
+def entry_kernel(level, share, packed, mates, weights, meets, own, mate, held, sent, blocks, sems):
+    *owners, _ = unpack(packed, level)
+    copies = [
+        pltpu.make_async_copy(mates.at[owners[half], :, pl.ds(1, 1)], blocks.at[half], sems.at[half])
+        for half in range(2)
+    ]
+    for copy in copies:
+        copy.start()
+
+    def arrived():
+        for copy in copies:
+            copy.wait()
+        return range(2), blocks, 0
+
+    sums = gathered_sums(level, share, packed, weights, arrived, meets, own[...], mate[...])
     pass_on(sums, held, sent)
 
 
@@ -141,21 +158,41 @@
     for total, vector, blocks in zip(joined(held, came), (solved, solved_mate), (weights, mates)):
         part = products(dot, share, owners, total.astype(BF16), blocks, 0)
         pair.append((vector[...].astype(F32) - part).astype(BF16))
-        if not outs:
-            break
     result[...] = pair[0]
-    if outs:
-        pass_on(pushed_sums(level, share, packed, weights, mates, targets, *pair), *outs)
-
-
-def call(kernel, outs, packed, weights, *rest, fetched=False):
+    pass_on(pushed_sums(level, share, packed, weights, mates, targets, *pair), *outs)
+
+
+def last_kernel(share, packed, weights, held, came, *rest):
+    *rest, out = rest
+    solved, results = rest[: packed.shape[0]], rest[packed.shape[0] :]
+    *owners, _ = unpack(packed, 0)
+    total = joined(held, came)[0].astype(BF16)
+    part = products(dot, share, owners, total, weights, 0)
+    result = (solved[0][...].astype(F32) - part).astype(BF16)
+    size = out.shape[1] // 2
+    for level in range(packed.shape[0]):
+        *owners, _ = unpack(packed, level)
+        for which, array in enumerate((solved[level], results[level - 1] if level else result)):
+            for half in range(2):
+                out[owners[half], which * size : (which + 1) * size] = array[half * size : (half + 1) * size]
+
+
+def deal_kernel(share, dealt, *outs):
+    parts = [dealt[source].astype(F32) for source in range(dealt.shape[0])]
+    for which, out in enumerate(outs):
+        for row in range(out.shape[0]):
+            at = (which * out.shape[0] + row) * share
+            out[row] = jnp.concatenate([part[at : at + share] for part in parts], axis=0).astype(BF16)
+
+
+def call(kernel, outs, packed, blocks, *rest, fetched=None):
     vmem = pl.BlockSpec(memory_space=pltpu.VMEM)
     specs = [vmem] * (2 + len(rest))
     scratch = []
     if fetched:
         specs[1] = pl.BlockSpec(memory_space=pltpu.HBM)
-        weights = pltpu.with_memory_space_constraint(weights, pltpu.HBM)
-        scratch = [pltpu.VMEM((2,) + weights.shape[1:], weights.dtype), pltpu.SemaphoreType.DMA((2,))]
+        blocks = pltpu.with_memory_space_constraint(blocks, pltpu.HBM)
+        scratch = [pltpu.VMEM(fetched, blocks.dtype), pltpu.SemaphoreType.DMA((2,))]
     return pl.pallas_call(
         kernel,
         out_shape=outs,
@@ -163,7 +200,7 @@
         out_specs=[vmem] * len(outs),
         scratch_shapes=scratch,
         compiler_params=pltpu.CompilerParams(vmem_limit_bytes=16 * 2**20),
-    )(packed, weights, *rest)
+    )(packed, blocks, *rest)
 
 
 def local(right_side, diag_inverse, off_blocks, columns, plan):
@@ -249,17 +286,19 @@
         if level > 1:
             own = solved[-1]
             far, near = swap(own, 0), swap(own, 1)
-        fetched = level == paired - 1
-        if fetched:
+        fetched = level in (1, paired - 1)
+        if level == paired - 1:
             far, near, mates = lax.optimization_barrier((far, near, mates))
         solved_mate.append(near if level % 2 == 0 else far)
         kernel = functools.partial(forward_kernel, level, share, fetched)
         args = packed, weights, places, side, far, own, near
+        fetched = (2,) + weights.shape[1:] if fetched else None
         solved += call(kernel, [vector], *args, fetched=fetched)
 
     solved_mate.append(swap(solved[-1], paired - 1))
     kernel = functools.partial(entry_kernel, paired, share)
-    held, sent = call(kernel, sums, packed, weights, mates, meets, solved[-1], solved_mate[-1])
+    args = packed, mates, weights, meets, solved[-1], solved_mate[-1]
+    held, sent = call(kernel, sums, *args, fetched=(2, rows, 1, width, width))
     for level in range(paired, levels):
         kernel = functools.partial(forward_pair_kernel, level, share, level == levels - 1)
         args = packed, weights, mates, meets, targets, side, side_mates[level - paired]
@@ -268,18 +307,23 @@
         solved_mate.append(mate)
 
     results = [own]
-    for level in range(levels - 2, -1, -1):
+    for level in range(levels - 2, 0, -1):
         kernel = functools.partial(backward_kernel, level, share)
         args = packed, weights, mates, targets, solved[level], solved_mate[level], held, swap(sent, level)
-        result, *rest = call(kernel, [vector] + (sums if level else []), *args)
+        result, held, sent = call(kernel, [vector] + sums, *args)
         results.append(result)
-        held, sent = rest or (held, sent)
-
-    both = jnp.stack([jnp.stack(solved), jnp.stack(results[::-1])])
-    both = both.reshape(2, levs, rows, share, width)[:, plan]
-    both = lax.all_to_all(both, "level", 1, 0, tiled=False)
-    both = both.transpose(1, 2, 0, 3, 4).reshape(2, rows, depth, width)
-    return both[0], both[1]
+
+    dealt = jax.ShapeDtypeStruct((levs, 2 * rows * share, width), BF16)
+    kernel = functools.partial(last_kernel, share)
+    (dealt,) = call(kernel, [dealt], packed, weights, held, swap(sent, 0), *solved, *results[::-1])
+    dealt = lax.all_to_all(dealt, "level", 0, 0, tiled=False)
+    vmem = pl.BlockSpec(memory_space=pltpu.VMEM)
+    return pl.pallas_call(
+        functools.partial(deal_kernel, share),
+        out_shape=[jax.ShapeDtypeStruct(right_side.shape, BF16)] * 2,
+        in_specs=[vmem],
+        out_specs=[vmem] * 2,
+    )(dealt)
 
 
 def solution(mesh):

time: 235 us -> 234 us (level)
  local copies, waits for them, and re-layouts: 15.7 us -> 10 us
  Pallas kernels: 13.2 us -> 17 us
    unnamed x20 -> x6, local copies, waits for them, and re-layouts: 6.88 us -> 3.39 us
  transfers between devices with their start and end apart: 25 -> 25, of which waited for: 19 -> 19; matrix products, arithmetic and copies ran while one was open for 6% -> 6% of each run, Pallas kernels for 1% -> 2%
where the time goes in v8:
time: 234 us; the launch traced here: 233 us
  starting transfers between devices  101 us (43%)
  waiting for transfers between devices  53.5 us (23%)
  blocking collectives  24.8 us (11%)
  between operations  17.1 us (7%)
  Pallas kernels  17 us (7%)
  local copies, waits for them, and re-layouts  10 us (4%)
  other arithmetic  7.94 us (3%)
    ppermute x18, starting transfers between devices, swap(): lax.ppermute(vector, 'dom', far_pairs if level % 2 == 0 else near_pairs)  72.9 us
    ppermute x18, waiting for transfers between devices, swap(): lax.ppermute(vector, 'dom', far_pairs if level % 2 == 0 else near_pairs)  25.4 us
    all_to_all x1, blocking collectives, local(): dealt = lax.all_to_all(dealt, 'level', 0, 0, tiled=False)  24.8 us
    all_gather x1, waiting for transfers between devices, local(): weights = lax.all_gather(weights, 'level')  17.4 us
    pallas_call x15, Pallas kernels, call(): pl.pallas_call(kernel, out_shape=outs, in_specs=specs, out_specs=[vmem] *...  15.5 us
    ppermute x1, starting transfers between devices, local(): by_far = lax.ppermute(mates, 'dom', far_pairs)  11 us
    all_to_all x1, starting transfers between devices, local(): side = lax.all_to_all(side, 'level', 1, 0, tiled=False)  8.35 us
    all_gather x1, waiting for transfers between devices, local(): mates = lax.all_gather(mates, 'level')  6.29 us
  transfers between devices with their start and end apart: 25, of which 19 were waited for; matrix products, arithmetic and copies ran while one was open for 6% of the time, Pallas kernels for 2%

profile of v8, /device:TPU:1, one launch (start us, length us, event | category | flops | bytes accessed | tf_op | source)
XLA Modules:
  0.0 232.5 jit_solution(1072701720119108393)
XLA Ops:
  7.2 1.9 pad_maximum_fusion
  9.2 1.3 fusion.7
  15.0 4.8 %collective-permute-start = (bf16[4,2,128,128]{3,2,1,0:T(8,128)(2,1)S(1)}, bf16[4,2,128,128]{3,2,1,0:T(8,128)(2,1)S(1)}, u32[]{:S(2)}, u32[]{:S(2)}) collective-permute-start(bf16[4,2,128,128]{3,2,1,0:T(8,128)(2,1)S(1)} %pad_maximum_fusion.1), channel_id=1, source_target_pairs={{0,16},{16,0},{32,48},{48,32},{64,80},{80,64},{96,112},{112,96},{1... | collective-permute-start | bytes 786440 | tf_op jit(solution)/shard_map/ppermute | solution.py:231
  19.9 11.0 %collective-permute-start.1 = (bf16[4,2,128,128]{3,2,1,0:T(8,128)(2,1)S(1)}, bf16[4,2,128,128]{3,2,1,0:T(8,128)(2,1)S(1)}, u32[]{:S(2)}, u32[]{:S(2)}) collective-permute-start(bf16[4,2,128,128]{3,2,1,0:T(8,128)(2,1)S(1)} %pad_maximum_fusion.1), channel_id=1, source_target_pairs={{16,32},{32,16},{48,64},{64,48},{80,96},{96,80},{112,128},{128,112... | collective-permute-start | bytes 786440 | tf_op jit(solution)/shard_map/ppermute | solution.py:232
  32.7 8.3 %all-to-all-start = ((bf16[1,4,16,4,128]{4,3,1,0,2:T(4,128)(2,1)}), bf16[1,4,16,4,128]{4,3,1,0,2:T(4,128)(2,1)S(1)}, u32[]{:S(2)}, u32[]{:S(2)}) async-start(bf16[1,4,16,4,128]{4,3,1,0,2:T(4,128)(2,1)} %copy.56), calls=%async_computation | async-start | bytes 131072 | tf_op jit(solution)/shard_map/all_to_all | solution.py:237
  48.6 1.1 all-to-all-done
  50.3 1.9 collective-permute-start.2
  52.3 1.9 collective-permute-start.3
  55.0 3.2 %collective-permute-done.2 = bf16[2,32,128]{2,1,0:T(8,128)(2,1)S(1)} collective-permute-done((bf16[2,32,128]{2,1,0:T(8,128)(2,1)S(1)}, bf16[2,32,128]{2,1,0:T(8,128)(2,1)S(1)}, u32[]{:S(2)}, u32[]{:S(2)}) %collective-permute-start.2) | collective-permute-done | bytes 16416 | tf_op jit(solution)/shard_map/ppermute | solution.py:271
  58.3 17.4 %all-gather.5.cloned.1.call-done = bf16[64,4,128,128]{3,2,1,0:T(8,128)(2,1)} async-done(((bf16[4,4,128,128]{3,2,1,0:T(8,128)(2,1)}), bf16[64,4,128,128]{3,2,1,0:T(8,128)(2,1)}) %all-gather.5.cloned.1.call-update) | async-done | bytes 8388624 | tf_op jit(solution)/shard_map/all_gather | solution.py:219
  75.7 2.0 shard_map.68.own.solved.rest_1_
  77.7 7.8 %collective-permute-start.4 = (bf16[32,128]{1,0:T(8,128)(2,1)S(1)}, bf16[32,128]{1,0:T(8,128)(2,1)S(1)}, u32[]{:S(2)}, u32[]{:S(2)}) collective-permute-start(bf16[32,128]{1,0:T(8,128)(2,1)S(1)} %shard_map.68.own.solved.rest_1_), channel_id=1, source_target_pairs={{16,32},{32,16},{48,64},{64,48},{80,96},{96,80},{112,128},{128,112... | collective-permute-start | bytes 24584 | tf_op jit(solution)/shard_map/ppermute | solution.py:281
  85.5 1.9 collective-permute-start.5
  87.5 2.5 %collective-permute-done.5.near.solved_mate = bf16[32,128]{1,0:T(8,128)(2,1)S(1)} collective-permute-done((bf16[32,128]{1,0:T(8,128)(2,1)S(1)}, bf16[32,128]{1,0:T(8,128)(2,1)S(1)}, u32[]{:S(2)}, u32[]{:S(2)}) %collective-permute-start.5) | collective-permute-done | bytes 8224 | tf_op jit(solution)/shard_map/ppermute | solution.py:281
  90.5 3.3 %collective-permute-start.6 = (bf16[32,128]{1,0:T(8,128)(2,1)S(1)}, bf16[32,128]{1,0:T(8,128)(2,1)S(1)}, u32[]{:S(2)}, u32[]{:S(2)}) collective-permute-start(bf16[32,128]{1,0:T(8,128)(2,1)S(1)} %shard_map.69.own.solved.rest_2_), channel_id=1, source_target_pairs={{16,32},{32,16},{48,64},{64,48},{80,96},{96,80},{112,128},{128,112... | collective-permute-start | bytes 24584 | tf_op jit(solution)/shard_map/ppermute | solution.py:281
  93.8 1.9 collective-permute-start.7
  95.8 2.5 %collective-permute-done.6.far.solved_mate = bf16[32,128]{1,0:T(8,128)(2,1)S(1)} collective-permute-done((bf16[32,128]{1,0:T(8,128)(2,1)S(1)}, bf16[32,128]{1,0:T(8,128)(2,1)S(1)}, u32[]{:S(2)}, u32[]{:S(2)}) %collective-permute-start.6) | collective-permute-done | bytes 8224 | tf_op jit(solution)/shard_map/ppermute | solution.py:281
  99.2 5.3 %collective-permute-start.8 = (bf16[32,128]{1,0:T(8,128)(2,1)S(1)}, bf16[32,128]{1,0:T(8,128)(2,1)S(1)}, u32[]{:S(2)}, u32[]{:S(2)}) collective-permute-start(bf16[32,128]{1,0:T(8,128)(2,1)S(1)} %shard_map.70.own.solved.rest_3_), channel_id=1, source_target_pairs={{16,32},{32,16},{48,64},{64,48},{80,96},{96,80},{112,128},{128,112... | collective-permute-start | bytes 24584 | tf_op jit(solution)/shard_map/ppermute | solution.py:281
  104.5 1.9 collective-permute-start.9
  107.0 2.4 %collective-permute-done.9.near.solved_mate = bf16[32,128]{1,0:T(8,128)(2,1)S(1)} collective-permute-done((bf16[32,128]{1,0:T(8,128)(2,1)S(1)}, bf16[32,128]{1,0:T(8,128)(2,1)S(1)}, u32[]{:S(2)}, u32[]{:S(2)}) %collective-permute-start.9) | collective-permute-done | bytes 8224 | tf_op jit(solution)/shard_map/ppermute | solution.py:281
  109.9 3.3 %collective-permute-start.10 = (bf16[32,128]{1,0:T(8,128)(2,1)S(1)}, bf16[32,128]{1,0:T(8,128)(2,1)S(1)}, u32[]{:S(2)}, u32[]{:S(2)}) collective-permute-start(bf16[32,128]{1,0:T(8,128)(2,1)S(1)} %shard_map.71.own.solved.rest_4_), channel_id=1, source_target_pairs={{16,32},{32,16},{48,64},{64,48},{80,96},{96,80},{112,128},{128,112... | collective-permute-start | bytes 24584 | tf_op jit(solution)/shard_map/ppermute | solution.py:281
  113.3 1.9 collective-permute-start.11
  115.2 6.3 %all-gather.7.cloned.1.call-done = bf16[64,2,128,128]{3,2,1,0:T(8,128)(2,1)} async-done(((bf16[4,2,128,128]{3,2,1,0:T(8,128)(2,1)}), bf16[64,2,128,128]{3,2,1,0:T(8,128)(2,1)}) %all-gather.7.cloned.1.call-update) | async-done | bytes 4194320 | tf_op jit(solution)/shard_map/all_gather | solution.py:278
  121.5 2.0 shard_map.72.own.solved.rest_5_
  123.5 3.3 %collective-permute-start.12 = (bf16[32,128]{1,0:T(8,128)(2,1)S(1)}, bf16[32,128]{1,0:T(8,128)(2,1)S(1)}, u32[]{:S(2)}, u32[]{:S(2)}) collective-permute-start(bf16[32,128]{1,0:T(8,128)(2,1)S(1)} %shard_map.72.own.solved.rest_5_), channel_id=1, source_target_pairs={{0,16},{16,0},{32,48},{48,32},{64,80},{80,64},{96,112},{112,96},{1... | collective-permute-start | bytes 24584 | tf_op jit(solution)/shard_map/ppermute | solution.py:281
  126.7 1.1 collective-permute-done.12.mate.solved_mate
  127.9 3.4 %copy-done.1 = bf16[64,4,128,128]{3,2,1,0:T(8,128)(2,1)S(1)} copy-done((bf16[64,4,128,128]{3,2,1,0:T(8,128)(2,1)S(1)}, bf16[64,4,128,128]{3,2,1,0:T(8,128)(2,1)}, u32[]{:S(2)}) %copy-start.1) | copy-done | bytes 8388632
  131.2 1.4 shard_map.73
  132.6 7.8 %collective-permute-start.13 = (bf16[64,128]{1,0:T(8,128)(2,1)S(1)}, bf16[64,128]{1,0:T(8,128)(2,1)S(1)}, u32[]{:S(2)}, u32[]{:S(2)}) collective-permute-start(bf16[64,128]{1,0:T(8,128)(2,1)S(1)} %get-tuple-element.54), channel_id=1, source_target_pairs={{16,32},{32,16},{48,64},{64,48},{80,96},{96,80},{112,128},{128,112... | collective-permute-start | bytes 49160 | tf_op jit(solution)/shard_map/ppermute | solution.py:281
  140.4 1.1 collective-permute-done.13.came
  142.4 1.9 collective-permute-start.14
  144.3 2.6 %collective-permute-done.14.came = bf16[64,128]{1,0:T(8,128)(2,1)S(1)} collective-permute-done((bf16[64,128]{1,0:T(8,128)(2,1)S(1)}, bf16[64,128]{1,0:T(8,128)(2,1)S(1)}, u32[]{:S(2)}, u32[]{:S(2)}) %collective-permute-start.14) | collective-permute-done | bytes 16416 | tf_op jit(solution)/shard_map/ppermute | solution.py:281
  146.9 1.3 shard_map.75
  148.2 6.7 %collective-permute-start.15 = (bf16[64,128]{1,0:T(8,128)(2,1)S(1)}, bf16[64,128]{1,0:T(8,128)(2,1)S(1)}, u32[]{:S(2)}, u32[]{:S(2)}) collective-permute-start(bf16[64,128]{1,0:T(8,128)(2,1)S(1)} %get-tuple-element.60), channel_id=1, source_target_pairs={{16,32},{32,16},{48,64},{64,48},{80,96},{96,80},{112,128},{128,112... | collective-permute-start | bytes 49160 | tf_op jit(solution)/shard_map/ppermute | solution.py:281
  154.8 1.1 collective-permute-done.15.came
  156.9 1.9 collective-permute-start.16
  158.9 2.6 %collective-permute-done.16.came = bf16[64,128]{1,0:T(8,128)(2,1)S(1)} collective-permute-done((bf16[64,128]{1,0:T(8,128)(2,1)S(1)}, bf16[64,128]{1,0:T(8,128)(2,1)S(1)}, u32[]{:S(2)}, u32[]{:S(2)}) %collective-permute-start.16) | collective-permute-done | bytes 16416 | tf_op jit(solution)/shard_map/ppermute | solution.py:281
  162.4 6.7 %collective-permute-start.17 = (bf16[64,128]{1,0:T(8,128)(2,1)S(1)}, bf16[64,128]{1,0:T(8,128)(2,1)S(1)}, u32[]{:S(2)}, u32[]{:S(2)}) collective-permute-start(bf16[64,128]{1,0:T(8,128)(2,1)S(1)} %get-tuple-element.64), channel_id=1, source_target_pairs={{16,32},{32,16},{48,64},{64,48},{80,96},{96,80},{112,128},{128,112... | collective-permute-start | bytes 49160 | tf_op jit(solution)/shard_map/ppermute | solution.py:281
  169.1 1.1 collective-permute-done.17.came
  171.2 1.9 collective-permute-start.18
  173.1 2.8 %collective-permute-done.18.came = bf16[64,128]{1,0:T(8,128)(2,1)S(1)} collective-permute-done((bf16[64,128]{1,0:T(8,128)(2,1)S(1)}, bf16[64,128]{1,0:T(8,128)(2,1)S(1)}, u32[]{:S(2)}, u32[]{:S(2)}) %collective-permute-start.18) | collective-permute-done | bytes 16416 | tf_op jit(solution)/shard_map/ppermute | solution.py:281
  176.9 6.7 %collective-permute-start.19 = (bf16[64,128]{1,0:T(8,128)(2,1)S(1)}, bf16[64,128]{1,0:T(8,128)(2,1)S(1)}, u32[]{:S(2)}, u32[]{:S(2)}) collective-permute-start(bf16[64,128]{1,0:T(8,128)(2,1)S(1)} %get-tuple-element.68), channel_id=1, source_target_pairs={{16,32},{32,16},{48,64},{64,48},{80,96},{96,80},{112,128},{128,112... | collective-permute-start | bytes 49160 | tf_op jit(solution)/shard_map/ppermute | solution.py:281
  183.6 1.1 collective-permute-done.19.came
  185.7 1.9 collective-permute-start.20
  187.6 2.6 %collective-permute-done.20.came = bf16[64,128]{1,0:T(8,128)(2,1)S(1)} collective-permute-done((bf16[64,128]{1,0:T(8,128)(2,1)S(1)}, bf16[64,128]{1,0:T(8,128)(2,1)S(1)}, u32[]{:S(2)}, u32[]{:S(2)}) %collective-permute-start.20) | collective-permute-done | bytes 16416 | tf_op jit(solution)/shard_map/ppermute | solution.py:281
  191.1 6.7 %collective-permute-start.21 = (bf16[64,128]{1,0:T(8,128)(2,1)S(1)}, bf16[64,128]{1,0:T(8,128)(2,1)S(1)}, u32[]{:S(2)}, u32[]{:S(2)}) collective-permute-start(bf16[64,128]{1,0:T(8,128)(2,1)S(1)} %get-tuple-element.72), channel_id=1, source_target_pairs={{16,32},{32,16},{48,64},{64,48},{80,96},{96,80},{112,128},{128,112... | collective-permute-start | bytes 49160 | tf_op jit(solution)/shard_map/ppermute | solution.py:281
  199.3 24.8 %all_to_all.20.dealt = bf16[16,32,128]{2,1,0:T(8,128)(2,1)} all-to-all(bf16[16,32,128]{2,1,0:T(8,128)(2,1)S(1)} %shard_map.82), channel_id=1, replica_groups=mesh['dom'=32,'level'=16] {'level'}, dimensions={0} | all-to-all | bytes 262144 | tf_op jit(solution)/shard_map/all_to_all | solution.py:319
  224.1 1.6 shard_map.83
  (81 shorter events, 23.4 us)
Async XLA Ops:
  7.2 68.5 %all-gather.5.cloned.1.call-start = ((), (), s32[]{:S(2)}) async-start(), calls=%async_computation.2 | async-start | bytes 8912896 | tf_op jit(solution)/shard_map/all_gather | solution.py:219
  15.0 39.2 %collective-permute-start = (bf16[4,2,128,128]{3,2,1,0:T(8,128)(2,1)S(1)}, bf16[4,2,128,128]{3,2,1,0:T(8,128)(2,1)S(1)}, u32[]{:S(2)}, u32[]{:S(2)}) collective-permute-start(bf16[4,2,128,128]{3,2,1,0:T(8,128)(2,1)S(1)} %pad_maximum_fusion.1), channel_id=1, source_target_pairs={{0,16},{16,0},{32,48},{48,32},{64,80},{80,64},{96,112},{112,96},{1... | collective-permute-start | bytes 786440 | tf_op jit(solution)/shard_map/ppermute | solution.py:231
  19.9 34.3 %collective-permute-start.1 = (bf16[4,2,128,128]{3,2,1,0:T(8,128)(2,1)S(1)}, bf16[4,2,128,128]{3,2,1,0:T(8,128)(2,1)S(1)}, u32[]{:S(2)}, u32[]{:S(2)}) collective-permute-start(bf16[4,2,128,128]{3,2,1,0:T(8,128)(2,1)S(1)} %pad_maximum_fusion.1), channel_id=1, source_target_pairs={{16,32},{32,16},{48,64},{64,48},{80,96},{96,80},{112,128},{128,112... | collective-permute-start | bytes 786440 | tf_op jit(solution)/shard_map/ppermute | solution.py:232
  32.7 17.0 %all-to-all-start = ((bf16[1,4,16,4,128]{4,3,1,0,2:T(4,128)(2,1)}), bf16[1,4,16,4,128]{4,3,1,0,2:T(4,128)(2,1)S(1)}, u32[]{:S(2)}, u32[]{:S(2)}) async-start(bf16[1,4,16,4,128]{4,3,1,0,2:T(4,128)(2,1)} %copy.56), calls=%async_computation | async-start | bytes 131072 | tf_op jit(solution)/shard_map/all_to_all | solution.py:237
  41.0 80.4 %all-gather.7.cloned.1.call-start = ((), (), s32[]{:S(2)}) async-start(), calls=%async_computation.3 | async-start | bytes 4456448 | tf_op jit(solution)/shard_map/all_gather | solution.py:278
  50.3 7.8 %collective-permute-start.2 = (bf16[2,32,128]{2,1,0:T(8,128)(2,1)S(1)}, bf16[2,32,128]{2,1,0:T(8,128)(2,1)S(1)}, u32[]{:S(2)}, u32[]{:S(2)}) collective-permute-start(bf16[2,32,128]{2,1,0:T(8,128)(2,1)S(1)} %get-tuple-element.98), channel_id=1, source_target_pairs={{16,32},{32,16},{48,64},{64,48},{80,96},{96,80},{112,128},{128,112... | collective-permute-start | bytes 49160 | tf_op jit(solution)/shard_map/ppermute | solution.py:271
  52.3 5.9 %collective-permute-start.3 = (bf16[2,32,128]{2,1,0:T(8,128)(2,1)S(1)}, bf16[2,32,128]{2,1,0:T(8,128)(2,1)S(1)}, u32[]{:S(2)}, u32[]{:S(2)}) collective-permute-start(bf16[2,32,128]{2,1,0:T(8,128)(2,1)S(1)} %get-tuple-element.97), channel_id=1, source_target_pairs={{0,16},{16,0},{32,48},{48,32},{64,80},{80,64},{96,112},{112,96},{1... | collective-permute-start | bytes 49160 | tf_op jit(solution)/shard_map/ppermute | solution.py:272
  75.7 14.2 %copy-start = (bf16[64,4,128,128]{3,2,1,0:T(8,128)(2,1)S(1)}, bf16[64,4,128,128]{3,2,1,0:T(8,128)(2,1)}, u32[]{:S(2)}) copy-start(bf16[64,4,128,128]{3,2,1,0:T(8,128)(2,1)} %all-gather.5.cloned.1.call-done) | copy-start | bytes 25165828
  77.7 9.8 %collective-permute-start.4 = (bf16[32,128]{1,0:T(8,128)(2,1)S(1)}, bf16[32,128]{1,0:T(8,128)(2,1)S(1)}, u32[]{:S(2)}, u32[]{:S(2)}) collective-permute-start(bf16[32,128]{1,0:T(8,128)(2,1)S(1)} %shard_map.68.own.solved.rest_1_), channel_id=1, source_target_pairs={{16,32},{32,16},{48,64},{64,48},{80,96},{96,80},{112,128},{128,112... | collective-permute-start | bytes 24584 | tf_op jit(solution)/shard_map/ppermute | solution.py:281
  85.5 4.4 %collective-permute-start.5 = (bf16[32,128]{1,0:T(8,128)(2,1)S(1)}, bf16[32,128]{1,0:T(8,128)(2,1)S(1)}, u32[]{:S(2)}, u32[]{:S(2)}) collective-permute-start(bf16[32,128]{1,0:T(8,128)(2,1)S(1)} %shard_map.68.own.solved.rest_1_), channel_id=1, source_target_pairs={{0,16},{16,0},{32,48},{48,32},{64,80},{80,64},{96,112},{112,96},{1... | collective-permute-start | bytes 24584 | tf_op jit(solution)/shard_map/ppermute | solution.py:281
  90.5 7.7 %collective-permute-start.6 = (bf16[32,128]{1,0:T(8,128)(2,1)S(1)}, bf16[32,128]{1,0:T(8,128)(2,1)S(1)}, u32[]{:S(2)}, u32[]{:S(2)}) collective-permute-start(bf16[32,128]{1,0:T(8,128)(2,1)S(1)} %shard_map.69.own.solved.rest_2_), channel_id=1, source_target_pairs={{16,32},{32,16},{48,64},{64,48},{80,96},{96,80},{112,128},{128,112... | collective-permute-start | bytes 24584 | tf_op jit(solution)/shard_map/ppermute | solution.py:281
  93.8 4.8 %collective-permute-start.7 = (bf16[32,128]{1,0:T(8,128)(2,1)S(1)}, bf16[32,128]{1,0:T(8,128)(2,1)S(1)}, u32[]{:S(2)}, u32[]{:S(2)}) collective-permute-start(bf16[32,128]{1,0:T(8,128)(2,1)S(1)} %shard_map.69.own.solved.rest_2_), channel_id=1, source_target_pairs={{0,16},{16,0},{32,48},{48,32},{64,80},{80,64},{96,112},{112,96},{1... | collective-permute-start | bytes 24584 | tf_op jit(solution)/shard_map/ppermute | solution.py:281
  99.2 7.7 %collective-permute-start.8 = (bf16[32,128]{1,0:T(8,128)(2,1)S(1)}, bf16[32,128]{1,0:T(8,128)(2,1)S(1)}, u32[]{:S(2)}, u32[]{:S(2)}) collective-permute-start(bf16[32,128]{1,0:T(8,128)(2,1)S(1)} %shard_map.70.own.solved.rest_3_), channel_id=1, source_target_pairs={{16,32},{32,16},{48,64},{64,48},{80,96},{96,80},{112,128},{128,112... | collective-permute-start | bytes 24584 | tf_op jit(solution)/shard_map/ppermute | solution.py:281
  104.5 4.8 %collective-permute-start.9 = (bf16[32,128]{1,0:T(8,128)(2,1)S(1)}, bf16[32,128]{1,0:T(8,128)(2,1)S(1)}, u32[]{:S(2)}, u32[]{:S(2)}) collective-permute-start(bf16[32,128]{1,0:T(8,128)(2,1)S(1)} %shard_map.70.own.solved.rest_3_), channel_id=1, source_target_pairs={{0,16},{16,0},{32,48},{48,32},{64,80},{80,64},{96,112},{112,96},{1... | collective-permute-start | bytes 24584 | tf_op jit(solution)/shard_map/ppermute | solution.py:281
  109.9 11.6 %collective-permute-start.10 = (bf16[32,128]{1,0:T(8,128)(2,1)S(1)}, bf16[32,128]{1,0:T(8,128)(2,1)S(1)}, u32[]{:S(2)}, u32[]{:S(2)}) collective-permute-start(bf16[32,128]{1,0:T(8,128)(2,1)S(1)} %shard_map.71.own.solved.rest_4_), channel_id=1, source_target_pairs={{16,32},{32,16},{48,64},{64,48},{80,96},{96,80},{112,128},{128,112... | collective-permute-start | bytes 24584 | tf_op jit(solution)/shard_map/ppermute | solution.py:281
  113.3 8.2 %collective-permute-start.11 = (bf16[32,128]{1,0:T(8,128)(2,1)S(1)}, bf16[32,128]{1,0:T(8,128)(2,1)S(1)}, u32[]{:S(2)}, u32[]{:S(2)}) collective-permute-start(bf16[32,128]{1,0:T(8,128)(2,1)S(1)} %shard_map.71.own.solved.rest_4_), channel_id=1, source_target_pairs={{0,16},{16,0},{32,48},{48,32},{64,80},{80,64},{96,112},{112,96},{1... | collective-permute-start | bytes 24584 | tf_op jit(solution)/shard_map/ppermute | solution.py:281
  121.5 20.0 %copy-start.2 = (bf16[64,2,128,128]{3,2,1,0:T(8,128)(2,1)S(1)}, bf16[64,2,128,128]{3,2,1,0:T(8,128)(2,1)}, u32[]{:S(2)}) copy-start(bf16[64,2,128,128]{3,2,1,0:T(8,128)(2,1)} %all-gather.7.cloned.1.call-done) | copy-start | bytes 12582916
  123.5 4.4 %collective-permute-start.12 = (bf16[32,128]{1,0:T(8,128)(2,1)S(1)}, bf16[32,128]{1,0:T(8,128)(2,1)S(1)}, u32[]{:S(2)}, u32[]{:S(2)}) collective-permute-start(bf16[32,128]{1,0:T(8,128)(2,1)S(1)} %shard_map.72.own.solved.rest_5_), channel_id=1, source_target_pairs={{0,16},{16,0},{32,48},{48,32},{64,80},{80,64},{96,112},{112,96},{1... | collective-permute-start | bytes 24584 | tf_op jit(solution)/shard_map/ppermute | solution.py:281
  127.9 3.4 %copy-start.1 = (bf16[64,4,128,128]{3,2,1,0:T(8,128)(2,1)S(1)}, bf16[64,4,128,128]{3,2,1,0:T(8,128)(2,1)}, u32[]{:S(2)}) copy-start(bf16[64,4,128,128]{3,2,1,0:T(8,128)(2,1)} %all-gather.5.cloned.1.call-done) | copy-start | bytes 25165828
  132.6 8.9 %collective-permute-start.13 = (bf16[64,128]{1,0:T(8,128)(2,1)S(1)}, bf16[64,128]{1,0:T(8,128)(2,1)S(1)}, u32[]{:S(2)}, u32[]{:S(2)}) collective-permute-start(bf16[64,128]{1,0:T(8,128)(2,1)S(1)} %get-tuple-element.54), channel_id=1, source_target_pairs={{16,32},{32,16},{48,64},{64,48},{80,96},{96,80},{112,128},{128,112... | collective-permute-start | bytes 49160 | tf_op jit(solution)/shard_map/ppermute | solution.py:281
  142.4 4.5 %collective-permute-start.14 = (bf16[64,128]{1,0:T(8,128)(2,1)S(1)}, bf16[64,128]{1,0:T(8,128)(2,1)S(1)}, u32[]{:S(2)}, u32[]{:S(2)}) collective-permute-start(bf16[64,128]{1,0:T(8,128)(2,1)S(1)} %get-tuple-element.58), channel_id=1, source_target_pairs={{0,16},{16,0},{32,48},{48,32},{64,80},{80,64},{96,112},{112,96},{1... | collective-permute-start | bytes 49160 | tf_op jit(solution)/shard_map/ppermute | solution.py:281
  148.2 7.8 %collective-permute-start.15 = (bf16[64,128]{1,0:T(8,128)(2,1)S(1)}, bf16[64,128]{1,0:T(8,128)(2,1)S(1)}, u32[]{:S(2)}, u32[]{:S(2)}) collective-permute-start(bf16[64,128]{1,0:T(8,128)(2,1)S(1)} %get-tuple-element.60), channel_id=1, source_target_pairs={{16,32},{32,16},{48,64},{64,48},{80,96},{96,80},{112,128},{128,112... | collective-permute-start | bytes 49160 | tf_op jit(solution)/shard_map/ppermute | solution.py:281
  156.9 4.5 %collective-permute-start.16 = (bf16[64,128]{1,0:T(8,128)(2,1)S(1)}, bf16[64,128]{1,0:T(8,128)(2,1)S(1)}, u32[]{:S(2)}, u32[]{:S(2)}) collective-permute-start(bf16[64,128]{1,0:T(8,128)(2,1)S(1)} %get-tuple-element.62), channel_id=1, source_target_pairs={{0,16},{16,0},{32,48},{48,32},{64,80},{80,64},{96,112},{112,96},{1... | collective-permute-start | bytes 49160 | tf_op jit(solution)/shard_map/ppermute | solution.py:281
  162.4 7.8 %collective-permute-start.17 = (bf16[64,128]{1,0:T(8,128)(2,1)S(1)}, bf16[64,128]{1,0:T(8,128)(2,1)S(1)}, u32[]{:S(2)}, u32[]{:S(2)}) collective-permute-start(bf16[64,128]{1,0:T(8,128)(2,1)S(1)} %get-tuple-element.64), channel_id=1, source_target_pairs={{16,32},{32,16},{48,64},{64,48},{80,96},{96,80},{112,128},{128,112... | collective-permute-start | bytes 49160 | tf_op jit(solution)/shard_map/ppermute | solution.py:281
  171.2 4.8 %collective-permute-start.18 = (bf16[64,128]{1,0:T(8,128)(2,1)S(1)}, bf16[64,128]{1,0:T(8,128)(2,1)S(1)}, u32[]{:S(2)}, u32[]{:S(2)}) collective-permute-start(bf16[64,128]{1,0:T(8,128)(2,1)S(1)} %get-tuple-element.66), channel_id=1, source_target_pairs={{0,16},{16,0},{32,48},{48,32},{64,80},{80,64},{96,112},{112,96},{1... | collective-permute-start | bytes 49160 | tf_op jit(solution)/shard_map/ppermute | solution.py:281
  176.9 7.8 %collective-permute-start.19 = (bf16[64,128]{1,0:T(8,128)(2,1)S(1)}, bf16[64,128]{1,0:T(8,128)(2,1)S(1)}, u32[]{:S(2)}, u32[]{:S(2)}) collective-permute-start(bf16[64,128]{1,0:T(8,128)(2,1)S(1)} %get-tuple-element.68), channel_id=1, source_target_pairs={{16,32},{32,16},{48,64},{64,48},{80,96},{96,80},{112,128},{128,112... | collective-permute-start | bytes 49160 | tf_op jit(solution)/shard_map/ppermute | solution.py:281
  185.7 4.5 %collective-permute-start.20 = (bf16[64,128]{1,0:T(8,128)(2,1)S(1)}, bf16[64,128]{1,0:T(8,128)(2,1)S(1)}, u32[]{:S(2)}, u32[]{:S(2)}) collective-permute-start(bf16[64,128]{1,0:T(8,128)(2,1)S(1)} %get-tuple-element.70), channel_id=1, source_target_pairs={{0,16},{16,0},{32,48},{48,32},{64,80},{80,64},{96,112},{112,96},{1... | collective-permute-start | bytes 49160 | tf_op jit(solution)/shard_map/ppermute | solution.py:281
  191.1 7.8 %collective-permute-start.21 = (bf16[64,128]{1,0:T(8,128)(2,1)S(1)}, bf16[64,128]{1,0:T(8,128)(2,1)S(1)}, u32[]{:S(2)}, u32[]{:S(2)}) collective-permute-start(bf16[64,128]{1,0:T(8,128)(2,1)S(1)} %get-tuple-element.72), channel_id=1, source_target_pairs={{16,32},{32,16},{48,64},{64,48},{80,96},{96,80},{112,128},{128,112... | collective-permute-start | bytes 49160 | tf_op jit(solution)/shard_map/ppermute | solution.py:281
Sparse Core Ops, SparseCore 0:
  10.1 65.5 all-gather.4
  77.8 43.6 all-gather.6

commit v9 on v8

--- a/solution.py
+++ b/solution.py
@@ -77,18 +77,15 @@
     out[...] = products(dot, share, owners, shifted, weights, 0).astype(BF16)
 
 
-def gathered_sums(level, share, packed, weights, mates, places, own, mate):
-    *owners, side = unpack(packed, level)
+def gathered_sums(level, share, places, own, mate, blocks):
     span = own.shape[0]
     picked = picked_from(places[level], jnp.concatenate([own, mate], axis=0)).astype(BF16)
-    sums = products(dot, share, owners, picked[:span], weights, 2)
-    sums += products(dot, share, owners, picked[2 * span :], weights, 1 + side)
-    if callable(mates):
-        owners, mates, kind = mates()
-    else:
-        kind = 1
-    sums_mate = products(dot, share, owners, picked[span : 2 * span], mates, kind)
-    return jnp.concatenate([sums, sums_mate], axis=0)
+    parts = [picked[n * span : (n + 1) * span] for n in range(3)]
+    sums = [
+        products(dot, share, owners, part, block, kind)
+        for part, (owners, block, kind) in zip(parts, blocks())
+    ]
+    return jnp.concatenate([sums[0] + sums[2], sums[1]], axis=0)
 
 
 def pushed_sums(level, share, packed, weights, mates, targets, own, mate):
@@ -115,22 +112,22 @@
     return held[:span] + came[span:], held[span:] + came[:span]
 
 
-def entry_kernel(level, share, packed, mates, weights, meets, own, mate, held, sent, blocks, sems):
-    *owners, _ = unpack(packed, level)
-    copies = [
-        pltpu.make_async_copy(mates.at[owners[half], :, pl.ds(1, 1)], blocks.at[half], sems.at[half])
-        for half in range(2)
-    ]
+def entry_kernel(level, share, packed, weights, mates, meets, own, mate, held, sent, blocks, sems):
+    *owners, side = unpack(packed, level)
+    copies = []
+    for which, (source, kind) in enumerate(((weights, 2), (mates, 1), (weights, 1 + side))):
+        for half in range(2):
+            rows = source.at[owners[half], :, pl.ds(kind, 1)]
+            copies.append(pltpu.make_async_copy(rows, blocks.at[which, half], sems.at[which, half]))
     for copy in copies:
         copy.start()
 
     def arrived():
         for copy in copies:
             copy.wait()
-        return range(2), blocks, 0
-
-    sums = gathered_sums(level, share, packed, weights, arrived, meets, own[...], mate[...])
-    pass_on(sums, held, sent)
+        return [(range(2), blocks.at[which], 0) for which in range(3)]
+
+    pass_on(gathered_sums(level, share, meets, own[...], mate[...], arrived), held, sent)
 
 
 def forward_pair_kernel(
@@ -146,7 +143,9 @@
     if last:
         sums = pushed_sums(level, share, packed, weights, mates, targets, *pair)
     else:
-        sums = gathered_sums(level + 1, share, packed, weights, mates, meets, *pair)
+        *owners, up = unpack(packed, level + 1)
+        blocks = [(owners, weights, 2), (owners, mates, 1), (owners, weights, 1 + up)]
+        sums = gathered_sums(level + 1, share, meets, *pair, lambda: blocks)
     pass_on(sums, to_hold, to_send)
 
 
@@ -177,30 +176,21 @@
                 out[owners[half], which * size : (which + 1) * size] = array[half * size : (half + 1) * size]
 
 
-def deal_kernel(share, dealt, *outs):
-    parts = [dealt[source].astype(F32) for source in range(dealt.shape[0])]
-    for which, out in enumerate(outs):
-        for row in range(out.shape[0]):
-            at = (which * out.shape[0] + row) * share
-            out[row] = jnp.concatenate([part[at : at + share] for part in parts], axis=0).astype(BF16)
-
-
-def call(kernel, outs, packed, blocks, *rest, fetched=None):
-    vmem = pl.BlockSpec(memory_space=pltpu.VMEM)
-    specs = [vmem] * (2 + len(rest))
-    scratch = []
-    if fetched:
-        specs[1] = pl.BlockSpec(memory_space=pltpu.HBM)
-        blocks = pltpu.with_memory_space_constraint(blocks, pltpu.HBM)
-        scratch = [pltpu.VMEM(fetched, blocks.dtype), pltpu.SemaphoreType.DMA((2,))]
+def call(kernel, outs, *args, fetched=0, scratch=(), cost=None):
+    specs = [pl.BlockSpec(memory_space=pltpu.VMEM)] * len(args)
+    args = list(args)
+    for at in range(1, 1 + fetched):
+        specs[at] = pl.BlockSpec(memory_space=pltpu.HBM)
+        args[at] = pltpu.with_memory_space_constraint(args[at], pltpu.HBM)
     return pl.pallas_call(
         kernel,
         out_shape=outs,
         in_specs=specs,
-        out_specs=[vmem] * len(outs),
+        out_specs=[pl.BlockSpec(memory_space=pltpu.VMEM)] * len(outs),
         scratch_shapes=scratch,
+        cost_estimate=cost,
         compiler_params=pltpu.CompilerParams(vmem_limit_bytes=16 * 2**20),
-    )(packed, blocks, *rest)
+    )(*args)
 
 
 def local(right_side, diag_inverse, off_blocks, columns, plan):
@@ -286,19 +276,25 @@
         if level > 1:
             own = solved[-1]
             far, near = swap(own, 0), swap(own, 1)
-        fetched = level in (1, paired - 1)
-        if level == paired - 1:
-            far, near, mates = lax.optimization_barrier((far, near, mates))
         solved_mate.append(near if level % 2 == 0 else far)
-        kernel = functools.partial(forward_kernel, level, share, fetched)
+        kernel = functools.partial(forward_kernel, level, share, level == 1)
         args = packed, weights, places, side, far, own, near
-        fetched = (2,) + weights.shape[1:] if fetched else None
-        solved += call(kernel, [vector], *args, fetched=fetched)
-
-    solved_mate.append(swap(solved[-1], paired - 1))
+        if level == 1:
+            scratch = [pltpu.VMEM((2,) + weights.shape[1:], BF16), pltpu.SemaphoreType.DMA((2,))]
+            solved += call(kernel, [vector], *args, fetched=1, scratch=scratch)
+        else:
+            solved += call(kernel, [vector], *args)
+
+    mate, mates = lax.optimization_barrier((swap(solved[-1], paired - 1), mates))
+    solved_mate.append(mate)
     kernel = functools.partial(entry_kernel, paired, share)
-    args = packed, mates, weights, meets, solved[-1], solved_mate[-1]
-    held, sent = call(kernel, sums, *args, fetched=(2, rows, 1, width, width))
+    args = packed, weights, mates, meets, solved[-1], mate
+    scratch = [
+        pltpu.VMEM((3, 2, rows, 1, width, width), BF16),
+        pltpu.SemaphoreType.DMA((3, 2)),
+    ]
+    cost = pl.CostEstimate(flops=0, transcendentals=0, bytes_accessed=3 * weights.size)
+    held, sent = call(kernel, sums, *args, fetched=2, scratch=scratch, cost=cost)
     for level in range(paired, levels):
         kernel = functools.partial(forward_pair_kernel, level, share, level == levels - 1)
         args = packed, weights, mates, meets, targets, side, side_mates[level - paired]
@@ -317,13 +313,9 @@
     kernel = functools.partial(last_kernel, share)
     (dealt,) = call(kernel, [dealt], packed, weights, held, swap(sent, 0), *solved, *results[::-1])
     dealt = lax.all_to_all(dealt, "level", 0, 0, tiled=False)
-    vmem = pl.BlockSpec(memory_space=pltpu.VMEM)
-    return pl.pallas_call(
-        functools.partial(deal_kernel, share),
-        out_shape=[jax.ShapeDtypeStruct(right_side.shape, BF16)] * 2,
-        in_specs=[vmem],
-        out_specs=[vmem] * 2,
-    )(dealt)
+    dealt = dealt.reshape(levs, 2, rows, share, width).transpose(1, 2, 0, 3, 4)
+    dealt = dealt.reshape(2, rows, depth, width)
+    return dealt[0], dealt[1]
 
 
 def solution(mesh):

time: 234 us -> 232 us (level)
  blocking collectives: 24.8 us -> 29.4 us
  starting transfers between devices: 101 us -> 96.9 us
  Pallas kernels: 17 us -> 14.5 us
    all_gather x1, waiting for transfers between devices: 6.29 us -> 0.89 us  [local(): mates = lax.all_gather(mates, 'level')]
    ppermute x18, waiting for transfers between devices: 25.4 us -> 30.1 us  [swap(): lax.ppermute(vector, 'dom', far_pairs if level % 2 == 0 else near_pairs)]
    all_to_all x1, blocking collectives: 24.8 us -> 29.4 us  [local(): dealt = lax.all_to_all(dealt, 'level', 0, 0, tiled=False)]
    ppermute x18, starting transfers between devices: 72.9 us -> 68.8 us  [swap(): lax.ppermute(vector, 'dom', far_pairs if level % 2 == 0 else near_pairs)]
    pallas_call x16 -> x15, Pallas kernels: 17 us -> 14.5 us  [call(): pl.pallas_call(kernel, out_shape=outs, in_specs=specs, out_specs=[pl.Bloc...]
  transfers between devices with their start and end apart: 25 -> 25, of which waited for: 19 -> 21; matrix products, arithmetic and copies ran while one was open for 6% -> 6% of each run, Pallas kernels for 2% -> 2%
where the time goes in v9:
time: 232 us; the launch traced here: 231 us
  starting transfers between devices  96.9 us (42%)
  waiting for transfers between devices  52.8 us (23%)
  blocking collectives  29.4 us (13%)
  between operations  17.1 us (7%)
  Pallas kernels  14.5 us (6%)
  local copies, waits for them, and re-layouts  11.4 us (5%)
  other arithmetic  7.91 us (3%)
    ppermute x18, starting transfers between devices, swap(): lax.ppermute(vector, 'dom', far_pairs if level % 2 == 0 else near_pairs)  68.8 us
    ppermute x18, waiting for transfers between devices, swap(): lax.ppermute(vector, 'dom', far_pairs if level % 2 == 0 else near_pairs)  30.1 us
    all_to_all x1, blocking collectives, local(): dealt = lax.all_to_all(dealt, 'level', 0, 0, tiled=False)  29.4 us
    all_gather x1, waiting for transfers between devices, local(): weights = lax.all_gather(weights, 'level')  17.4 us
    pallas_call x15, Pallas kernels, call(): pl.pallas_call(kernel, out_shape=outs, in_specs=specs, out_specs=[pl.Bloc...  14.5 us
    ppermute x1, starting transfers between devices, local(): by_far = lax.ppermute(mates, 'dom', far_pairs)  11 us
    all_to_all x1, starting transfers between devices, local(): side = lax.all_to_all(side, 'level', 1, 0, tiled=False)  8.35 us
    ppermute x1, starting transfers between devices, local(): by_near = lax.ppermute(mates, 'dom', near_pairs)  4.83 us
  transfers between devices with their start and end apart: 25, of which 21 were waited for; matrix products, arithmetic and copies ran while one was open for 6% of the time, Pallas kernels for 2%

profile of v9, /device:TPU:1, one launch (start us, length us, event | category | flops | bytes accessed | tf_op | source)
XLA Modules:
  0.0 231.2 jit_solution(7086164800588034616)
XLA Ops:
  7.2 1.9 pad_maximum_fusion
  9.2 1.3 fusion.7
  15.0 4.8 %collective-permute-start = (bf16[4,2,128,128]{3,2,1,0:T(8,128)(2,1)S(1)}, bf16[4,2,128,128]{3,2,1,0:T(8,128)(2,1)S(1)}, u32[]{:S(2)}, u32[]{:S(2)}) collective-permute-start(bf16[4,2,128,128]{3,2,1,0:T(8,128)(2,1)S(1)} %pad_maximum_fusion.1), channel_id=1, source_target_pairs={{0,16},{16,0},{32,48},{48,32},{64,80},{80,64},{96,112},{112,96},{1... | collective-permute-start | bytes 786440 | tf_op jit(solution)/shard_map/ppermute | solution.py:221
  19.9 11.0 %collective-permute-start.1 = (bf16[4,2,128,128]{3,2,1,0:T(8,128)(2,1)S(1)}, bf16[4,2,128,128]{3,2,1,0:T(8,128)(2,1)S(1)}, u32[]{:S(2)}, u32[]{:S(2)}) collective-permute-start(bf16[4,2,128,128]{3,2,1,0:T(8,128)(2,1)S(1)} %pad_maximum_fusion.1), channel_id=1, source_target_pairs={{16,32},{32,16},{48,64},{64,48},{80,96},{96,80},{112,128},{128,112... | collective-permute-start | bytes 786440 | tf_op jit(solution)/shard_map/ppermute | solution.py:222
  30.9 1.1 fusion
  32.7 8.3 %all-to-all-start = ((bf16[1,4,16,4,128]{4,3,1,0,2:T(4,128)(2,1)}), bf16[1,4,16,4,128]{4,3,1,0,2:T(4,128)(2,1)S(1)}, u32[]{:S(2)}, u32[]{:S(2)}) async-start(bf16[1,4,16,4,128]{4,3,1,0,2:T(4,128)(2,1)} %copy.64), calls=%async_computation | async-start | bytes 131072 | tf_op jit(solution)/shard_map/all_to_all | solution.py:227
  48.5 1.1 all-to-all-done
  50.3 1.9 collective-permute-start.2
  52.3 1.9 collective-permute-start.3
  54.9 3.2 %collective-permute-done.2 = bf16[2,32,128]{2,1,0:T(8,128)(2,1)S(1)} collective-permute-done((bf16[2,32,128]{2,1,0:T(8,128)(2,1)S(1)}, bf16[2,32,128]{2,1,0:T(8,128)(2,1)S(1)}, u32[]{:S(2)}, u32[]{:S(2)}) %collective-permute-start.2) | collective-permute-done | bytes 16416 | tf_op jit(solution)/shard_map/ppermute | solution.py:261
  58.2 17.4 %all-gather.5.cloned.1.call-done = bf16[64,4,128,128]{3,2,1,0:T(8,128)(2,1)} async-done(((bf16[4,4,128,128]{3,2,1,0:T(8,128)(2,1)}), bf16[64,4,128,128]{3,2,1,0:T(8,128)(2,1)}) %all-gather.5.cloned.1.call-update) | async-done | bytes 8388624 | tf_op jit(solution)/shard_map/all_gather | solution.py:209
  75.7 2.0 shard_map.68.own.solved.rest_1_
  77.7 7.8 %collective-permute-start.4 = (bf16[32,128]{1,0:T(8,128)(2,1)S(1)}, bf16[32,128]{1,0:T(8,128)(2,1)S(1)}, u32[]{:S(2)}, u32[]{:S(2)}) collective-permute-start(bf16[32,128]{1,0:T(8,128)(2,1)S(1)} %shard_map.68.own.solved.rest_1_), channel_id=1, source_target_pairs={{16,32},{32,16},{48,64},{64,48},{80,96},{96,80},{112,128},{128,112... | collective-permute-start | bytes 24584 | tf_op jit(solution)/shard_map/ppermute | solution.py:271
  85.5 1.9 collective-permute-start.5
  87.5 2.5 %collective-permute-done.5.near.solved_mate = bf16[32,128]{1,0:T(8,128)(2,1)S(1)} collective-permute-done((bf16[32,128]{1,0:T(8,128)(2,1)S(1)}, bf16[32,128]{1,0:T(8,128)(2,1)S(1)}, u32[]{:S(2)}, u32[]{:S(2)}) %collective-permute-start.5) | collective-permute-done | bytes 8224 | tf_op jit(solution)/shard_map/ppermute | solution.py:271
  90.5 3.3 %collective-permute-start.6 = (bf16[32,128]{1,0:T(8,128)(2,1)S(1)}, bf16[32,128]{1,0:T(8,128)(2,1)S(1)}, u32[]{:S(2)}, u32[]{:S(2)}) collective-permute-start(bf16[32,128]{1,0:T(8,128)(2,1)S(1)} %shard_map.69.own.solved.rest_2_), channel_id=1, source_target_pairs={{16,32},{32,16},{48,64},{64,48},{80,96},{96,80},{112,128},{128,112... | collective-permute-start | bytes 24584 | tf_op jit(solution)/shard_map/ppermute | solution.py:271
  93.8 1.9 collective-permute-start.7
  95.8 2.5 %collective-permute-done.6.far.solved_mate = bf16[32,128]{1,0:T(8,128)(2,1)S(1)} collective-permute-done((bf16[32,128]{1,0:T(8,128)(2,1)S(1)}, bf16[32,128]{1,0:T(8,128)(2,1)S(1)}, u32[]{:S(2)}, u32[]{:S(2)}) %collective-permute-start.6) | collective-permute-done | bytes 8224 | tf_op jit(solution)/shard_map/ppermute | solution.py:271
  99.2 5.3 %collective-permute-start.8 = (bf16[32,128]{1,0:T(8,128)(2,1)S(1)}, bf16[32,128]{1,0:T(8,128)(2,1)S(1)}, u32[]{:S(2)}, u32[]{:S(2)}) collective-permute-start(bf16[32,128]{1,0:T(8,128)(2,1)S(1)} %shard_map.70.own.solved.rest_3_), channel_id=1, source_target_pairs={{16,32},{32,16},{48,64},{64,48},{80,96},{96,80},{112,128},{128,112... | collective-permute-start | bytes 24584 | tf_op jit(solution)/shard_map/ppermute | solution.py:271
  104.5 1.9 collective-permute-start.9
  107.0 2.4 %collective-permute-done.9.near.solved_mate = bf16[32,128]{1,0:T(8,128)(2,1)S(1)} collective-permute-done((bf16[32,128]{1,0:T(8,128)(2,1)S(1)}, bf16[32,128]{1,0:T(8,128)(2,1)S(1)}, u32[]{:S(2)}, u32[]{:S(2)}) %collective-permute-start.9) | collective-permute-done | bytes 8224 | tf_op jit(solution)/shard_map/ppermute | solution.py:271
  109.9 3.3 %collective-permute-start.10 = (bf16[32,128]{1,0:T(8,128)(2,1)S(1)}, bf16[32,128]{1,0:T(8,128)(2,1)S(1)}, u32[]{:S(2)}, u32[]{:S(2)}) collective-permute-start(bf16[32,128]{1,0:T(8,128)(2,1)S(1)} %shard_map.71.own.solved.rest_4_), channel_id=1, source_target_pairs={{16,32},{32,16},{48,64},{64,48},{80,96},{96,80},{112,128},{128,112... | collective-permute-start | bytes 24584 | tf_op jit(solution)/shard_map/ppermute | solution.py:271
  113.3 1.9 collective-permute-start.11
  115.2 2.5 %collective-permute-done.10.far.solved_mate = bf16[32,128]{1,0:T(8,128)(2,1)S(1)} collective-permute-done((bf16[32,128]{1,0:T(8,128)(2,1)S(1)}, bf16[32,128]{1,0:T(8,128)(2,1)S(1)}, u32[]{:S(2)}, u32[]{:S(2)}) %collective-permute-start.10) | collective-permute-done | bytes 8224 | tf_op jit(solution)/shard_map/ppermute | solution.py:271
  118.7 1.9 collective-permute-start.12
  121.5 1.6 collective-permute-done.12.mate.solved_mate
  123.0 1.8 shard_map.73
  124.9 6.3 %collective-permute-start.13 = (bf16[64,128]{1,0:T(8,128)(2,1)S(1)}, bf16[64,128]{1,0:T(8,128)(2,1)S(1)}, u32[]{:S(2)}, u32[]{:S(2)}) collective-permute-start(bf16[64,128]{1,0:T(8,128)(2,1)S(1)} %get-tuple-element.52), channel_id=1, source_target_pairs={{16,32},{32,16},{48,64},{64,48},{80,96},{96,80},{112,128},{128,112... | collective-permute-start | bytes 49160 | tf_op jit(solution)/shard_map/ppermute | solution.py:271
  131.2 1.5 collective-permute-done.13.came
  132.7 3.4 %copy-done.1 = bf16[64,4,128,128]{3,2,1,0:T(8,128)(2,1)S(1)} copy-done((bf16[64,4,128,128]{3,2,1,0:T(8,128)(2,1)S(1)}, bf16[64,4,128,128]{3,2,1,0:T(8,128)(2,1)}, u32[]{:S(2)}) %copy-start.1) | copy-done | bytes 8388632
  136.9 1.9 collective-permute-start.14
  138.8 2.6 %collective-permute-done.14.came = bf16[64,128]{1,0:T(8,128)(2,1)S(1)} collective-permute-done((bf16[64,128]{1,0:T(8,128)(2,1)S(1)}, bf16[64,128]{1,0:T(8,128)(2,1)S(1)}, u32[]{:S(2)}, u32[]{:S(2)}) %collective-permute-start.14) | collective-permute-done | bytes 16416 | tf_op jit(solution)/shard_map/ppermute | solution.py:271
  141.4 1.3 shard_map.75
  142.7 6.3 %collective-permute-start.15 = (bf16[64,128]{1,0:T(8,128)(2,1)S(1)}, bf16[64,128]{1,0:T(8,128)(2,1)S(1)}, u32[]{:S(2)}, u32[]{:S(2)}) collective-permute-start(bf16[64,128]{1,0:T(8,128)(2,1)S(1)} %get-tuple-element.58), channel_id=1, source_target_pairs={{16,32},{32,16},{48,64},{64,48},{80,96},{96,80},{112,128},{128,112... | collective-permute-start | bytes 49160 | tf_op jit(solution)/shard_map/ppermute | solution.py:271
  149.0 1.5 collective-permute-done.15.came
  151.5 1.9 collective-permute-start.16
  153.4 2.6 %collective-permute-done.16.came = bf16[64,128]{1,0:T(8,128)(2,1)S(1)} collective-permute-done((bf16[64,128]{1,0:T(8,128)(2,1)S(1)}, bf16[64,128]{1,0:T(8,128)(2,1)S(1)}, u32[]{:S(2)}, u32[]{:S(2)}) %collective-permute-start.16) | collective-permute-done | bytes 16416 | tf_op jit(solution)/shard_map/ppermute | solution.py:271
  156.9 6.3 %collective-permute-start.17 = (bf16[64,128]{1,0:T(8,128)(2,1)S(1)}, bf16[64,128]{1,0:T(8,128)(2,1)S(1)}, u32[]{:S(2)}, u32[]{:S(2)}) collective-permute-start(bf16[64,128]{1,0:T(8,128)(2,1)S(1)} %get-tuple-element.62), channel_id=1, source_target_pairs={{16,32},{32,16},{48,64},{64,48},{80,96},{96,80},{112,128},{128,112... | collective-permute-start | bytes 49160 | tf_op jit(solution)/shard_map/ppermute | solution.py:271
  163.3 1.5 collective-permute-done.17.came
  165.7 1.9 collective-permute-start.18
  167.6 2.6 %collective-permute-done.18.came = bf16[64,128]{1,0:T(8,128)(2,1)S(1)} collective-permute-done((bf16[64,128]{1,0:T(8,128)(2,1)S(1)}, bf16[64,128]{1,0:T(8,128)(2,1)S(1)}, u32[]{:S(2)}, u32[]{:S(2)}) %collective-permute-start.18) | collective-permute-done | bytes 16416 | tf_op jit(solution)/shard_map/ppermute | solution.py:271
  171.1 6.3 %collective-permute-start.19 = (bf16[64,128]{1,0:T(8,128)(2,1)S(1)}, bf16[64,128]{1,0:T(8,128)(2,1)S(1)}, u32[]{:S(2)}, u32[]{:S(2)}) collective-permute-start(bf16[64,128]{1,0:T(8,128)(2,1)S(1)} %get-tuple-element.66), channel_id=1, source_target_pairs={{16,32},{32,16},{48,64},{64,48},{80,96},{96,80},{112,128},{128,112... | collective-permute-start | bytes 49160 | tf_op jit(solution)/shard_map/ppermute | solution.py:271
  177.5 1.5 collective-permute-done.19.came
  179.9 1.9 collective-permute-start.20
  181.8 2.6 %collective-permute-done.20.came = bf16[64,128]{1,0:T(8,128)(2,1)S(1)} collective-permute-done((bf16[64,128]{1,0:T(8,128)(2,1)S(1)}, bf16[64,128]{1,0:T(8,128)(2,1)S(1)}, u32[]{:S(2)}, u32[]{:S(2)}) %collective-permute-start.20) | collective-permute-done | bytes 16416 | tf_op jit(solution)/shard_map/ppermute | solution.py:271
  185.4 6.3 %collective-permute-start.21 = (bf16[64,128]{1,0:T(8,128)(2,1)S(1)}, bf16[64,128]{1,0:T(8,128)(2,1)S(1)}, u32[]{:S(2)}, u32[]{:S(2)}) collective-permute-start(bf16[64,128]{1,0:T(8,128)(2,1)S(1)} %get-tuple-element.70), channel_id=1, source_target_pairs={{16,32},{32,16},{48,64},{64,48},{80,96},{96,80},{112,128},{128,112... | collective-permute-start | bytes 49160 | tf_op jit(solution)/shard_map/ppermute | solution.py:271
  191.7 1.5 collective-permute-done.21.came
  193.6 29.4 %all_to_all.20 = bf16[16,32,128]{2,1,0:T(8,128)(2,1)S(1)} all-to-all(bf16[16,32,128]{2,1,0:T(8,128)(2,1)S(1)} %shard_map.82), channel_id=1, replica_groups=mesh['dom'=32,'level'=16] {'level'}, dimensions={0} | all-to-all | bytes 262144 | tf_op jit(solution)/shard_map/all_to_all | solution.py:315
  (83 shorter events, 24.5 us)
Async XLA Ops:
  7.2 68.5 %all-gather.5.cloned.1.call-start = ((), (), s32[]{:S(2)}) async-start(), calls=%async_computation.2 | async-start | bytes 8912896 | tf_op jit(solution)/shard_map/all_gather | solution.py:209
  15.0 39.2 %collective-permute-start = (bf16[4,2,128,128]{3,2,1,0:T(8,128)(2,1)S(1)}, bf16[4,2,128,128]{3,2,1,0:T(8,128)(2,1)S(1)}, u32[]{:S(2)}, u32[]{:S(2)}) collective-permute-start(bf16[4,2,128,128]{3,2,1,0:T(8,128)(2,1)S(1)} %pad_maximum_fusion.1), channel_id=1, source_target_pairs={{0,16},{16,0},{32,48},{48,32},{64,80},{80,64},{96,112},{112,96},{1... | collective-permute-start | bytes 786440 | tf_op jit(solution)/shard_map/ppermute | solution.py:221
  19.9 34.3 %collective-permute-start.1 = (bf16[4,2,128,128]{3,2,1,0:T(8,128)(2,1)S(1)}, bf16[4,2,128,128]{3,2,1,0:T(8,128)(2,1)S(1)}, u32[]{:S(2)}, u32[]{:S(2)}) collective-permute-start(bf16[4,2,128,128]{3,2,1,0:T(8,128)(2,1)S(1)} %pad_maximum_fusion.1), channel_id=1, source_target_pairs={{16,32},{32,16},{48,64},{64,48},{80,96},{96,80},{112,128},{128,112... | collective-permute-start | bytes 786440 | tf_op jit(solution)/shard_map/ppermute | solution.py:222
  32.7 17.0 %all-to-all-start = ((bf16[1,4,16,4,128]{4,3,1,0,2:T(4,128)(2,1)}), bf16[1,4,16,4,128]{4,3,1,0,2:T(4,128)(2,1)S(1)}, u32[]{:S(2)}, u32[]{:S(2)}) async-start(bf16[1,4,16,4,128]{4,3,1,0,2:T(4,128)(2,1)} %copy.64), calls=%async_computation | async-start | bytes 131072 | tf_op jit(solution)/shard_map/all_to_all | solution.py:227
  41.0 80.4 %all-gather.7.cloned.1.call-start = ((), (), s32[]{:S(2)}) async-start(), calls=%async_computation.3 | async-start | bytes 4456448 | tf_op jit(solution)/shard_map/all_gather | solution.py:268
  50.3 7.8 %collective-permute-start.2 = (bf16[2,32,128]{2,1,0:T(8,128)(2,1)S(1)}, bf16[2,32,128]{2,1,0:T(8,128)(2,1)S(1)}, u32[]{:S(2)}, u32[]{:S(2)}) collective-permute-start(bf16[2,32,128]{2,1,0:T(8,128)(2,1)S(1)} %get-tuple-element.98), channel_id=1, source_target_pairs={{16,32},{32,16},{48,64},{64,48},{80,96},{96,80},{112,128},{128,112... | collective-permute-start | bytes 49160 | tf_op jit(solution)/shard_map/ppermute | solution.py:261
  52.3 5.9 %collective-permute-start.3 = (bf16[2,32,128]{2,1,0:T(8,128)(2,1)S(1)}, bf16[2,32,128]{2,1,0:T(8,128)(2,1)S(1)}, u32[]{:S(2)}, u32[]{:S(2)}) collective-permute-start(bf16[2,32,128]{2,1,0:T(8,128)(2,1)S(1)} %get-tuple-element.97), channel_id=1, source_target_pairs={{0,16},{16,0},{32,48},{48,32},{64,80},{80,64},{96,112},{112,96},{1... | collective-permute-start | bytes 49160 | tf_op jit(solution)/shard_map/ppermute | solution.py:262
  75.7 14.2 %copy-start = (bf16[64,4,128,128]{3,2,1,0:T(8,128)(2,1)S(1)}, bf16[64,4,128,128]{3,2,1,0:T(8,128)(2,1)}, u32[]{:S(2)}) copy-start(bf16[64,4,128,128]{3,2,1,0:T(8,128)(2,1)} %all-gather.5.cloned.1.call-done) | copy-start | bytes 25165828
  77.7 9.8 %collective-permute-start.4 = (bf16[32,128]{1,0:T(8,128)(2,1)S(1)}, bf16[32,128]{1,0:T(8,128)(2,1)S(1)}, u32[]{:S(2)}, u32[]{:S(2)}) collective-permute-start(bf16[32,128]{1,0:T(8,128)(2,1)S(1)} %shard_map.68.own.solved.rest_1_), channel_id=1, source_target_pairs={{16,32},{32,16},{48,64},{64,48},{80,96},{96,80},{112,128},{128,112... | collective-permute-start | bytes 24584 | tf_op jit(solution)/shard_map/ppermute | solution.py:271
  85.5 4.4 %collective-permute-start.5 = (bf16[32,128]{1,0:T(8,128)(2,1)S(1)}, bf16[32,128]{1,0:T(8,128)(2,1)S(1)}, u32[]{:S(2)}, u32[]{:S(2)}) collective-permute-start(bf16[32,128]{1,0:T(8,128)(2,1)S(1)} %shard_map.68.own.solved.rest_1_), channel_id=1, source_target_pairs={{0,16},{16,0},{32,48},{48,32},{64,80},{80,64},{96,112},{112,96},{1... | collective-permute-start | bytes 24584 | tf_op jit(solution)/shard_map/ppermute | solution.py:271
  90.5 7.7 %collective-permute-start.6 = (bf16[32,128]{1,0:T(8,128)(2,1)S(1)}, bf16[32,128]{1,0:T(8,128)(2,1)S(1)}, u32[]{:S(2)}, u32[]{:S(2)}) collective-permute-start(bf16[32,128]{1,0:T(8,128)(2,1)S(1)} %shard_map.69.own.solved.rest_2_), channel_id=1, source_target_pairs={{16,32},{32,16},{48,64},{64,48},{80,96},{96,80},{112,128},{128,112... | collective-permute-start | bytes 24584 | tf_op jit(solution)/shard_map/ppermute | solution.py:271
  93.8 4.8 %collective-permute-start.7 = (bf16[32,128]{1,0:T(8,128)(2,1)S(1)}, bf16[32,128]{1,0:T(8,128)(2,1)S(1)}, u32[]{:S(2)}, u32[]{:S(2)}) collective-permute-start(bf16[32,128]{1,0:T(8,128)(2,1)S(1)} %shard_map.69.own.solved.rest_2_), channel_id=1, source_target_pairs={{0,16},{16,0},{32,48},{48,32},{64,80},{80,64},{96,112},{112,96},{1... | collective-permute-start | bytes 24584 | tf_op jit(solution)/shard_map/ppermute | solution.py:271
  99.2 7.7 %collective-permute-start.8 = (bf16[32,128]{1,0:T(8,128)(2,1)S(1)}, bf16[32,128]{1,0:T(8,128)(2,1)S(1)}, u32[]{:S(2)}, u32[]{:S(2)}) collective-permute-start(bf16[32,128]{1,0:T(8,128)(2,1)S(1)} %shard_map.70.own.solved.rest_3_), channel_id=1, source_target_pairs={{16,32},{32,16},{48,64},{64,48},{80,96},{96,80},{112,128},{128,112... | collective-permute-start | bytes 24584 | tf_op jit(solution)/shard_map/ppermute | solution.py:271
  104.5 4.8 %collective-permute-start.9 = (bf16[32,128]{1,0:T(8,128)(2,1)S(1)}, bf16[32,128]{1,0:T(8,128)(2,1)S(1)}, u32[]{:S(2)}, u32[]{:S(2)}) collective-permute-start(bf16[32,128]{1,0:T(8,128)(2,1)S(1)} %shard_map.70.own.solved.rest_3_), channel_id=1, source_target_pairs={{0,16},{16,0},{32,48},{48,32},{64,80},{80,64},{96,112},{112,96},{1... | collective-permute-start | bytes 24584 | tf_op jit(solution)/shard_map/ppermute | solution.py:271
  109.9 7.7 %collective-permute-start.10 = (bf16[32,128]{1,0:T(8,128)(2,1)S(1)}, bf16[32,128]{1,0:T(8,128)(2,1)S(1)}, u32[]{:S(2)}, u32[]{:S(2)}) collective-permute-start(bf16[32,128]{1,0:T(8,128)(2,1)S(1)} %shard_map.71.own.solved.rest_4_), channel_id=1, source_target_pairs={{16,32},{32,16},{48,64},{64,48},{80,96},{96,80},{112,128},{128,112... | collective-permute-start | bytes 24584 | tf_op jit(solution)/shard_map/ppermute | solution.py:271
  113.3 4.8 %collective-permute-start.11 = (bf16[32,128]{1,0:T(8,128)(2,1)S(1)}, bf16[32,128]{1,0:T(8,128)(2,1)S(1)}, u32[]{:S(2)}, u32[]{:S(2)}) collective-permute-start(bf16[32,128]{1,0:T(8,128)(2,1)S(1)} %shard_map.71.own.solved.rest_4_), channel_id=1, source_target_pairs={{0,16},{16,0},{32,48},{48,32},{64,80},{80,64},{96,112},{112,96},{1... | collective-permute-start | bytes 24584 | tf_op jit(solution)/shard_map/ppermute | solution.py:271
  118.7 4.4 %collective-permute-start.12 = (bf16[32,128]{1,0:T(8,128)(2,1)S(1)}, bf16[32,128]{1,0:T(8,128)(2,1)S(1)}, u32[]{:S(2)}, u32[]{:S(2)}) collective-permute-start(bf16[32,128]{1,0:T(8,128)(2,1)S(1)} %shard_map.72.own.solved.rest_5_), channel_id=1, source_target_pairs={{0,16},{16,0},{32,48},{48,32},{64,80},{80,64},{96,112},{112,96},{1... | collective-permute-start | bytes 24584 | tf_op jit(solution)/shard_map/ppermute | solution.py:271
  121.5 11.2 %copy-start.2 = (bf16[64,2,128,128]{3,2,1,0:T(8,128)(2,1)S(1)}, bf16[64,2,128,128]{3,2,1,0:T(8,128)(2,1)}, u32[]{:S(2)}) copy-start(bf16[64,2,128,128]{3,2,1,0:T(8,128)(2,1)} %all-gather.7.cloned.1.call-done) | copy-start | bytes 12582916
  124.9 7.8 %collective-permute-start.13 = (bf16[64,128]{1,0:T(8,128)(2,1)S(1)}, bf16[64,128]{1,0:T(8,128)(2,1)S(1)}, u32[]{:S(2)}, u32[]{:S(2)}) collective-permute-start(bf16[64,128]{1,0:T(8,128)(2,1)S(1)} %get-tuple-element.52), channel_id=1, source_target_pairs={{16,32},{32,16},{48,64},{64,48},{80,96},{96,80},{112,128},{128,112... | collective-permute-start | bytes 49160 | tf_op jit(solution)/shard_map/ppermute | solution.py:271
  132.7 3.4 %copy-start.1 = (bf16[64,4,128,128]{3,2,1,0:T(8,128)(2,1)S(1)}, bf16[64,4,128,128]{3,2,1,0:T(8,128)(2,1)}, u32[]{:S(2)}) copy-start(bf16[64,4,128,128]{3,2,1,0:T(8,128)(2,1)} %all-gather.5.cloned.1.call-done) | copy-start | bytes 25165828
  136.9 4.5 %collective-permute-start.14 = (bf16[64,128]{1,0:T(8,128)(2,1)S(1)}, bf16[64,128]{1,0:T(8,128)(2,1)S(1)}, u32[]{:S(2)}, u32[]{:S(2)}) collective-permute-start(bf16[64,128]{1,0:T(8,128)(2,1)S(1)} %get-tuple-element.56), channel_id=1, source_target_pairs={{0,16},{16,0},{32,48},{48,32},{64,80},{80,64},{96,112},{112,96},{1... | collective-permute-start | bytes 49160 | tf_op jit(solution)/shard_map/ppermute | solution.py:271
  142.7 7.8 %collective-permute-start.15 = (bf16[64,128]{1,0:T(8,128)(2,1)S(1)}, bf16[64,128]{1,0:T(8,128)(2,1)S(1)}, u32[]{:S(2)}, u32[]{:S(2)}) collective-permute-start(bf16[64,128]{1,0:T(8,128)(2,1)S(1)} %get-tuple-element.58), channel_id=1, source_target_pairs={{16,32},{32,16},{48,64},{64,48},{80,96},{96,80},{112,128},{128,112... | collective-permute-start | bytes 49160 | tf_op jit(solution)/shard_map/ppermute | solution.py:271
  151.5 4.5 %collective-permute-start.16 = (bf16[64,128]{1,0:T(8,128)(2,1)S(1)}, bf16[64,128]{1,0:T(8,128)(2,1)S(1)}, u32[]{:S(2)}, u32[]{:S(2)}) collective-permute-start(bf16[64,128]{1,0:T(8,128)(2,1)S(1)} %get-tuple-element.60), channel_id=1, source_target_pairs={{0,16},{16,0},{32,48},{48,32},{64,80},{80,64},{96,112},{112,96},{1... | collective-permute-start | bytes 49160 | tf_op jit(solution)/shard_map/ppermute | solution.py:271
  156.9 7.8 %collective-permute-start.17 = (bf16[64,128]{1,0:T(8,128)(2,1)S(1)}, bf16[64,128]{1,0:T(8,128)(2,1)S(1)}, u32[]{:S(2)}, u32[]{:S(2)}) collective-permute-start(bf16[64,128]{1,0:T(8,128)(2,1)S(1)} %get-tuple-element.62), channel_id=1, source_target_pairs={{16,32},{32,16},{48,64},{64,48},{80,96},{96,80},{112,128},{128,112... | collective-permute-start | bytes 49160 | tf_op jit(solution)/shard_map/ppermute | solution.py:271
  165.7 4.5 %collective-permute-start.18 = (bf16[64,128]{1,0:T(8,128)(2,1)S(1)}, bf16[64,128]{1,0:T(8,128)(2,1)S(1)}, u32[]{:S(2)}, u32[]{:S(2)}) collective-permute-start(bf16[64,128]{1,0:T(8,128)(2,1)S(1)} %get-tuple-element.64), channel_id=1, source_target_pairs={{0,16},{16,0},{32,48},{48,32},{64,80},{80,64},{96,112},{112,96},{1... | collective-permute-start | bytes 49160 | tf_op jit(solution)/shard_map/ppermute | solution.py:271
  171.1 7.8 %collective-permute-start.19 = (bf16[64,128]{1,0:T(8,128)(2,1)S(1)}, bf16[64,128]{1,0:T(8,128)(2,1)S(1)}, u32[]{:S(2)}, u32[]{:S(2)}) collective-permute-start(bf16[64,128]{1,0:T(8,128)(2,1)S(1)} %get-tuple-element.66), channel_id=1, source_target_pairs={{16,32},{32,16},{48,64},{64,48},{80,96},{96,80},{112,128},{128,112... | collective-permute-start | bytes 49160 | tf_op jit(solution)/shard_map/ppermute | solution.py:271
  179.9 4.5 %collective-permute-start.20 = (bf16[64,128]{1,0:T(8,128)(2,1)S(1)}, bf16[64,128]{1,0:T(8,128)(2,1)S(1)}, u32[]{:S(2)}, u32[]{:S(2)}) collective-permute-start(bf16[64,128]{1,0:T(8,128)(2,1)S(1)} %get-tuple-element.68), channel_id=1, source_target_pairs={{0,16},{16,0},{32,48},{48,32},{64,80},{80,64},{96,112},{112,96},{1... | collective-permute-start | bytes 49160 | tf_op jit(solution)/shard_map/ppermute | solution.py:271
  185.4 7.8 %collective-permute-start.21 = (bf16[64,128]{1,0:T(8,128)(2,1)S(1)}, bf16[64,128]{1,0:T(8,128)(2,1)S(1)}, u32[]{:S(2)}, u32[]{:S(2)}) collective-permute-start(bf16[64,128]{1,0:T(8,128)(2,1)S(1)} %get-tuple-element.70), channel_id=1, source_target_pairs={{16,32},{32,16},{48,64},{64,48},{80,96},{96,80},{112,128},{128,112... | collective-permute-start | bytes 49160 | tf_op jit(solution)/shard_map/ppermute | solution.py:271
Sparse Core Ops, SparseCore 0:
  10.1 65.5 all-gather.4
  77.8 43.6 all-gather.6

commit v10 on v9

--- a/solution.py
+++ b/solution.py
@@ -293,7 +293,7 @@
         pltpu.VMEM((3, 2, rows, 1, width, width), BF16),
         pltpu.SemaphoreType.DMA((3, 2)),
     ]
-    cost = pl.CostEstimate(flops=0, transcendentals=0, bytes_accessed=3 * weights.size)
+    cost = pl.CostEstimate(flops=0, transcendentals=0, bytes_accessed=12 * weights.size)
     held, sent = call(kernel, sums, *args, fetched=2, scratch=scratch, cost=cost)
     for level in range(paired, levels):
         kernel = functools.partial(forward_pair_kernel, level, share, level == levels - 1)

time: 232 us -> 232 us (level)
  no operation moved by 1% of the time
where the time goes in v10:
time: 232 us; the launch traced here: 231 us
  starting transfers between devices  96.9 us (42%)
  waiting for transfers between devices  52.8 us (23%)
  blocking collectives  29.4 us (13%)
  between operations  17.1 us (7%)
  Pallas kernels  14.5 us (6%)
  local copies, waits for them, and re-layouts  11.4 us (5%)
  other arithmetic  7.91 us (3%)
    ppermute x18, starting transfers between devices, swap(): lax.ppermute(vector, 'dom', far_pairs if level % 2 == 0 else near_pairs)  68.8 us
    ppermute x18, waiting for transfers between devices, swap(): lax.ppermute(vector, 'dom', far_pairs if level % 2 == 0 else near_pairs)  30.1 us
    all_to_all x1, blocking collectives, local(): dealt = lax.all_to_all(dealt, 'level', 0, 0, tiled=False)  29.4 us
    all_gather x1, waiting for transfers between devices, local(): weights = lax.all_gather(weights, 'level')  17.4 us
    pallas_call x15, Pallas kernels, call(): pl.pallas_call(kernel, out_shape=outs, in_specs=specs, out_specs=[pl.Bloc...  14.5 us
    ppermute x1, starting transfers between devices, local(): by_far = lax.ppermute(mates, 'dom', far_pairs)  11 us
    all_to_all x1, starting transfers between devices, local(): side = lax.all_to_all(side, 'level', 1, 0, tiled=False)  8.35 us
    ppermute x1, starting transfers between devices, local(): by_near = lax.ppermute(mates, 'dom', near_pairs)  4.83 us
  transfers between devices with their start and end apart: 25, of which 21 were waited for; matrix products, arithmetic and copies ran while one was open for 6% of the time, Pallas kernels for 2%

profile of v10, /device:TPU:1, one launch (start us, length us, event | category | flops | bytes accessed | tf_op | source)
XLA Modules:
  0.0 231.2 jit_solution(7086164800588034616)
XLA Ops:
  7.2 1.9 pad_maximum_fusion
  9.2 1.3 fusion.7
  15.0 4.8 %collective-permute-start = (bf16[4,2,128,128]{3,2,1,0:T(8,128)(2,1)S(1)}, bf16[4,2,128,128]{3,2,1,0:T(8,128)(2,1)S(1)}, u32[]{:S(2)}, u32[]{:S(2)}) collective-permute-start(bf16[4,2,128,128]{3,2,1,0:T(8,128)(2,1)S(1)} %pad_maximum_fusion.1), channel_id=1, source_target_pairs={{0,16},{16,0},{32,48},{48,32},{64,80},{80,64},{96,112},{112,96},{1... | collective-permute-start | bytes 786440 | tf_op jit(solution)/shard_map/ppermute | solution.py:221
  19.9 11.0 %collective-permute-start.1 = (bf16[4,2,128,128]{3,2,1,0:T(8,128)(2,1)S(1)}, bf16[4,2,128,128]{3,2,1,0:T(8,128)(2,1)S(1)}, u32[]{:S(2)}, u32[]{:S(2)}) collective-permute-start(bf16[4,2,128,128]{3,2,1,0:T(8,128)(2,1)S(1)} %pad_maximum_fusion.1), channel_id=1, source_target_pairs={{16,32},{32,16},{48,64},{64,48},{80,96},{96,80},{112,128},{128,112... | collective-permute-start | bytes 786440 | tf_op jit(solution)/shard_map/ppermute | solution.py:222
  30.9 1.1 fusion
  32.7 8.3 %all-to-all-start = ((bf16[1,4,16,4,128]{4,3,1,0,2:T(4,128)(2,1)}), bf16[1,4,16,4,128]{4,3,1,0,2:T(4,128)(2,1)S(1)}, u32[]{:S(2)}, u32[]{:S(2)}) async-start(bf16[1,4,16,4,128]{4,3,1,0,2:T(4,128)(2,1)} %copy.64), calls=%async_computation | async-start | bytes 131072 | tf_op jit(solution)/shard_map/all_to_all | solution.py:227
  48.5 1.1 all-to-all-done
  50.3 1.9 collective-permute-start.2
  52.3 1.9 collective-permute-start.3
  54.9 3.2 %collective-permute-done.2 = bf16[2,32,128]{2,1,0:T(8,128)(2,1)S(1)} collective-permute-done((bf16[2,32,128]{2,1,0:T(8,128)(2,1)S(1)}, bf16[2,32,128]{2,1,0:T(8,128)(2,1)S(1)}, u32[]{:S(2)}, u32[]{:S(2)}) %collective-permute-start.2) | collective-permute-done | bytes 16416 | tf_op jit(solution)/shard_map/ppermute | solution.py:261
  58.2 17.4 %all-gather.5.cloned.1.call-done = bf16[64,4,128,128]{3,2,1,0:T(8,128)(2,1)} async-done(((bf16[4,4,128,128]{3,2,1,0:T(8,128)(2,1)}), bf16[64,4,128,128]{3,2,1,0:T(8,128)(2,1)}) %all-gather.5.cloned.1.call-update) | async-done | bytes 8388624 | tf_op jit(solution)/shard_map/all_gather | solution.py:209
  75.7 2.0 shard_map.68.own.solved.rest_1_
  77.7 7.8 %collective-permute-start.4 = (bf16[32,128]{1,0:T(8,128)(2,1)S(1)}, bf16[32,128]{1,0:T(8,128)(2,1)S(1)}, u32[]{:S(2)}, u32[]{:S(2)}) collective-permute-start(bf16[32,128]{1,0:T(8,128)(2,1)S(1)} %shard_map.68.own.solved.rest_1_), channel_id=1, source_target_pairs={{16,32},{32,16},{48,64},{64,48},{80,96},{96,80},{112,128},{128,112... | collective-permute-start | bytes 24584 | tf_op jit(solution)/shard_map/ppermute | solution.py:271
  85.5 1.9 collective-permute-start.5
  87.5 2.5 %collective-permute-done.5.near.solved_mate = bf16[32,128]{1,0:T(8,128)(2,1)S(1)} collective-permute-done((bf16[32,128]{1,0:T(8,128)(2,1)S(1)}, bf16[32,128]{1,0:T(8,128)(2,1)S(1)}, u32[]{:S(2)}, u32[]{:S(2)}) %collective-permute-start.5) | collective-permute-done | bytes 8224 | tf_op jit(solution)/shard_map/ppermute | solution.py:271
  90.5 3.3 %collective-permute-start.6 = (bf16[32,128]{1,0:T(8,128)(2,1)S(1)}, bf16[32,128]{1,0:T(8,128)(2,1)S(1)}, u32[]{:S(2)}, u32[]{:S(2)}) collective-permute-start(bf16[32,128]{1,0:T(8,128)(2,1)S(1)} %shard_map.69.own.solved.rest_2_), channel_id=1, source_target_pairs={{16,32},{32,16},{48,64},{64,48},{80,96},{96,80},{112,128},{128,112... | collective-permute-start | bytes 24584 | tf_op jit(solution)/shard_map/ppermute | solution.py:271
  93.8 1.9 collective-permute-start.7
  95.8 2.5 %collective-permute-done.6.far.solved_mate = bf16[32,128]{1,0:T(8,128)(2,1)S(1)} collective-permute-done((bf16[32,128]{1,0:T(8,128)(2,1)S(1)}, bf16[32,128]{1,0:T(8,128)(2,1)S(1)}, u32[]{:S(2)}, u32[]{:S(2)}) %collective-permute-start.6) | collective-permute-done | bytes 8224 | tf_op jit(solution)/shard_map/ppermute | solution.py:271
  99.2 5.3 %collective-permute-start.8 = (bf16[32,128]{1,0:T(8,128)(2,1)S(1)}, bf16[32,128]{1,0:T(8,128)(2,1)S(1)}, u32[]{:S(2)}, u32[]{:S(2)}) collective-permute-start(bf16[32,128]{1,0:T(8,128)(2,1)S(1)} %shard_map.70.own.solved.rest_3_), channel_id=1, source_target_pairs={{16,32},{32,16},{48,64},{64,48},{80,96},{96,80},{112,128},{128,112... | collective-permute-start | bytes 24584 | tf_op jit(solution)/shard_map/ppermute | solution.py:271
  104.5 1.9 collective-permute-start.9
  107.0 2.4 %collective-permute-done.9.near.solved_mate = bf16[32,128]{1,0:T(8,128)(2,1)S(1)} collective-permute-done((bf16[32,128]{1,0:T(8,128)(2,1)S(1)}, bf16[32,128]{1,0:T(8,128)(2,1)S(1)}, u32[]{:S(2)}, u32[]{:S(2)}) %collective-permute-start.9) | collective-permute-done | bytes 8224 | tf_op jit(solution)/shard_map/ppermute | solution.py:271
  109.9 3.3 %collective-permute-start.10 = (bf16[32,128]{1,0:T(8,128)(2,1)S(1)}, bf16[32,128]{1,0:T(8,128)(2,1)S(1)}, u32[]{:S(2)}, u32[]{:S(2)}) collective-permute-start(bf16[32,128]{1,0:T(8,128)(2,1)S(1)} %shard_map.71.own.solved.rest_4_), channel_id=1, source_target_pairs={{16,32},{32,16},{48,64},{64,48},{80,96},{96,80},{112,128},{128,112... | collective-permute-start | bytes 24584 | tf_op jit(solution)/shard_map/ppermute | solution.py:271
  113.3 1.9 collective-permute-start.11
  115.2 2.5 %collective-permute-done.10.far.solved_mate = bf16[32,128]{1,0:T(8,128)(2,1)S(1)} collective-permute-done((bf16[32,128]{1,0:T(8,128)(2,1)S(1)}, bf16[32,128]{1,0:T(8,128)(2,1)S(1)}, u32[]{:S(2)}, u32[]{:S(2)}) %collective-permute-start.10) | collective-permute-done | bytes 8224 | tf_op jit(solution)/shard_map/ppermute | solution.py:271
  118.7 1.9 collective-permute-start.12
  121.5 1.6 collective-permute-done.12.mate.solved_mate
  123.0 1.8 shard_map.73
  124.9 6.3 %collective-permute-start.13 = (bf16[64,128]{1,0:T(8,128)(2,1)S(1)}, bf16[64,128]{1,0:T(8,128)(2,1)S(1)}, u32[]{:S(2)}, u32[]{:S(2)}) collective-permute-start(bf16[64,128]{1,0:T(8,128)(2,1)S(1)} %get-tuple-element.52), channel_id=1, source_target_pairs={{16,32},{32,16},{48,64},{64,48},{80,96},{96,80},{112,128},{128,112... | collective-permute-start | bytes 49160 | tf_op jit(solution)/shard_map/ppermute | solution.py:271
  131.2 1.5 collective-permute-done.13.came
  132.7 3.4 %copy-done.1 = bf16[64,4,128,128]{3,2,1,0:T(8,128)(2,1)S(1)} copy-done((bf16[64,4,128,128]{3,2,1,0:T(8,128)(2,1)S(1)}, bf16[64,4,128,128]{3,2,1,0:T(8,128)(2,1)}, u32[]{:S(2)}) %copy-start.1) | copy-done | bytes 8388632
  136.9 1.9 collective-permute-start.14
  138.8 2.6 %collective-permute-done.14.came = bf16[64,128]{1,0:T(8,128)(2,1)S(1)} collective-permute-done((bf16[64,128]{1,0:T(8,128)(2,1)S(1)}, bf16[64,128]{1,0:T(8,128)(2,1)S(1)}, u32[]{:S(2)}, u32[]{:S(2)}) %collective-permute-start.14) | collective-permute-done | bytes 16416 | tf_op jit(solution)/shard_map/ppermute | solution.py:271
  141.4 1.3 shard_map.75
  142.7 6.3 %collective-permute-start.15 = (bf16[64,128]{1,0:T(8,128)(2,1)S(1)}, bf16[64,128]{1,0:T(8,128)(2,1)S(1)}, u32[]{:S(2)}, u32[]{:S(2)}) collective-permute-start(bf16[64,128]{1,0:T(8,128)(2,1)S(1)} %get-tuple-element.58), channel_id=1, source_target_pairs={{16,32},{32,16},{48,64},{64,48},{80,96},{96,80},{112,128},{128,112... | collective-permute-start | bytes 49160 | tf_op jit(solution)/shard_map/ppermute | solution.py:271
  149.0 1.5 collective-permute-done.15.came
  151.5 1.9 collective-permute-start.16
  153.4 2.6 %collective-permute-done.16.came = bf16[64,128]{1,0:T(8,128)(2,1)S(1)} collective-permute-done((bf16[64,128]{1,0:T(8,128)(2,1)S(1)}, bf16[64,128]{1,0:T(8,128)(2,1)S(1)}, u32[]{:S(2)}, u32[]{:S(2)}) %collective-permute-start.16) | collective-permute-done | bytes 16416 | tf_op jit(solution)/shard_map/ppermute | solution.py:271
  156.9 6.3 %collective-permute-start.17 = (bf16[64,128]{1,0:T(8,128)(2,1)S(1)}, bf16[64,128]{1,0:T(8,128)(2,1)S(1)}, u32[]{:S(2)}, u32[]{:S(2)}) collective-permute-start(bf16[64,128]{1,0:T(8,128)(2,1)S(1)} %get-tuple-element.62), channel_id=1, source_target_pairs={{16,32},{32,16},{48,64},{64,48},{80,96},{96,80},{112,128},{128,112... | collective-permute-start | bytes 49160 | tf_op jit(solution)/shard_map/ppermute | solution.py:271
  163.3 1.5 collective-permute-done.17.came
  165.7 1.9 collective-permute-start.18
  167.6 2.6 %collective-permute-done.18.came = bf16[64,128]{1,0:T(8,128)(2,1)S(1)} collective-permute-done((bf16[64,128]{1,0:T(8,128)(2,1)S(1)}, bf16[64,128]{1,0:T(8,128)(2,1)S(1)}, u32[]{:S(2)}, u32[]{:S(2)}) %collective-permute-start.18) | collective-permute-done | bytes 16416 | tf_op jit(solution)/shard_map/ppermute | solution.py:271
  171.1 6.3 %collective-permute-start.19 = (bf16[64,128]{1,0:T(8,128)(2,1)S(1)}, bf16[64,128]{1,0:T(8,128)(2,1)S(1)}, u32[]{:S(2)}, u32[]{:S(2)}) collective-permute-start(bf16[64,128]{1,0:T(8,128)(2,1)S(1)} %get-tuple-element.66), channel_id=1, source_target_pairs={{16,32},{32,16},{48,64},{64,48},{80,96},{96,80},{112,128},{128,112... | collective-permute-start | bytes 49160 | tf_op jit(solution)/shard_map/ppermute | solution.py:271
  177.5 1.5 collective-permute-done.19.came
  179.9 1.9 collective-permute-start.20
  181.8 2.6 %collective-permute-done.20.came = bf16[64,128]{1,0:T(8,128)(2,1)S(1)} collective-permute-done((bf16[64,128]{1,0:T(8,128)(2,1)S(1)}, bf16[64,128]{1,0:T(8,128)(2,1)S(1)}, u32[]{:S(2)}, u32[]{:S(2)}) %collective-permute-start.20) | collective-permute-done | bytes 16416 | tf_op jit(solution)/shard_map/ppermute | solution.py:271
  185.4 6.3 %collective-permute-start.21 = (bf16[64,128]{1,0:T(8,128)(2,1)S(1)}, bf16[64,128]{1,0:T(8,128)(2,1)S(1)}, u32[]{:S(2)}, u32[]{:S(2)}) collective-permute-start(bf16[64,128]{1,0:T(8,128)(2,1)S(1)} %get-tuple-element.70), channel_id=1, source_target_pairs={{16,32},{32,16},{48,64},{64,48},{80,96},{96,80},{112,128},{128,112... | collective-permute-start | bytes 49160 | tf_op jit(solution)/shard_map/ppermute | solution.py:271
  191.7 1.5 collective-permute-done.21.came
  193.6 29.4 %all_to_all.20 = bf16[16,32,128]{2,1,0:T(8,128)(2,1)S(1)} all-to-all(bf16[16,32,128]{2,1,0:T(8,128)(2,1)S(1)} %shard_map.82), channel_id=1, replica_groups=mesh['dom'=32,'level'=16] {'level'}, dimensions={0} | all-to-all | bytes 262144 | tf_op jit(solution)/shard_map/all_to_all | solution.py:315
  (83 shorter events, 24.5 us)
Async XLA Ops:
  7.2 68.5 %all-gather.5.cloned.1.call-start = ((), (), s32[]{:S(2)}) async-start(), calls=%async_computation.2 | async-start | bytes 8912896 | tf_op jit(solution)/shard_map/all_gather | solution.py:209
  15.0 39.2 %collective-permute-start = (bf16[4,2,128,128]{3,2,1,0:T(8,128)(2,1)S(1)}, bf16[4,2,128,128]{3,2,1,0:T(8,128)(2,1)S(1)}, u32[]{:S(2)}, u32[]{:S(2)}) collective-permute-start(bf16[4,2,128,128]{3,2,1,0:T(8,128)(2,1)S(1)} %pad_maximum_fusion.1), channel_id=1, source_target_pairs={{0,16},{16,0},{32,48},{48,32},{64,80},{80,64},{96,112},{112,96},{1... | collective-permute-start | bytes 786440 | tf_op jit(solution)/shard_map/ppermute | solution.py:221
  19.9 34.3 %collective-permute-start.1 = (bf16[4,2,128,128]{3,2,1,0:T(8,128)(2,1)S(1)}, bf16[4,2,128,128]{3,2,1,0:T(8,128)(2,1)S(1)}, u32[]{:S(2)}, u32[]{:S(2)}) collective-permute-start(bf16[4,2,128,128]{3,2,1,0:T(8,128)(2,1)S(1)} %pad_maximum_fusion.1), channel_id=1, source_target_pairs={{16,32},{32,16},{48,64},{64,48},{80,96},{96,80},{112,128},{128,112... | collective-permute-start | bytes 786440 | tf_op jit(solution)/shard_map/ppermute | solution.py:222
  32.7 17.0 %all-to-all-start = ((bf16[1,4,16,4,128]{4,3,1,0,2:T(4,128)(2,1)}), bf16[1,4,16,4,128]{4,3,1,0,2:T(4,128)(2,1)S(1)}, u32[]{:S(2)}, u32[]{:S(2)}) async-start(bf16[1,4,16,4,128]{4,3,1,0,2:T(4,128)(2,1)} %copy.64), calls=%async_computation | async-start | bytes 131072 | tf_op jit(solution)/shard_map/all_to_all | solution.py:227
  41.0 80.4 %all-gather.7.cloned.1.call-start = ((), (), s32[]{:S(2)}) async-start(), calls=%async_computation.3 | async-start | bytes 4456448 | tf_op jit(solution)/shard_map/all_gather | solution.py:268
  50.3 7.8 %collective-permute-start.2 = (bf16[2,32,128]{2,1,0:T(8,128)(2,1)S(1)}, bf16[2,32,128]{2,1,0:T(8,128)(2,1)S(1)}, u32[]{:S(2)}, u32[]{:S(2)}) collective-permute-start(bf16[2,32,128]{2,1,0:T(8,128)(2,1)S(1)} %get-tuple-element.98), channel_id=1, source_target_pairs={{16,32},{32,16},{48,64},{64,48},{80,96},{96,80},{112,128},{128,112... | collective-permute-start | bytes 49160 | tf_op jit(solution)/shard_map/ppermute | solution.py:261
  52.3 5.9 %collective-permute-start.3 = (bf16[2,32,128]{2,1,0:T(8,128)(2,1)S(1)}, bf16[2,32,128]{2,1,0:T(8,128)(2,1)S(1)}, u32[]{:S(2)}, u32[]{:S(2)}) collective-permute-start(bf16[2,32,128]{2,1,0:T(8,128)(2,1)S(1)} %get-tuple-element.97), channel_id=1, source_target_pairs={{0,16},{16,0},{32,48},{48,32},{64,80},{80,64},{96,112},{112,96},{1... | collective-permute-start | bytes 49160 | tf_op jit(solution)/shard_map/ppermute | solution.py:262
  75.7 14.2 %copy-start = (bf16[64,4,128,128]{3,2,1,0:T(8,128)(2,1)S(1)}, bf16[64,4,128,128]{3,2,1,0:T(8,128)(2,1)}, u32[]{:S(2)}) copy-start(bf16[64,4,128,128]{3,2,1,0:T(8,128)(2,1)} %all-gather.5.cloned.1.call-done) | copy-start | bytes 25165828
  77.7 9.8 %collective-permute-start.4 = (bf16[32,128]{1,0:T(8,128)(2,1)S(1)}, bf16[32,128]{1,0:T(8,128)(2,1)S(1)}, u32[]{:S(2)}, u32[]{:S(2)}) collective-permute-start(bf16[32,128]{1,0:T(8,128)(2,1)S(1)} %shard_map.68.own.solved.rest_1_), channel_id=1, source_target_pairs={{16,32},{32,16},{48,64},{64,48},{80,96},{96,80},{112,128},{128,112... | collective-permute-start | bytes 24584 | tf_op jit(solution)/shard_map/ppermute | solution.py:271
  85.5 4.4 %collective-permute-start.5 = (bf16[32,128]{1,0:T(8,128)(2,1)S(1)}, bf16[32,128]{1,0:T(8,128)(2,1)S(1)}, u32[]{:S(2)}, u32[]{:S(2)}) collective-permute-start(bf16[32,128]{1,0:T(8,128)(2,1)S(1)} %shard_map.68.own.solved.rest_1_), channel_id=1, source_target_pairs={{0,16},{16,0},{32,48},{48,32},{64,80},{80,64},{96,112},{112,96},{1... | collective-permute-start | bytes 24584 | tf_op jit(solution)/shard_map/ppermute | solution.py:271
  90.5 7.7 %collective-permute-start.6 = (bf16[32,128]{1,0:T(8,128)(2,1)S(1)}, bf16[32,128]{1,0:T(8,128)(2,1)S(1)}, u32[]{:S(2)}, u32[]{:S(2)}) collective-permute-start(bf16[32,128]{1,0:T(8,128)(2,1)S(1)} %shard_map.69.own.solved.rest_2_), channel_id=1, source_target_pairs={{16,32},{32,16},{48,64},{64,48},{80,96},{96,80},{112,128},{128,112... | collective-permute-start | bytes 24584 | tf_op jit(solution)/shard_map/ppermute | solution.py:271
  93.8 4.8 %collective-permute-start.7 = (bf16[32,128]{1,0:T(8,128)(2,1)S(1)}, bf16[32,128]{1,0:T(8,128)(2,1)S(1)}, u32[]{:S(2)}, u32[]{:S(2)}) collective-permute-start(bf16[32,128]{1,0:T(8,128)(2,1)S(1)} %shard_map.69.own.solved.rest_2_), channel_id=1, source_target_pairs={{0,16},{16,0},{32,48},{48,32},{64,80},{80,64},{96,112},{112,96},{1... | collective-permute-start | bytes 24584 | tf_op jit(solution)/shard_map/ppermute | solution.py:271
  99.2 7.7 %collective-permute-start.8 = (bf16[32,128]{1,0:T(8,128)(2,1)S(1)}, bf16[32,128]{1,0:T(8,128)(2,1)S(1)}, u32[]{:S(2)}, u32[]{:S(2)}) collective-permute-start(bf16[32,128]{1,0:T(8,128)(2,1)S(1)} %shard_map.70.own.solved.rest_3_), channel_id=1, source_target_pairs={{16,32},{32,16},{48,64},{64,48},{80,96},{96,80},{112,128},{128,112... | collective-permute-start | bytes 24584 | tf_op jit(solution)/shard_map/ppermute | solution.py:271
  104.5 4.8 %collective-permute-start.9 = (bf16[32,128]{1,0:T(8,128)(2,1)S(1)}, bf16[32,128]{1,0:T(8,128)(2,1)S(1)}, u32[]{:S(2)}, u32[]{:S(2)}) collective-permute-start(bf16[32,128]{1,0:T(8,128)(2,1)S(1)} %shard_map.70.own.solved.rest_3_), channel_id=1, source_target_pairs={{0,16},{16,0},{32,48},{48,32},{64,80},{80,64},{96,112},{112,96},{1... | collective-permute-start | bytes 24584 | tf_op jit(solution)/shard_map/ppermute | solution.py:271
  109.9 7.7 %collective-permute-start.10 = (bf16[32,128]{1,0:T(8,128)(2,1)S(1)}, bf16[32,128]{1,0:T(8,128)(2,1)S(1)}, u32[]{:S(2)}, u32[]{:S(2)}) collective-permute-start(bf16[32,128]{1,0:T(8,128)(2,1)S(1)} %shard_map.71.own.solved.rest_4_), channel_id=1, source_target_pairs={{16,32},{32,16},{48,64},{64,48},{80,96},{96,80},{112,128},{128,112... | collective-permute-start | bytes 24584 | tf_op jit(solution)/shard_map/ppermute | solution.py:271
  113.3 4.8 %collective-permute-start.11 = (bf16[32,128]{1,0:T(8,128)(2,1)S(1)}, bf16[32,128]{1,0:T(8,128)(2,1)S(1)}, u32[]{:S(2)}, u32[]{:S(2)}) collective-permute-start(bf16[32,128]{1,0:T(8,128)(2,1)S(1)} %shard_map.71.own.solved.rest_4_), channel_id=1, source_target_pairs={{0,16},{16,0},{32,48},{48,32},{64,80},{80,64},{96,112},{112,96},{1... | collective-permute-start | bytes 24584 | tf_op jit(solution)/shard_map/ppermute | solution.py:271
  118.7 4.4 %collective-permute-start.12 = (bf16[32,128]{1,0:T(8,128)(2,1)S(1)}, bf16[32,128]{1,0:T(8,128)(2,1)S(1)}, u32[]{:S(2)}, u32[]{:S(2)}) collective-permute-start(bf16[32,128]{1,0:T(8,128)(2,1)S(1)} %shard_map.72.own.solved.rest_5_), channel_id=1, source_target_pairs={{0,16},{16,0},{32,48},{48,32},{64,80},{80,64},{96,112},{112,96},{1... | collective-permute-start | bytes 24584 | tf_op jit(solution)/shard_map/ppermute | solution.py:271
  121.5 11.2 %copy-start.2 = (bf16[64,2,128,128]{3,2,1,0:T(8,128)(2,1)S(1)}, bf16[64,2,128,128]{3,2,1,0:T(8,128)(2,1)}, u32[]{:S(2)}) copy-start(bf16[64,2,128,128]{3,2,1,0:T(8,128)(2,1)} %all-gather.7.cloned.1.call-done) | copy-start | bytes 12582916
  124.9 7.8 %collective-permute-start.13 = (bf16[64,128]{1,0:T(8,128)(2,1)S(1)}, bf16[64,128]{1,0:T(8,128)(2,1)S(1)}, u32[]{:S(2)}, u32[]{:S(2)}) collective-permute-start(bf16[64,128]{1,0:T(8,128)(2,1)S(1)} %get-tuple-element.52), channel_id=1, source_target_pairs={{16,32},{32,16},{48,64},{64,48},{80,96},{96,80},{112,128},{128,112... | collective-permute-start | bytes 49160 | tf_op jit(solution)/shard_map/ppermute | solution.py:271
  132.7 3.4 %copy-start.1 = (bf16[64,4,128,128]{3,2,1,0:T(8,128)(2,1)S(1)}, bf16[64,4,128,128]{3,2,1,0:T(8,128)(2,1)}, u32[]{:S(2)}) copy-start(bf16[64,4,128,128]{3,2,1,0:T(8,128)(2,1)} %all-gather.5.cloned.1.call-done) | copy-start | bytes 25165828
  136.9 4.5 %collective-permute-start.14 = (bf16[64,128]{1,0:T(8,128)(2,1)S(1)}, bf16[64,128]{1,0:T(8,128)(2,1)S(1)}, u32[]{:S(2)}, u32[]{:S(2)}) collective-permute-start(bf16[64,128]{1,0:T(8,128)(2,1)S(1)} %get-tuple-element.56), channel_id=1, source_target_pairs={{0,16},{16,0},{32,48},{48,32},{64,80},{80,64},{96,112},{112,96},{1... | collective-permute-start | bytes 49160 | tf_op jit(solution)/shard_map/ppermute | solution.py:271
  142.7 7.8 %collective-permute-start.15 = (bf16[64,128]{1,0:T(8,128)(2,1)S(1)}, bf16[64,128]{1,0:T(8,128)(2,1)S(1)}, u32[]{:S(2)}, u32[]{:S(2)}) collective-permute-start(bf16[64,128]{1,0:T(8,128)(2,1)S(1)} %get-tuple-element.58), channel_id=1, source_target_pairs={{16,32},{32,16},{48,64},{64,48},{80,96},{96,80},{112,128},{128,112... | collective-permute-start | bytes 49160 | tf_op jit(solution)/shard_map/ppermute | solution.py:271
  151.5 4.5 %collective-permute-start.16 = (bf16[64,128]{1,0:T(8,128)(2,1)S(1)}, bf16[64,128]{1,0:T(8,128)(2,1)S(1)}, u32[]{:S(2)}, u32[]{:S(2)}) collective-permute-start(bf16[64,128]{1,0:T(8,128)(2,1)S(1)} %get-tuple-element.60), channel_id=1, source_target_pairs={{0,16},{16,0},{32,48},{48,32},{64,80},{80,64},{96,112},{112,96},{1... | collective-permute-start | bytes 49160 | tf_op jit(solution)/shard_map/ppermute | solution.py:271
  156.9 7.8 %collective-permute-start.17 = (bf16[64,128]{1,0:T(8,128)(2,1)S(1)}, bf16[64,128]{1,0:T(8,128)(2,1)S(1)}, u32[]{:S(2)}, u32[]{:S(2)}) collective-permute-start(bf16[64,128]{1,0:T(8,128)(2,1)S(1)} %get-tuple-element.62), channel_id=1, source_target_pairs={{16,32},{32,16},{48,64},{64,48},{80,96},{96,80},{112,128},{128,112... | collective-permute-start | bytes 49160 | tf_op jit(solution)/shard_map/ppermute | solution.py:271
  165.7 4.5 %collective-permute-start.18 = (bf16[64,128]{1,0:T(8,128)(2,1)S(1)}, bf16[64,128]{1,0:T(8,128)(2,1)S(1)}, u32[]{:S(2)}, u32[]{:S(2)}) collective-permute-start(bf16[64,128]{1,0:T(8,128)(2,1)S(1)} %get-tuple-element.64), channel_id=1, source_target_pairs={{0,16},{16,0},{32,48},{48,32},{64,80},{80,64},{96,112},{112,96},{1... | collective-permute-start | bytes 49160 | tf_op jit(solution)/shard_map/ppermute | solution.py:271
  171.1 7.8 %collective-permute-start.19 = (bf16[64,128]{1,0:T(8,128)(2,1)S(1)}, bf16[64,128]{1,0:T(8,128)(2,1)S(1)}, u32[]{:S(2)}, u32[]{:S(2)}) collective-permute-start(bf16[64,128]{1,0:T(8,128)(2,1)S(1)} %get-tuple-element.66), channel_id=1, source_target_pairs={{16,32},{32,16},{48,64},{64,48},{80,96},{96,80},{112,128},{128,112... | collective-permute-start | bytes 49160 | tf_op jit(solution)/shard_map/ppermute | solution.py:271
  179.9 4.5 %collective-permute-start.20 = (bf16[64,128]{1,0:T(8,128)(2,1)S(1)}, bf16[64,128]{1,0:T(8,128)(2,1)S(1)}, u32[]{:S(2)}, u32[]{:S(2)}) collective-permute-start(bf16[64,128]{1,0:T(8,128)(2,1)S(1)} %get-tuple-element.68), channel_id=1, source_target_pairs={{0,16},{16,0},{32,48},{48,32},{64,80},{80,64},{96,112},{112,96},{1... | collective-permute-start | bytes 49160 | tf_op jit(solution)/shard_map/ppermute | solution.py:271
  185.4 7.8 %collective-permute-start.21 = (bf16[64,128]{1,0:T(8,128)(2,1)S(1)}, bf16[64,128]{1,0:T(8,128)(2,1)S(1)}, u32[]{:S(2)}, u32[]{:S(2)}) collective-permute-start(bf16[64,128]{1,0:T(8,128)(2,1)S(1)} %get-tuple-element.70), channel_id=1, source_target_pairs={{16,32},{32,16},{48,64},{64,48},{80,96},{96,80},{112,128},{128,112... | collective-permute-start | bytes 49160 | tf_op jit(solution)/shard_map/ppermute | solution.py:271
Sparse Core Ops, SparseCore 0:
  10.1 65.5 all-gather.4
  77.8 43.6 all-gather.6

commit v11 on v10

--- a/solution.py
+++ b/solution.py
@@ -37,64 +37,92 @@
     return value & mask, (value >> BITS) & mask, value >> (2 * BITS)
 
 
-def products(product, share, owners, vectors, blocks, kind):
-    rows = blocks.shape[1]
+def products(product, share, vectors, blocks, level, kind):
     totals = []
-    for pair in range(rows):
-        half, row = divmod(2 * pair, rows)
-        part = vectors[2 * share * pair : 2 * share * (pair + 1)]
-        wide = [blocks[owners[half], row + one, kind] for one in range(2)]
+    for row in range(0, blocks.shape[1], 2):
+        part = vectors[share * row : share * (row + 2)]
+        wide = [blocks[level, row + one, kind] for one in range(2)]
         if isinstance(kind, slice):
             wide = [block.reshape(-1, block.shape[-1]) for block in wide]
         totals.append(either(*[product(part, block) for block in wide], share))
     return jnp.concatenate(totals, axis=0)
 
 
+def run(copies, sems):
+    copies = [pltpu.make_async_copy(*ends, sems.at[which]) for which, ends in enumerate(copies)]
+    for copy in copies:
+        copy.start()
+    return lambda: [copy.wait() for copy in copies]
+
+
+OWN_DIAG, OWN_OWN, OWN_MATE, MATE_DIAG, MATE_OWN = range(5)
+
+
+def level_copies(levels, packed, weights, out):
+    rows = weights.shape[1]
+    copies = []
+    for at, level in enumerate(levels):
+        *owners, _ = unpack(packed, level)
+        for half in range(2):
+            copies.append((weights.at[owners[half]], out.at[at, pl.ds(half * rows, rows)]))
+    return copies
+
+
+def arrange_kernel(levels, packed, weights, out, sems):
+    run(level_copies(levels, packed, weights, out), sems)()
+
+
+def arrange_pairs_kernel(levels, packed, weights, mates, out, sems):
+    rows = weights.shape[1]
+    copies = []
+    for at, level in enumerate(levels):
+        *owners, side = unpack(packed, level)
+        for half in range(2):
+            here = pl.ds(half * rows, rows)
+            kinds = [(OWN_DIAG, 0), (OWN_OWN, 2), (OWN_MATE, 1 + side)] if level else [(OWN_DIAG, 0)]
+            for kind, block in kinds:
+                source = weights.at[owners[half], :, pl.ds(block, 1)]
+                copies.append((source, out.at[at, here, pl.ds(kind, 1)]))
+            if level:
+                copies.append((mates.at[owners[half]], out.at[at, here, pl.ds(MATE_DIAG, 2)]))
+    run(copies, sems)()
+
+
 def picked_from(places, around):
     at = lax.broadcasted_iota(jnp.int32, (places.shape[0], around.shape[0]), 1)
     return dot(ones_where(at == places), around)
 
 
-def forward_kernel(level, share, fetched, packed, weights, places, side, far, own, near, out, *held):
-    *owners, _ = unpack(packed, level)
+def forward_kernel(level, at, share, fetched, packed, weights, places, side, far, own, near, out, *held):
     if fetched:
         held, sems = held
-        copies = [
-            pltpu.make_async_copy(weights.at[owners[half]], held.at[half], sems.at[half])
-            for half in range(2)
-        ]
-        for copy in copies:
-            copy.start()
+        wait = run(level_copies([level], packed, weights, held), sems)
+        weights = held
     span = out.shape[0]
     picked = picked_from(places[level], jnp.concatenate([far[...], own[...], near[...]], axis=0))
     picked = jnp.concatenate([picked[n * span : (n + 1) * span] for n in range(3)], axis=1)
     if fetched:
-        for copy in copies:
-            copy.wait()
-        owners, weights = range(2), held
-    total = products(dot, share, owners, picked.astype(BF16), weights, slice(1, None))
+        wait()
+    total = products(dot, share, picked.astype(BF16), weights, at, slice(1, None))
     shifted = (side[level].astype(F32) - total).astype(BF16)
-    out[...] = products(dot, share, owners, shifted, weights, 0).astype(BF16)
-
-
-def gathered_sums(level, share, places, own, mate, blocks):
+    out[...] = products(dot, share, shifted, weights, at, 0).astype(BF16)
+
+
+def gathered_sums(level, at, share, blocks, places, own, mate):
     span = own.shape[0]
     picked = picked_from(places[level], jnp.concatenate([own, mate], axis=0)).astype(BF16)
-    parts = [picked[n * span : (n + 1) * span] for n in range(3)]
-    sums = [
-        products(dot, share, owners, part, block, kind)
-        for part, (owners, block, kind) in zip(parts, blocks())
+    parts = [
+        products(dot, share, picked[n * span : (n + 1) * span], blocks, at, kind)
+        for n, kind in enumerate((OWN_OWN, MATE_OWN, OWN_MATE))
     ]
-    return jnp.concatenate([sums[0] + sums[2], sums[1]], axis=0)
-
-
-def pushed_sums(level, share, packed, weights, mates, targets, own, mate):
-    *owners, side = unpack(packed, level)
+    return jnp.concatenate([parts[0] + parts[2], parts[1]], axis=0)
+
+
+def pushed_sums(level, at, share, blocks, targets, own, mate):
     span = own.shape[0]
     pushed = [
-        products(dot_t, share, owners, own, weights, 2),
-        products(dot_t, share, owners, mate, mates, 1),
-        products(dot_t, share, owners, own, weights, 1 + side),
+        products(dot_t, share, vectors, blocks, at, kind)
+        for vectors, kind in ((own, OWN_OWN), (mate, MATE_OWN), (own, OWN_MATE))
     ]
     pushed = jnp.concatenate(pushed, axis=0).astype(BF16)
     to = lax.broadcasted_iota(jnp.int32, (2 * span, 3 * span), 0)
@@ -112,61 +140,43 @@
     return held[:span] + came[span:], held[span:] + came[:span]
 
 
-def entry_kernel(level, share, packed, weights, mates, meets, own, mate, held, sent, blocks, sems):
-    *owners, side = unpack(packed, level)
-    copies = []
-    for which, (source, kind) in enumerate(((weights, 2), (mates, 1), (weights, 1 + side))):
-        for half in range(2):
-            rows = source.at[owners[half], :, pl.ds(kind, 1)]
-            copies.append(pltpu.make_async_copy(rows, blocks.at[which, half], sems.at[which, half]))
-    for copy in copies:
-        copy.start()
-
-    def arrived():
-        for copy in copies:
-            copy.wait()
-        return [(range(2), blocks.at[which], 0) for which in range(3)]
-
-    pass_on(gathered_sums(level, share, meets, own[...], mate[...], arrived), held, sent)
+def entry_kernel(level, at, share, blocks, meets, own, mate, held, sent):
+    pass_on(gathered_sums(level, at, share, blocks, meets, own[...], mate[...]), held, sent)
 
 
 def forward_pair_kernel(
-    level, share, last, packed, weights, mates, meets, targets, side, side_mate, held, came,
+    level, at, share, last, blocks, meets, targets, side, side_mate, held, came,
     solved, solved_mate, to_hold, to_send,
 ):
-    *owners, _ = unpack(packed, level)
     pair = []
-    for total, right, blocks in zip(joined(held, came), (side[level], side_mate[...]), (weights, mates)):
+    diags = OWN_DIAG, MATE_DIAG
+    for total, right, diag in zip(joined(held, came), (side[level], side_mate[...]), diags):
         shifted = (right.astype(F32) - total).astype(BF16)
-        pair.append(products(dot, share, owners, shifted, blocks, 0).astype(BF16))
+        pair.append(products(dot, share, shifted, blocks, at, diag).astype(BF16))
     solved[...], solved_mate[...] = pair
     if last:
-        sums = pushed_sums(level, share, packed, weights, mates, targets, *pair)
+        sums = pushed_sums(level, at, share, blocks, targets, *pair)
     else:
-        *owners, up = unpack(packed, level + 1)
-        blocks = [(owners, weights, 2), (owners, mates, 1), (owners, weights, 1 + up)]
-        sums = gathered_sums(level + 1, share, meets, *pair, lambda: blocks)
+        sums = gathered_sums(level + 1, at + 1, share, blocks, meets, *pair)
     pass_on(sums, to_hold, to_send)
 
 
 def backward_kernel(
-    level, share, packed, weights, mates, targets, solved, solved_mate, held, came, result, *outs
+    level, at, share, blocks, targets, solved, solved_mate, held, came, result, *outs
 ):
-    *owners, _ = unpack(packed, level)
     pair = []
-    for total, vector, blocks in zip(joined(held, came), (solved, solved_mate), (weights, mates)):
-        part = products(dot, share, owners, total.astype(BF16), blocks, 0)
+    diags = OWN_DIAG, MATE_DIAG
+    for total, vector, diag in zip(joined(held, came), (solved, solved_mate), diags):
+        part = products(dot, share, total.astype(BF16), blocks, at, diag)
         pair.append((vector[...].astype(F32) - part).astype(BF16))
     result[...] = pair[0]
-    pass_on(pushed_sums(level, share, packed, weights, mates, targets, *pair), *outs)
-
-
-def last_kernel(share, packed, weights, held, came, *rest):
+    pass_on(pushed_sums(level, at, share, blocks, targets, *pair), *outs)
+
+
+def last_kernel(share, packed, blocks, held, came, *rest):
     *rest, out = rest
     solved, results = rest[: packed.shape[0]], rest[packed.shape[0] :]
-    *owners, _ = unpack(packed, 0)
-    total = joined(held, came)[0].astype(BF16)
-    part = products(dot, share, owners, total, weights, 0)
+    part = products(dot, share, joined(held, came)[0].astype(BF16), blocks, 0, OWN_DIAG)
     result = (solved[0][...].astype(F32) - part).astype(BF16)
     size = out.shape[1] // 2
     for level in range(packed.shape[0]):
@@ -176,7 +186,7 @@
                 out[owners[half], which * size : (which + 1) * size] = array[half * size : (half + 1) * size]
 
 
-def call(kernel, outs, *args, fetched=0, scratch=(), cost=None):
+def call(kernel, outs, *args, fetched=0, scratch=()):
     specs = [pl.BlockSpec(memory_space=pltpu.VMEM)] * len(args)
     args = list(args)
     for at in range(1, 1 + fetched):
@@ -188,7 +198,6 @@
         in_specs=specs,
         out_specs=[pl.BlockSpec(memory_space=pltpu.VMEM)] * len(outs),
         scratch_shapes=scratch,
-        cost_estimate=cost,
         compiler_params=pltpu.CompilerParams(vmem_limit_bytes=16 * 2**20),
     )(*args)
 
@@ -270,6 +279,14 @@
     def swap(vector, level):
         return lax.ppermute(vector, "dom", far_pairs if level % 2 == 0 else near_pairs)
 
+    def arranged(kernel, levels_now, kinds, copies, behind, *blocks):
+        _, *blocks = lax.optimization_barrier((behind, *blocks))
+        shape = (len(levels_now), count, kinds, width, width)
+        kernel = functools.partial(kernel, levels_now)
+        scratch = [pltpu.SemaphoreType.DMA((copies,))]
+        outs = [jax.ShapeDtypeStruct(shape, BF16)]
+        return call(kernel, outs, packed, *blocks, fetched=len(blocks), scratch=scratch)[0]
+
     solved = [own]
     solved_mate = []
     for level in range(1, paired):
@@ -277,41 +294,42 @@
             own = solved[-1]
             far, near = swap(own, 0), swap(own, 1)
         solved_mate.append(near if level % 2 == 0 else far)
-        kernel = functools.partial(forward_kernel, level, share, level == 1)
-        args = packed, weights, places, side, far, own, near
+        args = places, side, far, own, near
         if level == 1:
-            scratch = [pltpu.VMEM((2,) + weights.shape[1:], BF16), pltpu.SemaphoreType.DMA((2,))]
-            solved += call(kernel, [vector], *args, fetched=1, scratch=scratch)
+            scratch = [pltpu.VMEM((1, count, 4, width, width), BF16), pltpu.SemaphoreType.DMA((2,))]
+            kernel = functools.partial(forward_kernel, level, 0, share, True)
+            solved += call(kernel, [vector], packed, weights, *args, fetched=1, scratch=scratch)
+            singles = range(2, paired)
+            blocks = arranged(arrange_kernel, singles, 4, 2 * len(singles), solved[-1], weights)
         else:
-            solved += call(kernel, [vector], *args)
-
-    mate, mates = lax.optimization_barrier((swap(solved[-1], paired - 1), mates))
-    solved_mate.append(mate)
-    kernel = functools.partial(entry_kernel, paired, share)
-    args = packed, weights, mates, meets, solved[-1], mate
-    scratch = [
-        pltpu.VMEM((3, 2, rows, 1, width, width), BF16),
-        pltpu.SemaphoreType.DMA((3, 2)),
-    ]
-    cost = pl.CostEstimate(flops=0, transcendentals=0, bytes_accessed=12 * weights.size)
-    held, sent = call(kernel, sums, *args, fetched=2, scratch=scratch, cost=cost)
-    for level in range(paired, levels):
-        kernel = functools.partial(forward_pair_kernel, level, share, level == levels - 1)
-        args = packed, weights, mates, meets, targets, side, side_mates[level - paired]
+            kernel = functools.partial(forward_kernel, level, level - 2, share, False)
+            solved += call(kernel, [vector], packed, blocks, *args)
+
+    solved_mate.append(swap(solved[-1], paired - 1))
+    upper = range(paired, levels)
+    blocks = arranged(arrange_pairs_kernel, upper, 5, 8 * len(upper), solved[-1], weights, mates)
+    kernel = functools.partial(entry_kernel, paired, 0, share)
+    held, sent = call(kernel, sums, blocks, meets, solved[-1], solved_mate[-1])
+    lower = range(paired)
+    below = arranged(arrange_pairs_kernel, lower, 5, 8 * len(lower) - 6, held, weights, mates)
+    for level in upper:
+        kernel = functools.partial(forward_pair_kernel, level, level - paired, share, level == levels - 1)
+        args = blocks, meets, targets, side, side_mates[level - paired]
         own, mate, held, sent = call(kernel, [vector] * 2 + sums, *args, held, swap(sent, level))
         solved.append(own)
         solved_mate.append(mate)
 
     results = [own]
     for level in range(levels - 2, 0, -1):
-        kernel = functools.partial(backward_kernel, level, share)
-        args = packed, weights, mates, targets, solved[level], solved_mate[level], held, swap(sent, level)
-        result, held, sent = call(kernel, [vector] + sums, *args)
+        at = level - paired if level in upper else level
+        kernel = functools.partial(backward_kernel, level, at, share)
+        args = blocks if level in upper else below, targets, solved[level], solved_mate[level]
+        result, held, sent = call(kernel, [vector] + sums, *args, held, swap(sent, level))
         results.append(result)
 
     dealt = jax.ShapeDtypeStruct((levs, 2 * rows * share, width), BF16)
     kernel = functools.partial(last_kernel, share)
-    (dealt,) = call(kernel, [dealt], packed, weights, held, swap(sent, 0), *solved, *results[::-1])
+    (dealt,) = call(kernel, [dealt], packed, below, held, swap(sent, 0), *solved, *results[::-1])
     dealt = lax.all_to_all(dealt, "level", 0, 0, tiled=False)
     dealt = dealt.reshape(levs, 2, rows, share, width).transpose(1, 2, 0, 3, 4)
     dealt = dealt.reshape(2, rows, depth, width)

time: 232 us -> 225 us (0.970)
  waiting for transfers between devices: 52.8 us -> 44.6 us
  Pallas kernels: 14.5 us -> 19.2 us
  local copies, waits for them, and re-layouts: 11.4 us -> 8.01 us
  blocking collectives: 29.4 us -> 26.1 us
  starting transfers between devices: 96.9 us -> 100 us
    ppermute x18, waiting for transfers between devices: 30.1 us -> 21.9 us  [swap(): lax.ppermute(vector, 'dom', far_pairs if level % 2 == 0 else near_pairs)]
    pallas_call x15 -> x18, Pallas kernels: 14.5 us -> 19.2 us  [call(): pl.pallas_call(kernel, out_shape=outs, in_specs=specs, out_specs=[pl.Bloc...]
    unnamed x6 -> x0, local copies, waits for them, and re-layouts: 3.39 us -> none
    all_to_all x1, blocking collectives: 29.4 us -> 26.1 us  [local(): dealt = lax.all_to_all(dealt, 'level', 0, 0, tiled=False)]
    ppermute x18, starting transfers between devices: 68.8 us -> 72 us  [swap(): lax.ppermute(vector, 'dom', far_pairs if level % 2 == 0 else near_pairs)]
  transfers between devices with their start and end apart: 25 -> 25, of which waited for: 21 -> 18; matrix products, arithmetic and copies ran while one was open for 6% -> 6% of each run, Pallas kernels for 2% -> 5%
where the time goes in v11:
time: 225 us; the launch traced here: 224 us
  starting transfers between devices  100 us (44%)
  waiting for transfers between devices  44.6 us (20%)
  blocking collectives  26.1 us (12%)
  Pallas kernels  19.2 us (9%)
  between operations  17.1 us (8%)
  local copies, waits for them, and re-layouts  8.01 us (4%)
  other arithmetic  7.92 us (4%)
    ppermute x18, starting transfers between devices, swap(): lax.ppermute(vector, 'dom', far_pairs if level % 2 == 0 else near_pairs)  72 us
    all_to_all x1, blocking collectives, local(): dealt = lax.all_to_all(dealt, 'level', 0, 0, tiled=False)  26.1 us
    ppermute x18, waiting for transfers between devices, swap(): lax.ppermute(vector, 'dom', far_pairs if level % 2 == 0 else near_pairs)  21.9 us
    pallas_call x18, Pallas kernels, call(): pl.pallas_call(kernel, out_shape=outs, in_specs=specs, out_specs=[pl.Bloc...  19.2 us
    all_gather x1, waiting for transfers between devices, local(): weights = lax.all_gather(weights, 'level')  17.4 us
    ppermute x1, starting transfers between devices, local(): by_far = lax.ppermute(mates, 'dom', far_pairs)  11 us
    all_to_all x1, starting transfers between devices, local(): side = lax.all_to_all(side, 'level', 1, 0, tiled=False)  8.35 us
    ppermute x1, starting transfers between devices, local(): by_near = lax.ppermute(mates, 'dom', near_pairs)  4.83 us
  transfers between devices with their start and end apart: 25, of which 18 were waited for; matrix products, arithmetic and copies ran while one was open for 6% of the time, Pallas kernels for 5%

profile of v11, /device:TPU:1, one launch (start us, length us, event | category | flops | bytes accessed | tf_op | source)
XLA Modules:
  0.0 224.3 jit_solution(1561586063009476726)
XLA Ops:
  7.2 1.9 pad_maximum_fusion
  9.2 1.3 fusion.7
  13.1 1.0 slice_select_fusion
  15.0 4.8 %collective-permute-start = (bf16[4,2,128,128]{3,2,1,0:T(8,128)(2,1)S(1)}, bf16[4,2,128,128]{3,2,1,0:T(8,128)(2,1)S(1)}, u32[]{:S(2)}, u32[]{:S(2)}) collective-permute-start(bf16[4,2,128,128]{3,2,1,0:T(8,128)(2,1)S(1)} %pad_maximum_fusion.1), channel_id=1, source_target_pairs={{0,16},{16,0},{32,48},{48,32},{64,80},{80,64},{96,112},{112,96},{1... | collective-permute-start | bytes 786440 | tf_op jit(solution)/shard_map/ppermute | solution.py:230
  19.9 11.0 %collective-permute-start.1 = (bf16[4,2,128,128]{3,2,1,0:T(8,128)(2,1)S(1)}, bf16[4,2,128,128]{3,2,1,0:T(8,128)(2,1)S(1)}, u32[]{:S(2)}, u32[]{:S(2)}) collective-permute-start(bf16[4,2,128,128]{3,2,1,0:T(8,128)(2,1)S(1)} %pad_maximum_fusion.1), channel_id=1, source_target_pairs={{16,32},{32,16},{48,64},{64,48},{80,96},{96,80},{112,128},{128,112... | collective-permute-start | bytes 786440 | tf_op jit(solution)/shard_map/ppermute | solution.py:231
  30.9 1.1 fusion
  32.7 8.3 %all-to-all-start = ((bf16[1,4,16,4,128]{4,3,1,0,2:T(4,128)(2,1)}), bf16[1,4,16,4,128]{4,3,1,0,2:T(4,128)(2,1)S(1)}, u32[]{:S(2)}, u32[]{:S(2)}) async-start(bf16[1,4,16,4,128]{4,3,1,0,2:T(4,128)(2,1)} %copy.64), calls=%async_computation | async-start | bytes 131072 | tf_op jit(solution)/shard_map/all_to_all | solution.py:236
  48.6 1.1 all-to-all-done
  50.3 1.9 collective-permute-start.2
  52.3 1.9 collective-permute-start.3
  54.9 3.2 %collective-permute-done.2 = bf16[2,32,128]{2,1,0:T(8,128)(2,1)S(1)} collective-permute-done((bf16[2,32,128]{2,1,0:T(8,128)(2,1)S(1)}, bf16[2,32,128]{2,1,0:T(8,128)(2,1)S(1)}, u32[]{:S(2)}, u32[]{:S(2)}) %collective-permute-start.2) | collective-permute-done | bytes 16416 | tf_op jit(solution)/shard_map/ppermute | solution.py:270
  58.3 17.4 %all-gather.5.cloned.1.call-done = bf16[64,4,128,128]{3,2,1,0:T(8,128)(2,1)} async-done(((bf16[4,4,128,128]{3,2,1,0:T(8,128)(2,1)}), bf16[64,4,128,128]{3,2,1,0:T(8,128)(2,1)}) %all-gather.5.cloned.1.call-update) | async-done | bytes 8388624 | tf_op jit(solution)/shard_map/all_gather | solution.py:218
  75.7 1.8 shard_map.68.own.solved.rest_1_
  77.5 7.7 %collective-permute-start.4 = (bf16[32,128]{1,0:T(8,128)(2,1)S(1)}, bf16[32,128]{1,0:T(8,128)(2,1)S(1)}, u32[]{:S(2)}, u32[]{:S(2)}) collective-permute-start(bf16[32,128]{1,0:T(8,128)(2,1)S(1)} %shard_map.68.own.solved.rest_1_), channel_id=1, source_target_pairs={{16,32},{32,16},{48,64},{64,48},{80,96},{96,80},{112,128},{128,112... | collective-permute-start | bytes 24584 | tf_op jit(solution)/shard_map/ppermute | solution.py:280
  85.2 1.9 collective-permute-start.5
  87.2 2.4 %shard_map.69.weights = bf16[4,8,4,128,128]{4,3,2,1,0:T(8,128)(2,1)S(1)} custom-call(s32[8,128]{1,0:T(8,128)S(1)} %broadcast_in_dim.73.packed, bf16[16,4,4,128,128]{4,3,2,1,0:T(8,128)(2,1)} %bitcast.77), custom_call_target="tpu_custom_call" | custom-call | tf_op jit(solution)/shard_map/pallas_call | solution.py:195
  90.2 3.9 %collective-permute-start.6 = (bf16[32,128]{1,0:T(8,128)(2,1)S(1)}, bf16[32,128]{1,0:T(8,128)(2,1)S(1)}, u32[]{:S(2)}, u32[]{:S(2)}) collective-permute-start(bf16[32,128]{1,0:T(8,128)(2,1)S(1)} %shard_map.70.own.solved.rest_2_), channel_id=1, source_target_pairs={{16,32},{32,16},{48,64},{64,48},{80,96},{96,80},{112,128},{128,112... | collective-permute-start | bytes 24584 | tf_op jit(solution)/shard_map/ppermute | solution.py:280
  94.1 1.9 collective-permute-start.7
  96.0 1.9 collective-permute-done.6.far.solved_mate
  99.4 4.7 %collective-permute-start.8 = (bf16[32,128]{1,0:T(8,128)(2,1)S(1)}, bf16[32,128]{1,0:T(8,128)(2,1)S(1)}, u32[]{:S(2)}, u32[]{:S(2)}) collective-permute-start(bf16[32,128]{1,0:T(8,128)(2,1)S(1)} %shard_map.71.own.solved.rest_3_), channel_id=1, source_target_pairs={{16,32},{32,16},{48,64},{64,48},{80,96},{96,80},{112,128},{128,112... | collective-permute-start | bytes 24584 | tf_op jit(solution)/shard_map/ppermute | solution.py:280
  104.2 1.9 collective-permute-start.9
  106.1 1.1 collective-permute-done.8.far
  107.1 1.8 collective-permute-done.9.near.solved_mate
  109.5 3.8 %collective-permute-start.10 = (bf16[32,128]{1,0:T(8,128)(2,1)S(1)}, bf16[32,128]{1,0:T(8,128)(2,1)S(1)}, u32[]{:S(2)}, u32[]{:S(2)}) collective-permute-start(bf16[32,128]{1,0:T(8,128)(2,1)S(1)} %shard_map.72.own.solved.rest_4_), channel_id=1, source_target_pairs={{16,32},{32,16},{48,64},{64,48},{80,96},{96,80},{112,128},{128,112... | collective-permute-start | bytes 24584 | tf_op jit(solution)/shard_map/ppermute | solution.py:280
  113.3 1.9 collective-permute-start.11
  115.2 2.0 collective-permute-done.10.far.solved_mate
  118.6 1.9 collective-permute-start.12
  121.5 2.1 shard_map.74.blocks
  124.1 7.7 %collective-permute-start.13 = (bf16[64,128]{1,0:T(8,128)(2,1)S(1)}, bf16[64,128]{1,0:T(8,128)(2,1)S(1)}, u32[]{:S(2)}, u32[]{:S(2)}) collective-permute-start(bf16[64,128]{1,0:T(8,128)(2,1)S(1)} %get-tuple-element.58), channel_id=1, source_target_pairs={{16,32},{32,16},{48,64},{64,48},{80,96},{96,80},{112,128},{128,112... | collective-permute-start | bytes 49160 | tf_op jit(solution)/shard_map/ppermute | solution.py:280
  131.7 1.1 collective-permute-done.13.came
  133.5 1.9 collective-permute-start.14
  135.4 2.6 %collective-permute-done.14.came = bf16[64,128]{1,0:T(8,128)(2,1)S(1)} collective-permute-done((bf16[64,128]{1,0:T(8,128)(2,1)S(1)}, bf16[64,128]{1,0:T(8,128)(2,1)S(1)}, u32[]{:S(2)}, u32[]{:S(2)}) %collective-permute-start.14) | collective-permute-done | bytes 16416 | tf_op jit(solution)/shard_map/ppermute | solution.py:280
  138.0 1.1 shard_map.78
  139.1 6.7 %collective-permute-start.15 = (bf16[64,128]{1,0:T(8,128)(2,1)S(1)}, bf16[64,128]{1,0:T(8,128)(2,1)S(1)}, u32[]{:S(2)}, u32[]{:S(2)}) collective-permute-start(bf16[64,128]{1,0:T(8,128)(2,1)S(1)} %get-tuple-element.64), channel_id=1, source_target_pairs={{16,32},{32,16},{48,64},{64,48},{80,96},{96,80},{112,128},{128,112... | collective-permute-start | bytes 49160 | tf_op jit(solution)/shard_map/ppermute | solution.py:280
  145.8 1.1 collective-permute-done.15.came
  147.6 1.9 collective-permute-start.16
  149.6 3.6 %shard_map.76.blocks = bf16[6,8,5,128,128]{4,3,2,1,0:T(8,128)(2,1)S(1)} custom-call(s32[8,128]{1,0:T(8,128)S(1)} %broadcast_in_dim.73.packed, bf16[16,4,4,128,128]{4,3,2,1,0:T(8,128)(2,1)} %bitcast.79, bf16[16,4,2,128,128]{4,3,2,1,0:T(8,128)(2,1)} %bitcast.81), custom_call_target="tpu_custom_call" | custom-call | tf_op jit(solution)/shard_map/pallas_call | solution.py:195
  154.0 6.7 %collective-permute-start.17 = (bf16[64,128]{1,0:T(8,128)(2,1)S(1)}, bf16[64,128]{1,0:T(8,128)(2,1)S(1)}, u32[]{:S(2)}, u32[]{:S(2)}) collective-permute-start(bf16[64,128]{1,0:T(8,128)(2,1)S(1)} %get-tuple-element.68), channel_id=1, source_target_pairs={{16,32},{32,16},{48,64},{64,48},{80,96},{96,80},{112,128},{128,112... | collective-permute-start | bytes 49160 | tf_op jit(solution)/shard_map/ppermute | solution.py:280
  160.7 1.1 collective-permute-done.17.came
  162.6 1.9 collective-permute-start.18
  164.5 2.6 %collective-permute-done.18.came = bf16[64,128]{1,0:T(8,128)(2,1)S(1)} collective-permute-done((bf16[64,128]{1,0:T(8,128)(2,1)S(1)}, bf16[64,128]{1,0:T(8,128)(2,1)S(1)}, u32[]{:S(2)}, u32[]{:S(2)}) %collective-permute-start.18) | collective-permute-done | bytes 16416 | tf_op jit(solution)/shard_map/ppermute | solution.py:280
  167.8 7.0 %collective-permute-start.19 = (bf16[64,128]{1,0:T(8,128)(2,1)S(1)}, bf16[64,128]{1,0:T(8,128)(2,1)S(1)}, u32[]{:S(2)}, u32[]{:S(2)}) collective-permute-start(bf16[64,128]{1,0:T(8,128)(2,1)S(1)} %get-tuple-element.72), channel_id=1, source_target_pairs={{16,32},{32,16},{48,64},{64,48},{80,96},{96,80},{112,128},{128,112... | collective-permute-start | bytes 49160 | tf_op jit(solution)/shard_map/ppermute | solution.py:280
  174.8 1.1 collective-permute-done.19.came
  176.7 1.9 collective-permute-start.20
  178.6 2.6 %collective-permute-done.20.came = bf16[64,128]{1,0:T(8,128)(2,1)S(1)} collective-permute-done((bf16[64,128]{1,0:T(8,128)(2,1)S(1)}, bf16[64,128]{1,0:T(8,128)(2,1)S(1)}, u32[]{:S(2)}, u32[]{:S(2)}) %collective-permute-start.20) | collective-permute-done | bytes 16416 | tf_op jit(solution)/shard_map/ppermute | solution.py:280
  181.9 6.7 %collective-permute-start.21 = (bf16[64,128]{1,0:T(8,128)(2,1)S(1)}, bf16[64,128]{1,0:T(8,128)(2,1)S(1)}, u32[]{:S(2)}, u32[]{:S(2)}) collective-permute-start(bf16[64,128]{1,0:T(8,128)(2,1)S(1)} %get-tuple-element.76), channel_id=1, source_target_pairs={{16,32},{32,16},{48,64},{64,48},{80,96},{96,80},{112,128},{128,112... | collective-permute-start | bytes 49160 | tf_op jit(solution)/shard_map/ppermute | solution.py:280
  188.6 1.1 collective-permute-done.21.came
  190.0 26.1 %all_to_all.20 = bf16[16,32,128]{2,1,0:T(8,128)(2,1)S(1)} all-to-all(bf16[16,32,128]{2,1,0:T(8,128)(2,1)S(1)} %shard_map.85), channel_id=1, replica_groups=mesh['dom'=32,'level'=16] {'level'}, dimensions={0} | all-to-all | bytes 262144 | tf_op jit(solution)/shard_map/all_to_all | solution.py:333
  (80 shorter events, 22.8 us)
Async XLA Ops:
  7.2 68.5 %all-gather.5.cloned.1.call-start = ((), (), s32[]{:S(2)}) async-start(), calls=%async_computation.2 | async-start | bytes 8912896 | tf_op jit(solution)/shard_map/all_gather | solution.py:218
  15.0 39.2 %collective-permute-start = (bf16[4,2,128,128]{3,2,1,0:T(8,128)(2,1)S(1)}, bf16[4,2,128,128]{3,2,1,0:T(8,128)(2,1)S(1)}, u32[]{:S(2)}, u32[]{:S(2)}) collective-permute-start(bf16[4,2,128,128]{3,2,1,0:T(8,128)(2,1)S(1)} %pad_maximum_fusion.1), channel_id=1, source_target_pairs={{0,16},{16,0},{32,48},{48,32},{64,80},{80,64},{96,112},{112,96},{1... | collective-permute-start | bytes 786440 | tf_op jit(solution)/shard_map/ppermute | solution.py:230
  19.9 34.3 %collective-permute-start.1 = (bf16[4,2,128,128]{3,2,1,0:T(8,128)(2,1)S(1)}, bf16[4,2,128,128]{3,2,1,0:T(8,128)(2,1)S(1)}, u32[]{:S(2)}, u32[]{:S(2)}) collective-permute-start(bf16[4,2,128,128]{3,2,1,0:T(8,128)(2,1)S(1)} %pad_maximum_fusion.1), channel_id=1, source_target_pairs={{16,32},{32,16},{48,64},{64,48},{80,96},{96,80},{112,128},{128,112... | collective-permute-start | bytes 786440 | tf_op jit(solution)/shard_map/ppermute | solution.py:231
  32.7 17.0 %all-to-all-start = ((bf16[1,4,16,4,128]{4,3,1,0,2:T(4,128)(2,1)}), bf16[1,4,16,4,128]{4,3,1,0,2:T(4,128)(2,1)S(1)}, u32[]{:S(2)}, u32[]{:S(2)}) async-start(bf16[1,4,16,4,128]{4,3,1,0,2:T(4,128)(2,1)} %copy.64), calls=%async_computation | async-start | bytes 131072 | tf_op jit(solution)/shard_map/all_to_all | solution.py:236
  41.0 80.4 %all-gather.7.cloned.1.call-start = ((), (), s32[]{:S(2)}) async-start(), calls=%async_computation.3 | async-start | bytes 4456448 | tf_op jit(solution)/shard_map/all_gather | solution.py:277
  50.3 7.8 %collective-permute-start.2 = (bf16[2,32,128]{2,1,0:T(8,128)(2,1)S(1)}, bf16[2,32,128]{2,1,0:T(8,128)(2,1)S(1)}, u32[]{:S(2)}, u32[]{:S(2)}) collective-permute-start(bf16[2,32,128]{2,1,0:T(8,128)(2,1)S(1)} %get-tuple-element.104), channel_id=1, source_target_pairs={{16,32},{32,16},{48,64},{64,48},{80,96},{96,80},{112,128},{128,112... | collective-permute-start | bytes 49160 | tf_op jit(solution)/shard_map/ppermute | solution.py:270
  52.3 5.9 %collective-permute-start.3 = (bf16[2,32,128]{2,1,0:T(8,128)(2,1)S(1)}, bf16[2,32,128]{2,1,0:T(8,128)(2,1)S(1)}, u32[]{:S(2)}, u32[]{:S(2)}) collective-permute-start(bf16[2,32,128]{2,1,0:T(8,128)(2,1)S(1)} %get-tuple-element.103), channel_id=1, source_target_pairs={{0,16},{16,0},{32,48},{48,32},{64,80},{80,64},{96,112},{112,96},{1... | collective-permute-start | bytes 49160 | tf_op jit(solution)/shard_map/ppermute | solution.py:271
  77.5 12.1 %collective-permute-start.4 = (bf16[32,128]{1,0:T(8,128)(2,1)S(1)}, bf16[32,128]{1,0:T(8,128)(2,1)S(1)}, u32[]{:S(2)}, u32[]{:S(2)}) collective-permute-start(bf16[32,128]{1,0:T(8,128)(2,1)S(1)} %shard_map.68.own.solved.rest_1_), channel_id=1, source_target_pairs={{16,32},{32,16},{48,64},{64,48},{80,96},{96,80},{112,128},{128,112... | collective-permute-start | bytes 24584 | tf_op jit(solution)/shard_map/ppermute | solution.py:280
  85.2 4.4 %collective-permute-start.5 = (bf16[32,128]{1,0:T(8,128)(2,1)S(1)}, bf16[32,128]{1,0:T(8,128)(2,1)S(1)}, u32[]{:S(2)}, u32[]{:S(2)}) collective-permute-start(bf16[32,128]{1,0:T(8,128)(2,1)S(1)} %shard_map.68.own.solved.rest_1_), channel_id=1, source_target_pairs={{0,16},{16,0},{32,48},{48,32},{64,80},{80,64},{96,112},{112,96},{1... | collective-permute-start | bytes 24584 | tf_op jit(solution)/shard_map/ppermute | solution.py:280
  90.2 7.7 %collective-permute-start.6 = (bf16[32,128]{1,0:T(8,128)(2,1)S(1)}, bf16[32,128]{1,0:T(8,128)(2,1)S(1)}, u32[]{:S(2)}, u32[]{:S(2)}) collective-permute-start(bf16[32,128]{1,0:T(8,128)(2,1)S(1)} %shard_map.70.own.solved.rest_2_), channel_id=1, source_target_pairs={{16,32},{32,16},{48,64},{64,48},{80,96},{96,80},{112,128},{128,112... | collective-permute-start | bytes 24584 | tf_op jit(solution)/shard_map/ppermute | solution.py:280
  94.1 4.8 %collective-permute-start.7 = (bf16[32,128]{1,0:T(8,128)(2,1)S(1)}, bf16[32,128]{1,0:T(8,128)(2,1)S(1)}, u32[]{:S(2)}, u32[]{:S(2)}) collective-permute-start(bf16[32,128]{1,0:T(8,128)(2,1)S(1)} %shard_map.70.own.solved.rest_2_), channel_id=1, source_target_pairs={{0,16},{16,0},{32,48},{48,32},{64,80},{80,64},{96,112},{112,96},{1... | collective-permute-start | bytes 24584 | tf_op jit(solution)/shard_map/ppermute | solution.py:280
  99.4 7.7 %collective-permute-start.8 = (bf16[32,128]{1,0:T(8,128)(2,1)S(1)}, bf16[32,128]{1,0:T(8,128)(2,1)S(1)}, u32[]{:S(2)}, u32[]{:S(2)}) collective-permute-start(bf16[32,128]{1,0:T(8,128)(2,1)S(1)} %shard_map.71.own.solved.rest_3_), channel_id=1, source_target_pairs={{16,32},{32,16},{48,64},{64,48},{80,96},{96,80},{112,128},{128,112... | collective-permute-start | bytes 24584 | tf_op jit(solution)/shard_map/ppermute | solution.py:280
  104.2 4.8 %collective-permute-start.9 = (bf16[32,128]{1,0:T(8,128)(2,1)S(1)}, bf16[32,128]{1,0:T(8,128)(2,1)S(1)}, u32[]{:S(2)}, u32[]{:S(2)}) collective-permute-start(bf16[32,128]{1,0:T(8,128)(2,1)S(1)} %shard_map.71.own.solved.rest_3_), channel_id=1, source_target_pairs={{0,16},{16,0},{32,48},{48,32},{64,80},{80,64},{96,112},{112,96},{1... | collective-permute-start | bytes 24584 | tf_op jit(solution)/shard_map/ppermute | solution.py:280
  109.5 7.7 %collective-permute-start.10 = (bf16[32,128]{1,0:T(8,128)(2,1)S(1)}, bf16[32,128]{1,0:T(8,128)(2,1)S(1)}, u32[]{:S(2)}, u32[]{:S(2)}) collective-permute-start(bf16[32,128]{1,0:T(8,128)(2,1)S(1)} %shard_map.72.own.solved.rest_4_), channel_id=1, source_target_pairs={{16,32},{32,16},{48,64},{64,48},{80,96},{96,80},{112,128},{128,112... | collective-permute-start | bytes 24584 | tf_op jit(solution)/shard_map/ppermute | solution.py:280
  113.3 4.8 %collective-permute-start.11 = (bf16[32,128]{1,0:T(8,128)(2,1)S(1)}, bf16[32,128]{1,0:T(8,128)(2,1)S(1)}, u32[]{:S(2)}, u32[]{:S(2)}) collective-permute-start(bf16[32,128]{1,0:T(8,128)(2,1)S(1)} %shard_map.72.own.solved.rest_4_), channel_id=1, source_target_pairs={{0,16},{16,0},{32,48},{48,32},{64,80},{80,64},{96,112},{112,96},{1... | collective-permute-start | bytes 24584 | tf_op jit(solution)/shard_map/ppermute | solution.py:280
  118.6 4.9 %collective-permute-start.12 = (bf16[32,128]{1,0:T(8,128)(2,1)S(1)}, bf16[32,128]{1,0:T(8,128)(2,1)S(1)}, u32[]{:S(2)}, u32[]{:S(2)}) collective-permute-start(bf16[32,128]{1,0:T(8,128)(2,1)S(1)} %shard_map.73.own.solved.rest_5_), channel_id=1, source_target_pairs={{0,16},{16,0},{32,48},{48,32},{64,80},{80,64},{96,112},{112,96},{1... | collective-permute-start | bytes 24584 | tf_op jit(solution)/shard_map/ppermute | solution.py:280
  124.1 8.8 %collective-permute-start.13 = (bf16[64,128]{1,0:T(8,128)(2,1)S(1)}, bf16[64,128]{1,0:T(8,128)(2,1)S(1)}, u32[]{:S(2)}, u32[]{:S(2)}) collective-permute-start(bf16[64,128]{1,0:T(8,128)(2,1)S(1)} %get-tuple-element.58), channel_id=1, source_target_pairs={{16,32},{32,16},{48,64},{64,48},{80,96},{96,80},{112,128},{128,112... | collective-permute-start | bytes 49160 | tf_op jit(solution)/shard_map/ppermute | solution.py:280
  133.5 4.5 %collective-permute-start.14 = (bf16[64,128]{1,0:T(8,128)(2,1)S(1)}, bf16[64,128]{1,0:T(8,128)(2,1)S(1)}, u32[]{:S(2)}, u32[]{:S(2)}) collective-permute-start(bf16[64,128]{1,0:T(8,128)(2,1)S(1)} %get-tuple-element.62), channel_id=1, source_target_pairs={{0,16},{16,0},{32,48},{48,32},{64,80},{80,64},{96,112},{112,96},{1... | collective-permute-start | bytes 49160 | tf_op jit(solution)/shard_map/ppermute | solution.py:280
  139.1 7.8 %collective-permute-start.15 = (bf16[64,128]{1,0:T(8,128)(2,1)S(1)}, bf16[64,128]{1,0:T(8,128)(2,1)S(1)}, u32[]{:S(2)}, u32[]{:S(2)}) collective-permute-start(bf16[64,128]{1,0:T(8,128)(2,1)S(1)} %get-tuple-element.64), channel_id=1, source_target_pairs={{16,32},{32,16},{48,64},{64,48},{80,96},{96,80},{112,128},{128,112... | collective-permute-start | bytes 49160 | tf_op jit(solution)/shard_map/ppermute | solution.py:280
  147.6 5.6 %collective-permute-start.16 = (bf16[64,128]{1,0:T(8,128)(2,1)S(1)}, bf16[64,128]{1,0:T(8,128)(2,1)S(1)}, u32[]{:S(2)}, u32[]{:S(2)}) collective-permute-start(bf16[64,128]{1,0:T(8,128)(2,1)S(1)} %get-tuple-element.66), channel_id=1, source_target_pairs={{0,16},{16,0},{32,48},{48,32},{64,80},{80,64},{96,112},{112,96},{1... | collective-permute-start | bytes 49160 | tf_op jit(solution)/shard_map/ppermute | solution.py:280
  154.0 7.8 %collective-permute-start.17 = (bf16[64,128]{1,0:T(8,128)(2,1)S(1)}, bf16[64,128]{1,0:T(8,128)(2,1)S(1)}, u32[]{:S(2)}, u32[]{:S(2)}) collective-permute-start(bf16[64,128]{1,0:T(8,128)(2,1)S(1)} %get-tuple-element.68), channel_id=1, source_target_pairs={{16,32},{32,16},{48,64},{64,48},{80,96},{96,80},{112,128},{128,112... | collective-permute-start | bytes 49160 | tf_op jit(solution)/shard_map/ppermute | solution.py:280
  162.6 4.5 %collective-permute-start.18 = (bf16[64,128]{1,0:T(8,128)(2,1)S(1)}, bf16[64,128]{1,0:T(8,128)(2,1)S(1)}, u32[]{:S(2)}, u32[]{:S(2)}) collective-permute-start(bf16[64,128]{1,0:T(8,128)(2,1)S(1)} %get-tuple-element.70), channel_id=1, source_target_pairs={{0,16},{16,0},{32,48},{48,32},{64,80},{80,64},{96,112},{112,96},{1... | collective-permute-start | bytes 49160 | tf_op jit(solution)/shard_map/ppermute | solution.py:280
  167.8 8.1 %collective-permute-start.19 = (bf16[64,128]{1,0:T(8,128)(2,1)S(1)}, bf16[64,128]{1,0:T(8,128)(2,1)S(1)}, u32[]{:S(2)}, u32[]{:S(2)}) collective-permute-start(bf16[64,128]{1,0:T(8,128)(2,1)S(1)} %get-tuple-element.72), channel_id=1, source_target_pairs={{16,32},{32,16},{48,64},{64,48},{80,96},{96,80},{112,128},{128,112... | collective-permute-start | bytes 49160 | tf_op jit(solution)/shard_map/ppermute | solution.py:280
  176.7 4.5 %collective-permute-start.20 = (bf16[64,128]{1,0:T(8,128)(2,1)S(1)}, bf16[64,128]{1,0:T(8,128)(2,1)S(1)}, u32[]{:S(2)}, u32[]{:S(2)}) collective-permute-start(bf16[64,128]{1,0:T(8,128)(2,1)S(1)} %get-tuple-element.74), channel_id=1, source_target_pairs={{0,16},{16,0},{32,48},{48,32},{64,80},{80,64},{96,112},{112,96},{1... | collective-permute-start | bytes 49160 | tf_op jit(solution)/shard_map/ppermute | solution.py:280
  181.9 7.8 %collective-permute-start.21 = (bf16[64,128]{1,0:T(8,128)(2,1)S(1)}, bf16[64,128]{1,0:T(8,128)(2,1)S(1)}, u32[]{:S(2)}, u32[]{:S(2)}) collective-permute-start(bf16[64,128]{1,0:T(8,128)(2,1)S(1)} %get-tuple-element.76), channel_id=1, source_target_pairs={{16,32},{32,16},{48,64},{64,48},{80,96},{96,80},{112,128},{128,112... | collective-permute-start | bytes 49160 | tf_op jit(solution)/shard_map/ppermute | solution.py:280
Sparse Core Ops, SparseCore 0:
  10.1 65.5 all-gather.4
  77.8 43.6 all-gather.6

commit v12 on v11

v12 whole, which is shorter than its diff:
```python
import functools

import jax
import jax.numpy as jnp
from jax import lax
from jax.experimental import pallas as pl
from jax.experimental.pallas import tpu as pltpu
from jax.sharding import PartitionSpec as P

BF16 = jnp.bfloat16
F32 = jnp.float32


def dot(a, b):
    return lax.dot_general(a, b, (((1,), (0,)), ((), ())), preferred_element_type=F32)


def dot_t(a, b):
    return lax.dot_general(a, b, (((1,), (1,)), ((), ())), preferred_element_type=F32)


def either(low, high, share):
    top = lax.broadcasted_iota(jnp.int32, low.shape, 0) < share
    return jnp.where(top, low, high)


def ones_where(condition):
    return jnp.where(condition, 1.0, 0.0).astype(BF16)


BITS = 8


def unpack(packed, level):
    value = jnp.max(packed[level : level + 1])
    mask = (1 << BITS) - 1
    return value & mask, (value >> BITS) & mask, value >> (2 * BITS)


def products(product, share, vectors, blocks, level, kind):
    totals = []
    for row in range(0, blocks.shape[1], 2):
        part = vectors[share * row : share * (row + 2)]
        wide = [blocks[level, row + one, kind] for one in range(2)]
        if isinstance(kind, slice):
            wide = [block.reshape(-1, block.shape[-1]) for block in wide]
        totals.append(either(*[product(part, block) for block in wide], share))
    return jnp.concatenate(totals, axis=0)


OWN_DIAG, OWN_OWN, OWN_MATE, MATE_DIAG, MATE_OWN = range(5)


def arrange_kernel(slots, *rest):
    *pieces, out, sems = rest
    copies = []
    at = 0
    for piece in pieces:
        kinds = pl.ds(MATE_DIAG if piece.shape[2] == 2 else 0, piece.shape[2])
        for sub in range(piece.shape[0]):
            which = at + sub - (2 if piece.shape[2] == 2 else 0)
            slot = jnp.max(slots[which : which + 1])
            copies.append(
                pltpu.make_async_copy(piece.at[sub], out.at[slot, :, kinds], sems.at[len(copies)])
            )
        at += 0 if piece.shape[2] == 2 else piece.shape[0]
    for copy in copies:
        copy.start()
    for copy in copies:
        copy.wait()


def picked_from(places, around):
    at = lax.broadcasted_iota(jnp.int32, (places.shape[0], around.shape[0]), 1)
    return dot(ones_where(at == places), around)


def gathered_sums(level, at, share, blocks, places, own, mate):
    span = own.shape[0]
    picked = picked_from(places[level], jnp.concatenate([own, mate], axis=0)).astype(BF16)
    parts = [
        products(dot, share, picked[n * span : (n + 1) * span], blocks, at, kind)
        for n, kind in enumerate((OWN_OWN, MATE_OWN, OWN_MATE))
    ]
    return jnp.concatenate([parts[0] + parts[2], parts[1]], axis=0)


def pushed_sums(level, at, share, blocks, targets, own, mate):
    span = own.shape[0]
    pushed = [
        products(dot_t, share, vectors, blocks, at, kind)
        for vectors, kind in ((own, OWN_OWN), (mate, MATE_OWN), (own, OWN_MATE))
    ]
    pushed = jnp.concatenate(pushed, axis=0).astype(BF16)
    to = lax.broadcasted_iota(jnp.int32, (2 * span, 3 * span), 0)
    return dot(ones_where(to == targets[level]), pushed)


def pass_on(sums, held, sent):
    held[...] = sums
    sent[...] = sums.astype(BF16)


def joined(held, came):
    span = held.shape[0] // 2
    came = came[...].astype(F32)
    return held[:span] + came[span:], held[span:] + came[:span]


def entry_kernel(level, at, share, blocks, meets, own, mate, held, sent):
    pass_on(gathered_sums(level, at, share, blocks, meets, own[...], mate[...]), held, sent)


def forward_pair_kernel(
    level, at, share, last, blocks, meets, targets, side, side_mate, held, came,
    solved, solved_mate, to_hold, to_send,
):
    pair = []
    diags = OWN_DIAG, MATE_DIAG
    for total, right, diag in zip(joined(held, came), (side[level], side_mate[...]), diags):
        shifted = (right.astype(F32) - total).astype(BF16)
        pair.append(products(dot, share, shifted, blocks, at, diag).astype(BF16))
    solved[...], solved_mate[...] = pair
    if last:
        sums = pushed_sums(level, at, share, blocks, targets, *pair)
    else:
        sums = gathered_sums(level + 1, at + 1, share, blocks, meets, *pair)
    pass_on(sums, to_hold, to_send)


def backward_kernel(
    level, at, share, blocks, targets, solved, solved_mate, held, came, result, *outs
):
    pair = []
    diags = OWN_DIAG, MATE_DIAG
    for total, vector, diag in zip(joined(held, came), (solved, solved_mate), diags):
        part = products(dot, share, total.astype(BF16), blocks, at, diag)
        pair.append((vector[...].astype(F32) - part).astype(BF16))
    result[...] = pair[0]
    pass_on(pushed_sums(level, at, share, blocks, targets, *pair), *outs)


def last_kernel(share, packed, blocks, held, came, *rest):
    *rest, out = rest
    solved, results = rest[: packed.shape[0]], rest[packed.shape[0] :]
    part = products(dot, share, joined(held, came)[0].astype(BF16), blocks, 0, OWN_DIAG)
    result = (solved[0][...].astype(F32) - part).astype(BF16)
    size = out.shape[1] // 2
    for level in range(packed.shape[0]):
        *owners, _ = unpack(packed, level)
        for which, array in enumerate((solved[level], results[level - 1] if level else result)):
            for half in range(2):
                out[owners[half], which * size : (which + 1) * size] = array[half * size : (half + 1) * size]


def call(kernel, outs, *args, anywhere=0, scratch=()):
    vmem, kept = [pl.BlockSpec(memory_space=space) for space in (pltpu.VMEM, pl.ANY)]
    specs = [vmem] + [kept] * anywhere + [vmem] * (len(args) - 1 - anywhere)
    return pl.pallas_call(
        kernel,
        out_shape=outs,
        in_specs=specs,
        out_specs=[vmem] * len(outs),
        scratch_shapes=scratch,
        compiler_params=pltpu.CompilerParams(vmem_limit_bytes=16 * 2**20),
    )(*args)


def local(right_side, diag_inverse, off_blocks, columns, plan):
    rows, depth, width = right_side.shape
    doms = lax.axis_size("dom")
    levs = lax.axis_size("level")
    levels = levs // 2
    share = depth // levs
    count = 2 * rows
    dom = lax.axis_index("dom")
    turn = dom % 2
    lev = lax.axis_index("level")
    near_pairs = [(i, i ^ 1) for i in range(doms)]
    far_pairs = [(i, ((i + 1) ^ 1) - 1) for i in range(1, doms - 1)] + [(0, doms - 1), (doms - 1, 0)]

    ids = jnp.arange(levs, dtype=jnp.int32)
    own_level = jnp.sum(jnp.where(ids == lev, plan, 0)) // 2
    inverse = jnp.sum(jnp.where(plan[None, :] == ids[:, None], ids[None, :], 0), axis=1)
    side_of = jnp.where(jnp.arange(levels) % 2 == 1, 2 * turn, 2 - 2 * turn)
    packed = inverse[0::2] + (inverse[1::2] << BITS) + (side_of << (2 * BITS))
    packed = jnp.broadcast_to(packed[:, None], (levels, 128)).astype(jnp.int32)

    low = own_level % 2 == turn
    pieces = jnp.where(low, off_blocks[:, 2], off_blocks[:, 0])
    pieces = jnp.stack([diag_inverse, off_blocks[:, 1], pieces], axis=1)
    mates = jnp.stack([diag_inverse, jnp.where(low, off_blocks[:, 0], off_blocks[:, 2])], axis=1)

    chips = levs // 2
    ring = [(2 * y, 2 * ((y + 1) % chips)) for y in range(chips)]
    ring += [(2 * y + 1, 2 * ((y - 1) % chips) + 1) for y in range(chips)]
    cores = [(i, i ^ 1) for i in range(levs)]
    pieces = jnp.stack([pieces, lax.ppermute(pieces, "level", cores)])
    came = lax.ppermute(pieces, "level", ring)
    by_near = lax.ppermute(mates, "dom", near_pairs)
    by_far = lax.ppermute(mates, "dom", far_pairs)
    mates = jnp.where(own_level % 2 == 1, by_near, by_far)
    mates = jnp.stack([mates, lax.ppermute(mates, "level", cores)])
    came = jnp.concatenate([came, lax.ppermute(mates, "level", ring)], axis=2)
    core, chip = lev % 2, lev // 2
    arrays = [pieces, mates]
    places = [2 * chip + core, 2 * chip + 1 - core]
    for step in range(1, chips // 2 + 1):
        if step > 1:
            came = lax.ppermute(came if step < chips // 2 else came[:1], "level", ring)
        shared = lax.ppermute(came, "level", cores)
        for array, side in ((came, core), (shared, 1 - core)):
            arrays.append(array)
            there = (chip - step + 2 * step * side) % chips
            places += [2 * there + side, 2 * there + 1 - side][: array.shape[0]]
    places = jnp.stack(places)
    slots = jnp.sum(jnp.where(places[:, None] == ids, plan, 0), axis=1)
    slots = jnp.broadcast_to(slots[:, None], (levs, 128)).astype(jnp.int32)

    first = jnp.einsum("rkb,rbc->rkc", right_side, diag_inverse, preferred_element_type=F32)
    side = jnp.where(own_level == 0, first.astype(BF16), right_side)
    side = side.reshape(rows, levs, share, width)
    side = lax.all_to_all(side, "level", 1, 0, tiled=False)
    side = side.reshape(levs, rows * share, width)[inverse].reshape(levels, count * share, width)

    near_dom = dom + 1 - 2 * turn
    far_dom = (dom - 1 + 2 * turn) % doms
    part = jnp.stack(
        [
            lax.dynamic_slice_in_dim(columns, which * levs * rows, levs * rows, 0)
            for which in (dom, near_dom, far_dom)
        ]
    )
    part = part.reshape(3, levs, rows * 3)[:, inverse].reshape(3, levels, count, 3)
    second = jnp.roll(inverse[1::2], 1)[None, :, None, None]
    met = jnp.where(part // rows % levs == second, rows, 0) + part % rows
    odd = (jnp.arange(levels) % 2 == 1)[:, None]
    meets_own = met[0]
    meets_mate = jnp.where(odd[..., None], met[1], met[2])
    ahead = odd == (turn == 0)
    own_mate = jnp.where(ahead, meets_own[..., 0], meets_own[..., 2])
    mate_own = jnp.where(ahead, meets_mate[..., 0], meets_mate[..., 2])
    k = jnp.arange(share, dtype=jnp.int32)
    span = count * share
    targets = jnp.stack([meets_own[..., 1], mate_own, own_mate + count], axis=1) * share
    targets = (targets[..., None] + k).reshape(levels, 3 * span)
    targets, meets = targets[:, None, :], targets[:, :, None]

    vector = jax.ShapeDtypeStruct((count * share, width), BF16)
    sums = [jax.ShapeDtypeStruct((2 * span, width), kind) for kind in (F32, BF16)]

    def swap(vector, level):
        return lax.ppermute(vector, "dom", far_pairs if level % 2 == 0 else near_pairs)

    side_mates = swap(side[0::2], 0), swap(side[1::2], 1)
    packed, slots, side, targets, meets, side_mates, arrays = lax.optimization_barrier(
        (packed, slots, side, targets, meets, side_mates, arrays)
    )
    kernel_scratch = [pltpu.SemaphoreType.DMA((levs + 2,))]
    outs = [jax.ShapeDtypeStruct((levs, rows, 5, width, width), BF16)]
    (blocks,) = call(arrange_kernel, outs, slots, *arrays, anywhere=len(arrays), scratch=kernel_scratch)
    blocks = blocks.reshape(levels, count, 5, width, width)

    solved = [side[0]]
    solved_mate = [side_mates[0][0]]
    kernel = functools.partial(entry_kernel, 1, 1, share)
    held, sent = call(kernel, sums, blocks, meets, solved[0], solved_mate[0])
    for level in range(1, levels):
        kernel = functools.partial(forward_pair_kernel, level, level, share, level == levels - 1)
        args = blocks, meets, targets, side, side_mates[level % 2][level // 2]
        own, mate, held, sent = call(kernel, [vector] * 2 + sums, *args, held, swap(sent, level))
        solved.append(own)
        solved_mate.append(mate)

    results = [own]
    for level in range(levels - 2, 0, -1):
        kernel = functools.partial(backward_kernel, level, level, share)
        args = blocks, targets, solved[level], solved_mate[level]
        result, held, sent = call(kernel, [vector] + sums, *args, held, swap(sent, level))
        results.append(result)

    dealt = jax.ShapeDtypeStruct((levs, 2 * rows * share, width), BF16)
    kernel = functools.partial(last_kernel, share)
    (dealt,) = call(kernel, [dealt], packed, blocks, held, swap(sent, 0), *solved, *results[::-1])
    dealt = lax.all_to_all(dealt, "level", 0, 0, tiled=False)
    dealt = dealt.reshape(levs, 2, rows, share, width).transpose(1, 2, 0, 3, 4)
    dealt = dealt.reshape(2, rows, depth, width)
    return dealt[0], dealt[1]


def solution(mesh):
    return jax.shard_map(
        local,
        mesh=mesh,
        in_specs=(
            P(("dom", "level"), None, None),
            P(("dom", "level"), None, None),
            P(("dom", "level"), None, None, None),
            P(),
            P(),
        ),
        out_specs=(P(("dom", "level"), None, None), P(("dom", "level"), None, None)),
        check_vma=False,
    )
```

time: 225 us -> 260 us (1.16)
  starting transfers between devices: 100 us -> 135 us
  between operations: 17.1 us -> 3.82 us
  waiting for transfers between devices: 44.6 us -> 56.7 us
  blocking collectives: 26.1 us -> 34.1 us
  Pallas kernels: 19.2 us -> 14.5 us
  other arithmetic: 7.92 us -> 4.9 us
    ppermute x2 -> x11, starting transfers between devices: 3.84 us -> 50.3 us  [the longest x3 15.2 us: local(): came = lax.ppermute(came if step < chips // 2 else came[:1], 'level', ring)]
    ppermute x2 -> x11, waiting for transfers between devices: 3.2 us -> 25.3 us  [the longest x3 18.1 us: local(): came = lax.ppermute(came if step < chips // 2 else came[:1], 'level', ring)]
    all_gather x2 -> x0, waiting for transfers between devices: 18.3 us -> none  [the longest x1 17.4 us: local(): weights = lax.all_gather(weights, 'level')]
    ppermute x18 -> x16, waiting for transfers between devices: 21.9 us -> 30.2 us  [swap(): lax.ppermute(vector, 'dom', far_pairs if level % 2 == 0 else near_pairs)]
    all_to_all x1, blocking collectives: 26.1 us -> 34.1 us  [local(): dealt = lax.all_to_all(dealt, 'level', 0, 0, tiled=False)]
    pallas_call x18 -> x16, Pallas kernels: 19.2 us -> 14.5 us  [call(): pl.pallas_call(kernel, out_shape=outs, in_specs=specs, out_specs=[vmem] *...]
    ppermute x1, starting transfers between devices: 11 us -> 7.75 us  [local(): by_far = lax.ppermute(mates, 'dom', far_pairs)]
    ppermute x18 -> x16, starting transfers between devices: 72 us -> 68.8 us  [swap(): lax.ppermute(vector, 'dom', far_pairs if level % 2 == 0 else near_pairs)]
  transfers between devices with their start and end apart: 25 -> 30, of which waited for: 18 -> 22; matrix products, arithmetic and copies ran while one was open for 6% -> 4% of each run, Pallas kernels for 5% -> 0%
where the time goes in v12:
time: 260 us; the launch traced here: 259 us
  starting transfers between devices  135 us (52%)
  waiting for transfers between devices  56.7 us (22%)
  blocking collectives  34.1 us (13%)
  Pallas kernels  14.5 us (6%)
  local copies, waits for them, and re-layouts  9.68 us (4%)
  other arithmetic  4.9 us (2%)
  between operations  3.82 us (1%)
    ppermute x16, starting transfers between devices, swap(): lax.ppermute(vector, 'dom', far_pairs if level % 2 == 0 else near_pairs)  68.8 us
    all_to_all x1, blocking collectives, local(): dealt = lax.all_to_all(dealt, 'level', 0, 0, tiled=False)  34.1 us
    ppermute x16, waiting for transfers between devices, swap(): lax.ppermute(vector, 'dom', far_pairs if level % 2 == 0 else near_pairs)  30.2 us
    ppermute x3, waiting for transfers between devices, local(): came = lax.ppermute(came if step < chips // 2 else came[:1], 'level', ring)  18.1 us
    ppermute x3, starting transfers between devices, local(): came = lax.ppermute(came if step < chips // 2 else came[:1], 'level', ring)  15.2 us
    pallas_call x16, Pallas kernels, call(): pl.pallas_call(kernel, out_shape=outs, in_specs=specs, out_specs=[vmem] *...  14.5 us
    ppermute x4, starting transfers between devices, local(): shared = lax.ppermute(came, 'level', cores)  13.3 us
    ppermute x1, starting transfers between devices, local(): pieces = jnp.stack([pieces, lax.ppermute(pieces, 'level', cores)])  8.79 us
  transfers between devices with their start and end apart: 30, of which 22 were waited for; matrix products, arithmetic and copies ran while one was open for 4% of the time, Pallas kernels for 0%

profile of v12, /device:TPU:1, one launch (start us, length us, event | category | flops | bytes accessed | tf_op | source)
XLA Modules:
  0.0 258.6 jit_solution(8289825767917058407)
XLA Ops:
  0.6 1.3 fusion.8
  6.6 8.8 %collective-permute-start.2 = (bf16[4,3,128,128]{3,2,1,0:T(8,128)(2,1)S(1)}, bf16[4,3,128,128]{3,2,1,0:T(8,128)(2,1)S(1)}, u32[]{:S(2)}, u32[]{:S(2)}) collective-permute-start(bf16[4,3,128,128]{3,2,1,0:T(8,128)(2,1)S(1)} %get-tuple-element.141), channel_id=1, source_target_pairs={{0,1},{1,0},{2,3},{3,2},{4,5},{5,4},{6,7},{7,6},{8,9},{9,8},{10,11... | collective-permute-start | bytes 1179656 | tf_op jit(solution)/shard_map/ppermute | solution.py:198
  15.5 1.9 collective-permute-start.3
  17.4 7.7 %collective-permute-start.4 = (bf16[4,2,128,128]{3,2,1,0:T(8,128)(2,1)S(1)}, bf16[4,2,128,128]{3,2,1,0:T(8,128)(2,1)S(1)}, u32[]{:S(2)}, u32[]{:S(2)}) collective-permute-start(bf16[4,2,128,128]{3,2,1,0:T(8,128)(2,1)S(1)} %pad_maximum_fusion.3), channel_id=1, source_target_pairs={{16,32},{32,16},{48,64},{64,48},{80,96},{96,80},{112,128},{128,112... | collective-permute-start | bytes 786440 | tf_op jit(solution)/shard_map/ppermute | solution.py:201
  25.3 5.1 %collective-permute-start.6 = (bf16[2,4,3,128,128]{4,3,2,1,0:T(8,128)(2,1)S(1)}, bf16[2,4,3,128,128]{4,3,2,1,0:T(8,128)(2,1)S(1)}, u32[]{:S(2)}, u32[]{:S(2)}) collective-permute-start(bf16[2,4,3,128,128]{4,3,2,1,0:T(8,128)(2,1)S(1)} %pad_maximum_fusion.rest_0_), channel_id=1, source_target_pairs={{0,2},{2,4},{4,6},{6,8},{8,10},{10,12},{12,14},{14,0},{1,15},{3,1}... | collective-permute-start | bytes 2359304 | tf_op jit(solution)/shard_map/ppermute | solution.py:199
  30.4 1.2 collective-permute-done.4
  31.7 2.7 %collective-permute-start.5 = (bf16[4,2,128,128]{3,2,1,0:T(8,128)(2,1)S(1)}, bf16[4,2,128,128]{3,2,1,0:T(8,128)(2,1)S(1)}, u32[]{:S(2)}, u32[]{:S(2)}) collective-permute-start(bf16[4,2,128,128]{3,2,1,0:T(8,128)(2,1)S(1)} %broadcast_select_fusion), channel_id=1, source_target_pairs={{0,1},{1,0},{2,3},{3,2},{4,5},{5,4},{6,7},{7,6},{8,9},{9,8},{10,11... | collective-permute-start | bytes 786440 | tf_op jit(solution)/shard_map/ppermute | solution.py:203
  35.6 5.2 %collective-permute-start.7 = (bf16[2,4,2,128,128]{4,3,2,1,0:T(8,128)(2,1)S(1)}, bf16[2,4,2,128,128]{4,3,2,1,0:T(8,128)(2,1)S(1)}, u32[]{:S(2)}, u32[]{:S(2)}) collective-permute-start(bf16[2,4,2,128,128]{4,3,2,1,0:T(8,128)(2,1)S(1)} %pad_maximum_fusion.1.rest_1_), channel_id=1, source_target_pairs={{0,2},{2,4},{4,6},{6,8},{8,10},{10,12},{12,14},{14,0},{1,15},{3,1}... | collective-permute-start | bytes 1572872 | tf_op jit(solution)/shard_map/ppermute | solution.py:204
  40.9 6.0 %collective-permute-done.7 = bf16[2,4,2,128,128]{4,3,2,1,0:T(8,128)(2,1)S(1)} collective-permute-done((bf16[2,4,2,128,128]{4,3,2,1,0:T(8,128)(2,1)S(1)}, bf16[2,4,2,128,128]{4,3,2,1,0:T(8,128)(2,1)S(1)}, u32[]{:S(2)}, u32[]{:S(2)}) %collective-permute-start.7) | collective-permute-done | bytes 524320 | tf_op jit(solution)/shard_map/ppermute | solution.py:204
  47.0 5.0 %collective-permute-start.9 = (bf16[2,4,5,128,128]{4,3,2,1,0:T(8,128)(2,1)S(1)}, bf16[2,4,5,128,128]{4,3,2,1,0:T(8,128)(2,1)}, u32[]{:S(2)}, u32[]{:S(2)}) collective-permute-start(bf16[2,4,5,128,128]{4,3,2,1,0:T(8,128)(2,1)S(1)} %constant_dynamic-update-slice_fusion.rest_2_), channel_id=1, source_target_pairs={{0,2},{2,4},{4,6},{6,8},{8,10},{10,12},{12,14},{14,0},{1,15},{3,1}... | collective-permute-start | bytes 3932168 | tf_op jit(solution)/shard_map/ppermute | solution.py:210
  52.9 6.0 %all-to-all-start = ((bf16[1,4,16,4,128]{4,3,1,0,2:T(4,128)(2,1)}), bf16[1,4,16,4,128]{4,3,1,0,2:T(4,128)(2,1)S(1)}, u32[]{:S(2)}, u32[]{:S(2)}) async-start(bf16[1,4,16,4,128]{4,3,1,0,2:T(4,128)(2,1)} %copy.53), calls=%async_computation | async-start | bytes 131072 | tf_op jit(solution)/shard_map/all_to_all | solution.py:223
  59.3 8.4 %collective-permute-done.9.rest_4_ = bf16[2,4,5,128,128]{4,3,2,1,0:T(8,128)(2,1)} collective-permute-done((bf16[2,4,5,128,128]{4,3,2,1,0:T(8,128)(2,1)S(1)}, bf16[2,4,5,128,128]{4,3,2,1,0:T(8,128)(2,1)}, u32[]{:S(2)}, u32[]{:S(2)}) %collective-permute-start.9) | collective-permute-done | bytes 1310752 | tf_op jit(solution)/shard_map/ppermute | solution.py:210
  67.7 5.1 %collective-permute-start.11 = (bf16[2,4,5,128,128]{4,3,2,1,0:T(8,128)(2,1)}, bf16[2,4,5,128,128]{4,3,2,1,0:T(8,128)(2,1)}, u32[]{:S(2)}, u32[]{:S(2)}) collective-permute-start(bf16[2,4,5,128,128]{4,3,2,1,0:T(8,128)(2,1)} %collective-permute-done.9.rest_4_), channel_id=1, source_target_pairs={{0,2},{2,4},{4,6},{6,8},{8,10},{10,12},{12,14},{14,0},{1,15},{3,1}... | collective-permute-start | bytes 3932168 | tf_op jit(solution)/shard_map/ppermute | solution.py:210
  77.0 1.9 collective-permute-start.8
  78.9 2.4 collective-permute-start.10
  81.4 6.3 %collective-permute-done.11.rest_6_ = bf16[2,4,5,128,128]{4,3,2,1,0:T(8,128)(2,1)} collective-permute-done((bf16[2,4,5,128,128]{4,3,2,1,0:T(8,128)(2,1)}, bf16[2,4,5,128,128]{4,3,2,1,0:T(8,128)(2,1)}, u32[]{:S(2)}, u32[]{:S(2)}) %collective-permute-start.11) | collective-permute-done | bytes 1310752 | tf_op jit(solution)/shard_map/ppermute | solution.py:210
  87.7 2.0 slice.135
  89.7 5.0 %collective-permute-start.13 = (bf16[1,4,5,128,128]{4,3,2,1,0:T(8,128)(2,1)}, bf16[1,4,5,128,128]{4,3,2,1,0:T(8,128)(2,1)}, u32[]{:S(2)}, u32[]{:S(2)}) collective-permute-start(bf16[1,4,5,128,128]{4,3,2,1,0:T(8,128)(2,1)} %slice.135), channel_id=1, source_target_pairs={{0,2},{2,4},{4,6},{6,8},{8,10},{10,12},{12,14},{14,0},{1,15},{3,1}... | collective-permute-start | bytes 1966088 | tf_op jit(solution)/shard_map/ppermute | solution.py:210
  94.7 2.4 collective-permute-start.12
  99.2 3.3 %collective-permute-done.13.rest_8_ = bf16[1,4,5,128,128]{4,3,2,1,0:T(8,128)(2,1)} collective-permute-done((bf16[1,4,5,128,128]{4,3,2,1,0:T(8,128)(2,1)}, bf16[1,4,5,128,128]{4,3,2,1,0:T(8,128)(2,1)}, u32[]{:S(2)}, u32[]{:S(2)}) %collective-permute-start.13) | collective-permute-done | bytes 655392 | tf_op jit(solution)/shard_map/ppermute | solution.py:210
  102.6 6.6 %collective-permute-start.14 = (bf16[1,4,5,128,128]{4,3,2,1,0:T(8,128)(2,1)}, bf16[1,4,5,128,128]{4,3,2,1,0:T(8,128)(2,1)}, u32[]{:S(2)}, u32[]{:S(2)}) collective-permute-start(bf16[1,4,5,128,128]{4,3,2,1,0:T(8,128)(2,1)} %collective-permute-done.13.rest_8_), channel_id=1, source_target_pairs={{0,1},{1,0},{2,3},{3,2},{4,5},{5,4},{6,7},{7,6},{8,9},{9,8},{10,11... | collective-permute-start | bytes 1966088 | tf_op jit(solution)/shard_map/ppermute | solution.py:211
  109.2 6.7 %collective-permute-start = (bf16[4,32,128]{2,1,0:T(8,128)(2,1)S(1)}, bf16[4,32,128]{2,1,0:T(8,128)(2,1)S(1)}, u32[]{:S(2)}, u32[]{:S(2)}) collective-permute-start(bf16[4,32,128]{2,1,0:T(8,128)(2,1)S(1)} %get-tuple-element.145), channel_id=1, source_target_pairs={{16,32},{32,16},{48,64},{64,48},{80,96},{96,80},{112,128},{128,112... | collective-permute-start | bytes 98312 | tf_op jit(solution)/shard_map/ppermute | solution.py:253
  116.0 1.2 collective-permute-done
  117.2 1.9 collective-permute-start.1
  119.1 2.7 %collective-permute-done.1 = bf16[4,32,128]{2,1,0:T(8,128)(2,1)S(1)} collective-permute-done((bf16[4,32,128]{2,1,0:T(8,128)(2,1)S(1)}, bf16[4,32,128]{2,1,0:T(8,128)(2,1)S(1)}, u32[]{:S(2)}, u32[]{:S(2)}) %collective-permute-start.1) | collective-permute-done | bytes 32800 | tf_op jit(solution)/shard_map/ppermute | solution.py:253
  122.0 4.2 %shard_map.68 = bf16[16,4,5,128,128]{4,3,2,1,0:T(8,128)(2,1)S(1)} custom-call(s32[16,128]{1,0:T(8,128)S(1)} %broadcast_in_dim.84.slots, bf16[2,4,3,128,128]{4,3,2,1,0:T(8,128)(2,1)S(1)} %pad_maximum_fusion.rest_0_, bf16[2,4,2,128,128]{4,3,2,1,0:T(8,128)(2,1)S(1)} %pad_maximum_fusion.1.rest_1_, ...), custom_call_target="tpu_custom_call" | custom-call | tf_op jit(solution)/shard_map/pallas_call | solution.py:159
  126.6 1.9 collective-permute-start.15
  128.6 2.5 collective-permute-done.15.came
  131.8 6.7 %collective-permute-start.16 = (bf16[64,128]{1,0:T(8,128)(2,1)S(1)}, bf16[64,128]{1,0:T(8,128)(2,1)S(1)}, u32[]{:S(2)}, u32[]{:S(2)}) collective-permute-start(bf16[64,128]{1,0:T(8,128)(2,1)S(1)} %get-tuple-element.88), channel_id=1, source_target_pairs={{16,32},{32,16},{48,64},{64,48},{80,96},{96,80},{112,128},{128,112... | collective-permute-start | bytes 49160 | tf_op jit(solution)/shard_map/ppermute | solution.py:253
  140.3 1.9 collective-permute-start.17
  142.2 2.6 collective-permute-done.17.came
  145.4 6.7 %collective-permute-start.18 = (bf16[64,128]{1,0:T(8,128)(2,1)S(1)}, bf16[64,128]{1,0:T(8,128)(2,1)S(1)}, u32[]{:S(2)}, u32[]{:S(2)}) collective-permute-start(bf16[64,128]{1,0:T(8,128)(2,1)S(1)} %get-tuple-element.96), channel_id=1, source_target_pairs={{16,32},{32,16},{48,64},{64,48},{80,96},{96,80},{112,128},{128,112... | collective-permute-start | bytes 49160 | tf_op jit(solution)/shard_map/ppermute | solution.py:253
  153.9 1.9 collective-permute-start.19
  155.8 2.8 %collective-permute-done.19.came = bf16[64,128]{1,0:T(8,128)(2,1)S(1)} collective-permute-done((bf16[64,128]{1,0:T(8,128)(2,1)S(1)}, bf16[64,128]{1,0:T(8,128)(2,1)S(1)}, u32[]{:S(2)}, u32[]{:S(2)}) %collective-permute-start.19) | collective-permute-done | bytes 16416 | tf_op jit(solution)/shard_map/ppermute | solution.py:253
  159.3 6.7 %collective-permute-start.20 = (bf16[64,128]{1,0:T(8,128)(2,1)S(1)}, bf16[64,128]{1,0:T(8,128)(2,1)S(1)}, u32[]{:S(2)}, u32[]{:S(2)}) collective-permute-start(bf16[64,128]{1,0:T(8,128)(2,1)S(1)} %get-tuple-element.104), channel_id=1, source_target_pairs={{16,32},{32,16},{48,64},{64,48},{80,96},{96,80},{112,128},{128,112... | collective-permute-start | bytes 49160 | tf_op jit(solution)/shard_map/ppermute | solution.py:253
  167.8 1.9 collective-permute-start.21
  169.7 2.6 collective-permute-done.21.came
  173.4 6.7 %collective-permute-start.22 = (bf16[64,128]{1,0:T(8,128)(2,1)S(1)}, bf16[64,128]{1,0:T(8,128)(2,1)S(1)}, u32[]{:S(2)}, u32[]{:S(2)}) collective-permute-start(bf16[64,128]{1,0:T(8,128)(2,1)S(1)} %get-tuple-element.110), channel_id=1, source_target_pairs={{16,32},{32,16},{48,64},{64,48},{80,96},{96,80},{112,128},{128,112... | collective-permute-start | bytes 49160 | tf_op jit(solution)/shard_map/ppermute | solution.py:253
  181.9 1.9 collective-permute-start.23
  183.9 2.6 collective-permute-done.23.came
  187.2 6.7 %collective-permute-start.24 = (bf16[64,128]{1,0:T(8,128)(2,1)S(1)}, bf16[64,128]{1,0:T(8,128)(2,1)S(1)}, u32[]{:S(2)}, u32[]{:S(2)}) collective-permute-start(bf16[64,128]{1,0:T(8,128)(2,1)S(1)} %get-tuple-element.114), channel_id=1, source_target_pairs={{16,32},{32,16},{48,64},{64,48},{80,96},{96,80},{112,128},{128,112... | collective-permute-start | bytes 49160 | tf_op jit(solution)/shard_map/ppermute | solution.py:253
  195.8 1.9 collective-permute-start.25
  197.7 2.6 collective-permute-done.25.came
  201.0 6.7 %collective-permute-start.26 = (bf16[64,128]{1,0:T(8,128)(2,1)S(1)}, bf16[64,128]{1,0:T(8,128)(2,1)S(1)}, u32[]{:S(2)}, u32[]{:S(2)}) collective-permute-start(bf16[64,128]{1,0:T(8,128)(2,1)S(1)} %get-tuple-element.118), channel_id=1, source_target_pairs={{16,32},{32,16},{48,64},{64,48},{80,96},{96,80},{112,128},{128,112... | collective-permute-start | bytes 49160 | tf_op jit(solution)/shard_map/ppermute | solution.py:253
  209.6 1.9 collective-permute-start.27
  211.5 2.9 %collective-permute-done.27.came = bf16[64,128]{1,0:T(8,128)(2,1)S(1)} collective-permute-done((bf16[64,128]{1,0:T(8,128)(2,1)S(1)}, bf16[64,128]{1,0:T(8,128)(2,1)S(1)}, u32[]{:S(2)}, u32[]{:S(2)}) %collective-permute-start.27) | collective-permute-done | bytes 16416 | tf_op jit(solution)/shard_map/ppermute | solution.py:253
  215.2 6.7 %collective-permute-start.28 = (bf16[64,128]{1,0:T(8,128)(2,1)S(1)}, bf16[64,128]{1,0:T(8,128)(2,1)S(1)}, u32[]{:S(2)}, u32[]{:S(2)}) collective-permute-start(bf16[64,128]{1,0:T(8,128)(2,1)S(1)} %get-tuple-element.122), channel_id=1, source_target_pairs={{16,32},{32,16},{48,64},{64,48},{80,96},{96,80},{112,128},{128,112... | collective-permute-start | bytes 49160 | tf_op jit(solution)/shard_map/ppermute | solution.py:253
  223.2 34.1 %all_to_all.20 = bf16[16,32,128]{2,1,0:T(8,128)(2,1)S(1)} all-to-all(bf16[16,32,128]{2,1,0:T(8,128)(2,1)S(1)} %shard_map.83), channel_id=1, replica_groups=mesh['dom'=32,'level'=16] {'level'}, dimensions={0} | all-to-all | bytes 262144 | tf_op jit(solution)/shard_map/all_to_all | solution.py:285
  (95 shorter events, 30.7 us)
Async XLA Ops:
  0.6 14.8 %copy-start = (bf16[4,128,128]{2,1,0:T(8,128)(2,1)S(1)}, bf16[4,128,128]{2,1,0:T(8,128)(2,1)}, u32[]{:S(2)}) copy-start(bf16[4,128,128]{2,1,0:T(8,128)(2,1)} %param.6) | copy-start | bytes 393220
  6.6 18.5 %collective-permute-start.2 = (bf16[4,3,128,128]{3,2,1,0:T(8,128)(2,1)S(1)}, bf16[4,3,128,128]{3,2,1,0:T(8,128)(2,1)S(1)}, u32[]{:S(2)}, u32[]{:S(2)}) collective-permute-start(bf16[4,3,128,128]{3,2,1,0:T(8,128)(2,1)S(1)} %get-tuple-element.141), channel_id=1, source_target_pairs={{0,1},{1,0},{2,3},{3,2},{4,5},{5,4},{6,7},{7,6},{8,9},{9,8},{10,11... | collective-permute-start | bytes 1179656 | tf_op jit(solution)/shard_map/ppermute | solution.py:198
  15.5 14.9 %collective-permute-start.3 = (bf16[4,2,128,128]{3,2,1,0:T(8,128)(2,1)S(1)}, bf16[4,2,128,128]{3,2,1,0:T(8,128)(2,1)S(1)}, u32[]{:S(2)}, u32[]{:S(2)}) collective-permute-start(bf16[4,2,128,128]{3,2,1,0:T(8,128)(2,1)S(1)} %pad_maximum_fusion.3), channel_id=1, source_target_pairs={{0,16},{16,0},{32,48},{48,32},{64,80},{80,64},{96,112},{112,96},{1... | collective-permute-start | bytes 786440 | tf_op jit(solution)/shard_map/ppermute | solution.py:200
  17.4 14.2 %collective-permute-start.4 = (bf16[4,2,128,128]{3,2,1,0:T(8,128)(2,1)S(1)}, bf16[4,2,128,128]{3,2,1,0:T(8,128)(2,1)S(1)}, u32[]{:S(2)}, u32[]{:S(2)}) collective-permute-start(bf16[4,2,128,128]{3,2,1,0:T(8,128)(2,1)S(1)} %pad_maximum_fusion.3), channel_id=1, source_target_pairs={{16,32},{32,16},{48,64},{64,48},{80,96},{96,80},{112,128},{128,112... | collective-permute-start | bytes 786440 | tf_op jit(solution)/shard_map/ppermute | solution.py:201
  25.3 15.5 %collective-permute-start.6 = (bf16[2,4,3,128,128]{4,3,2,1,0:T(8,128)(2,1)S(1)}, bf16[2,4,3,128,128]{4,3,2,1,0:T(8,128)(2,1)S(1)}, u32[]{:S(2)}, u32[]{:S(2)}) collective-permute-start(bf16[2,4,3,128,128]{4,3,2,1,0:T(8,128)(2,1)S(1)} %pad_maximum_fusion.rest_0_), channel_id=1, source_target_pairs={{0,2},{2,4},{4,6},{6,8},{8,10},{10,12},{12,14},{14,0},{1,15},{3,1}... | collective-permute-start | bytes 2359304 | tf_op jit(solution)/shard_map/ppermute | solution.py:199
  31.7 3.9 %collective-permute-start.5 = (bf16[4,2,128,128]{3,2,1,0:T(8,128)(2,1)S(1)}, bf16[4,2,128,128]{3,2,1,0:T(8,128)(2,1)S(1)}, u32[]{:S(2)}, u32[]{:S(2)}) collective-permute-start(bf16[4,2,128,128]{3,2,1,0:T(8,128)(2,1)S(1)} %broadcast_select_fusion), channel_id=1, source_target_pairs={{0,1},{1,0},{2,3},{3,2},{4,5},{5,4},{6,7},{7,6},{8,9},{9,8},{10,11... | collective-permute-start | bytes 786440 | tf_op jit(solution)/shard_map/ppermute | solution.py:203
  35.6 16.5 %copy-start.1 = (bf16[4,64,128]{2,1,0:T(8,128)(2,1)S(1)}, bf16[4,64,128]{2,1,0:T(8,128)(2,1)}, u32[]{:S(2)}) copy-start(bf16[4,64,128]{2,1,0:T(8,128)(2,1)} %param.5) | copy-start | bytes 196612
  35.6 11.3 %collective-permute-start.7 = (bf16[2,4,2,128,128]{4,3,2,1,0:T(8,128)(2,1)S(1)}, bf16[2,4,2,128,128]{4,3,2,1,0:T(8,128)(2,1)S(1)}, u32[]{:S(2)}, u32[]{:S(2)}) collective-permute-start(bf16[2,4,2,128,128]{4,3,2,1,0:T(8,128)(2,1)S(1)} %pad_maximum_fusion.1.rest_1_), channel_id=1, source_target_pairs={{0,2},{2,4},{4,6},{6,8},{8,10},{10,12},{12,14},{14,0},{1,15},{3,1}... | collective-permute-start | bytes 1572872 | tf_op jit(solution)/shard_map/ppermute | solution.py:204
  40.9 18.1 %copy-start.2 = (s32[16]{0:T(128)S(1)}, s32[16]{0:T(128)}, u32[]{:S(2)}) copy-start(s32[16]{0:T(128)} %param.9) | copy-start | bytes 196
  47.0 20.7 %collective-permute-start.9 = (bf16[2,4,5,128,128]{4,3,2,1,0:T(8,128)(2,1)S(1)}, bf16[2,4,5,128,128]{4,3,2,1,0:T(8,128)(2,1)}, u32[]{:S(2)}, u32[]{:S(2)}) collective-permute-start(bf16[2,4,5,128,128]{4,3,2,1,0:T(8,128)(2,1)S(1)} %constant_dynamic-update-slice_fusion.rest_2_), channel_id=1, source_target_pairs={{0,2},{2,4},{4,6},{6,8},{8,10},{10,12},{12,14},{14,0},{1,15},{3,1}... | collective-permute-start | bytes 3932168 | tf_op jit(solution)/shard_map/ppermute | solution.py:210
  52.9 45.7 %all-to-all-start = ((bf16[1,4,16,4,128]{4,3,1,0,2:T(4,128)(2,1)}), bf16[1,4,16,4,128]{4,3,1,0,2:T(4,128)(2,1)S(1)}, u32[]{:S(2)}, u32[]{:S(2)}) async-start(bf16[1,4,16,4,128]{4,3,1,0,2:T(4,128)(2,1)} %copy.53), calls=%async_computation | async-start | bytes 131072 | tf_op jit(solution)/shard_map/all_to_all | solution.py:223
  67.7 20.0 %collective-permute-start.11 = (bf16[2,4,5,128,128]{4,3,2,1,0:T(8,128)(2,1)}, bf16[2,4,5,128,128]{4,3,2,1,0:T(8,128)(2,1)}, u32[]{:S(2)}, u32[]{:S(2)}) collective-permute-start(bf16[2,4,5,128,128]{4,3,2,1,0:T(8,128)(2,1)} %collective-permute-done.9.rest_4_), channel_id=1, source_target_pairs={{0,2},{2,4},{4,6},{6,8},{8,10},{10,12},{12,14},{14,0},{1,15},{3,1}... | collective-permute-start | bytes 3932168 | tf_op jit(solution)/shard_map/ppermute | solution.py:210
  77.0 44.8 %collective-permute-start.8 = (bf16[2,4,5,128,128]{4,3,2,1,0:T(8,128)(2,1)S(1)}, bf16[2,4,5,128,128]{4,3,2,1,0:T(8,128)(2,1)}, u32[]{:S(2)}, u32[]{:S(2)}) collective-permute-start(bf16[2,4,5,128,128]{4,3,2,1,0:T(8,128)(2,1)S(1)} %constant_dynamic-update-slice_fusion.rest_2_), channel_id=1, source_target_pairs={{0,1},{1,0},{2,3},{3,2},{4,5},{5,4},{6,7},{7,6},{8,9},{9,8},{10,11... | collective-permute-start | bytes 3932168 | tf_op jit(solution)/shard_map/ppermute | solution.py:211
  78.9 42.9 %collective-permute-start.10 = (bf16[2,4,5,128,128]{4,3,2,1,0:T(8,128)(2,1)}, bf16[2,4,5,128,128]{4,3,2,1,0:T(8,128)(2,1)}, u32[]{:S(2)}, u32[]{:S(2)}) collective-permute-start(bf16[2,4,5,128,128]{4,3,2,1,0:T(8,128)(2,1)} %collective-permute-done.9.rest_4_), channel_id=1, source_target_pairs={{0,1},{1,0},{2,3},{3,2},{4,5},{5,4},{6,7},{7,6},{8,9},{9,8},{10,11... | collective-permute-start | bytes 3932168 | tf_op jit(solution)/shard_map/ppermute | solution.py:211
  89.7 12.8 %collective-permute-start.13 = (bf16[1,4,5,128,128]{4,3,2,1,0:T(8,128)(2,1)}, bf16[1,4,5,128,128]{4,3,2,1,0:T(8,128)(2,1)}, u32[]{:S(2)}, u32[]{:S(2)}) collective-permute-start(bf16[1,4,5,128,128]{4,3,2,1,0:T(8,128)(2,1)} %slice.135), channel_id=1, source_target_pairs={{0,2},{2,4},{4,6},{6,8},{8,10},{10,12},{12,14},{14,0},{1,15},{3,1}... | collective-permute-start | bytes 1966088 | tf_op jit(solution)/shard_map/ppermute | solution.py:210
  94.7 27.1 %collective-permute-start.12 = (bf16[2,4,5,128,128]{4,3,2,1,0:T(8,128)(2,1)}, bf16[2,4,5,128,128]{4,3,2,1,0:T(8,128)(2,1)}, u32[]{:S(2)}, u32[]{:S(2)}) collective-permute-start(bf16[2,4,5,128,128]{4,3,2,1,0:T(8,128)(2,1)} %collective-permute-done.11.rest_6_), channel_id=1, source_target_pairs={{0,1},{1,0},{2,3},{3,2},{4,5},{5,4},{6,7},{7,6},{8,9},{9,8},{10,11... | collective-permute-start | bytes 3932168 | tf_op jit(solution)/shard_map/ppermute | solution.py:211
  102.6 19.3 %collective-permute-start.14 = (bf16[1,4,5,128,128]{4,3,2,1,0:T(8,128)(2,1)}, bf16[1,4,5,128,128]{4,3,2,1,0:T(8,128)(2,1)}, u32[]{:S(2)}, u32[]{:S(2)}) collective-permute-start(bf16[1,4,5,128,128]{4,3,2,1,0:T(8,128)(2,1)} %collective-permute-done.13.rest_8_), channel_id=1, source_target_pairs={{0,1},{1,0},{2,3},{3,2},{4,5},{5,4},{6,7},{7,6},{8,9},{9,8},{10,11... | collective-permute-start | bytes 1966088 | tf_op jit(solution)/shard_map/ppermute | solution.py:211
  109.2 8.0 %collective-permute-start = (bf16[4,32,128]{2,1,0:T(8,128)(2,1)S(1)}, bf16[4,32,128]{2,1,0:T(8,128)(2,1)S(1)}, u32[]{:S(2)}, u32[]{:S(2)}) collective-permute-start(bf16[4,32,128]{2,1,0:T(8,128)(2,1)S(1)} %get-tuple-element.145), channel_id=1, source_target_pairs={{16,32},{32,16},{48,64},{64,48},{80,96},{96,80},{112,128},{128,112... | collective-permute-start | bytes 98312 | tf_op jit(solution)/shard_map/ppermute | solution.py:253
  117.2 4.6 %collective-permute-start.1 = (bf16[4,32,128]{2,1,0:T(8,128)(2,1)S(1)}, bf16[4,32,128]{2,1,0:T(8,128)(2,1)S(1)}, u32[]{:S(2)}, u32[]{:S(2)}) collective-permute-start(bf16[4,32,128]{2,1,0:T(8,128)(2,1)S(1)} %get-tuple-element.144), channel_id=1, source_target_pairs={{0,16},{16,0},{32,48},{48,32},{64,80},{80,64},{96,112},{112,96},{1... | collective-permute-start | bytes 98312 | tf_op jit(solution)/shard_map/ppermute | solution.py:253
  126.6 4.5 %collective-permute-start.15 = (bf16[64,128]{1,0:T(8,128)(2,1)S(1)}, bf16[64,128]{1,0:T(8,128)(2,1)S(1)}, u32[]{:S(2)}, u32[]{:S(2)}) collective-permute-start(bf16[64,128]{1,0:T(8,128)(2,1)S(1)} %get-tuple-element.84), channel_id=1, source_target_pairs={{0,16},{16,0},{32,48},{48,32},{64,80},{80,64},{96,112},{112,96},{1... | collective-permute-start | bytes 49160 | tf_op jit(solution)/shard_map/ppermute | solution.py:253
  131.8 7.8 %collective-permute-start.16 = (bf16[64,128]{1,0:T(8,128)(2,1)S(1)}, bf16[64,128]{1,0:T(8,128)(2,1)S(1)}, u32[]{:S(2)}, u32[]{:S(2)}) collective-permute-start(bf16[64,128]{1,0:T(8,128)(2,1)S(1)} %get-tuple-element.88), channel_id=1, source_target_pairs={{16,32},{32,16},{48,64},{64,48},{80,96},{96,80},{112,128},{128,112... | collective-permute-start | bytes 49160 | tf_op jit(solution)/shard_map/ppermute | solution.py:253
  140.3 4.5 %collective-permute-start.17 = (bf16[64,128]{1,0:T(8,128)(2,1)S(1)}, bf16[64,128]{1,0:T(8,128)(2,1)S(1)}, u32[]{:S(2)}, u32[]{:S(2)}) collective-permute-start(bf16[64,128]{1,0:T(8,128)(2,1)S(1)} %get-tuple-element.92), channel_id=1, source_target_pairs={{0,16},{16,0},{32,48},{48,32},{64,80},{80,64},{96,112},{112,96},{1... | collective-permute-start | bytes 49160 | tf_op jit(solution)/shard_map/ppermute | solution.py:253
  145.4 7.8 %collective-permute-start.18 = (bf16[64,128]{1,0:T(8,128)(2,1)S(1)}, bf16[64,128]{1,0:T(8,128)(2,1)S(1)}, u32[]{:S(2)}, u32[]{:S(2)}) collective-permute-start(bf16[64,128]{1,0:T(8,128)(2,1)S(1)} %get-tuple-element.96), channel_id=1, source_target_pairs={{16,32},{32,16},{48,64},{64,48},{80,96},{96,80},{112,128},{128,112... | collective-permute-start | bytes 49160 | tf_op jit(solution)/shard_map/ppermute | solution.py:253
  153.9 4.8 %collective-permute-start.19 = (bf16[64,128]{1,0:T(8,128)(2,1)S(1)}, bf16[64,128]{1,0:T(8,128)(2,1)S(1)}, u32[]{:S(2)}, u32[]{:S(2)}) collective-permute-start(bf16[64,128]{1,0:T(8,128)(2,1)S(1)} %get-tuple-element.100), channel_id=1, source_target_pairs={{0,16},{16,0},{32,48},{48,32},{64,80},{80,64},{96,112},{112,96},{1... | collective-permute-start | bytes 49160 | tf_op jit(solution)/shard_map/ppermute | solution.py:253
  159.3 7.8 %collective-permute-start.20 = (bf16[64,128]{1,0:T(8,128)(2,1)S(1)}, bf16[64,128]{1,0:T(8,128)(2,1)S(1)}, u32[]{:S(2)}, u32[]{:S(2)}) collective-permute-start(bf16[64,128]{1,0:T(8,128)(2,1)S(1)} %get-tuple-element.104), channel_id=1, source_target_pairs={{16,32},{32,16},{48,64},{64,48},{80,96},{96,80},{112,128},{128,112... | collective-permute-start | bytes 49160 | tf_op jit(solution)/shard_map/ppermute | solution.py:253
  167.8 4.5 %collective-permute-start.21 = (bf16[64,128]{1,0:T(8,128)(2,1)S(1)}, bf16[64,128]{1,0:T(8,128)(2,1)S(1)}, u32[]{:S(2)}, u32[]{:S(2)}) collective-permute-start(bf16[64,128]{1,0:T(8,128)(2,1)S(1)} %get-tuple-element.108), channel_id=1, source_target_pairs={{0,16},{16,0},{32,48},{48,32},{64,80},{80,64},{96,112},{112,96},{1... | collective-permute-start | bytes 49160 | tf_op jit(solution)/shard_map/ppermute | solution.py:253
  173.4 7.8 %collective-permute-start.22 = (bf16[64,128]{1,0:T(8,128)(2,1)S(1)}, bf16[64,128]{1,0:T(8,128)(2,1)S(1)}, u32[]{:S(2)}, u32[]{:S(2)}) collective-permute-start(bf16[64,128]{1,0:T(8,128)(2,1)S(1)} %get-tuple-element.110), channel_id=1, source_target_pairs={{16,32},{32,16},{48,64},{64,48},{80,96},{96,80},{112,128},{128,112... | collective-permute-start | bytes 49160 | tf_op jit(solution)/shard_map/ppermute | solution.py:253
  181.9 4.5 %collective-permute-start.23 = (bf16[64,128]{1,0:T(8,128)(2,1)S(1)}, bf16[64,128]{1,0:T(8,128)(2,1)S(1)}, u32[]{:S(2)}, u32[]{:S(2)}) collective-permute-start(bf16[64,128]{1,0:T(8,128)(2,1)S(1)} %get-tuple-element.112), channel_id=1, source_target_pairs={{0,16},{16,0},{32,48},{48,32},{64,80},{80,64},{96,112},{112,96},{1... | collective-permute-start | bytes 49160 | tf_op jit(solution)/shard_map/ppermute | solution.py:253
  187.2 7.8 %collective-permute-start.24 = (bf16[64,128]{1,0:T(8,128)(2,1)S(1)}, bf16[64,128]{1,0:T(8,128)(2,1)S(1)}, u32[]{:S(2)}, u32[]{:S(2)}) collective-permute-start(bf16[64,128]{1,0:T(8,128)(2,1)S(1)} %get-tuple-element.114), channel_id=1, source_target_pairs={{16,32},{32,16},{48,64},{64,48},{80,96},{96,80},{112,128},{128,112... | collective-permute-start | bytes 49160 | tf_op jit(solution)/shard_map/ppermute | solution.py:253
  195.8 4.5 %collective-permute-start.25 = (bf16[64,128]{1,0:T(8,128)(2,1)S(1)}, bf16[64,128]{1,0:T(8,128)(2,1)S(1)}, u32[]{:S(2)}, u32[]{:S(2)}) collective-permute-start(bf16[64,128]{1,0:T(8,128)(2,1)S(1)} %get-tuple-element.116), channel_id=1, source_target_pairs={{0,16},{16,0},{32,48},{48,32},{64,80},{80,64},{96,112},{112,96},{1... | collective-permute-start | bytes 49160 | tf_op jit(solution)/shard_map/ppermute | solution.py:253
  201.0 7.8 %collective-permute-start.26 = (bf16[64,128]{1,0:T(8,128)(2,1)S(1)}, bf16[64,128]{1,0:T(8,128)(2,1)S(1)}, u32[]{:S(2)}, u32[]{:S(2)}) collective-permute-start(bf16[64,128]{1,0:T(8,128)(2,1)S(1)} %get-tuple-element.118), channel_id=1, source_target_pairs={{16,32},{32,16},{48,64},{64,48},{80,96},{96,80},{112,128},{128,112... | collective-permute-start | bytes 49160 | tf_op jit(solution)/shard_map/ppermute | solution.py:253
  209.6 4.8 %collective-permute-start.27 = (bf16[64,128]{1,0:T(8,128)(2,1)S(1)}, bf16[64,128]{1,0:T(8,128)(2,1)S(1)}, u32[]{:S(2)}, u32[]{:S(2)}) collective-permute-start(bf16[64,128]{1,0:T(8,128)(2,1)S(1)} %get-tuple-element.120), channel_id=1, source_target_pairs={{0,16},{16,0},{32,48},{48,32},{64,80},{80,64},{96,112},{112,96},{1... | collective-permute-start | bytes 49160 | tf_op jit(solution)/shard_map/ppermute | solution.py:253
  215.2 7.8 %collective-permute-start.28 = (bf16[64,128]{1,0:T(8,128)(2,1)S(1)}, bf16[64,128]{1,0:T(8,128)(2,1)S(1)}, u32[]{:S(2)}, u32[]{:S(2)}) collective-permute-start(bf16[64,128]{1,0:T(8,128)(2,1)S(1)} %get-tuple-element.122), channel_id=1, source_target_pairs={{16,32},{32,16},{48,64},{64,48},{80,96},{96,80},{112,128},{128,112... | collective-permute-start | bytes 49160 | tf_op jit(solution)/shard_map/ppermute | solution.py:253

commit v13 on v11

--- a/solution.py
+++ b/solution.py
@@ -221,15 +221,15 @@
     ids = jnp.arange(levs, dtype=jnp.int32)
     own_level = jnp.sum(jnp.where(ids == lev, plan, 0)) // 2
     inverse = jnp.sum(jnp.where(plan[None, :] == ids[:, None], ids[None, :], 0), axis=1)
-    side_of = jnp.where(jnp.arange(levels) % 2 == 1, 2 * turn, 2 - 2 * turn)
+    side_of = jnp.where(jnp.arange(levels) % 2 == 0, 2 * turn, 2 - 2 * turn)
     packed = inverse[0::2] + (inverse[1::2] << BITS) + (side_of << (2 * BITS))
     packed = jnp.broadcast_to(packed[:, None], (levels, 128)).astype(jnp.int32)
 
-    here = jnp.where(own_level % 2 == turn, off_blocks[:, 0], off_blocks[:, 2])
+    here = jnp.where(own_level % 2 == turn, off_blocks[:, 2], off_blocks[:, 0])
     mates = jnp.stack([diag_inverse, here], axis=1)
     by_near = lax.ppermute(mates, "dom", near_pairs)
     by_far = lax.ppermute(mates, "dom", far_pairs)
-    mates = jnp.where(own_level % 2 == 1, by_near, by_far)
+    mates = jnp.where(own_level % 2 == 1, by_far, by_near)
     first = jnp.einsum("rkb,rbc->rkc", right_side, diag_inverse, preferred_element_type=F32)
     side = jnp.where(own_level == 0, first.astype(BF16), right_side)
     side = side.reshape(rows, levs, share, width)
@@ -249,8 +249,8 @@
     met = jnp.where(part // rows % levs == second, rows, 0) + part % rows
     odd = (jnp.arange(levels) % 2 == 1)[:, None]
     meets_own = met[0]
-    meets_mate = jnp.where(odd[..., None], met[1], met[2])
-    ahead = odd == (turn == 0)
+    meets_mate = jnp.where(odd[..., None], met[2], met[1])
+    ahead = odd == (turn == 1)
     own_mate = jnp.where(ahead, meets_own[..., 0], meets_own[..., 2])
     mate_own = jnp.where(ahead, meets_mate[..., 0], meets_mate[..., 2])
     k = jnp.arange(share, dtype=jnp.int32)
@@ -267,17 +267,17 @@
     paired = levels - 2
 
     own = side[0]
-    far = lax.ppermute(jnp.stack([own, side[paired]]), "dom", far_pairs)
-    near = lax.ppermute(jnp.stack([own, side[paired + 1]]), "dom", near_pairs)
+    far = lax.ppermute(jnp.stack([own, side[paired + 1]]), "dom", far_pairs)
+    near = lax.ppermute(jnp.stack([own, side[paired]]), "dom", near_pairs)
     mates, packed, side, places, targets, meets, own, far, near = lax.optimization_barrier(
         (mates, packed, side, places, targets, meets, own, far, near)
     )
-    side_mates = [far[1], near[1]]
+    side_mates = [near[1], far[1]]
     far, near = far[0], near[0]
     mates = lax.all_gather(mates, "level")
 
     def swap(vector, level):
-        return lax.ppermute(vector, "dom", far_pairs if level % 2 == 0 else near_pairs)
+        return lax.ppermute(vector, "dom", far_pairs if level % 2 else near_pairs)
 
     def arranged(kernel, levels_now, kinds, copies, behind, *blocks):
         _, *blocks = lax.optimization_barrier((behind, *blocks))
@@ -292,8 +292,8 @@
     for level in range(1, paired):
         if level > 1:
             own = solved[-1]
-            far, near = swap(own, 0), swap(own, 1)
-        solved_mate.append(near if level % 2 == 0 else far)
+            far, near = swap(own, 1), swap(own, 0)
+        solved_mate.append(far if level % 2 == 0 else near)
         args = places, side, far, own, near
         if level == 1:
             scratch = [pltpu.VMEM((1, count, 4, width, width), BF16), pltpu.SemaphoreType.DMA((2,))]

time: 225 us -> 226 us (level)
  starting transfers between devices: 100 us -> 89.9 us
  waiting for transfers between devices: 44.6 us -> 53.3 us
    ppermute x20, starting transfers between devices: 75.9 us -> 66.1 us  [the longest x18 60.6 us: swap(): return lax.ppermute(vector, 'dom', far_pairs if level % 2 else near_pairs)]
    ppermute x20, waiting for transfers between devices: 25.1 us -> 34.2 us  [the longest x18 32.7 us: swap(): return lax.ppermute(vector, 'dom', far_pairs if level % 2 else near_pairs)]
    ppermute x1, starting transfers between devices: 4.83 us -> 1.92 us  [local(): by_near = lax.ppermute(mates, 'dom', near_pairs)]
    ppermute x1, starting transfers between devices: 11 us -> 13.7 us  [local(): by_far = lax.ppermute(mates, 'dom', far_pairs)]
where the time goes in v13:
time: 226 us; the launch traced here: 225 us
  starting transfers between devices  89.9 us (40%)
  waiting for transfers between devices  53.3 us (24%)
  blocking collectives  28.2 us (12%)
  Pallas kernels  19.2 us (8%)
  between operations  17.1 us (8%)
  local copies, waits for them, and re-layouts  8.01 us (4%)
  other arithmetic  7.92 us (4%)
    ppermute x18, starting transfers between devices, swap(): return lax.ppermute(vector, 'dom', far_pairs if level % 2 else near_pairs)  60.6 us
    ppermute x18, waiting for transfers between devices, swap(): return lax.ppermute(vector, 'dom', far_pairs if level % 2 else near_pairs)  32.7 us
    all_to_all x1, blocking collectives, local(): dealt = lax.all_to_all(dealt, 'level', 0, 0, tiled=False)  28.2 us
    pallas_call x18, Pallas kernels, call(): pl.pallas_call(kernel, out_shape=outs, in_specs=specs, out_specs=[pl.Bloc...  19.2 us
    all_gather x1, waiting for transfers between devices, local(): weights = lax.all_gather(weights, 'level')  17.9 us
    ppermute x1, starting transfers between devices, local(): by_far = lax.ppermute(mates, 'dom', far_pairs)  13.7 us
    all_to_all x1, starting transfers between devices, local(): side = lax.all_to_all(side, 'level', 1, 0, tiled=False)  8.07 us
  transfers between devices with their start and end apart: 25, of which 18 were waited for; matrix products, arithmetic and copies ran while one was open for 6% of the time, Pallas kernels for 5%

profile of v13, /device:TPU:1, one launch (start us, length us, event | category | flops | bytes accessed | tf_op | source)
XLA Modules:
  0.0 224.8 jit_solution(6412193924932217995)
XLA Ops:
  7.2 1.9 pad_maximum_fusion
  9.2 1.3 fusion.7
  15.0 13.7 %collective-permute-start = (bf16[4,2,128,128]{3,2,1,0:T(8,128)(2,1)S(1)}, bf16[4,2,128,128]{3,2,1,0:T(8,128)(2,1)S(1)}, u32[]{:S(2)}, u32[]{:S(2)}) collective-permute-start(bf16[4,2,128,128]{3,2,1,0:T(8,128)(2,1)S(1)} %pad_maximum_fusion.1), channel_id=1, source_target_pairs={{16,32},{32,16},{48,64},{64,48},{80,96},{96,80},{112,128},{128,112... | collective-permute-start | bytes 786440 | tf_op jit(solution)/shard_map/ppermute | solution.py:231
  28.7 1.9 collective-permute-start.1
  30.7 1.1 fusion
  32.4 8.1 %all-to-all-start = ((bf16[1,4,16,4,128]{4,3,1,0,2:T(4,128)(2,1)}), bf16[1,4,16,4,128]{4,3,1,0,2:T(4,128)(2,1)S(1)}, u32[]{:S(2)}, u32[]{:S(2)}) async-start(bf16[1,4,16,4,128]{4,3,1,0,2:T(4,128)(2,1)} %copy.64), calls=%async_computation | async-start | bytes 131072 | tf_op jit(solution)/shard_map/all_to_all | solution.py:236
  48.0 1.2 all-to-all-done
  49.8 2.7 %collective-permute-start.2 = (bf16[2,32,128]{2,1,0:T(8,128)(2,1)S(1)}, bf16[2,32,128]{2,1,0:T(8,128)(2,1)S(1)}, u32[]{:S(2)}, u32[]{:S(2)}) collective-permute-start(bf16[2,32,128]{2,1,0:T(8,128)(2,1)S(1)} %get-tuple-element.104), channel_id=1, source_target_pairs={{16,32},{32,16},{48,64},{64,48},{80,96},{96,80},{112,128},{128,112... | collective-permute-start | bytes 49160 | tf_op jit(solution)/shard_map/ppermute | solution.py:270
  52.5 2.8 %collective-permute-start.3 = (bf16[2,32,128]{2,1,0:T(8,128)(2,1)S(1)}, bf16[2,32,128]{2,1,0:T(8,128)(2,1)S(1)}, u32[]{:S(2)}, u32[]{:S(2)}) collective-permute-start(bf16[2,32,128]{2,1,0:T(8,128)(2,1)S(1)} %get-tuple-element.103), channel_id=1, source_target_pairs={{0,16},{16,0},{32,48},{48,32},{64,80},{80,64},{96,112},{112,96},{1... | collective-permute-start | bytes 49160 | tf_op jit(solution)/shard_map/ppermute | solution.py:271
  56.1 1.5 collective-permute-done.2
  57.7 17.9 %all-gather.5.cloned.1.call-done = bf16[64,4,128,128]{3,2,1,0:T(8,128)(2,1)} async-done(((bf16[4,4,128,128]{3,2,1,0:T(8,128)(2,1)}), bf16[64,4,128,128]{3,2,1,0:T(8,128)(2,1)}) %all-gather.5.cloned.1.call-update) | async-done | bytes 8388624 | tf_op jit(solution)/shard_map/all_gather | solution.py:218
  75.7 1.8 shard_map.68.own.solved.rest_1_
  77.5 7.7 %collective-permute-start.4 = (bf16[32,128]{1,0:T(8,128)(2,1)S(1)}, bf16[32,128]{1,0:T(8,128)(2,1)S(1)}, u32[]{:S(2)}, u32[]{:S(2)}) collective-permute-start(bf16[32,128]{1,0:T(8,128)(2,1)S(1)} %shard_map.68.own.solved.rest_1_), channel_id=1, source_target_pairs={{16,32},{32,16},{48,64},{64,48},{80,96},{96,80},{112,128},{128,112... | collective-permute-start | bytes 24584 | tf_op jit(solution)/shard_map/ppermute | solution.py:280
  85.2 1.9 collective-permute-start.5
  87.2 2.4 %shard_map.69.weights = bf16[4,8,4,128,128]{4,3,2,1,0:T(8,128)(2,1)S(1)} custom-call(s32[8,128]{1,0:T(8,128)S(1)} %broadcast_in_dim.73.packed, bf16[16,4,4,128,128]{4,3,2,1,0:T(8,128)(2,1)} %bitcast.77), custom_call_target="tpu_custom_call" | custom-call | tf_op jit(solution)/shard_map/pallas_call | solution.py:195
  90.2 3.9 %collective-permute-start.6 = (bf16[32,128]{1,0:T(8,128)(2,1)S(1)}, bf16[32,128]{1,0:T(8,128)(2,1)S(1)}, u32[]{:S(2)}, u32[]{:S(2)}) collective-permute-start(bf16[32,128]{1,0:T(8,128)(2,1)S(1)} %shard_map.70.own.solved.rest_2_), channel_id=1, source_target_pairs={{16,32},{32,16},{48,64},{64,48},{80,96},{96,80},{112,128},{128,112... | collective-permute-start | bytes 24584 | tf_op jit(solution)/shard_map/ppermute | solution.py:280
  94.1 1.9 collective-permute-start.7
  96.0 1.9 collective-permute-done.6.far
  99.4 4.7 %collective-permute-start.8 = (bf16[32,128]{1,0:T(8,128)(2,1)S(1)}, bf16[32,128]{1,0:T(8,128)(2,1)S(1)}, u32[]{:S(2)}, u32[]{:S(2)}) collective-permute-start(bf16[32,128]{1,0:T(8,128)(2,1)S(1)} %shard_map.71.own.solved.rest_3_), channel_id=1, source_target_pairs={{16,32},{32,16},{48,64},{64,48},{80,96},{96,80},{112,128},{128,112... | collective-permute-start | bytes 24584 | tf_op jit(solution)/shard_map/ppermute | solution.py:280
  104.2 1.9 collective-permute-start.9
  106.1 1.1 collective-permute-done.8.far.solved_mate
  107.1 1.8 collective-permute-done.9.near
  109.5 3.8 %collective-permute-start.10 = (bf16[32,128]{1,0:T(8,128)(2,1)S(1)}, bf16[32,128]{1,0:T(8,128)(2,1)S(1)}, u32[]{:S(2)}, u32[]{:S(2)}) collective-permute-start(bf16[32,128]{1,0:T(8,128)(2,1)S(1)} %shard_map.72.own.solved.rest_4_), channel_id=1, source_target_pairs={{16,32},{32,16},{48,64},{64,48},{80,96},{96,80},{112,128},{128,112... | collective-permute-start | bytes 24584 | tf_op jit(solution)/shard_map/ppermute | solution.py:280
  113.3 1.9 collective-permute-start.11
  115.2 2.0 collective-permute-done.10.far
  118.6 4.5 %collective-permute-start.12 = (bf16[32,128]{1,0:T(8,128)(2,1)S(1)}, bf16[32,128]{1,0:T(8,128)(2,1)S(1)}, u32[]{:S(2)}, u32[]{:S(2)}) collective-permute-start(bf16[32,128]{1,0:T(8,128)(2,1)S(1)} %shard_map.73.own.solved.rest_5_), channel_id=1, source_target_pairs={{16,32},{32,16},{48,64},{64,48},{80,96},{96,80},{112,128},{128,112... | collective-permute-start | bytes 24584 | tf_op jit(solution)/shard_map/ppermute | solution.py:280
  123.2 2.1 shard_map.74.blocks
  125.3 1.1 collective-permute-done.12.mate.solved_mate
  126.8 1.9 collective-permute-start.13
  128.8 2.6 %collective-permute-done.13.came = bf16[64,128]{1,0:T(8,128)(2,1)S(1)} collective-permute-done((bf16[64,128]{1,0:T(8,128)(2,1)S(1)}, bf16[64,128]{1,0:T(8,128)(2,1)S(1)}, u32[]{:S(2)}, u32[]{:S(2)}) %collective-permute-start.13) | collective-permute-done | bytes 16416 | tf_op jit(solution)/shard_map/ppermute | solution.py:280
  132.0 5.2 %collective-permute-start.14 = (bf16[64,128]{1,0:T(8,128)(2,1)S(1)}, bf16[64,128]{1,0:T(8,128)(2,1)S(1)}, u32[]{:S(2)}, u32[]{:S(2)}) collective-permute-start(bf16[64,128]{1,0:T(8,128)(2,1)S(1)} %get-tuple-element.62), channel_id=1, source_target_pairs={{16,32},{32,16},{48,64},{64,48},{80,96},{96,80},{112,128},{128,112... | collective-permute-start | bytes 49160 | tf_op jit(solution)/shard_map/ppermute | solution.py:280
  137.2 2.6 %collective-permute-done.14.came = bf16[64,128]{1,0:T(8,128)(2,1)S(1)} collective-permute-done((bf16[64,128]{1,0:T(8,128)(2,1)S(1)}, bf16[64,128]{1,0:T(8,128)(2,1)S(1)}, u32[]{:S(2)}, u32[]{:S(2)}) %collective-permute-start.14) | collective-permute-done | bytes 16416 | tf_op jit(solution)/shard_map/ppermute | solution.py:280
  139.8 1.1 shard_map.78
  140.9 1.9 collective-permute-start.15
  142.8 2.8 %collective-permute-done.15.came = bf16[64,128]{1,0:T(8,128)(2,1)S(1)} collective-permute-done((bf16[64,128]{1,0:T(8,128)(2,1)S(1)}, bf16[64,128]{1,0:T(8,128)(2,1)S(1)}, u32[]{:S(2)}, u32[]{:S(2)}) %collective-permute-start.15) | collective-permute-done | bytes 16416 | tf_op jit(solution)/shard_map/ppermute | solution.py:280
  146.4 5.2 %collective-permute-start.16 = (bf16[64,128]{1,0:T(8,128)(2,1)S(1)}, bf16[64,128]{1,0:T(8,128)(2,1)S(1)}, u32[]{:S(2)}, u32[]{:S(2)}) collective-permute-start(bf16[64,128]{1,0:T(8,128)(2,1)S(1)} %get-tuple-element.66), channel_id=1, source_target_pairs={{16,32},{32,16},{48,64},{64,48},{80,96},{96,80},{112,128},{128,112... | collective-permute-start | bytes 49160 | tf_op jit(solution)/shard_map/ppermute | solution.py:280
  151.6 3.6 %shard_map.76.blocks = bf16[6,8,5,128,128]{4,3,2,1,0:T(8,128)(2,1)S(1)} custom-call(s32[8,128]{1,0:T(8,128)S(1)} %broadcast_in_dim.73.packed, bf16[16,4,4,128,128]{4,3,2,1,0:T(8,128)(2,1)} %bitcast.79, bf16[16,4,2,128,128]{4,3,2,1,0:T(8,128)(2,1)} %bitcast.81), custom_call_target="tpu_custom_call" | custom-call | tf_op jit(solution)/shard_map/pallas_call | solution.py:195
  156.0 1.9 collective-permute-start.17
  157.9 2.6 %collective-permute-done.17.came = bf16[64,128]{1,0:T(8,128)(2,1)S(1)} collective-permute-done((bf16[64,128]{1,0:T(8,128)(2,1)S(1)}, bf16[64,128]{1,0:T(8,128)(2,1)S(1)}, u32[]{:S(2)}, u32[]{:S(2)}) %collective-permute-start.17) | collective-permute-done | bytes 16416 | tf_op jit(solution)/shard_map/ppermute | solution.py:280
  161.3 4.2 %collective-permute-start.18 = (bf16[64,128]{1,0:T(8,128)(2,1)S(1)}, bf16[64,128]{1,0:T(8,128)(2,1)S(1)}, u32[]{:S(2)}, u32[]{:S(2)}) collective-permute-start(bf16[64,128]{1,0:T(8,128)(2,1)S(1)} %get-tuple-element.70), channel_id=1, source_target_pairs={{16,32},{32,16},{48,64},{64,48},{80,96},{96,80},{112,128},{128,112... | collective-permute-start | bytes 49160 | tf_op jit(solution)/shard_map/ppermute | solution.py:280
  165.4 3.6 %collective-permute-done.18.came = bf16[64,128]{1,0:T(8,128)(2,1)S(1)} collective-permute-done((bf16[64,128]{1,0:T(8,128)(2,1)S(1)}, bf16[64,128]{1,0:T(8,128)(2,1)S(1)}, u32[]{:S(2)}, u32[]{:S(2)}) %collective-permute-start.18) | collective-permute-done | bytes 16416 | tf_op jit(solution)/shard_map/ppermute | solution.py:280
  169.8 1.9 collective-permute-start.19
  171.8 2.6 %collective-permute-done.19.came = bf16[64,128]{1,0:T(8,128)(2,1)S(1)} collective-permute-done((bf16[64,128]{1,0:T(8,128)(2,1)S(1)}, bf16[64,128]{1,0:T(8,128)(2,1)S(1)}, u32[]{:S(2)}, u32[]{:S(2)}) %collective-permute-start.19) | collective-permute-done | bytes 16416 | tf_op jit(solution)/shard_map/ppermute | solution.py:280
  175.1 4.2 %collective-permute-start.20 = (bf16[64,128]{1,0:T(8,128)(2,1)S(1)}, bf16[64,128]{1,0:T(8,128)(2,1)S(1)}, u32[]{:S(2)}, u32[]{:S(2)}) collective-permute-start(bf16[64,128]{1,0:T(8,128)(2,1)S(1)} %get-tuple-element.74), channel_id=1, source_target_pairs={{16,32},{32,16},{48,64},{64,48},{80,96},{96,80},{112,128},{128,112... | collective-permute-start | bytes 49160 | tf_op jit(solution)/shard_map/ppermute | solution.py:280
  179.3 3.6 %collective-permute-done.20.came = bf16[64,128]{1,0:T(8,128)(2,1)S(1)} collective-permute-done((bf16[64,128]{1,0:T(8,128)(2,1)S(1)}, bf16[64,128]{1,0:T(8,128)(2,1)S(1)}, u32[]{:S(2)}, u32[]{:S(2)}) %collective-permute-start.20) | collective-permute-done | bytes 16416 | tf_op jit(solution)/shard_map/ppermute | solution.py:280
  183.7 1.9 collective-permute-start.21
  185.6 2.6 %collective-permute-done.21.came = bf16[64,128]{1,0:T(8,128)(2,1)S(1)} collective-permute-done((bf16[64,128]{1,0:T(8,128)(2,1)S(1)}, bf16[64,128]{1,0:T(8,128)(2,1)S(1)}, u32[]{:S(2)}, u32[]{:S(2)}) %collective-permute-start.21) | collective-permute-done | bytes 16416 | tf_op jit(solution)/shard_map/ppermute | solution.py:280
  188.4 28.2 %all_to_all.20 = bf16[16,32,128]{2,1,0:T(8,128)(2,1)S(1)} all-to-all(bf16[16,32,128]{2,1,0:T(8,128)(2,1)S(1)} %shard_map.85), channel_id=1, replica_groups=mesh['dom'=32,'level'=16] {'level'}, dimensions={0} | all-to-all | bytes 262144 | tf_op jit(solution)/shard_map/all_to_all | solution.py:333
  (80 shorter events, 22.9 us)
Async XLA Ops:
  7.2 68.5 %all-gather.5.cloned.1.call-start = ((), (), s32[]{:S(2)}) async-start(), calls=%async_computation.2 | async-start | bytes 8912896 | tf_op jit(solution)/shard_map/all_gather | solution.py:218
  15.0 40.3 %collective-permute-start = (bf16[4,2,128,128]{3,2,1,0:T(8,128)(2,1)S(1)}, bf16[4,2,128,128]{3,2,1,0:T(8,128)(2,1)S(1)}, u32[]{:S(2)}, u32[]{:S(2)}) collective-permute-start(bf16[4,2,128,128]{3,2,1,0:T(8,128)(2,1)S(1)} %pad_maximum_fusion.1), channel_id=1, source_target_pairs={{16,32},{32,16},{48,64},{64,48},{80,96},{96,80},{112,128},{128,112... | collective-permute-start | bytes 786440 | tf_op jit(solution)/shard_map/ppermute | solution.py:231
  28.7 26.7 %collective-permute-start.1 = (bf16[4,2,128,128]{3,2,1,0:T(8,128)(2,1)S(1)}, bf16[4,2,128,128]{3,2,1,0:T(8,128)(2,1)S(1)}, u32[]{:S(2)}, u32[]{:S(2)}) collective-permute-start(bf16[4,2,128,128]{3,2,1,0:T(8,128)(2,1)S(1)} %pad_maximum_fusion.1), channel_id=1, source_target_pairs={{0,16},{16,0},{32,48},{48,32},{64,80},{80,64},{96,112},{112,96},{1... | collective-permute-start | bytes 786440 | tf_op jit(solution)/shard_map/ppermute | solution.py:230
  32.4 16.7 %all-to-all-start = ((bf16[1,4,16,4,128]{4,3,1,0,2:T(4,128)(2,1)}), bf16[1,4,16,4,128]{4,3,1,0,2:T(4,128)(2,1)S(1)}, u32[]{:S(2)}, u32[]{:S(2)}) async-start(bf16[1,4,16,4,128]{4,3,1,0,2:T(4,128)(2,1)} %copy.64), calls=%async_computation | async-start | bytes 131072 | tf_op jit(solution)/shard_map/all_to_all | solution.py:236
  40.5 82.7 %all-gather.7.cloned.1.call-start = ((), (), s32[]{:S(2)}) async-start(), calls=%async_computation.3 | async-start | bytes 4456448 | tf_op jit(solution)/shard_map/all_gather | solution.py:277
  49.8 7.8 %collective-permute-start.2 = (bf16[2,32,128]{2,1,0:T(8,128)(2,1)S(1)}, bf16[2,32,128]{2,1,0:T(8,128)(2,1)S(1)}, u32[]{:S(2)}, u32[]{:S(2)}) collective-permute-start(bf16[2,32,128]{2,1,0:T(8,128)(2,1)S(1)} %get-tuple-element.104), channel_id=1, source_target_pairs={{16,32},{32,16},{48,64},{64,48},{80,96},{96,80},{112,128},{128,112... | collective-permute-start | bytes 49160 | tf_op jit(solution)/shard_map/ppermute | solution.py:270
  52.5 5.1 %collective-permute-start.3 = (bf16[2,32,128]{2,1,0:T(8,128)(2,1)S(1)}, bf16[2,32,128]{2,1,0:T(8,128)(2,1)S(1)}, u32[]{:S(2)}, u32[]{:S(2)}) collective-permute-start(bf16[2,32,128]{2,1,0:T(8,128)(2,1)S(1)} %get-tuple-element.103), channel_id=1, source_target_pairs={{0,16},{16,0},{32,48},{48,32},{64,80},{80,64},{96,112},{112,96},{1... | collective-permute-start | bytes 49160 | tf_op jit(solution)/shard_map/ppermute | solution.py:271
  77.5 12.1 %collective-permute-start.4 = (bf16[32,128]{1,0:T(8,128)(2,1)S(1)}, bf16[32,128]{1,0:T(8,128)(2,1)S(1)}, u32[]{:S(2)}, u32[]{:S(2)}) collective-permute-start(bf16[32,128]{1,0:T(8,128)(2,1)S(1)} %shard_map.68.own.solved.rest_1_), channel_id=1, source_target_pairs={{16,32},{32,16},{48,64},{64,48},{80,96},{96,80},{112,128},{128,112... | collective-permute-start | bytes 24584 | tf_op jit(solution)/shard_map/ppermute | solution.py:280
  85.2 4.4 %collective-permute-start.5 = (bf16[32,128]{1,0:T(8,128)(2,1)S(1)}, bf16[32,128]{1,0:T(8,128)(2,1)S(1)}, u32[]{:S(2)}, u32[]{:S(2)}) collective-permute-start(bf16[32,128]{1,0:T(8,128)(2,1)S(1)} %shard_map.68.own.solved.rest_1_), channel_id=1, source_target_pairs={{0,16},{16,0},{32,48},{48,32},{64,80},{80,64},{96,112},{112,96},{1... | collective-permute-start | bytes 24584 | tf_op jit(solution)/shard_map/ppermute | solution.py:280
  90.2 7.7 %collective-permute-start.6 = (bf16[32,128]{1,0:T(8,128)(2,1)S(1)}, bf16[32,128]{1,0:T(8,128)(2,1)S(1)}, u32[]{:S(2)}, u32[]{:S(2)}) collective-permute-start(bf16[32,128]{1,0:T(8,128)(2,1)S(1)} %shard_map.70.own.solved.rest_2_), channel_id=1, source_target_pairs={{16,32},{32,16},{48,64},{64,48},{80,96},{96,80},{112,128},{128,112... | collective-permute-start | bytes 24584 | tf_op jit(solution)/shard_map/ppermute | solution.py:280
  94.1 4.8 %collective-permute-start.7 = (bf16[32,128]{1,0:T(8,128)(2,1)S(1)}, bf16[32,128]{1,0:T(8,128)(2,1)S(1)}, u32[]{:S(2)}, u32[]{:S(2)}) collective-permute-start(bf16[32,128]{1,0:T(8,128)(2,1)S(1)} %shard_map.70.own.solved.rest_2_), channel_id=1, source_target_pairs={{0,16},{16,0},{32,48},{48,32},{64,80},{80,64},{96,112},{112,96},{1... | collective-permute-start | bytes 24584 | tf_op jit(solution)/shard_map/ppermute | solution.py:280
  99.4 7.7 %collective-permute-start.8 = (bf16[32,128]{1,0:T(8,128)(2,1)S(1)}, bf16[32,128]{1,0:T(8,128)(2,1)S(1)}, u32[]{:S(2)}, u32[]{:S(2)}) collective-permute-start(bf16[32,128]{1,0:T(8,128)(2,1)S(1)} %shard_map.71.own.solved.rest_3_), channel_id=1, source_target_pairs={{16,32},{32,16},{48,64},{64,48},{80,96},{96,80},{112,128},{128,112... | collective-permute-start | bytes 24584 | tf_op jit(solution)/shard_map/ppermute | solution.py:280
  104.2 4.8 %collective-permute-start.9 = (bf16[32,128]{1,0:T(8,128)(2,1)S(1)}, bf16[32,128]{1,0:T(8,128)(2,1)S(1)}, u32[]{:S(2)}, u32[]{:S(2)}) collective-permute-start(bf16[32,128]{1,0:T(8,128)(2,1)S(1)} %shard_map.71.own.solved.rest_3_), channel_id=1, source_target_pairs={{0,16},{16,0},{32,48},{48,32},{64,80},{80,64},{96,112},{112,96},{1... | collective-permute-start | bytes 24584 | tf_op jit(solution)/shard_map/ppermute | solution.py:280
  109.5 7.7 %collective-permute-start.10 = (bf16[32,128]{1,0:T(8,128)(2,1)S(1)}, bf16[32,128]{1,0:T(8,128)(2,1)S(1)}, u32[]{:S(2)}, u32[]{:S(2)}) collective-permute-start(bf16[32,128]{1,0:T(8,128)(2,1)S(1)} %shard_map.72.own.solved.rest_4_), channel_id=1, source_target_pairs={{16,32},{32,16},{48,64},{64,48},{80,96},{96,80},{112,128},{128,112... | collective-permute-start | bytes 24584 | tf_op jit(solution)/shard_map/ppermute | solution.py:280
  113.3 4.8 %collective-permute-start.11 = (bf16[32,128]{1,0:T(8,128)(2,1)S(1)}, bf16[32,128]{1,0:T(8,128)(2,1)S(1)}, u32[]{:S(2)}, u32[]{:S(2)}) collective-permute-start(bf16[32,128]{1,0:T(8,128)(2,1)S(1)} %shard_map.72.own.solved.rest_4_), channel_id=1, source_target_pairs={{0,16},{16,0},{32,48},{48,32},{64,80},{80,64},{96,112},{112,96},{1... | collective-permute-start | bytes 24584 | tf_op jit(solution)/shard_map/ppermute | solution.py:280
  118.6 7.7 %collective-permute-start.12 = (bf16[32,128]{1,0:T(8,128)(2,1)S(1)}, bf16[32,128]{1,0:T(8,128)(2,1)S(1)}, u32[]{:S(2)}, u32[]{:S(2)}) collective-permute-start(bf16[32,128]{1,0:T(8,128)(2,1)S(1)} %shard_map.73.own.solved.rest_5_), channel_id=1, source_target_pairs={{16,32},{32,16},{48,64},{64,48},{80,96},{96,80},{112,128},{128,112... | collective-permute-start | bytes 24584 | tf_op jit(solution)/shard_map/ppermute | solution.py:280
  126.8 4.5 %collective-permute-start.13 = (bf16[64,128]{1,0:T(8,128)(2,1)S(1)}, bf16[64,128]{1,0:T(8,128)(2,1)S(1)}, u32[]{:S(2)}, u32[]{:S(2)}) collective-permute-start(bf16[64,128]{1,0:T(8,128)(2,1)S(1)} %get-tuple-element.58), channel_id=1, source_target_pairs={{0,16},{16,0},{32,48},{48,32},{64,80},{80,64},{96,112},{112,96},{1... | collective-permute-start | bytes 49160 | tf_op jit(solution)/shard_map/ppermute | solution.py:280
  132.0 7.8 %collective-permute-start.14 = (bf16[64,128]{1,0:T(8,128)(2,1)S(1)}, bf16[64,128]{1,0:T(8,128)(2,1)S(1)}, u32[]{:S(2)}, u32[]{:S(2)}) collective-permute-start(bf16[64,128]{1,0:T(8,128)(2,1)S(1)} %get-tuple-element.62), channel_id=1, source_target_pairs={{16,32},{32,16},{48,64},{64,48},{80,96},{96,80},{112,128},{128,112... | collective-permute-start | bytes 49160 | tf_op jit(solution)/shard_map/ppermute | solution.py:280
  140.9 4.8 %collective-permute-start.15 = (bf16[64,128]{1,0:T(8,128)(2,1)S(1)}, bf16[64,128]{1,0:T(8,128)(2,1)S(1)}, u32[]{:S(2)}, u32[]{:S(2)}) collective-permute-start(bf16[64,128]{1,0:T(8,128)(2,1)S(1)} %get-tuple-element.64), channel_id=1, source_target_pairs={{0,16},{16,0},{32,48},{48,32},{64,80},{80,64},{96,112},{112,96},{1... | collective-permute-start | bytes 49160 | tf_op jit(solution)/shard_map/ppermute | solution.py:280
  146.4 8.8 %collective-permute-start.16 = (bf16[64,128]{1,0:T(8,128)(2,1)S(1)}, bf16[64,128]{1,0:T(8,128)(2,1)S(1)}, u32[]{:S(2)}, u32[]{:S(2)}) collective-permute-start(bf16[64,128]{1,0:T(8,128)(2,1)S(1)} %get-tuple-element.66), channel_id=1, source_target_pairs={{16,32},{32,16},{48,64},{64,48},{80,96},{96,80},{112,128},{128,112... | collective-permute-start | bytes 49160 | tf_op jit(solution)/shard_map/ppermute | solution.py:280
  156.0 4.5 %collective-permute-start.17 = (bf16[64,128]{1,0:T(8,128)(2,1)S(1)}, bf16[64,128]{1,0:T(8,128)(2,1)S(1)}, u32[]{:S(2)}, u32[]{:S(2)}) collective-permute-start(bf16[64,128]{1,0:T(8,128)(2,1)S(1)} %get-tuple-element.68), channel_id=1, source_target_pairs={{0,16},{16,0},{32,48},{48,32},{64,80},{80,64},{96,112},{112,96},{1... | collective-permute-start | bytes 49160 | tf_op jit(solution)/shard_map/ppermute | solution.py:280
  161.3 7.8 %collective-permute-start.18 = (bf16[64,128]{1,0:T(8,128)(2,1)S(1)}, bf16[64,128]{1,0:T(8,128)(2,1)S(1)}, u32[]{:S(2)}, u32[]{:S(2)}) collective-permute-start(bf16[64,128]{1,0:T(8,128)(2,1)S(1)} %get-tuple-element.70), channel_id=1, source_target_pairs={{16,32},{32,16},{48,64},{64,48},{80,96},{96,80},{112,128},{128,112... | collective-permute-start | bytes 49160 | tf_op jit(solution)/shard_map/ppermute | solution.py:280
  169.8 4.5 %collective-permute-start.19 = (bf16[64,128]{1,0:T(8,128)(2,1)S(1)}, bf16[64,128]{1,0:T(8,128)(2,1)S(1)}, u32[]{:S(2)}, u32[]{:S(2)}) collective-permute-start(bf16[64,128]{1,0:T(8,128)(2,1)S(1)} %get-tuple-element.72), channel_id=1, source_target_pairs={{0,16},{16,0},{32,48},{48,32},{64,80},{80,64},{96,112},{112,96},{1... | collective-permute-start | bytes 49160 | tf_op jit(solution)/shard_map/ppermute | solution.py:280
  175.1 7.8 %collective-permute-start.20 = (bf16[64,128]{1,0:T(8,128)(2,1)S(1)}, bf16[64,128]{1,0:T(8,128)(2,1)S(1)}, u32[]{:S(2)}, u32[]{:S(2)}) collective-permute-start(bf16[64,128]{1,0:T(8,128)(2,1)S(1)} %get-tuple-element.74), channel_id=1, source_target_pairs={{16,32},{32,16},{48,64},{64,48},{80,96},{96,80},{112,128},{128,112... | collective-permute-start | bytes 49160 | tf_op jit(solution)/shard_map/ppermute | solution.py:280
  183.7 4.5 %collective-permute-start.21 = (bf16[64,128]{1,0:T(8,128)(2,1)S(1)}, bf16[64,128]{1,0:T(8,128)(2,1)S(1)}, u32[]{:S(2)}, u32[]{:S(2)}) collective-permute-start(bf16[64,128]{1,0:T(8,128)(2,1)S(1)} %get-tuple-element.76), channel_id=1, source_target_pairs={{0,16},{16,0},{32,48},{48,32},{64,80},{80,64},{96,112},{112,96},{1... | collective-permute-start | bytes 49160 | tf_op jit(solution)/shard_map/ppermute | solution.py:280
Sparse Core Ops, SparseCore 0:
  10.1 65.5 all-gather.4
  77.8 43.6 all-gather.6

commit v14 on v11

--- a/solution.py
+++ b/solution.py
@@ -42,9 +42,25 @@
     for row in range(0, blocks.shape[1], 2):
         part = vectors[share * row : share * (row + 2)]
         wide = [blocks[level, row + one, kind] for one in range(2)]
-        if isinstance(kind, slice):
-            wide = [block.reshape(-1, block.shape[-1]) for block in wide]
         totals.append(either(*[product(part, block) for block in wide], share))
+    return jnp.concatenate(totals, axis=0)
+
+
+def flat_products(share, vectors, blocks, level, off):
+    totals = []
+    rows = vectors.shape[0] // (2 * share)
+    for row in range(0, 2 * rows, 2):
+        part = vectors[share * row : share * (row + 2)]
+        wide = []
+        for one in range(2):
+            half, at = divmod(row + one, rows)
+            if off:
+                n = blocks.shape[2] // rows - 1
+                block = blocks[level, half, rows + n * at : rows + n * (at + 1)]
+                wide.append(block.reshape(-1, block.shape[-1]))
+            else:
+                wide.append(blocks[level, half, at])
+        totals.append(either(*[dot(part, block) for block in wide], share))
     return jnp.concatenate(totals, axis=0)
 
 
@@ -59,12 +75,10 @@
 
 
 def level_copies(levels, packed, weights, out):
-    rows = weights.shape[1]
     copies = []
     for at, level in enumerate(levels):
         *owners, _ = unpack(packed, level)
-        for half in range(2):
-            copies.append((weights.at[owners[half]], out.at[at, pl.ds(half * rows, rows)]))
+        copies += [(weights.at[owners[half]], out.at[at, half]) for half in range(2)]
     return copies
 
 
@@ -73,17 +87,19 @@
 
 
 def arrange_pairs_kernel(levels, packed, weights, mates, out, sems):
-    rows = weights.shape[1]
+    rows = mates.shape[1]
+    off = weights.shape[1] - rows
     copies = []
     for at, level in enumerate(levels):
         *owners, side = unpack(packed, level)
         for half in range(2):
             here = pl.ds(half * rows, rows)
-            kinds = [(OWN_DIAG, 0), (OWN_OWN, 2), (OWN_MATE, 1 + side)] if level else [(OWN_DIAG, 0)]
-            for kind, block in kinds:
-                source = weights.at[owners[half], :, pl.ds(block, 1)]
-                copies.append((source, out.at[at, here, pl.ds(kind, 1)]))
+            copies.append((weights.at[owners[half], pl.ds(0, rows)], out.at[at, here, OWN_DIAG]))
             if level:
+                offs = weights.at[owners[half], pl.ds(rows, off)]
+                offs = offs.reshape((rows, off // rows) + weights.shape[2:])
+                copies.append((offs.at[:, 1], out.at[at, here, OWN_OWN]))
+                copies.append((offs.at[:, side], out.at[at, here, OWN_MATE]))
                 copies.append((mates.at[owners[half]], out.at[at, here, pl.ds(MATE_DIAG, 2)]))
     run(copies, sems)()
 
@@ -103,9 +119,9 @@
     picked = jnp.concatenate([picked[n * span : (n + 1) * span] for n in range(3)], axis=1)
     if fetched:
         wait()
-    total = products(dot, share, picked.astype(BF16), weights, at, slice(1, None))
+    total = flat_products(share, picked.astype(BF16), weights, at, True)
     shifted = (side[level].astype(F32) - total).astype(BF16)
-    out[...] = products(dot, share, shifted, weights, at, 0).astype(BF16)
+    out[...] = flat_products(share, shifted, weights, at, False).astype(BF16)
 
 
 def gathered_sums(level, at, share, blocks, places, own, mate):
@@ -214,7 +230,7 @@
     near_pairs = [(i, i ^ 1) for i in range(doms)]
     far_pairs = [(i, ((i + 1) ^ 1) - 1) for i in range(1, doms - 1)] + [(0, doms - 1), (doms - 1, 0)]
 
-    weights = jnp.concatenate([diag_inverse[:, None], off_blocks], axis=1)
+    weights = jnp.concatenate([diag_inverse, off_blocks.reshape((-1,) + off_blocks.shape[2:])], axis=0)
     weights = lax.all_gather(weights, "level")
 
     turn = dom % 2
@@ -279,9 +295,9 @@
     def swap(vector, level):
         return lax.ppermute(vector, "dom", far_pairs if level % 2 == 0 else near_pairs)
 
-    def arranged(kernel, levels_now, kinds, copies, behind, *blocks):
+    def arranged(kernel, levels_now, dims, copies, behind, *blocks):
         _, *blocks = lax.optimization_barrier((behind, *blocks))
-        shape = (len(levels_now), count, kinds, width, width)
+        shape = (len(levels_now), *dims, width, width)
         kernel = functools.partial(kernel, levels_now)
         scratch = [pltpu.SemaphoreType.DMA((copies,))]
         outs = [jax.ShapeDtypeStruct(shape, BF16)]
@@ -296,22 +312,22 @@
         solved_mate.append(near if level % 2 == 0 else far)
         args = places, side, far, own, near
         if level == 1:
-            scratch = [pltpu.VMEM((1, count, 4, width, width), BF16), pltpu.SemaphoreType.DMA((2,))]
+            scratch = [pltpu.VMEM((1, 2, 4 * rows, width, width), BF16), pltpu.SemaphoreType.DMA((2,))]
             kernel = functools.partial(forward_kernel, level, 0, share, True)
             solved += call(kernel, [vector], packed, weights, *args, fetched=1, scratch=scratch)
             singles = range(2, paired)
-            blocks = arranged(arrange_kernel, singles, 4, 2 * len(singles), solved[-1], weights)
+            blocks = arranged(arrange_kernel, singles, (2, 4 * rows), 2 * len(singles), solved[-1], weights)
         else:
             kernel = functools.partial(forward_kernel, level, level - 2, share, False)
             solved += call(kernel, [vector], packed, blocks, *args)
 
     solved_mate.append(swap(solved[-1], paired - 1))
     upper = range(paired, levels)
-    blocks = arranged(arrange_pairs_kernel, upper, 5, 8 * len(upper), solved[-1], weights, mates)
+    blocks = arranged(arrange_pairs_kernel, upper, (count, 5), 8 * len(upper), solved[-1], weights, mates)
     kernel = functools.partial(entry_kernel, paired, 0, share)
     held, sent = call(kernel, sums, blocks, meets, solved[-1], solved_mate[-1])
     lower = range(paired)
-    below = arranged(arrange_pairs_kernel, lower, 5, 8 * len(lower) - 6, held, weights, mates)
+    below = arranged(arrange_pairs_kernel, lower, (count, 5), 8 * len(lower) - 6, held, weights, mates)
     for level in upper:
         kernel = functools.partial(forward_pair_kernel, level, level - paired, share, level == levels - 1)
         args = blocks, meets, targets, side, side_mates[level - paired]

time: 225 us -> 225 us (level)
  no operation moved by 1% of the time
where the time goes in v14:
time: 225 us; the launch traced here: 224 us
  starting transfers between devices  100 us (44%)
  waiting for transfers between devices  44.6 us (20%)
  blocking collectives  26.1 us (12%)
  Pallas kernels  19.2 us (9%)
  between operations  17.1 us (8%)
  local copies, waits for them, and re-layouts  8.01 us (4%)
  other arithmetic  7.92 us (4%)
    ppermute x18, starting transfers between devices, swap(): lax.ppermute(vector, 'dom', far_pairs if level % 2 == 0 else near_pairs)  72 us
    all_to_all x1, blocking collectives, local(): dealt = lax.all_to_all(dealt, 'level', 0, 0, tiled=False)  26.1 us
    ppermute x18, waiting for transfers between devices, swap(): lax.ppermute(vector, 'dom', far_pairs if level % 2 == 0 else near_pairs)  21.9 us
    pallas_call x18, Pallas kernels, call(): pl.pallas_call(kernel, out_shape=outs, in_specs=specs, out_specs=[pl.Bloc...  19.2 us
    all_gather x1, waiting for transfers between devices, local(): weights = lax.all_gather(weights, 'level')  17.4 us
    ppermute x1, starting transfers between devices, local(): by_far = lax.ppermute(mates, 'dom', far_pairs)  11 us
    all_to_all x1, starting transfers between devices, local(): side = lax.all_to_all(side, 'level', 1, 0, tiled=False)  8.35 us
    ppermute x1, starting transfers between devices, local(): by_near = lax.ppermute(mates, 'dom', near_pairs)  4.83 us
  transfers between devices with their start and end apart: 25, of which 18 were waited for; matrix products, arithmetic and copies ran while one was open for 6% of the time, Pallas kernels for 5%

profile of v14, /device:TPU:1, one launch (start us, length us, event | category | flops | bytes accessed | tf_op | source)
XLA Modules:
  0.0 224.3 jit_solution(3110924286919167844)
XLA Ops:
  7.2 1.9 pad_maximum_fusion
  9.2 1.3 fusion.7
  13.1 1.0 slice_select_fusion
  15.0 4.8 %collective-permute-start = (bf16[4,2,128,128]{3,2,1,0:T(8,128)(2,1)S(1)}, bf16[4,2,128,128]{3,2,1,0:T(8,128)(2,1)S(1)}, u32[]{:S(2)}, u32[]{:S(2)}) collective-permute-start(bf16[4,2,128,128]{3,2,1,0:T(8,128)(2,1)S(1)} %pad_maximum_fusion.1), channel_id=1, source_target_pairs={{0,16},{16,0},{32,48},{48,32},{64,80},{80,64},{96,112},{112,96},{1... | collective-permute-start | bytes 786440 | tf_op jit(solution)/shard_map/ppermute | solution.py:246
  19.9 11.0 %collective-permute-start.1 = (bf16[4,2,128,128]{3,2,1,0:T(8,128)(2,1)S(1)}, bf16[4,2,128,128]{3,2,1,0:T(8,128)(2,1)S(1)}, u32[]{:S(2)}, u32[]{:S(2)}) collective-permute-start(bf16[4,2,128,128]{3,2,1,0:T(8,128)(2,1)S(1)} %pad_maximum_fusion.1), channel_id=1, source_target_pairs={{16,32},{32,16},{48,64},{64,48},{80,96},{96,80},{112,128},{128,112... | collective-permute-start | bytes 786440 | tf_op jit(solution)/shard_map/ppermute | solution.py:247
  30.9 1.1 fusion
  32.7 8.3 %all-to-all-start = ((bf16[1,4,16,4,128]{4,3,1,0,2:T(4,128)(2,1)}), bf16[1,4,16,4,128]{4,3,1,0,2:T(4,128)(2,1)S(1)}, u32[]{:S(2)}, u32[]{:S(2)}) async-start(bf16[1,4,16,4,128]{4,3,1,0,2:T(4,128)(2,1)} %copy.64), calls=%async_computation | async-start | bytes 131072 | tf_op jit(solution)/shard_map/all_to_all | solution.py:252
  48.5 1.1 all-to-all-done
  50.3 1.9 collective-permute-start.2
  52.3 1.9 collective-permute-start.3
  54.9 3.2 %collective-permute-done.2 = bf16[2,32,128]{2,1,0:T(8,128)(2,1)S(1)} collective-permute-done((bf16[2,32,128]{2,1,0:T(8,128)(2,1)S(1)}, bf16[2,32,128]{2,1,0:T(8,128)(2,1)S(1)}, u32[]{:S(2)}, u32[]{:S(2)}) %collective-permute-start.2) | collective-permute-done | bytes 16416 | tf_op jit(solution)/shard_map/ppermute | solution.py:286
  58.3 17.4 %all-gather.5.cloned.1.call-done = bf16[256,128,128]{2,1,0:T(8,128)(2,1)} async-done(((bf16[16,128,128]{2,1,0:T(8,128)(2,1)}), bf16[256,128,128]{2,1,0:T(8,128)(2,1)}) %all-gather.5.cloned.1.call-update) | async-done | bytes 8388624 | tf_op jit(solution)/shard_map/all_gather | solution.py:234
  75.7 1.8 shard_map.68.own.solved.rest_1_
  77.5 7.7 %collective-permute-start.4 = (bf16[32,128]{1,0:T(8,128)(2,1)S(1)}, bf16[32,128]{1,0:T(8,128)(2,1)S(1)}, u32[]{:S(2)}, u32[]{:S(2)}) collective-permute-start(bf16[32,128]{1,0:T(8,128)(2,1)S(1)} %shard_map.68.own.solved.rest_1_), channel_id=1, source_target_pairs={{16,32},{32,16},{48,64},{64,48},{80,96},{96,80},{112,128},{128,112... | collective-permute-start | bytes 24584 | tf_op jit(solution)/shard_map/ppermute | solution.py:296
  85.2 1.9 collective-permute-start.5
  87.2 2.4 %shard_map.69.weights = bf16[4,2,16,128,128]{4,3,2,1,0:T(8,128)(2,1)S(1)} custom-call(s32[8,128]{1,0:T(8,128)S(1)} %broadcast_in_dim.72.packed, bf16[16,16,128,128]{3,2,1,0:T(8,128)(2,1)} %bitcast.78), custom_call_target="tpu_custom_call" | custom-call | tf_op jit(solution)/shard_map/pallas_call | solution.py:211
  90.2 3.9 %collective-permute-start.6 = (bf16[32,128]{1,0:T(8,128)(2,1)S(1)}, bf16[32,128]{1,0:T(8,128)(2,1)S(1)}, u32[]{:S(2)}, u32[]{:S(2)}) collective-permute-start(bf16[32,128]{1,0:T(8,128)(2,1)S(1)} %shard_map.70.own.solved.rest_2_), channel_id=1, source_target_pairs={{16,32},{32,16},{48,64},{64,48},{80,96},{96,80},{112,128},{128,112... | collective-permute-start | bytes 24584 | tf_op jit(solution)/shard_map/ppermute | solution.py:296
  94.1 1.9 collective-permute-start.7
  96.0 1.9 collective-permute-done.6.far.solved_mate
  99.4 4.7 %collective-permute-start.8 = (bf16[32,128]{1,0:T(8,128)(2,1)S(1)}, bf16[32,128]{1,0:T(8,128)(2,1)S(1)}, u32[]{:S(2)}, u32[]{:S(2)}) collective-permute-start(bf16[32,128]{1,0:T(8,128)(2,1)S(1)} %shard_map.71.own.solved.rest_3_), channel_id=1, source_target_pairs={{16,32},{32,16},{48,64},{64,48},{80,96},{96,80},{112,128},{128,112... | collective-permute-start | bytes 24584 | tf_op jit(solution)/shard_map/ppermute | solution.py:296
  104.2 1.9 collective-permute-start.9
  106.1 1.1 collective-permute-done.8.far
  107.1 1.8 collective-permute-done.9.near.solved_mate
  109.5 3.8 %collective-permute-start.10 = (bf16[32,128]{1,0:T(8,128)(2,1)S(1)}, bf16[32,128]{1,0:T(8,128)(2,1)S(1)}, u32[]{:S(2)}, u32[]{:S(2)}) collective-permute-start(bf16[32,128]{1,0:T(8,128)(2,1)S(1)} %shard_map.72.own.solved.rest_4_), channel_id=1, source_target_pairs={{16,32},{32,16},{48,64},{64,48},{80,96},{96,80},{112,128},{128,112... | collective-permute-start | bytes 24584 | tf_op jit(solution)/shard_map/ppermute | solution.py:296
  113.3 1.9 collective-permute-start.11
  115.2 2.0 collective-permute-done.10.far.solved_mate
  118.6 1.9 collective-permute-start.12
  121.5 2.1 shard_map.74.blocks
  124.1 7.7 %collective-permute-start.13 = (bf16[64,128]{1,0:T(8,128)(2,1)S(1)}, bf16[64,128]{1,0:T(8,128)(2,1)S(1)}, u32[]{:S(2)}, u32[]{:S(2)}) collective-permute-start(bf16[64,128]{1,0:T(8,128)(2,1)S(1)} %get-tuple-element.58), channel_id=1, source_target_pairs={{16,32},{32,16},{48,64},{64,48},{80,96},{96,80},{112,128},{128,112... | collective-permute-start | bytes 49160 | tf_op jit(solution)/shard_map/ppermute | solution.py:296
  131.7 1.1 collective-permute-done.13.came
  133.5 1.9 collective-permute-start.14
  135.4 2.6 %collective-permute-done.14.came = bf16[64,128]{1,0:T(8,128)(2,1)S(1)} collective-permute-done((bf16[64,128]{1,0:T(8,128)(2,1)S(1)}, bf16[64,128]{1,0:T(8,128)(2,1)S(1)}, u32[]{:S(2)}, u32[]{:S(2)}) %collective-permute-start.14) | collective-permute-done | bytes 16416 | tf_op jit(solution)/shard_map/ppermute | solution.py:296
  138.0 1.1 shard_map.78
  139.1 6.7 %collective-permute-start.15 = (bf16[64,128]{1,0:T(8,128)(2,1)S(1)}, bf16[64,128]{1,0:T(8,128)(2,1)S(1)}, u32[]{:S(2)}, u32[]{:S(2)}) collective-permute-start(bf16[64,128]{1,0:T(8,128)(2,1)S(1)} %get-tuple-element.64), channel_id=1, source_target_pairs={{16,32},{32,16},{48,64},{64,48},{80,96},{96,80},{112,128},{128,112... | collective-permute-start | bytes 49160 | tf_op jit(solution)/shard_map/ppermute | solution.py:296
  145.8 1.1 collective-permute-done.15.came
  147.6 1.9 collective-permute-start.16
  149.6 3.6 %shard_map.76.blocks = bf16[6,8,5,128,128]{4,3,2,1,0:T(8,128)(2,1)S(1)} custom-call(s32[8,128]{1,0:T(8,128)S(1)} %broadcast_in_dim.72.packed, bf16[16,16,128,128]{3,2,1,0:T(8,128)(2,1)} %bitcast.80, bf16[16,4,2,128,128]{4,3,2,1,0:T(8,128)(2,1)} %bitcast.82), custom_call_target="tpu_custom_call" | custom-call | tf_op jit(solution)/shard_map/pallas_call | solution.py:211
  154.0 6.7 %collective-permute-start.17 = (bf16[64,128]{1,0:T(8,128)(2,1)S(1)}, bf16[64,128]{1,0:T(8,128)(2,1)S(1)}, u32[]{:S(2)}, u32[]{:S(2)}) collective-permute-start(bf16[64,128]{1,0:T(8,128)(2,1)S(1)} %get-tuple-element.68), channel_id=1, source_target_pairs={{16,32},{32,16},{48,64},{64,48},{80,96},{96,80},{112,128},{128,112... | collective-permute-start | bytes 49160 | tf_op jit(solution)/shard_map/ppermute | solution.py:296
  160.7 1.1 collective-permute-done.17.came
  162.5 1.9 collective-permute-start.18
  164.5 2.6 %collective-permute-done.18.came = bf16[64,128]{1,0:T(8,128)(2,1)S(1)} collective-permute-done((bf16[64,128]{1,0:T(8,128)(2,1)S(1)}, bf16[64,128]{1,0:T(8,128)(2,1)S(1)}, u32[]{:S(2)}, u32[]{:S(2)}) %collective-permute-start.18) | collective-permute-done | bytes 16416 | tf_op jit(solution)/shard_map/ppermute | solution.py:296
  167.8 7.0 %collective-permute-start.19 = (bf16[64,128]{1,0:T(8,128)(2,1)S(1)}, bf16[64,128]{1,0:T(8,128)(2,1)S(1)}, u32[]{:S(2)}, u32[]{:S(2)}) collective-permute-start(bf16[64,128]{1,0:T(8,128)(2,1)S(1)} %get-tuple-element.72), channel_id=1, source_target_pairs={{16,32},{32,16},{48,64},{64,48},{80,96},{96,80},{112,128},{128,112... | collective-permute-start | bytes 49160 | tf_op jit(solution)/shard_map/ppermute | solution.py:296
  174.8 1.1 collective-permute-done.19.came
  176.7 1.9 collective-permute-start.20
  178.6 2.6 %collective-permute-done.20.came = bf16[64,128]{1,0:T(8,128)(2,1)S(1)} collective-permute-done((bf16[64,128]{1,0:T(8,128)(2,1)S(1)}, bf16[64,128]{1,0:T(8,128)(2,1)S(1)}, u32[]{:S(2)}, u32[]{:S(2)}) %collective-permute-start.20) | collective-permute-done | bytes 16416 | tf_op jit(solution)/shard_map/ppermute | solution.py:296
  181.9 6.7 %collective-permute-start.21 = (bf16[64,128]{1,0:T(8,128)(2,1)S(1)}, bf16[64,128]{1,0:T(8,128)(2,1)S(1)}, u32[]{:S(2)}, u32[]{:S(2)}) collective-permute-start(bf16[64,128]{1,0:T(8,128)(2,1)S(1)} %get-tuple-element.76), channel_id=1, source_target_pairs={{16,32},{32,16},{48,64},{64,48},{80,96},{96,80},{112,128},{128,112... | collective-permute-start | bytes 49160 | tf_op jit(solution)/shard_map/ppermute | solution.py:296
  188.6 1.1 collective-permute-done.21.came
  190.0 26.1 %all_to_all.20 = bf16[16,32,128]{2,1,0:T(8,128)(2,1)S(1)} all-to-all(bf16[16,32,128]{2,1,0:T(8,128)(2,1)S(1)} %shard_map.85), channel_id=1, replica_groups=mesh['dom'=32,'level'=16] {'level'}, dimensions={0} | all-to-all | bytes 262144 | tf_op jit(solution)/shard_map/all_to_all | solution.py:349
  (80 shorter events, 22.8 us)
Async XLA Ops:
  7.2 68.5 %all-gather.5.cloned.1.call-start = ((), (), s32[]{:S(2)}) async-start(), calls=%async_computation.2 | async-start | bytes 8912896 | tf_op jit(solution)/shard_map/all_gather | solution.py:234
  15.0 39.2 %collective-permute-start = (bf16[4,2,128,128]{3,2,1,0:T(8,128)(2,1)S(1)}, bf16[4,2,128,128]{3,2,1,0:T(8,128)(2,1)S(1)}, u32[]{:S(2)}, u32[]{:S(2)}) collective-permute-start(bf16[4,2,128,128]{3,2,1,0:T(8,128)(2,1)S(1)} %pad_maximum_fusion.1), channel_id=1, source_target_pairs={{0,16},{16,0},{32,48},{48,32},{64,80},{80,64},{96,112},{112,96},{1... | collective-permute-start | bytes 786440 | tf_op jit(solution)/shard_map/ppermute | solution.py:246
  19.9 34.3 %collective-permute-start.1 = (bf16[4,2,128,128]{3,2,1,0:T(8,128)(2,1)S(1)}, bf16[4,2,128,128]{3,2,1,0:T(8,128)(2,1)S(1)}, u32[]{:S(2)}, u32[]{:S(2)}) collective-permute-start(bf16[4,2,128,128]{3,2,1,0:T(8,128)(2,1)S(1)} %pad_maximum_fusion.1), channel_id=1, source_target_pairs={{16,32},{32,16},{48,64},{64,48},{80,96},{96,80},{112,128},{128,112... | collective-permute-start | bytes 786440 | tf_op jit(solution)/shard_map/ppermute | solution.py:247
  32.7 17.0 %all-to-all-start = ((bf16[1,4,16,4,128]{4,3,1,0,2:T(4,128)(2,1)}), bf16[1,4,16,4,128]{4,3,1,0,2:T(4,128)(2,1)S(1)}, u32[]{:S(2)}, u32[]{:S(2)}) async-start(bf16[1,4,16,4,128]{4,3,1,0,2:T(4,128)(2,1)} %copy.64), calls=%async_computation | async-start | bytes 131072 | tf_op jit(solution)/shard_map/all_to_all | solution.py:252
  41.0 80.4 %all-gather.7.cloned.1.call-start = ((), (), s32[]{:S(2)}) async-start(), calls=%async_computation.3 | async-start | bytes 4456448 | tf_op jit(solution)/shard_map/all_gather | solution.py:293
  50.3 7.8 %collective-permute-start.2 = (bf16[2,32,128]{2,1,0:T(8,128)(2,1)S(1)}, bf16[2,32,128]{2,1,0:T(8,128)(2,1)S(1)}, u32[]{:S(2)}, u32[]{:S(2)}) collective-permute-start(bf16[2,32,128]{2,1,0:T(8,128)(2,1)S(1)} %get-tuple-element.104), channel_id=1, source_target_pairs={{16,32},{32,16},{48,64},{64,48},{80,96},{96,80},{112,128},{128,112... | collective-permute-start | bytes 49160 | tf_op jit(solution)/shard_map/ppermute | solution.py:286
  52.3 5.9 %collective-permute-start.3 = (bf16[2,32,128]{2,1,0:T(8,128)(2,1)S(1)}, bf16[2,32,128]{2,1,0:T(8,128)(2,1)S(1)}, u32[]{:S(2)}, u32[]{:S(2)}) collective-permute-start(bf16[2,32,128]{2,1,0:T(8,128)(2,1)S(1)} %get-tuple-element.103), channel_id=1, source_target_pairs={{0,16},{16,0},{32,48},{48,32},{64,80},{80,64},{96,112},{112,96},{1... | collective-permute-start | bytes 49160 | tf_op jit(solution)/shard_map/ppermute | solution.py:287
  77.5 12.1 %collective-permute-start.4 = (bf16[32,128]{1,0:T(8,128)(2,1)S(1)}, bf16[32,128]{1,0:T(8,128)(2,1)S(1)}, u32[]{:S(2)}, u32[]{:S(2)}) collective-permute-start(bf16[32,128]{1,0:T(8,128)(2,1)S(1)} %shard_map.68.own.solved.rest_1_), channel_id=1, source_target_pairs={{16,32},{32,16},{48,64},{64,48},{80,96},{96,80},{112,128},{128,112... | collective-permute-start | bytes 24584 | tf_op jit(solution)/shard_map/ppermute | solution.py:296
  85.2 4.4 %collective-permute-start.5 = (bf16[32,128]{1,0:T(8,128)(2,1)S(1)}, bf16[32,128]{1,0:T(8,128)(2,1)S(1)}, u32[]{:S(2)}, u32[]{:S(2)}) collective-permute-start(bf16[32,128]{1,0:T(8,128)(2,1)S(1)} %shard_map.68.own.solved.rest_1_), channel_id=1, source_target_pairs={{0,16},{16,0},{32,48},{48,32},{64,80},{80,64},{96,112},{112,96},{1... | collective-permute-start | bytes 24584 | tf_op jit(solution)/shard_map/ppermute | solution.py:296
  90.2 7.7 %collective-permute-start.6 = (bf16[32,128]{1,0:T(8,128)(2,1)S(1)}, bf16[32,128]{1,0:T(8,128)(2,1)S(1)}, u32[]{:S(2)}, u32[]{:S(2)}) collective-permute-start(bf16[32,128]{1,0:T(8,128)(2,1)S(1)} %shard_map.70.own.solved.rest_2_), channel_id=1, source_target_pairs={{16,32},{32,16},{48,64},{64,48},{80,96},{96,80},{112,128},{128,112... | collective-permute-start | bytes 24584 | tf_op jit(solution)/shard_map/ppermute | solution.py:296
  94.1 4.8 %collective-permute-start.7 = (bf16[32,128]{1,0:T(8,128)(2,1)S(1)}, bf16[32,128]{1,0:T(8,128)(2,1)S(1)}, u32[]{:S(2)}, u32[]{:S(2)}) collective-permute-start(bf16[32,128]{1,0:T(8,128)(2,1)S(1)} %shard_map.70.own.solved.rest_2_), channel_id=1, source_target_pairs={{0,16},{16,0},{32,48},{48,32},{64,80},{80,64},{96,112},{112,96},{1... | collective-permute-start | bytes 24584 | tf_op jit(solution)/shard_map/ppermute | solution.py:296
  99.4 7.7 %collective-permute-start.8 = (bf16[32,128]{1,0:T(8,128)(2,1)S(1)}, bf16[32,128]{1,0:T(8,128)(2,1)S(1)}, u32[]{:S(2)}, u32[]{:S(2)}) collective-permute-start(bf16[32,128]{1,0:T(8,128)(2,1)S(1)} %shard_map.71.own.solved.rest_3_), channel_id=1, source_target_pairs={{16,32},{32,16},{48,64},{64,48},{80,96},{96,80},{112,128},{128,112... | collective-permute-start | bytes 24584 | tf_op jit(solution)/shard_map/ppermute | solution.py:296
  104.2 4.8 %collective-permute-start.9 = (bf16[32,128]{1,0:T(8,128)(2,1)S(1)}, bf16[32,128]{1,0:T(8,128)(2,1)S(1)}, u32[]{:S(2)}, u32[]{:S(2)}) collective-permute-start(bf16[32,128]{1,0:T(8,128)(2,1)S(1)} %shard_map.71.own.solved.rest_3_), channel_id=1, source_target_pairs={{0,16},{16,0},{32,48},{48,32},{64,80},{80,64},{96,112},{112,96},{1... | collective-permute-start | bytes 24584 | tf_op jit(solution)/shard_map/ppermute | solution.py:296
  109.5 7.7 %collective-permute-start.10 = (bf16[32,128]{1,0:T(8,128)(2,1)S(1)}, bf16[32,128]{1,0:T(8,128)(2,1)S(1)}, u32[]{:S(2)}, u32[]{:S(2)}) collective-permute-start(bf16[32,128]{1,0:T(8,128)(2,1)S(1)} %shard_map.72.own.solved.rest_4_), channel_id=1, source_target_pairs={{16,32},{32,16},{48,64},{64,48},{80,96},{96,80},{112,128},{128,112... | collective-permute-start | bytes 24584 | tf_op jit(solution)/shard_map/ppermute | solution.py:296
  113.3 4.8 %collective-permute-start.11 = (bf16[32,128]{1,0:T(8,128)(2,1)S(1)}, bf16[32,128]{1,0:T(8,128)(2,1)S(1)}, u32[]{:S(2)}, u32[]{:S(2)}) collective-permute-start(bf16[32,128]{1,0:T(8,128)(2,1)S(1)} %shard_map.72.own.solved.rest_4_), channel_id=1, source_target_pairs={{0,16},{16,0},{32,48},{48,32},{64,80},{80,64},{96,112},{112,96},{1... | collective-permute-start | bytes 24584 | tf_op jit(solution)/shard_map/ppermute | solution.py:296
  118.6 4.9 %collective-permute-start.12 = (bf16[32,128]{1,0:T(8,128)(2,1)S(1)}, bf16[32,128]{1,0:T(8,128)(2,1)S(1)}, u32[]{:S(2)}, u32[]{:S(2)}) collective-permute-start(bf16[32,128]{1,0:T(8,128)(2,1)S(1)} %shard_map.73.own.solved.rest_5_), channel_id=1, source_target_pairs={{0,16},{16,0},{32,48},{48,32},{64,80},{80,64},{96,112},{112,96},{1... | collective-permute-start | bytes 24584 | tf_op jit(solution)/shard_map/ppermute | solution.py:296
  124.1 8.8 %collective-permute-start.13 = (bf16[64,128]{1,0:T(8,128)(2,1)S(1)}, bf16[64,128]{1,0:T(8,128)(2,1)S(1)}, u32[]{:S(2)}, u32[]{:S(2)}) collective-permute-start(bf16[64,128]{1,0:T(8,128)(2,1)S(1)} %get-tuple-element.58), channel_id=1, source_target_pairs={{16,32},{32,16},{48,64},{64,48},{80,96},{96,80},{112,128},{128,112... | collective-permute-start | bytes 49160 | tf_op jit(solution)/shard_map/ppermute | solution.py:296
  133.5 4.5 %collective-permute-start.14 = (bf16[64,128]{1,0:T(8,128)(2,1)S(1)}, bf16[64,128]{1,0:T(8,128)(2,1)S(1)}, u32[]{:S(2)}, u32[]{:S(2)}) collective-permute-start(bf16[64,128]{1,0:T(8,128)(2,1)S(1)} %get-tuple-element.62), channel_id=1, source_target_pairs={{0,16},{16,0},{32,48},{48,32},{64,80},{80,64},{96,112},{112,96},{1... | collective-permute-start | bytes 49160 | tf_op jit(solution)/shard_map/ppermute | solution.py:296
  139.1 7.8 %collective-permute-start.15 = (bf16[64,128]{1,0:T(8,128)(2,1)S(1)}, bf16[64,128]{1,0:T(8,128)(2,1)S(1)}, u32[]{:S(2)}, u32[]{:S(2)}) collective-permute-start(bf16[64,128]{1,0:T(8,128)(2,1)S(1)} %get-tuple-element.64), channel_id=1, source_target_pairs={{16,32},{32,16},{48,64},{64,48},{80,96},{96,80},{112,128},{128,112... | collective-permute-start | bytes 49160 | tf_op jit(solution)/shard_map/ppermute | solution.py:296
  147.6 5.6 %collective-permute-start.16 = (bf16[64,128]{1,0:T(8,128)(2,1)S(1)}, bf16[64,128]{1,0:T(8,128)(2,1)S(1)}, u32[]{:S(2)}, u32[]{:S(2)}) collective-permute-start(bf16[64,128]{1,0:T(8,128)(2,1)S(1)} %get-tuple-element.66), channel_id=1, source_target_pairs={{0,16},{16,0},{32,48},{48,32},{64,80},{80,64},{96,112},{112,96},{1... | collective-permute-start | bytes 49160 | tf_op jit(solution)/shard_map/ppermute | solution.py:296
  154.0 7.8 %collective-permute-start.17 = (bf16[64,128]{1,0:T(8,128)(2,1)S(1)}, bf16[64,128]{1,0:T(8,128)(2,1)S(1)}, u32[]{:S(2)}, u32[]{:S(2)}) collective-permute-start(bf16[64,128]{1,0:T(8,128)(2,1)S(1)} %get-tuple-element.68), channel_id=1, source_target_pairs={{16,32},{32,16},{48,64},{64,48},{80,96},{96,80},{112,128},{128,112... | collective-permute-start | bytes 49160 | tf_op jit(solution)/shard_map/ppermute | solution.py:296
  162.5 4.5 %collective-permute-start.18 = (bf16[64,128]{1,0:T(8,128)(2,1)S(1)}, bf16[64,128]{1,0:T(8,128)(2,1)S(1)}, u32[]{:S(2)}, u32[]{:S(2)}) collective-permute-start(bf16[64,128]{1,0:T(8,128)(2,1)S(1)} %get-tuple-element.70), channel_id=1, source_target_pairs={{0,16},{16,0},{32,48},{48,32},{64,80},{80,64},{96,112},{112,96},{1... | collective-permute-start | bytes 49160 | tf_op jit(solution)/shard_map/ppermute | solution.py:296
  167.8 8.1 %collective-permute-start.19 = (bf16[64,128]{1,0:T(8,128)(2,1)S(1)}, bf16[64,128]{1,0:T(8,128)(2,1)S(1)}, u32[]{:S(2)}, u32[]{:S(2)}) collective-permute-start(bf16[64,128]{1,0:T(8,128)(2,1)S(1)} %get-tuple-element.72), channel_id=1, source_target_pairs={{16,32},{32,16},{48,64},{64,48},{80,96},{96,80},{112,128},{128,112... | collective-permute-start | bytes 49160 | tf_op jit(solution)/shard_map/ppermute | solution.py:296
  176.7 4.5 %collective-permute-start.20 = (bf16[64,128]{1,0:T(8,128)(2,1)S(1)}, bf16[64,128]{1,0:T(8,128)(2,1)S(1)}, u32[]{:S(2)}, u32[]{:S(2)}) collective-permute-start(bf16[64,128]{1,0:T(8,128)(2,1)S(1)} %get-tuple-element.74), channel_id=1, source_target_pairs={{0,16},{16,0},{32,48},{48,32},{64,80},{80,64},{96,112},{112,96},{1... | collective-permute-start | bytes 49160 | tf_op jit(solution)/shard_map/ppermute | solution.py:296
  181.9 7.8 %collective-permute-start.21 = (bf16[64,128]{1,0:T(8,128)(2,1)S(1)}, bf16[64,128]{1,0:T(8,128)(2,1)S(1)}, u32[]{:S(2)}, u32[]{:S(2)}) collective-permute-start(bf16[64,128]{1,0:T(8,128)(2,1)S(1)} %get-tuple-element.76), channel_id=1, source_target_pairs={{16,32},{32,16},{48,64},{64,48},{80,96},{96,80},{112,128},{128,112... | collective-permute-start | bytes 49160 | tf_op jit(solution)/shard_map/ppermute | solution.py:296
Sparse Core Ops, SparseCore 0:
  10.1 65.5 all-gather.4
  77.8 43.6 all-gather.6

commit v15 on v11

--- a/solution.py
+++ b/solution.py
@@ -15,10 +15,6 @@
     return lax.dot_general(a, b, (((1,), (0,)), ((), ())), preferred_element_type=F32)
 
 
-def dot_t(a, b):
-    return lax.dot_general(a, b, (((1,), (1,)), ((), ())), preferred_element_type=F32)
-
-
 def either(low, high, share):
     top = lax.broadcasted_iota(jnp.int32, low.shape, 0) < share
     return jnp.where(top, low, high)
@@ -37,14 +33,14 @@
     return value & mask, (value >> BITS) & mask, value >> (2 * BITS)
 
 
-def products(product, share, vectors, blocks, level, kind):
+def products(share, vectors, blocks, level, kind):
     totals = []
     for row in range(0, blocks.shape[1], 2):
         part = vectors[share * row : share * (row + 2)]
         wide = [blocks[level, row + one, kind] for one in range(2)]
         if isinstance(kind, slice):
             wide = [block.reshape(-1, block.shape[-1]) for block in wide]
-        totals.append(either(*[product(part, block) for block in wide], share))
+        totals.append(either(*[dot(part, block) for block in wide], share))
     return jnp.concatenate(totals, axis=0)
 
 
@@ -103,26 +99,35 @@
     picked = jnp.concatenate([picked[n * span : (n + 1) * span] for n in range(3)], axis=1)
     if fetched:
         wait()
-    total = products(dot, share, picked.astype(BF16), weights, at, slice(1, None))
+    total = products(share, picked.astype(BF16), weights, at, slice(1, None))
     shifted = (side[level].astype(F32) - total).astype(BF16)
-    out[...] = products(dot, share, shifted, weights, at, 0).astype(BF16)
+    out[...] = products(share, shifted, weights, at, 0).astype(BF16)
 
 
 def gathered_sums(level, at, share, blocks, places, own, mate):
     span = own.shape[0]
     picked = picked_from(places[level], jnp.concatenate([own, mate], axis=0)).astype(BF16)
     parts = [
-        products(dot, share, picked[n * span : (n + 1) * span], blocks, at, kind)
+        products(share, picked[n * span : (n + 1) * span], blocks, at, kind)
         for n, kind in enumerate((OWN_OWN, MATE_OWN, OWN_MATE))
     ]
     return jnp.concatenate([parts[0] + parts[2], parts[1]], axis=0)
 
 
-def pushed_sums(level, at, share, blocks, targets, own, mate):
+PUSHED = OWN_OWN, MATE_OWN, OWN_MATE
+
+
+def turn_kernel(at, blocks, out):
+    for row in range(out.shape[1]):
+        for which, kind in enumerate(PUSHED):
+            out[0, row, which] = blocks[at, row, kind].T
+
+
+def pushed_sums(level, share, turned, targets, own, mate):
     span = own.shape[0]
     pushed = [
-        products(dot_t, share, vectors, blocks, at, kind)
-        for vectors, kind in ((own, OWN_OWN), (mate, MATE_OWN), (own, OWN_MATE))
+        products(share, vectors, turned, 0, which)
+        for which, vectors in enumerate((own, mate, own))
     ]
     pushed = jnp.concatenate(pushed, axis=0).astype(BF16)
     to = lax.broadcasted_iota(jnp.int32, (2 * span, 3 * span), 0)
@@ -145,38 +150,38 @@
 
 
 def forward_pair_kernel(
-    level, at, share, last, blocks, meets, targets, side, side_mate, held, came,
+    level, at, share, last, blocks, turned, meets, targets, side, side_mate, held, came,
     solved, solved_mate, to_hold, to_send,
 ):
     pair = []
     diags = OWN_DIAG, MATE_DIAG
     for total, right, diag in zip(joined(held, came), (side[level], side_mate[...]), diags):
         shifted = (right.astype(F32) - total).astype(BF16)
-        pair.append(products(dot, share, shifted, blocks, at, diag).astype(BF16))
+        pair.append(products(share, shifted, blocks, at, diag).astype(BF16))
     solved[...], solved_mate[...] = pair
     if last:
-        sums = pushed_sums(level, at, share, blocks, targets, *pair)
+        sums = pushed_sums(level, share, turned, targets, *pair)
     else:
         sums = gathered_sums(level + 1, at + 1, share, blocks, meets, *pair)
     pass_on(sums, to_hold, to_send)
 
 
 def backward_kernel(
-    level, at, share, blocks, targets, solved, solved_mate, held, came, result, *outs
+    level, at, share, blocks, turned, targets, solved, solved_mate, held, came, result, *outs
 ):
     pair = []
     diags = OWN_DIAG, MATE_DIAG
     for total, vector, diag in zip(joined(held, came), (solved, solved_mate), diags):
-        part = products(dot, share, total.astype(BF16), blocks, at, diag)
+        part = products(share, total.astype(BF16), blocks, at, diag)
         pair.append((vector[...].astype(F32) - part).astype(BF16))
     result[...] = pair[0]
-    pass_on(pushed_sums(level, at, share, blocks, targets, *pair), *outs)
+    pass_on(pushed_sums(level, share, turned, targets, *pair), *outs)
 
 
 def last_kernel(share, packed, blocks, held, came, *rest):
     *rest, out = rest
     solved, results = rest[: packed.shape[0]], rest[packed.shape[0] :]
-    part = products(dot, share, joined(held, came)[0].astype(BF16), blocks, 0, OWN_DIAG)
+    part = products(share, joined(held, came)[0].astype(BF16), blocks, 0, OWN_DIAG)
     result = (solved[0][...].astype(F32) - part).astype(BF16)
     size = out.shape[1] // 2
     for level in range(packed.shape[0]):
@@ -312,9 +317,18 @@
     held, sent = call(kernel, sums, blocks, meets, solved[-1], solved_mate[-1])
     lower = range(paired)
     below = arranged(arrange_pairs_kernel, lower, 5, 8 * len(lower) - 6, held, weights, mates)
+    blocks, below = lax.optimization_barrier((blocks, below))
+
+    def turned(blocks, at, behind):
+        _, blocks = lax.optimization_barrier((behind, blocks))
+        outs = [jax.ShapeDtypeStruct((1, count, len(PUSHED), width, width), BF16)]
+        return call(functools.partial(turn_kernel, at), outs, blocks)[0]
+
     for level in upper:
         kernel = functools.partial(forward_pair_kernel, level, level - paired, share, level == levels - 1)
-        args = blocks, meets, targets, side, side_mates[level - paired]
+        last = level == levels - 1
+        ready = turned(blocks, level - paired, sent) if last else targets
+        args = blocks, ready, meets, targets, side, side_mates[level - paired]
         own, mate, held, sent = call(kernel, [vector] * 2 + sums, *args, held, swap(sent, level))
         solved.append(own)
         solved_mate.append(mate)
@@ -323,7 +337,8 @@
     for level in range(levels - 2, 0, -1):
         at = level - paired if level in upper else level
         kernel = functools.partial(backward_kernel, level, at, share)
-        args = blocks if level in upper else below, targets, solved[level], solved_mate[level]
+        here = blocks if level in upper else below
+        args = here, turned(here, at, sent), targets, solved[level], solved_mate[level]
         result, held, sent = call(kernel, [vector] + sums, *args, held, swap(sent, level))
         results.append(result)
 

time: 225 us -> 228 us (1.013)
  starting transfers between devices: 100 us -> 94.2 us
  waiting for transfers between devices: 44.6 us -> 50 us
  blocking collectives: 26.1 us -> 29.2 us
    ppermute x18, waiting for transfers between devices: 21.9 us -> 29.4 us  [swap(): lax.ppermute(vector, 'dom', far_pairs if level % 2 == 0 else near_pairs)]
    ppermute x18, starting transfers between devices: 72 us -> 64.9 us  [swap(): lax.ppermute(vector, 'dom', far_pairs if level % 2 == 0 else near_pairs)]
    all_to_all x1, blocking collectives: 26.1 us -> 29.2 us  [local(): dealt = lax.all_to_all(dealt, 'level', 0, 0, tiled=False)]
    all_gather x1, waiting for transfers between devices: 17.4 us -> 14.3 us  [local(): weights = lax.all_gather(weights, 'level')]
    ppermute x1, starting transfers between devices: 4.83 us -> 1.92 us  [local(): by_near = lax.ppermute(mates, 'dom', near_pairs)]
    ppermute x1, starting transfers between devices: 11 us -> 13.7 us  [local(): by_far = lax.ppermute(mates, 'dom', far_pairs)]
    pallas_call x18 -> x25, Pallas kernels: 19.2 us -> 19.6 us  [call(): pl.pallas_call(kernel, out_shape=outs, in_specs=specs, out_specs=[pl.Bloc...]
  transfers between devices with their start and end apart: 25 -> 25, of which waited for: 18 -> 15; matrix products, arithmetic and copies ran while one was open for 6% -> 6% of each run, Pallas kernels for 5% -> 6%
where the time goes in v15:
time: 228 us; the launch traced here: 227 us
  starting transfers between devices  94.2 us (41%)
  waiting for transfers between devices  50 us (22%)
  blocking collectives  29.2 us (13%)
  Pallas kernels  19.6 us (9%)
  between operations  17.3 us (8%)
  local copies, waits for them, and re-layouts  8.03 us (4%)
  other arithmetic  7.91 us (3%)
    ppermute x18, starting transfers between devices, swap(): lax.ppermute(vector, 'dom', far_pairs if level % 2 == 0 else near_pairs)  64.9 us
    ppermute x18, waiting for transfers between devices, swap(): lax.ppermute(vector, 'dom', far_pairs if level % 2 == 0 else near_pairs)  29.4 us
    all_to_all x1, blocking collectives, local(): dealt = lax.all_to_all(dealt, 'level', 0, 0, tiled=False)  29.2 us
    pallas_call x25, Pallas kernels, call(): pl.pallas_call(kernel, out_shape=outs, in_specs=specs, out_specs=[pl.Bloc...  19.6 us
    all_gather x1, waiting for transfers between devices, local(): weights = lax.all_gather(weights, 'level')  14.3 us
    ppermute x1, starting transfers between devices, local(): by_far = lax.ppermute(mates, 'dom', far_pairs)  13.7 us
    all_to_all x1, starting transfers between devices, local(): side = lax.all_to_all(side, 'level', 1, 0, tiled=False)  8.07 us
    ppermute x1, waiting for transfers between devices, local(): far = lax.ppermute(jnp.stack([own, side[paired]]), 'dom', far_pairs)  5.13 us
  transfers between devices with their start and end apart: 25, of which 15 were waited for; matrix products, arithmetic and copies ran while one was open for 6% of the time, Pallas kernels for 6%

profile of v15, /device:TPU:1, one launch (start us, length us, event | category | flops | bytes accessed | tf_op | source)
XLA Modules:
  0.0 227.3 jit_solution(9854779536360171166)
XLA Ops:
  7.2 1.9 pad_maximum_fusion
  9.2 1.3 fusion.7
  13.1 1.0 slice_select_fusion
  14.1 0.9 pad_maximum_fusion.1
  15.0 13.7 %collective-permute-start.1 = (bf16[4,2,128,128]{3,2,1,0:T(8,128)(2,1)S(1)}, bf16[4,2,128,128]{3,2,1,0:T(8,128)(2,1)S(1)}, u32[]{:S(2)}, u32[]{:S(2)}) collective-permute-start(bf16[4,2,128,128]{3,2,1,0:T(8,128)(2,1)S(1)} %pad_maximum_fusion.1), channel_id=1, source_target_pairs={{16,32},{32,16},{48,64},{64,48},{80,96},{96,80},{112,128},{128,112... | collective-permute-start | bytes 786440 | tf_op jit(solution)/shard_map/ppermute | solution.py:236
  28.7 1.9 collective-permute-start
  30.7 1.1 fusion
  32.4 8.1 %all-to-all-start = ((bf16[1,4,16,4,128]{4,3,1,0,2:T(4,128)(2,1)}), bf16[1,4,16,4,128]{4,3,1,0,2:T(4,128)(2,1)S(1)}, u32[]{:S(2)}, u32[]{:S(2)}) async-start(bf16[1,4,16,4,128]{4,3,1,0,2:T(4,128)(2,1)} %copy.64), calls=%async_computation | async-start | bytes 131072 | tf_op jit(solution)/shard_map/all_to_all | solution.py:241
  48.1 1.1 all-to-all-done
  49.8 3.6 %collective-permute-start.3 = (bf16[2,32,128]{2,1,0:T(8,128)(2,1)S(1)}, bf16[2,32,128]{2,1,0:T(8,128)(2,1)S(1)}, u32[]{:S(2)}, u32[]{:S(2)}) collective-permute-start(bf16[2,32,128]{2,1,0:T(8,128)(2,1)S(1)} %get-tuple-element.121), channel_id=1, source_target_pairs={{0,16},{16,0},{32,48},{48,32},{64,80},{80,64},{96,112},{112,96},{1... | collective-permute-start | bytes 49160 | tf_op jit(solution)/shard_map/ppermute | solution.py:276
  53.4 1.9 collective-permute-start.2
  56.1 5.1 %collective-permute-done.2 = bf16[2,32,128]{2,1,0:T(8,128)(2,1)S(1)} collective-permute-done((bf16[2,32,128]{2,1,0:T(8,128)(2,1)S(1)}, bf16[2,32,128]{2,1,0:T(8,128)(2,1)S(1)}, u32[]{:S(2)}, u32[]{:S(2)}) %collective-permute-start.2) | collective-permute-done | bytes 16416 | tf_op jit(solution)/shard_map/ppermute | solution.py:275
  61.4 14.3 %all-gather.5.cloned.1.call-done = bf16[64,4,128,128]{3,2,1,0:T(8,128)(2,1)} async-done(((bf16[4,4,128,128]{3,2,1,0:T(8,128)(2,1)}), bf16[64,4,128,128]{3,2,1,0:T(8,128)(2,1)}) %all-gather.5.cloned.1.call-update) | async-done | bytes 8388624 | tf_op jit(solution)/shard_map/all_gather | solution.py:223
  75.7 1.8 shard_map.68.own.solved.rest_1_
  77.5 3.3 %collective-permute-start.5 = (bf16[32,128]{1,0:T(8,128)(2,1)S(1)}, bf16[32,128]{1,0:T(8,128)(2,1)S(1)}, u32[]{:S(2)}, u32[]{:S(2)}) collective-permute-start(bf16[32,128]{1,0:T(8,128)(2,1)S(1)} %shard_map.68.own.solved.rest_1_), channel_id=1, source_target_pairs={{0,16},{16,0},{32,48},{48,32},{64,80},{80,64},{96,112},{112,96},{1... | collective-permute-start | bytes 24584 | tf_op jit(solution)/shard_map/ppermute | solution.py:285
  80.8 7.3 %collective-permute-start.4 = (bf16[32,128]{1,0:T(8,128)(2,1)S(1)}, bf16[32,128]{1,0:T(8,128)(2,1)S(1)}, u32[]{:S(2)}, u32[]{:S(2)}) collective-permute-start(bf16[32,128]{1,0:T(8,128)(2,1)S(1)} %shard_map.68.own.solved.rest_1_), channel_id=1, source_target_pairs={{16,32},{32,16},{48,64},{64,48},{80,96},{96,80},{112,128},{128,112... | collective-permute-start | bytes 24584 | tf_op jit(solution)/shard_map/ppermute | solution.py:285
  88.1 2.4 %shard_map.69.weights = bf16[4,8,4,128,128]{4,3,2,1,0:T(8,128)(2,1)S(1)} custom-call(s32[8,128]{1,0:T(8,128)S(1)} %broadcast_in_dim.73.packed, bf16[16,4,4,128,128]{4,3,2,1,0:T(8,128)(2,1)} %bitcast.77), custom_call_target="tpu_custom_call" | custom-call | tf_op jit(solution)/shard_map/pallas_call | solution.py:200
  91.1 1.9 collective-permute-start.7
  93.1 5.3 %collective-permute-start.6 = (bf16[32,128]{1,0:T(8,128)(2,1)S(1)}, bf16[32,128]{1,0:T(8,128)(2,1)S(1)}, u32[]{:S(2)}, u32[]{:S(2)}) collective-permute-start(bf16[32,128]{1,0:T(8,128)(2,1)S(1)} %shard_map.70.own.solved.rest_2_), channel_id=1, source_target_pairs={{16,32},{32,16},{48,64},{64,48},{80,96},{96,80},{112,128},{128,112... | collective-permute-start | bytes 24584 | tf_op jit(solution)/shard_map/ppermute | solution.py:285
  98.4 2.4 %collective-permute-done.6.far.solved_mate = bf16[32,128]{1,0:T(8,128)(2,1)S(1)} collective-permute-done((bf16[32,128]{1,0:T(8,128)(2,1)S(1)}, bf16[32,128]{1,0:T(8,128)(2,1)S(1)}, u32[]{:S(2)}, u32[]{:S(2)}) %collective-permute-start.6) | collective-permute-done | bytes 8224 | tf_op jit(solution)/shard_map/ppermute | solution.py:285
  101.3 1.9 collective-permute-start.9
  103.3 5.3 %collective-permute-start.8 = (bf16[32,128]{1,0:T(8,128)(2,1)S(1)}, bf16[32,128]{1,0:T(8,128)(2,1)S(1)}, u32[]{:S(2)}, u32[]{:S(2)}) collective-permute-start(bf16[32,128]{1,0:T(8,128)(2,1)S(1)} %shard_map.71.own.solved.rest_3_), channel_id=1, source_target_pairs={{16,32},{32,16},{48,64},{64,48},{80,96},{96,80},{112,128},{128,112... | collective-permute-start | bytes 24584 | tf_op jit(solution)/shard_map/ppermute | solution.py:285
  108.6 2.4 %collective-permute-done.8.far = bf16[32,128]{1,0:T(8,128)(2,1)S(1)} collective-permute-done((bf16[32,128]{1,0:T(8,128)(2,1)S(1)}, bf16[32,128]{1,0:T(8,128)(2,1)S(1)}, u32[]{:S(2)}, u32[]{:S(2)}) %collective-permute-start.8) | collective-permute-done | bytes 8224 | tf_op jit(solution)/shard_map/ppermute | solution.py:285
  111.5 1.9 collective-permute-start.11
  113.5 5.3 %collective-permute-start.10 = (bf16[32,128]{1,0:T(8,128)(2,1)S(1)}, bf16[32,128]{1,0:T(8,128)(2,1)S(1)}, u32[]{:S(2)}, u32[]{:S(2)}) collective-permute-start(bf16[32,128]{1,0:T(8,128)(2,1)S(1)} %shard_map.72.own.solved.rest_4_), channel_id=1, source_target_pairs={{16,32},{32,16},{48,64},{64,48},{80,96},{96,80},{112,128},{128,112... | collective-permute-start | bytes 24584 | tf_op jit(solution)/shard_map/ppermute | solution.py:285
  118.8 2.4 %collective-permute-done.10.far.solved_mate = bf16[32,128]{1,0:T(8,128)(2,1)S(1)} collective-permute-done((bf16[32,128]{1,0:T(8,128)(2,1)S(1)}, bf16[32,128]{1,0:T(8,128)(2,1)S(1)}, u32[]{:S(2)}, u32[]{:S(2)}) %collective-permute-start.10) | collective-permute-done | bytes 8224 | tf_op jit(solution)/shard_map/ppermute | solution.py:285
  121.7 1.9 collective-permute-start.12
  123.7 2.1 shard_map.74.blocks
  126.6 5.3 %collective-permute-start.13 = (bf16[64,128]{1,0:T(8,128)(2,1)S(1)}, bf16[64,128]{1,0:T(8,128)(2,1)S(1)}, u32[]{:S(2)}, u32[]{:S(2)}) collective-permute-start(bf16[64,128]{1,0:T(8,128)(2,1)S(1)} %get-tuple-element.69), channel_id=1, source_target_pairs={{16,32},{32,16},{48,64},{64,48},{80,96},{96,80},{112,128},{128,112... | collective-permute-start | bytes 49160 | tf_op jit(solution)/shard_map/ppermute | solution.py:285
  131.9 3.6 %shard_map.76.blocks = bf16[6,8,5,128,128]{4,3,2,1,0:T(8,128)(2,1)S(1)} custom-call(s32[8,128]{1,0:T(8,128)S(1)} %broadcast_in_dim.73.packed, bf16[16,4,4,128,128]{4,3,2,1,0:T(8,128)(2,1)} %bitcast.79, bf16[16,4,2,128,128]{4,3,2,1,0:T(8,128)(2,1)} %bitcast.81), custom_call_target="tpu_custom_call" | custom-call | tf_op jit(solution)/shard_map/pallas_call | solution.py:200
  136.2 1.9 collective-permute-start.14
  138.4 2.3 %collective-permute-done.14.came = bf16[64,128]{1,0:T(8,128)(2,1)S(1)} collective-permute-done((bf16[64,128]{1,0:T(8,128)(2,1)S(1)}, bf16[64,128]{1,0:T(8,128)(2,1)S(1)}, u32[]{:S(2)}, u32[]{:S(2)}) %collective-permute-start.14) | collective-permute-done | bytes 16416 | tf_op jit(solution)/shard_map/ppermute | solution.py:285
  140.7 0.9 shard_map.79
  141.6 4.4 %collective-permute-start.15 = (bf16[64,128]{1,0:T(8,128)(2,1)S(1)}, bf16[64,128]{1,0:T(8,128)(2,1)S(1)}, u32[]{:S(2)}, u32[]{:S(2)}) collective-permute-start(bf16[64,128]{1,0:T(8,128)(2,1)S(1)} %get-tuple-element.73), channel_id=1, source_target_pairs={{16,32},{32,16},{48,64},{64,48},{80,96},{96,80},{112,128},{128,112... | collective-permute-start | bytes 49160 | tf_op jit(solution)/shard_map/ppermute | solution.py:285
  146.3 3.1 %collective-permute-done.15.came = bf16[64,128]{1,0:T(8,128)(2,1)S(1)} collective-permute-done((bf16[64,128]{1,0:T(8,128)(2,1)S(1)}, bf16[64,128]{1,0:T(8,128)(2,1)S(1)}, u32[]{:S(2)}, u32[]{:S(2)}) %collective-permute-start.15) | collective-permute-done | bytes 16416 | tf_op jit(solution)/shard_map/ppermute | solution.py:285
  150.0 1.9 collective-permute-start.16
  152.2 2.3 %collective-permute-done.16.came = bf16[64,128]{1,0:T(8,128)(2,1)S(1)} collective-permute-done((bf16[64,128]{1,0:T(8,128)(2,1)S(1)}, bf16[64,128]{1,0:T(8,128)(2,1)S(1)}, u32[]{:S(2)}, u32[]{:S(2)}) %collective-permute-start.16) | collective-permute-done | bytes 16416 | tf_op jit(solution)/shard_map/ppermute | solution.py:285
  155.0 4.5 %collective-permute-start.17 = (bf16[64,128]{1,0:T(8,128)(2,1)S(1)}, bf16[64,128]{1,0:T(8,128)(2,1)S(1)}, u32[]{:S(2)}, u32[]{:S(2)}) collective-permute-start(bf16[64,128]{1,0:T(8,128)(2,1)S(1)} %get-tuple-element.81), channel_id=1, source_target_pairs={{16,32},{32,16},{48,64},{64,48},{80,96},{96,80},{112,128},{128,112... | collective-permute-start | bytes 49160 | tf_op jit(solution)/shard_map/ppermute | solution.py:285
  159.7 3.1 %collective-permute-done.17.came = bf16[64,128]{1,0:T(8,128)(2,1)S(1)} collective-permute-done((bf16[64,128]{1,0:T(8,128)(2,1)S(1)}, bf16[64,128]{1,0:T(8,128)(2,1)S(1)}, u32[]{:S(2)}, u32[]{:S(2)}) %collective-permute-start.17) | collective-permute-done | bytes 16416 | tf_op jit(solution)/shard_map/ppermute | solution.py:285
  163.4 1.9 collective-permute-start.18
  165.6 2.3 %collective-permute-done.18.came = bf16[64,128]{1,0:T(8,128)(2,1)S(1)} collective-permute-done((bf16[64,128]{1,0:T(8,128)(2,1)S(1)}, bf16[64,128]{1,0:T(8,128)(2,1)S(1)}, u32[]{:S(2)}, u32[]{:S(2)}) %collective-permute-start.18) | collective-permute-done | bytes 16416 | tf_op jit(solution)/shard_map/ppermute | solution.py:285
  168.4 4.5 %collective-permute-start.19 = (bf16[64,128]{1,0:T(8,128)(2,1)S(1)}, bf16[64,128]{1,0:T(8,128)(2,1)S(1)}, u32[]{:S(2)}, u32[]{:S(2)}) collective-permute-start(bf16[64,128]{1,0:T(8,128)(2,1)S(1)} %get-tuple-element.87), channel_id=1, source_target_pairs={{16,32},{32,16},{48,64},{64,48},{80,96},{96,80},{112,128},{128,112... | collective-permute-start | bytes 49160 | tf_op jit(solution)/shard_map/ppermute | solution.py:285
  173.1 3.1 %collective-permute-done.19.came = bf16[64,128]{1,0:T(8,128)(2,1)S(1)} collective-permute-done((bf16[64,128]{1,0:T(8,128)(2,1)S(1)}, bf16[64,128]{1,0:T(8,128)(2,1)S(1)}, u32[]{:S(2)}, u32[]{:S(2)}) %collective-permute-start.19) | collective-permute-done | bytes 16416 | tf_op jit(solution)/shard_map/ppermute | solution.py:285
  176.8 1.9 collective-permute-start.20
  179.0 2.3 %collective-permute-done.20.came = bf16[64,128]{1,0:T(8,128)(2,1)S(1)} collective-permute-done((bf16[64,128]{1,0:T(8,128)(2,1)S(1)}, bf16[64,128]{1,0:T(8,128)(2,1)S(1)}, u32[]{:S(2)}, u32[]{:S(2)}) %collective-permute-start.20) | collective-permute-done | bytes 16416 | tf_op jit(solution)/shard_map/ppermute | solution.py:285
  181.8 4.5 %collective-permute-start.21 = (bf16[64,128]{1,0:T(8,128)(2,1)S(1)}, bf16[64,128]{1,0:T(8,128)(2,1)S(1)}, u32[]{:S(2)}, u32[]{:S(2)}) collective-permute-start(bf16[64,128]{1,0:T(8,128)(2,1)S(1)} %get-tuple-element.94), channel_id=1, source_target_pairs={{16,32},{32,16},{48,64},{64,48},{80,96},{96,80},{112,128},{128,112... | collective-permute-start | bytes 49160 | tf_op jit(solution)/shard_map/ppermute | solution.py:285
  186.3 3.3 %collective-permute-done.21.came = bf16[64,128]{1,0:T(8,128)(2,1)S(1)} collective-permute-done((bf16[64,128]{1,0:T(8,128)(2,1)S(1)}, bf16[64,128]{1,0:T(8,128)(2,1)S(1)}, u32[]{:S(2)}, u32[]{:S(2)}) %collective-permute-start.21) | collective-permute-done | bytes 16416 | tf_op jit(solution)/shard_map/ppermute | solution.py:285
  189.9 29.2 %all_to_all.20 = bf16[16,32,128]{2,1,0:T(8,128)(2,1)S(1)} all-to-all(bf16[16,32,128]{2,1,0:T(8,128)(2,1)S(1)} %shard_map.92), channel_id=1, replica_groups=mesh['dom'=32,'level'=16] {'level'}, dimensions={0} | all-to-all | bytes 262144 | tf_op jit(solution)/shard_map/all_to_all | solution.py:348
  (87 shorter events, 20.0 us)
Async XLA Ops:
  7.2 68.5 %all-gather.5.cloned.1.call-start = ((), (), s32[]{:S(2)}) async-start(), calls=%async_computation.2 | async-start | bytes 8912896 | tf_op jit(solution)/shard_map/all_gather | solution.py:223
  15.0 40.3 %collective-permute-start.1 = (bf16[4,2,128,128]{3,2,1,0:T(8,128)(2,1)S(1)}, bf16[4,2,128,128]{3,2,1,0:T(8,128)(2,1)S(1)}, u32[]{:S(2)}, u32[]{:S(2)}) collective-permute-start(bf16[4,2,128,128]{3,2,1,0:T(8,128)(2,1)S(1)} %pad_maximum_fusion.1), channel_id=1, source_target_pairs={{16,32},{32,16},{48,64},{64,48},{80,96},{96,80},{112,128},{128,112... | collective-permute-start | bytes 786440 | tf_op jit(solution)/shard_map/ppermute | solution.py:236
  28.7 26.7 %collective-permute-start = (bf16[4,2,128,128]{3,2,1,0:T(8,128)(2,1)S(1)}, bf16[4,2,128,128]{3,2,1,0:T(8,128)(2,1)S(1)}, u32[]{:S(2)}, u32[]{:S(2)}) collective-permute-start(bf16[4,2,128,128]{3,2,1,0:T(8,128)(2,1)S(1)} %pad_maximum_fusion.1), channel_id=1, source_target_pairs={{0,16},{16,0},{32,48},{48,32},{64,80},{80,64},{96,112},{112,96},{1... | collective-permute-start | bytes 786440 | tf_op jit(solution)/shard_map/ppermute | solution.py:235
  32.4 16.7 %all-to-all-start = ((bf16[1,4,16,4,128]{4,3,1,0,2:T(4,128)(2,1)}), bf16[1,4,16,4,128]{4,3,1,0,2:T(4,128)(2,1)S(1)}, u32[]{:S(2)}, u32[]{:S(2)}) async-start(bf16[1,4,16,4,128]{4,3,1,0,2:T(4,128)(2,1)} %copy.64), calls=%async_computation | async-start | bytes 131072 | tf_op jit(solution)/shard_map/all_to_all | solution.py:241
  40.5 83.2 %all-gather.7.cloned.1.call-start = ((), (), s32[]{:S(2)}) async-start(), calls=%async_computation.3 | async-start | bytes 4456448 | tf_op jit(solution)/shard_map/all_gather | solution.py:282
  49.8 6.3 %collective-permute-start.3 = (bf16[2,32,128]{2,1,0:T(8,128)(2,1)S(1)}, bf16[2,32,128]{2,1,0:T(8,128)(2,1)S(1)}, u32[]{:S(2)}, u32[]{:S(2)}) collective-permute-start(bf16[2,32,128]{2,1,0:T(8,128)(2,1)S(1)} %get-tuple-element.121), channel_id=1, source_target_pairs={{0,16},{16,0},{32,48},{48,32},{64,80},{80,64},{96,112},{112,96},{1... | collective-permute-start | bytes 49160 | tf_op jit(solution)/shard_map/ppermute | solution.py:276
  53.4 7.8 %collective-permute-start.2 = (bf16[2,32,128]{2,1,0:T(8,128)(2,1)S(1)}, bf16[2,32,128]{2,1,0:T(8,128)(2,1)S(1)}, u32[]{:S(2)}, u32[]{:S(2)}) collective-permute-start(bf16[2,32,128]{2,1,0:T(8,128)(2,1)S(1)} %get-tuple-element.122), channel_id=1, source_target_pairs={{16,32},{32,16},{48,64},{64,48},{80,96},{96,80},{112,128},{128,112... | collective-permute-start | bytes 49160 | tf_op jit(solution)/shard_map/ppermute | solution.py:275
  77.5 13.1 %collective-permute-start.5 = (bf16[32,128]{1,0:T(8,128)(2,1)S(1)}, bf16[32,128]{1,0:T(8,128)(2,1)S(1)}, u32[]{:S(2)}, u32[]{:S(2)}) collective-permute-start(bf16[32,128]{1,0:T(8,128)(2,1)S(1)} %shard_map.68.own.solved.rest_1_), channel_id=1, source_target_pairs={{0,16},{16,0},{32,48},{48,32},{64,80},{80,64},{96,112},{112,96},{1... | collective-permute-start | bytes 24584 | tf_op jit(solution)/shard_map/ppermute | solution.py:285
  80.8 9.8 %collective-permute-start.4 = (bf16[32,128]{1,0:T(8,128)(2,1)S(1)}, bf16[32,128]{1,0:T(8,128)(2,1)S(1)}, u32[]{:S(2)}, u32[]{:S(2)}) collective-permute-start(bf16[32,128]{1,0:T(8,128)(2,1)S(1)} %shard_map.68.own.solved.rest_1_), channel_id=1, source_target_pairs={{16,32},{32,16},{48,64},{64,48},{80,96},{96,80},{112,128},{128,112... | collective-permute-start | bytes 24584 | tf_op jit(solution)/shard_map/ppermute | solution.py:285
  91.1 7.2 %collective-permute-start.7 = (bf16[32,128]{1,0:T(8,128)(2,1)S(1)}, bf16[32,128]{1,0:T(8,128)(2,1)S(1)}, u32[]{:S(2)}, u32[]{:S(2)}) collective-permute-start(bf16[32,128]{1,0:T(8,128)(2,1)S(1)} %shard_map.70.own.solved.rest_2_), channel_id=1, source_target_pairs={{0,16},{16,0},{32,48},{48,32},{64,80},{80,64},{96,112},{112,96},{1... | collective-permute-start | bytes 24584 | tf_op jit(solution)/shard_map/ppermute | solution.py:285
  93.1 7.7 %collective-permute-start.6 = (bf16[32,128]{1,0:T(8,128)(2,1)S(1)}, bf16[32,128]{1,0:T(8,128)(2,1)S(1)}, u32[]{:S(2)}, u32[]{:S(2)}) collective-permute-start(bf16[32,128]{1,0:T(8,128)(2,1)S(1)} %shard_map.70.own.solved.rest_2_), channel_id=1, source_target_pairs={{16,32},{32,16},{48,64},{64,48},{80,96},{96,80},{112,128},{128,112... | collective-permute-start | bytes 24584 | tf_op jit(solution)/shard_map/ppermute | solution.py:285
  101.3 7.2 %collective-permute-start.9 = (bf16[32,128]{1,0:T(8,128)(2,1)S(1)}, bf16[32,128]{1,0:T(8,128)(2,1)S(1)}, u32[]{:S(2)}, u32[]{:S(2)}) collective-permute-start(bf16[32,128]{1,0:T(8,128)(2,1)S(1)} %shard_map.71.own.solved.rest_3_), channel_id=1, source_target_pairs={{0,16},{16,0},{32,48},{48,32},{64,80},{80,64},{96,112},{112,96},{1... | collective-permute-start | bytes 24584 | tf_op jit(solution)/shard_map/ppermute | solution.py:285
  103.3 7.7 %collective-permute-start.8 = (bf16[32,128]{1,0:T(8,128)(2,1)S(1)}, bf16[32,128]{1,0:T(8,128)(2,1)S(1)}, u32[]{:S(2)}, u32[]{:S(2)}) collective-permute-start(bf16[32,128]{1,0:T(8,128)(2,1)S(1)} %shard_map.71.own.solved.rest_3_), channel_id=1, source_target_pairs={{16,32},{32,16},{48,64},{64,48},{80,96},{96,80},{112,128},{128,112... | collective-permute-start | bytes 24584 | tf_op jit(solution)/shard_map/ppermute | solution.py:285
  111.5 7.2 %collective-permute-start.11 = (bf16[32,128]{1,0:T(8,128)(2,1)S(1)}, bf16[32,128]{1,0:T(8,128)(2,1)S(1)}, u32[]{:S(2)}, u32[]{:S(2)}) collective-permute-start(bf16[32,128]{1,0:T(8,128)(2,1)S(1)} %shard_map.72.own.solved.rest_4_), channel_id=1, source_target_pairs={{0,16},{16,0},{32,48},{48,32},{64,80},{80,64},{96,112},{112,96},{1... | collective-permute-start | bytes 24584 | tf_op jit(solution)/shard_map/ppermute | solution.py:285
  113.5 7.7 %collective-permute-start.10 = (bf16[32,128]{1,0:T(8,128)(2,1)S(1)}, bf16[32,128]{1,0:T(8,128)(2,1)S(1)}, u32[]{:S(2)}, u32[]{:S(2)}) collective-permute-start(bf16[32,128]{1,0:T(8,128)(2,1)S(1)} %shard_map.72.own.solved.rest_4_), channel_id=1, source_target_pairs={{16,32},{32,16},{48,64},{64,48},{80,96},{96,80},{112,128},{128,112... | collective-permute-start | bytes 24584 | tf_op jit(solution)/shard_map/ppermute | solution.py:285
  121.7 4.4 %collective-permute-start.12 = (bf16[32,128]{1,0:T(8,128)(2,1)S(1)}, bf16[32,128]{1,0:T(8,128)(2,1)S(1)}, u32[]{:S(2)}, u32[]{:S(2)}) collective-permute-start(bf16[32,128]{1,0:T(8,128)(2,1)S(1)} %shard_map.73.own.solved.rest_5_), channel_id=1, source_target_pairs={{0,16},{16,0},{32,48},{48,32},{64,80},{80,64},{96,112},{112,96},{1... | collective-permute-start | bytes 24584 | tf_op jit(solution)/shard_map/ppermute | solution.py:285
  126.6 8.9 %collective-permute-start.13 = (bf16[64,128]{1,0:T(8,128)(2,1)S(1)}, bf16[64,128]{1,0:T(8,128)(2,1)S(1)}, u32[]{:S(2)}, u32[]{:S(2)}) collective-permute-start(bf16[64,128]{1,0:T(8,128)(2,1)S(1)} %get-tuple-element.69), channel_id=1, source_target_pairs={{16,32},{32,16},{48,64},{64,48},{80,96},{96,80},{112,128},{128,112... | collective-permute-start | bytes 49160 | tf_op jit(solution)/shard_map/ppermute | solution.py:285
  136.2 4.5 %collective-permute-start.14 = (bf16[64,128]{1,0:T(8,128)(2,1)S(1)}, bf16[64,128]{1,0:T(8,128)(2,1)S(1)}, u32[]{:S(2)}, u32[]{:S(2)}) collective-permute-start(bf16[64,128]{1,0:T(8,128)(2,1)S(1)} %get-tuple-element.70), channel_id=1, source_target_pairs={{0,16},{16,0},{32,48},{48,32},{64,80},{80,64},{96,112},{112,96},{1... | collective-permute-start | bytes 49160 | tf_op jit(solution)/shard_map/ppermute | solution.py:285
  141.6 7.8 %collective-permute-start.15 = (bf16[64,128]{1,0:T(8,128)(2,1)S(1)}, bf16[64,128]{1,0:T(8,128)(2,1)S(1)}, u32[]{:S(2)}, u32[]{:S(2)}) collective-permute-start(bf16[64,128]{1,0:T(8,128)(2,1)S(1)} %get-tuple-element.73), channel_id=1, source_target_pairs={{16,32},{32,16},{48,64},{64,48},{80,96},{96,80},{112,128},{128,112... | collective-permute-start | bytes 49160 | tf_op jit(solution)/shard_map/ppermute | solution.py:285
  150.0 4.5 %collective-permute-start.16 = (bf16[64,128]{1,0:T(8,128)(2,1)S(1)}, bf16[64,128]{1,0:T(8,128)(2,1)S(1)}, u32[]{:S(2)}, u32[]{:S(2)}) collective-permute-start(bf16[64,128]{1,0:T(8,128)(2,1)S(1)} %get-tuple-element.78), channel_id=1, source_target_pairs={{0,16},{16,0},{32,48},{48,32},{64,80},{80,64},{96,112},{112,96},{1... | collective-permute-start | bytes 49160 | tf_op jit(solution)/shard_map/ppermute | solution.py:285
  155.0 7.8 %collective-permute-start.17 = (bf16[64,128]{1,0:T(8,128)(2,1)S(1)}, bf16[64,128]{1,0:T(8,128)(2,1)S(1)}, u32[]{:S(2)}, u32[]{:S(2)}) collective-permute-start(bf16[64,128]{1,0:T(8,128)(2,1)S(1)} %get-tuple-element.81), channel_id=1, source_target_pairs={{16,32},{32,16},{48,64},{64,48},{80,96},{96,80},{112,128},{128,112... | collective-permute-start | bytes 49160 | tf_op jit(solution)/shard_map/ppermute | solution.py:285
  163.4 4.5 %collective-permute-start.18 = (bf16[64,128]{1,0:T(8,128)(2,1)S(1)}, bf16[64,128]{1,0:T(8,128)(2,1)S(1)}, u32[]{:S(2)}, u32[]{:S(2)}) collective-permute-start(bf16[64,128]{1,0:T(8,128)(2,1)S(1)} %get-tuple-element.84), channel_id=1, source_target_pairs={{0,16},{16,0},{32,48},{48,32},{64,80},{80,64},{96,112},{112,96},{1... | collective-permute-start | bytes 49160 | tf_op jit(solution)/shard_map/ppermute | solution.py:285
  168.4 7.8 %collective-permute-start.19 = (bf16[64,128]{1,0:T(8,128)(2,1)S(1)}, bf16[64,128]{1,0:T(8,128)(2,1)S(1)}, u32[]{:S(2)}, u32[]{:S(2)}) collective-permute-start(bf16[64,128]{1,0:T(8,128)(2,1)S(1)} %get-tuple-element.87), channel_id=1, source_target_pairs={{16,32},{32,16},{48,64},{64,48},{80,96},{96,80},{112,128},{128,112... | collective-permute-start | bytes 49160 | tf_op jit(solution)/shard_map/ppermute | solution.py:285
  176.8 4.5 %collective-permute-start.20 = (bf16[64,128]{1,0:T(8,128)(2,1)S(1)}, bf16[64,128]{1,0:T(8,128)(2,1)S(1)}, u32[]{:S(2)}, u32[]{:S(2)}) collective-permute-start(bf16[64,128]{1,0:T(8,128)(2,1)S(1)} %get-tuple-element.90), channel_id=1, source_target_pairs={{0,16},{16,0},{32,48},{48,32},{64,80},{80,64},{96,112},{112,96},{1... | collective-permute-start | bytes 49160 | tf_op jit(solution)/shard_map/ppermute | solution.py:285
  181.8 7.8 %collective-permute-start.21 = (bf16[64,128]{1,0:T(8,128)(2,1)S(1)}, bf16[64,128]{1,0:T(8,128)(2,1)S(1)}, u32[]{:S(2)}, u32[]{:S(2)}) collective-permute-start(bf16[64,128]{1,0:T(8,128)(2,1)S(1)} %get-tuple-element.94), channel_id=1, source_target_pairs={{16,32},{32,16},{48,64},{64,48},{80,96},{96,80},{112,128},{128,112... | collective-permute-start | bytes 49160 | tf_op jit(solution)/shard_map/ppermute | solution.py:285
Sparse Core Ops, SparseCore 0:
  10.1 65.5 all-gather.4
  77.8 43.5 all-gather.6

commit v16 on v15

--- a/solution.py
+++ b/solution.py
@@ -317,7 +317,6 @@
     held, sent = call(kernel, sums, blocks, meets, solved[-1], solved_mate[-1])
     lower = range(paired)
     below = arranged(arrange_pairs_kernel, lower, 5, 8 * len(lower) - 6, held, weights, mates)
-    blocks, below = lax.optimization_barrier((blocks, below))
 
     def turned(blocks, at, behind):
         _, blocks = lax.optimization_barrier((behind, blocks))

time: 228 us -> 224 us (0.982)
  waiting for transfers between devices: 50 us -> 43 us
  starting transfers between devices: 94.2 us -> 100 us
  blocking collectives: 29.2 us -> 25.9 us
    ppermute x18, waiting for transfers between devices: 29.4 us -> 20.3 us  [swap(): lax.ppermute(vector, 'dom', far_pairs if level % 2 == 0 else near_pairs)]
    ppermute x18, starting transfers between devices: 64.9 us -> 72.2 us  [swap(): lax.ppermute(vector, 'dom', far_pairs if level % 2 == 0 else near_pairs)]
    all_to_all x1, blocking collectives: 29.2 us -> 25.9 us  [local(): dealt = lax.all_to_all(dealt, 'level', 0, 0, tiled=False)]
    all_gather x1, waiting for transfers between devices: 14.3 us -> 17.4 us  [local(): weights = lax.all_gather(weights, 'level')]
    ppermute x1, starting transfers between devices: 1.92 us -> 4.83 us  [local(): by_near = lax.ppermute(mates, 'dom', near_pairs)]
    ppermute x1, starting transfers between devices: 13.7 us -> 11 us  [local(): by_far = lax.ppermute(mates, 'dom', far_pairs)]
  transfers between devices with their start and end apart: 25 -> 25, of which waited for: 15 -> 18; matrix products, arithmetic and copies ran while one was open for 6% -> 6% of each run, Pallas kernels for 6% -> 6%
where the time goes in v16:
time: 224 us; the launch traced here: 223 us
  starting transfers between devices  100 us (45%)
  waiting for transfers between devices  43 us (19%)
  blocking collectives  25.9 us (12%)
  Pallas kernels  19.6 us (9%)
  between operations  17.2 us (8%)
  local copies, waits for them, and re-layouts  8.03 us (4%)
  other arithmetic  7.92 us (4%)
    ppermute x18, starting transfers between devices, swap(): lax.ppermute(vector, 'dom', far_pairs if level % 2 == 0 else near_pairs)  72.2 us
    all_to_all x1, blocking collectives, local(): dealt = lax.all_to_all(dealt, 'level', 0, 0, tiled=False)  25.9 us
    ppermute x18, waiting for transfers between devices, swap(): lax.ppermute(vector, 'dom', far_pairs if level % 2 == 0 else near_pairs)  20.3 us
    pallas_call x25, Pallas kernels, call(): pl.pallas_call(kernel, out_shape=outs, in_specs=specs, out_specs=[pl.Bloc...  19.6 us
    all_gather x1, waiting for transfers between devices, local(): weights = lax.all_gather(weights, 'level')  17.4 us
    ppermute x1, starting transfers between devices, local(): by_far = lax.ppermute(mates, 'dom', far_pairs)  11 us
    all_to_all x1, starting transfers between devices, local(): side = lax.all_to_all(side, 'level', 1, 0, tiled=False)  8.35 us
    ppermute x1, starting transfers between devices, local(): by_near = lax.ppermute(mates, 'dom', near_pairs)  4.83 us
  transfers between devices with their start and end apart: 25, of which 18 were waited for; matrix products, arithmetic and copies ran while one was open for 6% of the time, Pallas kernels for 6%

profile of v16, /device:TPU:1, one launch (start us, length us, event | category | flops | bytes accessed | tf_op | source)
XLA Modules:
  0.0 223.0 jit_solution(2533766914988180619)
XLA Ops:
  7.2 1.9 pad_maximum_fusion
  9.2 1.3 fusion.7
  13.1 1.0 slice_select_fusion
  14.1 0.9 pad_maximum_fusion.1
  15.0 4.8 %collective-permute-start = (bf16[4,2,128,128]{3,2,1,0:T(8,128)(2,1)S(1)}, bf16[4,2,128,128]{3,2,1,0:T(8,128)(2,1)S(1)}, u32[]{:S(2)}, u32[]{:S(2)}) collective-permute-start(bf16[4,2,128,128]{3,2,1,0:T(8,128)(2,1)S(1)} %pad_maximum_fusion.1), channel_id=1, source_target_pairs={{0,16},{16,0},{32,48},{48,32},{64,80},{80,64},{96,112},{112,96},{1... | collective-permute-start | bytes 786440 | tf_op jit(solution)/shard_map/ppermute | solution.py:235
  19.9 11.0 %collective-permute-start.1 = (bf16[4,2,128,128]{3,2,1,0:T(8,128)(2,1)S(1)}, bf16[4,2,128,128]{3,2,1,0:T(8,128)(2,1)S(1)}, u32[]{:S(2)}, u32[]{:S(2)}) collective-permute-start(bf16[4,2,128,128]{3,2,1,0:T(8,128)(2,1)S(1)} %pad_maximum_fusion.1), channel_id=1, source_target_pairs={{16,32},{32,16},{48,64},{64,48},{80,96},{96,80},{112,128},{128,112... | collective-permute-start | bytes 786440 | tf_op jit(solution)/shard_map/ppermute | solution.py:236
  30.9 1.1 fusion
  32.7 8.3 %all-to-all-start = ((bf16[1,4,16,4,128]{4,3,1,0,2:T(4,128)(2,1)}), bf16[1,4,16,4,128]{4,3,1,0,2:T(4,128)(2,1)S(1)}, u32[]{:S(2)}, u32[]{:S(2)}) async-start(bf16[1,4,16,4,128]{4,3,1,0,2:T(4,128)(2,1)} %copy.64), calls=%async_computation | async-start | bytes 131072 | tf_op jit(solution)/shard_map/all_to_all | solution.py:241
  48.6 1.1 all-to-all-done
  50.3 1.9 collective-permute-start.2
  52.3 1.9 collective-permute-start.3
  54.9 3.2 %collective-permute-done.2 = bf16[2,32,128]{2,1,0:T(8,128)(2,1)S(1)} collective-permute-done((bf16[2,32,128]{2,1,0:T(8,128)(2,1)S(1)}, bf16[2,32,128]{2,1,0:T(8,128)(2,1)S(1)}, u32[]{:S(2)}, u32[]{:S(2)}) %collective-permute-start.2) | collective-permute-done | bytes 16416 | tf_op jit(solution)/shard_map/ppermute | solution.py:275
  58.3 17.4 %all-gather.5.cloned.1.call-done = bf16[64,4,128,128]{3,2,1,0:T(8,128)(2,1)} async-done(((bf16[4,4,128,128]{3,2,1,0:T(8,128)(2,1)}), bf16[64,4,128,128]{3,2,1,0:T(8,128)(2,1)}) %all-gather.5.cloned.1.call-update) | async-done | bytes 8388624 | tf_op jit(solution)/shard_map/all_gather | solution.py:223
  75.7 1.8 shard_map.68.own.solved.rest_1_
  77.5 7.7 %collective-permute-start.4 = (bf16[32,128]{1,0:T(8,128)(2,1)S(1)}, bf16[32,128]{1,0:T(8,128)(2,1)S(1)}, u32[]{:S(2)}, u32[]{:S(2)}) collective-permute-start(bf16[32,128]{1,0:T(8,128)(2,1)S(1)} %shard_map.68.own.solved.rest_1_), channel_id=1, source_target_pairs={{16,32},{32,16},{48,64},{64,48},{80,96},{96,80},{112,128},{128,112... | collective-permute-start | bytes 24584 | tf_op jit(solution)/shard_map/ppermute | solution.py:285
  85.2 1.9 collective-permute-start.5
  87.2 2.4 %shard_map.69.weights = bf16[4,8,4,128,128]{4,3,2,1,0:T(8,128)(2,1)S(1)} custom-call(s32[8,128]{1,0:T(8,128)S(1)} %broadcast_in_dim.73.packed, bf16[16,4,4,128,128]{4,3,2,1,0:T(8,128)(2,1)} %bitcast.77), custom_call_target="tpu_custom_call" | custom-call | tf_op jit(solution)/shard_map/pallas_call | solution.py:200
  90.2 3.9 %collective-permute-start.6 = (bf16[32,128]{1,0:T(8,128)(2,1)S(1)}, bf16[32,128]{1,0:T(8,128)(2,1)S(1)}, u32[]{:S(2)}, u32[]{:S(2)}) collective-permute-start(bf16[32,128]{1,0:T(8,128)(2,1)S(1)} %shard_map.70.own.solved.rest_2_), channel_id=1, source_target_pairs={{16,32},{32,16},{48,64},{64,48},{80,96},{96,80},{112,128},{128,112... | collective-permute-start | bytes 24584 | tf_op jit(solution)/shard_map/ppermute | solution.py:285
  94.1 1.9 collective-permute-start.7
  96.0 1.9 collective-permute-done.6.far.solved_mate
  97.9 1.0 collective-permute-done.7.near
  99.4 4.7 %collective-permute-start.8 = (bf16[32,128]{1,0:T(8,128)(2,1)S(1)}, bf16[32,128]{1,0:T(8,128)(2,1)S(1)}, u32[]{:S(2)}, u32[]{:S(2)}) collective-permute-start(bf16[32,128]{1,0:T(8,128)(2,1)S(1)} %shard_map.71.own.solved.rest_3_), channel_id=1, source_target_pairs={{16,32},{32,16},{48,64},{64,48},{80,96},{96,80},{112,128},{128,112... | collective-permute-start | bytes 24584 | tf_op jit(solution)/shard_map/ppermute | solution.py:285
  104.2 1.9 collective-permute-start.9
  106.1 1.1 collective-permute-done.8.far
  107.1 1.8 collective-permute-done.9.near.solved_mate
  109.5 3.8 %collective-permute-start.10 = (bf16[32,128]{1,0:T(8,128)(2,1)S(1)}, bf16[32,128]{1,0:T(8,128)(2,1)S(1)}, u32[]{:S(2)}, u32[]{:S(2)}) collective-permute-start(bf16[32,128]{1,0:T(8,128)(2,1)S(1)} %shard_map.72.own.solved.rest_4_), channel_id=1, source_target_pairs={{16,32},{32,16},{48,64},{64,48},{80,96},{96,80},{112,128},{128,112... | collective-permute-start | bytes 24584 | tf_op jit(solution)/shard_map/ppermute | solution.py:285
  113.3 1.9 collective-permute-start.11
  115.2 2.0 collective-permute-done.10.far.solved_mate
  118.6 1.9 collective-permute-start.12
  120.5 0.9 all-gather.7.cloned.1.call-done
  121.5 2.1 shard_map.74.blocks
  124.1 7.8 %collective-permute-start.13 = (bf16[64,128]{1,0:T(8,128)(2,1)S(1)}, bf16[64,128]{1,0:T(8,128)(2,1)S(1)}, u32[]{:S(2)}, u32[]{:S(2)}) collective-permute-start(bf16[64,128]{1,0:T(8,128)(2,1)S(1)} %get-tuple-element.65), channel_id=1, source_target_pairs={{16,32},{32,16},{48,64},{64,48},{80,96},{96,80},{112,128},{128,112... | collective-permute-start | bytes 49160 | tf_op jit(solution)/shard_map/ppermute | solution.py:285
  131.9 1.1 collective-permute-done.13.came
  133.7 1.9 collective-permute-start.14
  135.9 2.3 %collective-permute-done.14.came = bf16[64,128]{1,0:T(8,128)(2,1)S(1)} collective-permute-done((bf16[64,128]{1,0:T(8,128)(2,1)S(1)}, bf16[64,128]{1,0:T(8,128)(2,1)S(1)}, u32[]{:S(2)}, u32[]{:S(2)}) %collective-permute-start.14) | collective-permute-done | bytes 16416 | tf_op jit(solution)/shard_map/ppermute | solution.py:285
  138.1 0.9 shard_map.79
  139.1 6.7 %collective-permute-start.15 = (bf16[64,128]{1,0:T(8,128)(2,1)S(1)}, bf16[64,128]{1,0:T(8,128)(2,1)S(1)}, u32[]{:S(2)}, u32[]{:S(2)}) collective-permute-start(bf16[64,128]{1,0:T(8,128)(2,1)S(1)} %get-tuple-element.69), channel_id=1, source_target_pairs={{16,32},{32,16},{48,64},{64,48},{80,96},{96,80},{112,128},{128,112... | collective-permute-start | bytes 49160 | tf_op jit(solution)/shard_map/ppermute | solution.py:285
  147.4 1.9 collective-permute-start.16
  149.4 3.6 %shard_map.76.blocks = bf16[6,8,5,128,128]{4,3,2,1,0:T(8,128)(2,1)S(1)} custom-call(s32[8,128]{1,0:T(8,128)S(1)} %broadcast_in_dim.73.packed, bf16[16,4,4,128,128]{4,3,2,1,0:T(8,128)(2,1)} %bitcast.79, bf16[16,4,2,128,128]{4,3,2,1,0:T(8,128)(2,1)} %bitcast.81), custom_call_target="tpu_custom_call" | custom-call | tf_op jit(solution)/shard_map/pallas_call | solution.py:200
  153.8 6.7 %collective-permute-start.17 = (bf16[64,128]{1,0:T(8,128)(2,1)S(1)}, bf16[64,128]{1,0:T(8,128)(2,1)S(1)}, u32[]{:S(2)}, u32[]{:S(2)}) collective-permute-start(bf16[64,128]{1,0:T(8,128)(2,1)S(1)} %get-tuple-element.77), channel_id=1, source_target_pairs={{16,32},{32,16},{48,64},{64,48},{80,96},{96,80},{112,128},{128,112... | collective-permute-start | bytes 49160 | tf_op jit(solution)/shard_map/ppermute | solution.py:285
  162.2 1.9 collective-permute-start.18
  164.4 2.3 %collective-permute-done.18.came = bf16[64,128]{1,0:T(8,128)(2,1)S(1)} collective-permute-done((bf16[64,128]{1,0:T(8,128)(2,1)S(1)}, bf16[64,128]{1,0:T(8,128)(2,1)S(1)}, u32[]{:S(2)}, u32[]{:S(2)}) %collective-permute-start.18) | collective-permute-done | bytes 16416 | tf_op jit(solution)/shard_map/ppermute | solution.py:285
  167.2 7.0 %collective-permute-start.19 = (bf16[64,128]{1,0:T(8,128)(2,1)S(1)}, bf16[64,128]{1,0:T(8,128)(2,1)S(1)}, u32[]{:S(2)}, u32[]{:S(2)}) collective-permute-start(bf16[64,128]{1,0:T(8,128)(2,1)S(1)} %get-tuple-element.83), channel_id=1, source_target_pairs={{16,32},{32,16},{48,64},{64,48},{80,96},{96,80},{112,128},{128,112... | collective-permute-start | bytes 49160 | tf_op jit(solution)/shard_map/ppermute | solution.py:285
  175.9 1.9 collective-permute-start.20
  178.1 2.3 %collective-permute-done.20.came = bf16[64,128]{1,0:T(8,128)(2,1)S(1)} collective-permute-done((bf16[64,128]{1,0:T(8,128)(2,1)S(1)}, bf16[64,128]{1,0:T(8,128)(2,1)S(1)}, u32[]{:S(2)}, u32[]{:S(2)}) %collective-permute-start.20) | collective-permute-done | bytes 16416 | tf_op jit(solution)/shard_map/ppermute | solution.py:285
  180.9 6.7 %collective-permute-start.21 = (bf16[64,128]{1,0:T(8,128)(2,1)S(1)}, bf16[64,128]{1,0:T(8,128)(2,1)S(1)}, u32[]{:S(2)}, u32[]{:S(2)}) collective-permute-start(bf16[64,128]{1,0:T(8,128)(2,1)S(1)} %get-tuple-element.90), channel_id=1, source_target_pairs={{16,32},{32,16},{48,64},{64,48},{80,96},{96,80},{112,128},{128,112... | collective-permute-start | bytes 49160 | tf_op jit(solution)/shard_map/ppermute | solution.py:285
  187.6 1.1 collective-permute-done.21.came
  189.0 25.9 %all_to_all.20 = bf16[16,32,128]{2,1,0:T(8,128)(2,1)S(1)} all-to-all(bf16[16,32,128]{2,1,0:T(8,128)(2,1)S(1)} %shard_map.92), channel_id=1, replica_groups=mesh['dom'=32,'level'=16] {'level'}, dimensions={0} | all-to-all | bytes 262144 | tf_op jit(solution)/shard_map/all_to_all | solution.py:347
  (87 shorter events, 23.1 us)
Async XLA Ops:
  7.2 68.5 %all-gather.5.cloned.1.call-start = ((), (), s32[]{:S(2)}) async-start(), calls=%async_computation.2 | async-start | bytes 8912896 | tf_op jit(solution)/shard_map/all_gather | solution.py:223
  15.0 39.2 %collective-permute-start = (bf16[4,2,128,128]{3,2,1,0:T(8,128)(2,1)S(1)}, bf16[4,2,128,128]{3,2,1,0:T(8,128)(2,1)S(1)}, u32[]{:S(2)}, u32[]{:S(2)}) collective-permute-start(bf16[4,2,128,128]{3,2,1,0:T(8,128)(2,1)S(1)} %pad_maximum_fusion.1), channel_id=1, source_target_pairs={{0,16},{16,0},{32,48},{48,32},{64,80},{80,64},{96,112},{112,96},{1... | collective-permute-start | bytes 786440 | tf_op jit(solution)/shard_map/ppermute | solution.py:235
  19.9 34.3 %collective-permute-start.1 = (bf16[4,2,128,128]{3,2,1,0:T(8,128)(2,1)S(1)}, bf16[4,2,128,128]{3,2,1,0:T(8,128)(2,1)S(1)}, u32[]{:S(2)}, u32[]{:S(2)}) collective-permute-start(bf16[4,2,128,128]{3,2,1,0:T(8,128)(2,1)S(1)} %pad_maximum_fusion.1), channel_id=1, source_target_pairs={{16,32},{32,16},{48,64},{64,48},{80,96},{96,80},{112,128},{128,112... | collective-permute-start | bytes 786440 | tf_op jit(solution)/shard_map/ppermute | solution.py:236
  32.7 17.0 %all-to-all-start = ((bf16[1,4,16,4,128]{4,3,1,0,2:T(4,128)(2,1)}), bf16[1,4,16,4,128]{4,3,1,0,2:T(4,128)(2,1)S(1)}, u32[]{:S(2)}, u32[]{:S(2)}) async-start(bf16[1,4,16,4,128]{4,3,1,0,2:T(4,128)(2,1)} %copy.64), calls=%async_computation | async-start | bytes 131072 | tf_op jit(solution)/shard_map/all_to_all | solution.py:241
  41.0 80.4 %all-gather.7.cloned.1.call-start = ((), (), s32[]{:S(2)}) async-start(), calls=%async_computation.3 | async-start | bytes 4456448 | tf_op jit(solution)/shard_map/all_gather | solution.py:282
  50.3 7.8 %collective-permute-start.2 = (bf16[2,32,128]{2,1,0:T(8,128)(2,1)S(1)}, bf16[2,32,128]{2,1,0:T(8,128)(2,1)S(1)}, u32[]{:S(2)}, u32[]{:S(2)}) collective-permute-start(bf16[2,32,128]{2,1,0:T(8,128)(2,1)S(1)} %get-tuple-element.118), channel_id=1, source_target_pairs={{16,32},{32,16},{48,64},{64,48},{80,96},{96,80},{112,128},{128,112... | collective-permute-start | bytes 49160 | tf_op jit(solution)/shard_map/ppermute | solution.py:275
  52.3 5.9 %collective-permute-start.3 = (bf16[2,32,128]{2,1,0:T(8,128)(2,1)S(1)}, bf16[2,32,128]{2,1,0:T(8,128)(2,1)S(1)}, u32[]{:S(2)}, u32[]{:S(2)}) collective-permute-start(bf16[2,32,128]{2,1,0:T(8,128)(2,1)S(1)} %get-tuple-element.117), channel_id=1, source_target_pairs={{0,16},{16,0},{32,48},{48,32},{64,80},{80,64},{96,112},{112,96},{1... | collective-permute-start | bytes 49160 | tf_op jit(solution)/shard_map/ppermute | solution.py:276
  77.5 12.1 %collective-permute-start.4 = (bf16[32,128]{1,0:T(8,128)(2,1)S(1)}, bf16[32,128]{1,0:T(8,128)(2,1)S(1)}, u32[]{:S(2)}, u32[]{:S(2)}) collective-permute-start(bf16[32,128]{1,0:T(8,128)(2,1)S(1)} %shard_map.68.own.solved.rest_1_), channel_id=1, source_target_pairs={{16,32},{32,16},{48,64},{64,48},{80,96},{96,80},{112,128},{128,112... | collective-permute-start | bytes 24584 | tf_op jit(solution)/shard_map/ppermute | solution.py:285
  85.2 4.4 %collective-permute-start.5 = (bf16[32,128]{1,0:T(8,128)(2,1)S(1)}, bf16[32,128]{1,0:T(8,128)(2,1)S(1)}, u32[]{:S(2)}, u32[]{:S(2)}) collective-permute-start(bf16[32,128]{1,0:T(8,128)(2,1)S(1)} %shard_map.68.own.solved.rest_1_), channel_id=1, source_target_pairs={{0,16},{16,0},{32,48},{48,32},{64,80},{80,64},{96,112},{112,96},{1... | collective-permute-start | bytes 24584 | tf_op jit(solution)/shard_map/ppermute | solution.py:285
  90.2 7.7 %collective-permute-start.6 = (bf16[32,128]{1,0:T(8,128)(2,1)S(1)}, bf16[32,128]{1,0:T(8,128)(2,1)S(1)}, u32[]{:S(2)}, u32[]{:S(2)}) collective-permute-start(bf16[32,128]{1,0:T(8,128)(2,1)S(1)} %shard_map.70.own.solved.rest_2_), channel_id=1, source_target_pairs={{16,32},{32,16},{48,64},{64,48},{80,96},{96,80},{112,128},{128,112... | collective-permute-start | bytes 24584 | tf_op jit(solution)/shard_map/ppermute | solution.py:285
  94.1 4.8 %collective-permute-start.7 = (bf16[32,128]{1,0:T(8,128)(2,1)S(1)}, bf16[32,128]{1,0:T(8,128)(2,1)S(1)}, u32[]{:S(2)}, u32[]{:S(2)}) collective-permute-start(bf16[32,128]{1,0:T(8,128)(2,1)S(1)} %shard_map.70.own.solved.rest_2_), channel_id=1, source_target_pairs={{0,16},{16,0},{32,48},{48,32},{64,80},{80,64},{96,112},{112,96},{1... | collective-permute-start | bytes 24584 | tf_op jit(solution)/shard_map/ppermute | solution.py:285
  99.4 7.7 %collective-permute-start.8 = (bf16[32,128]{1,0:T(8,128)(2,1)S(1)}, bf16[32,128]{1,0:T(8,128)(2,1)S(1)}, u32[]{:S(2)}, u32[]{:S(2)}) collective-permute-start(bf16[32,128]{1,0:T(8,128)(2,1)S(1)} %shard_map.71.own.solved.rest_3_), channel_id=1, source_target_pairs={{16,32},{32,16},{48,64},{64,48},{80,96},{96,80},{112,128},{128,112... | collective-permute-start | bytes 24584 | tf_op jit(solution)/shard_map/ppermute | solution.py:285
  104.2 4.8 %collective-permute-start.9 = (bf16[32,128]{1,0:T(8,128)(2,1)S(1)}, bf16[32,128]{1,0:T(8,128)(2,1)S(1)}, u32[]{:S(2)}, u32[]{:S(2)}) collective-permute-start(bf16[32,128]{1,0:T(8,128)(2,1)S(1)} %shard_map.71.own.solved.rest_3_), channel_id=1, source_target_pairs={{0,16},{16,0},{32,48},{48,32},{64,80},{80,64},{96,112},{112,96},{1... | collective-permute-start | bytes 24584 | tf_op jit(solution)/shard_map/ppermute | solution.py:285
  109.5 7.7 %collective-permute-start.10 = (bf16[32,128]{1,0:T(8,128)(2,1)S(1)}, bf16[32,128]{1,0:T(8,128)(2,1)S(1)}, u32[]{:S(2)}, u32[]{:S(2)}) collective-permute-start(bf16[32,128]{1,0:T(8,128)(2,1)S(1)} %shard_map.72.own.solved.rest_4_), channel_id=1, source_target_pairs={{16,32},{32,16},{48,64},{64,48},{80,96},{96,80},{112,128},{128,112... | collective-permute-start | bytes 24584 | tf_op jit(solution)/shard_map/ppermute | solution.py:285
  113.3 4.8 %collective-permute-start.11 = (bf16[32,128]{1,0:T(8,128)(2,1)S(1)}, bf16[32,128]{1,0:T(8,128)(2,1)S(1)}, u32[]{:S(2)}, u32[]{:S(2)}) collective-permute-start(bf16[32,128]{1,0:T(8,128)(2,1)S(1)} %shard_map.72.own.solved.rest_4_), channel_id=1, source_target_pairs={{0,16},{16,0},{32,48},{48,32},{64,80},{80,64},{96,112},{112,96},{1... | collective-permute-start | bytes 24584 | tf_op jit(solution)/shard_map/ppermute | solution.py:285
  118.6 4.9 %collective-permute-start.12 = (bf16[32,128]{1,0:T(8,128)(2,1)S(1)}, bf16[32,128]{1,0:T(8,128)(2,1)S(1)}, u32[]{:S(2)}, u32[]{:S(2)}) collective-permute-start(bf16[32,128]{1,0:T(8,128)(2,1)S(1)} %shard_map.73.own.solved.rest_5_), channel_id=1, source_target_pairs={{0,16},{16,0},{32,48},{48,32},{64,80},{80,64},{96,112},{112,96},{1... | collective-permute-start | bytes 24584 | tf_op jit(solution)/shard_map/ppermute | solution.py:285
  124.1 8.9 %collective-permute-start.13 = (bf16[64,128]{1,0:T(8,128)(2,1)S(1)}, bf16[64,128]{1,0:T(8,128)(2,1)S(1)}, u32[]{:S(2)}, u32[]{:S(2)}) collective-permute-start(bf16[64,128]{1,0:T(8,128)(2,1)S(1)} %get-tuple-element.65), channel_id=1, source_target_pairs={{16,32},{32,16},{48,64},{64,48},{80,96},{96,80},{112,128},{128,112... | collective-permute-start | bytes 49160 | tf_op jit(solution)/shard_map/ppermute | solution.py:285
  133.7 4.5 %collective-permute-start.14 = (bf16[64,128]{1,0:T(8,128)(2,1)S(1)}, bf16[64,128]{1,0:T(8,128)(2,1)S(1)}, u32[]{:S(2)}, u32[]{:S(2)}) collective-permute-start(bf16[64,128]{1,0:T(8,128)(2,1)S(1)} %get-tuple-element.66), channel_id=1, source_target_pairs={{0,16},{16,0},{32,48},{48,32},{64,80},{80,64},{96,112},{112,96},{1... | collective-permute-start | bytes 49160 | tf_op jit(solution)/shard_map/ppermute | solution.py:285
  139.1 7.8 %collective-permute-start.15 = (bf16[64,128]{1,0:T(8,128)(2,1)S(1)}, bf16[64,128]{1,0:T(8,128)(2,1)S(1)}, u32[]{:S(2)}, u32[]{:S(2)}) collective-permute-start(bf16[64,128]{1,0:T(8,128)(2,1)S(1)} %get-tuple-element.69), channel_id=1, source_target_pairs={{16,32},{32,16},{48,64},{64,48},{80,96},{96,80},{112,128},{128,112... | collective-permute-start | bytes 49160 | tf_op jit(solution)/shard_map/ppermute | solution.py:285
  147.4 5.8 %collective-permute-start.16 = (bf16[64,128]{1,0:T(8,128)(2,1)S(1)}, bf16[64,128]{1,0:T(8,128)(2,1)S(1)}, u32[]{:S(2)}, u32[]{:S(2)}) collective-permute-start(bf16[64,128]{1,0:T(8,128)(2,1)S(1)} %get-tuple-element.74), channel_id=1, source_target_pairs={{0,16},{16,0},{32,48},{48,32},{64,80},{80,64},{96,112},{112,96},{1... | collective-permute-start | bytes 49160 | tf_op jit(solution)/shard_map/ppermute | solution.py:285
  153.8 7.8 %collective-permute-start.17 = (bf16[64,128]{1,0:T(8,128)(2,1)S(1)}, bf16[64,128]{1,0:T(8,128)(2,1)S(1)}, u32[]{:S(2)}, u32[]{:S(2)}) collective-permute-start(bf16[64,128]{1,0:T(8,128)(2,1)S(1)} %get-tuple-element.77), channel_id=1, source_target_pairs={{16,32},{32,16},{48,64},{64,48},{80,96},{96,80},{112,128},{128,112... | collective-permute-start | bytes 49160 | tf_op jit(solution)/shard_map/ppermute | solution.py:285
  162.2 4.5 %collective-permute-start.18 = (bf16[64,128]{1,0:T(8,128)(2,1)S(1)}, bf16[64,128]{1,0:T(8,128)(2,1)S(1)}, u32[]{:S(2)}, u32[]{:S(2)}) collective-permute-start(bf16[64,128]{1,0:T(8,128)(2,1)S(1)} %get-tuple-element.80), channel_id=1, source_target_pairs={{0,16},{16,0},{32,48},{48,32},{64,80},{80,64},{96,112},{112,96},{1... | collective-permute-start | bytes 49160 | tf_op jit(solution)/shard_map/ppermute | solution.py:285
  167.2 8.1 %collective-permute-start.19 = (bf16[64,128]{1,0:T(8,128)(2,1)S(1)}, bf16[64,128]{1,0:T(8,128)(2,1)S(1)}, u32[]{:S(2)}, u32[]{:S(2)}) collective-permute-start(bf16[64,128]{1,0:T(8,128)(2,1)S(1)} %get-tuple-element.83), channel_id=1, source_target_pairs={{16,32},{32,16},{48,64},{64,48},{80,96},{96,80},{112,128},{128,112... | collective-permute-start | bytes 49160 | tf_op jit(solution)/shard_map/ppermute | solution.py:285
  175.9 4.5 %collective-permute-start.20 = (bf16[64,128]{1,0:T(8,128)(2,1)S(1)}, bf16[64,128]{1,0:T(8,128)(2,1)S(1)}, u32[]{:S(2)}, u32[]{:S(2)}) collective-permute-start(bf16[64,128]{1,0:T(8,128)(2,1)S(1)} %get-tuple-element.86), channel_id=1, source_target_pairs={{0,16},{16,0},{32,48},{48,32},{64,80},{80,64},{96,112},{112,96},{1... | collective-permute-start | bytes 49160 | tf_op jit(solution)/shard_map/ppermute | solution.py:285
  180.9 7.8 %collective-permute-start.21 = (bf16[64,128]{1,0:T(8,128)(2,1)S(1)}, bf16[64,128]{1,0:T(8,128)(2,1)S(1)}, u32[]{:S(2)}, u32[]{:S(2)}) collective-permute-start(bf16[64,128]{1,0:T(8,128)(2,1)S(1)} %get-tuple-element.90), channel_id=1, source_target_pairs={{16,32},{32,16},{48,64},{64,48},{80,96},{96,80},{112,128},{128,112... | collective-permute-start | bytes 49160 | tf_op jit(solution)/shard_map/ppermute | solution.py:285
Sparse Core Ops, SparseCore 0:
  10.1 65.5 all-gather.4
  77.8 43.6 all-gather.6

commit v17 on v16

--- a/solution.py
+++ b/solution.py
@@ -60,7 +60,9 @@
     for at, level in enumerate(levels):
         *owners, _ = unpack(packed, level)
         for half in range(2):
-            copies.append((weights.at[owners[half]], out.at[at, pl.ds(half * rows, rows)]))
+            for row in range(0, rows, 2):
+                source = weights.at[owners[half], pl.ds(row, 2)]
+                copies.append((source, out.at[at, pl.ds(half * rows + row, 2)]))
     return copies
 
 
@@ -301,11 +303,11 @@
         solved_mate.append(near if level % 2 == 0 else far)
         args = places, side, far, own, near
         if level == 1:
-            scratch = [pltpu.VMEM((1, count, 4, width, width), BF16), pltpu.SemaphoreType.DMA((2,))]
+            scratch = [pltpu.VMEM((1, count, 4, width, width), BF16), pltpu.SemaphoreType.DMA((rows,))]
             kernel = functools.partial(forward_kernel, level, 0, share, True)
             solved += call(kernel, [vector], packed, weights, *args, fetched=1, scratch=scratch)
             singles = range(2, paired)
-            blocks = arranged(arrange_kernel, singles, 4, 2 * len(singles), solved[-1], weights)
+            blocks = arranged(arrange_kernel, singles, 4, rows * len(singles), solved[-1], weights)
         else:
             kernel = functools.partial(forward_kernel, level, level - 2, share, False)
             solved += call(kernel, [vector], packed, blocks, *args)

time: 224 us -> 224 us (level)
  no operation moved by 1% of the time
where the time goes in v17:
time: 224 us; the launch traced here: 223 us
  starting transfers between devices  100 us (45%)
  waiting for transfers between devices  43.2 us (19%)
  blocking collectives  26 us (12%)
  Pallas kernels  19.7 us (9%)
  between operations  17.2 us (8%)
  local copies, waits for them, and re-layouts  8.03 us (4%)
  other arithmetic  7.92 us (4%)
    ppermute x18, starting transfers between devices, swap(): lax.ppermute(vector, 'dom', far_pairs if level % 2 == 0 else near_pairs)  71.9 us
    all_to_all x1, blocking collectives, local(): dealt = lax.all_to_all(dealt, 'level', 0, 0, tiled=False)  26 us
    ppermute x18, waiting for transfers between devices, swap(): lax.ppermute(vector, 'dom', far_pairs if level % 2 == 0 else near_pairs)  20.3 us
    pallas_call x25, Pallas kernels, call(): pl.pallas_call(kernel, out_shape=outs, in_specs=specs, out_specs=[pl.Bloc...  19.7 us
    all_gather x1, waiting for transfers between devices, local(): weights = lax.all_gather(weights, 'level')  17.4 us
    ppermute x1, starting transfers between devices, local(): by_far = lax.ppermute(mates, 'dom', far_pairs)  11 us
    all_to_all x1, starting transfers between devices, local(): side = lax.all_to_all(side, 'level', 1, 0, tiled=False)  8.35 us
    ppermute x1, starting transfers between devices, local(): by_near = lax.ppermute(mates, 'dom', near_pairs)  4.83 us
  transfers between devices with their start and end apart: 25, of which 18 were waited for; matrix products, arithmetic and copies ran while one was open for 6% of the time, Pallas kernels for 6%

profile of v17, /device:TPU:1, one launch (start us, length us, event | category | flops | bytes accessed | tf_op | source)
XLA Modules:
  0.0 223.1 jit_solution(13738540170264602403)
XLA Ops:
  7.2 1.9 pad_maximum_fusion
  9.2 1.3 fusion.7
  13.1 1.0 slice_select_fusion
  14.1 0.9 pad_maximum_fusion.1
  15.0 4.8 %collective-permute-start = (bf16[4,2,128,128]{3,2,1,0:T(8,128)(2,1)S(1)}, bf16[4,2,128,128]{3,2,1,0:T(8,128)(2,1)S(1)}, u32[]{:S(2)}, u32[]{:S(2)}) collective-permute-start(bf16[4,2,128,128]{3,2,1,0:T(8,128)(2,1)S(1)} %pad_maximum_fusion.1), channel_id=1, source_target_pairs={{0,16},{16,0},{32,48},{48,32},{64,80},{80,64},{96,112},{112,96},{1... | collective-permute-start | bytes 786440 | tf_op jit(solution)/shard_map/ppermute | solution.py:237
  19.9 11.0 %collective-permute-start.1 = (bf16[4,2,128,128]{3,2,1,0:T(8,128)(2,1)S(1)}, bf16[4,2,128,128]{3,2,1,0:T(8,128)(2,1)S(1)}, u32[]{:S(2)}, u32[]{:S(2)}) collective-permute-start(bf16[4,2,128,128]{3,2,1,0:T(8,128)(2,1)S(1)} %pad_maximum_fusion.1), channel_id=1, source_target_pairs={{16,32},{32,16},{48,64},{64,48},{80,96},{96,80},{112,128},{128,112... | collective-permute-start | bytes 786440 | tf_op jit(solution)/shard_map/ppermute | solution.py:238
  30.9 1.1 fusion
  32.7 8.3 %all-to-all-start = ((bf16[1,4,16,4,128]{4,3,1,0,2:T(4,128)(2,1)}), bf16[1,4,16,4,128]{4,3,1,0,2:T(4,128)(2,1)S(1)}, u32[]{:S(2)}, u32[]{:S(2)}) async-start(bf16[1,4,16,4,128]{4,3,1,0,2:T(4,128)(2,1)} %copy.64), calls=%async_computation | async-start | bytes 131072 | tf_op jit(solution)/shard_map/all_to_all | solution.py:243
  48.6 1.1 all-to-all-done
  50.3 1.9 collective-permute-start.2
  52.3 1.9 collective-permute-start.3
  54.9 3.2 %collective-permute-done.2 = bf16[2,32,128]{2,1,0:T(8,128)(2,1)S(1)} collective-permute-done((bf16[2,32,128]{2,1,0:T(8,128)(2,1)S(1)}, bf16[2,32,128]{2,1,0:T(8,128)(2,1)S(1)}, u32[]{:S(2)}, u32[]{:S(2)}) %collective-permute-start.2) | collective-permute-done | bytes 16416 | tf_op jit(solution)/shard_map/ppermute | solution.py:277
  58.3 17.4 %all-gather.5.cloned.1.call-done = bf16[64,4,128,128]{3,2,1,0:T(8,128)(2,1)} async-done(((bf16[4,4,128,128]{3,2,1,0:T(8,128)(2,1)}), bf16[64,4,128,128]{3,2,1,0:T(8,128)(2,1)}) %all-gather.5.cloned.1.call-update) | async-done | bytes 8388624 | tf_op jit(solution)/shard_map/all_gather | solution.py:225
  75.7 1.8 shard_map.68.own.solved.rest_1_
  77.5 7.7 %collective-permute-start.4 = (bf16[32,128]{1,0:T(8,128)(2,1)S(1)}, bf16[32,128]{1,0:T(8,128)(2,1)S(1)}, u32[]{:S(2)}, u32[]{:S(2)}) collective-permute-start(bf16[32,128]{1,0:T(8,128)(2,1)S(1)} %shard_map.68.own.solved.rest_1_), channel_id=1, source_target_pairs={{16,32},{32,16},{48,64},{64,48},{80,96},{96,80},{112,128},{128,112... | collective-permute-start | bytes 24584 | tf_op jit(solution)/shard_map/ppermute | solution.py:287
  85.2 1.9 collective-permute-start.5
  87.2 2.5 %shard_map.69.weights = bf16[4,8,4,128,128]{4,3,2,1,0:T(8,128)(2,1)S(1)} custom-call(s32[8,128]{1,0:T(8,128)S(1)} %broadcast_in_dim.73.packed, bf16[16,4,4,128,128]{4,3,2,1,0:T(8,128)(2,1)} %bitcast.77), custom_call_target="tpu_custom_call" | custom-call | tf_op jit(solution)/shard_map/pallas_call | solution.py:202
  90.2 3.9 %collective-permute-start.6 = (bf16[32,128]{1,0:T(8,128)(2,1)S(1)}, bf16[32,128]{1,0:T(8,128)(2,1)S(1)}, u32[]{:S(2)}, u32[]{:S(2)}) collective-permute-start(bf16[32,128]{1,0:T(8,128)(2,1)S(1)} %shard_map.70.own.solved.rest_2_), channel_id=1, source_target_pairs={{16,32},{32,16},{48,64},{64,48},{80,96},{96,80},{112,128},{128,112... | collective-permute-start | bytes 24584 | tf_op jit(solution)/shard_map/ppermute | solution.py:287
  94.1 1.9 collective-permute-start.7
  96.1 1.9 collective-permute-done.6.far.solved_mate
  97.9 1.0 collective-permute-done.7.near
  99.5 4.7 %collective-permute-start.8 = (bf16[32,128]{1,0:T(8,128)(2,1)S(1)}, bf16[32,128]{1,0:T(8,128)(2,1)S(1)}, u32[]{:S(2)}, u32[]{:S(2)}) collective-permute-start(bf16[32,128]{1,0:T(8,128)(2,1)S(1)} %shard_map.71.own.solved.rest_3_), channel_id=1, source_target_pairs={{16,32},{32,16},{48,64},{64,48},{80,96},{96,80},{112,128},{128,112... | collective-permute-start | bytes 24584 | tf_op jit(solution)/shard_map/ppermute | solution.py:287
  104.2 1.9 collective-permute-start.9
  106.1 1.1 collective-permute-done.8.far
  107.2 1.8 collective-permute-done.9.near.solved_mate
  109.5 3.7 %collective-permute-start.10 = (bf16[32,128]{1,0:T(8,128)(2,1)S(1)}, bf16[32,128]{1,0:T(8,128)(2,1)S(1)}, u32[]{:S(2)}, u32[]{:S(2)}) collective-permute-start(bf16[32,128]{1,0:T(8,128)(2,1)S(1)} %shard_map.72.own.solved.rest_4_), channel_id=1, source_target_pairs={{16,32},{32,16},{48,64},{64,48},{80,96},{96,80},{112,128},{128,112... | collective-permute-start | bytes 24584 | tf_op jit(solution)/shard_map/ppermute | solution.py:287
  113.3 1.9 collective-permute-start.11
  115.2 2.1 collective-permute-done.10.far.solved_mate
  118.6 1.9 collective-permute-start.12
  120.5 1.1 all-gather.7.cloned.1.call-done
  121.7 2.1 shard_map.74.blocks
  124.3 7.5 %collective-permute-start.13 = (bf16[64,128]{1,0:T(8,128)(2,1)S(1)}, bf16[64,128]{1,0:T(8,128)(2,1)S(1)}, u32[]{:S(2)}, u32[]{:S(2)}) collective-permute-start(bf16[64,128]{1,0:T(8,128)(2,1)S(1)} %get-tuple-element.65), channel_id=1, source_target_pairs={{16,32},{32,16},{48,64},{64,48},{80,96},{96,80},{112,128},{128,112... | collective-permute-start | bytes 49160 | tf_op jit(solution)/shard_map/ppermute | solution.py:287
  131.8 1.1 collective-permute-done.13.came
  133.6 1.9 collective-permute-start.14
  135.8 2.3 %collective-permute-done.14.came = bf16[64,128]{1,0:T(8,128)(2,1)S(1)} collective-permute-done((bf16[64,128]{1,0:T(8,128)(2,1)S(1)}, bf16[64,128]{1,0:T(8,128)(2,1)S(1)}, u32[]{:S(2)}, u32[]{:S(2)}) %collective-permute-start.14) | collective-permute-done | bytes 16416 | tf_op jit(solution)/shard_map/ppermute | solution.py:287
  138.0 0.9 shard_map.79
  139.0 6.7 %collective-permute-start.15 = (bf16[64,128]{1,0:T(8,128)(2,1)S(1)}, bf16[64,128]{1,0:T(8,128)(2,1)S(1)}, u32[]{:S(2)}, u32[]{:S(2)}) collective-permute-start(bf16[64,128]{1,0:T(8,128)(2,1)S(1)} %get-tuple-element.69), channel_id=1, source_target_pairs={{16,32},{32,16},{48,64},{64,48},{80,96},{96,80},{112,128},{128,112... | collective-permute-start | bytes 49160 | tf_op jit(solution)/shard_map/ppermute | solution.py:287
  147.3 1.9 collective-permute-start.16
  149.2 3.6 %shard_map.76.blocks = bf16[6,8,5,128,128]{4,3,2,1,0:T(8,128)(2,1)S(1)} custom-call(s32[8,128]{1,0:T(8,128)S(1)} %broadcast_in_dim.73.packed, bf16[16,4,4,128,128]{4,3,2,1,0:T(8,128)(2,1)} %bitcast.79, bf16[16,4,2,128,128]{4,3,2,1,0:T(8,128)(2,1)} %bitcast.81), custom_call_target="tpu_custom_call" | custom-call | tf_op jit(solution)/shard_map/pallas_call | solution.py:202
  153.7 6.7 %collective-permute-start.17 = (bf16[64,128]{1,0:T(8,128)(2,1)S(1)}, bf16[64,128]{1,0:T(8,128)(2,1)S(1)}, u32[]{:S(2)}, u32[]{:S(2)}) collective-permute-start(bf16[64,128]{1,0:T(8,128)(2,1)S(1)} %get-tuple-element.77), channel_id=1, source_target_pairs={{16,32},{32,16},{48,64},{64,48},{80,96},{96,80},{112,128},{128,112... | collective-permute-start | bytes 49160 | tf_op jit(solution)/shard_map/ppermute | solution.py:287
  162.1 1.9 collective-permute-start.18
  164.3 2.3 %collective-permute-done.18.came = bf16[64,128]{1,0:T(8,128)(2,1)S(1)} collective-permute-done((bf16[64,128]{1,0:T(8,128)(2,1)S(1)}, bf16[64,128]{1,0:T(8,128)(2,1)S(1)}, u32[]{:S(2)}, u32[]{:S(2)}) %collective-permute-start.18) | collective-permute-done | bytes 16416 | tf_op jit(solution)/shard_map/ppermute | solution.py:287
  167.1 7.0 %collective-permute-start.19 = (bf16[64,128]{1,0:T(8,128)(2,1)S(1)}, bf16[64,128]{1,0:T(8,128)(2,1)S(1)}, u32[]{:S(2)}, u32[]{:S(2)}) collective-permute-start(bf16[64,128]{1,0:T(8,128)(2,1)S(1)} %get-tuple-element.83), channel_id=1, source_target_pairs={{16,32},{32,16},{48,64},{64,48},{80,96},{96,80},{112,128},{128,112... | collective-permute-start | bytes 49160 | tf_op jit(solution)/shard_map/ppermute | solution.py:287
  175.8 1.9 collective-permute-start.20
  178.0 2.3 %collective-permute-done.20.came = bf16[64,128]{1,0:T(8,128)(2,1)S(1)} collective-permute-done((bf16[64,128]{1,0:T(8,128)(2,1)S(1)}, bf16[64,128]{1,0:T(8,128)(2,1)S(1)}, u32[]{:S(2)}, u32[]{:S(2)}) %collective-permute-start.20) | collective-permute-done | bytes 16416 | tf_op jit(solution)/shard_map/ppermute | solution.py:287
  180.8 6.7 %collective-permute-start.21 = (bf16[64,128]{1,0:T(8,128)(2,1)S(1)}, bf16[64,128]{1,0:T(8,128)(2,1)S(1)}, u32[]{:S(2)}, u32[]{:S(2)}) collective-permute-start(bf16[64,128]{1,0:T(8,128)(2,1)S(1)} %get-tuple-element.90), channel_id=1, source_target_pairs={{16,32},{32,16},{48,64},{64,48},{80,96},{96,80},{112,128},{128,112... | collective-permute-start | bytes 49160 | tf_op jit(solution)/shard_map/ppermute | solution.py:287
  187.5 1.1 collective-permute-done.21.came
  188.9 26.0 %all_to_all.20 = bf16[16,32,128]{2,1,0:T(8,128)(2,1)S(1)} all-to-all(bf16[16,32,128]{2,1,0:T(8,128)(2,1)S(1)} %shard_map.92), channel_id=1, replica_groups=mesh['dom'=32,'level'=16] {'level'}, dimensions={0} | all-to-all | bytes 262144 | tf_op jit(solution)/shard_map/all_to_all | solution.py:349
  (87 shorter events, 23.0 us)
Async XLA Ops:
  7.2 68.5 %all-gather.5.cloned.1.call-start = ((), (), s32[]{:S(2)}) async-start(), calls=%async_computation.2 | async-start | bytes 8912896 | tf_op jit(solution)/shard_map/all_gather | solution.py:225
  15.0 39.2 %collective-permute-start = (bf16[4,2,128,128]{3,2,1,0:T(8,128)(2,1)S(1)}, bf16[4,2,128,128]{3,2,1,0:T(8,128)(2,1)S(1)}, u32[]{:S(2)}, u32[]{:S(2)}) collective-permute-start(bf16[4,2,128,128]{3,2,1,0:T(8,128)(2,1)S(1)} %pad_maximum_fusion.1), channel_id=1, source_target_pairs={{0,16},{16,0},{32,48},{48,32},{64,80},{80,64},{96,112},{112,96},{1... | collective-permute-start | bytes 786440 | tf_op jit(solution)/shard_map/ppermute | solution.py:237
  19.9 34.3 %collective-permute-start.1 = (bf16[4,2,128,128]{3,2,1,0:T(8,128)(2,1)S(1)}, bf16[4,2,128,128]{3,2,1,0:T(8,128)(2,1)S(1)}, u32[]{:S(2)}, u32[]{:S(2)}) collective-permute-start(bf16[4,2,128,128]{3,2,1,0:T(8,128)(2,1)S(1)} %pad_maximum_fusion.1), channel_id=1, source_target_pairs={{16,32},{32,16},{48,64},{64,48},{80,96},{96,80},{112,128},{128,112... | collective-permute-start | bytes 786440 | tf_op jit(solution)/shard_map/ppermute | solution.py:238
  32.7 17.0 %all-to-all-start = ((bf16[1,4,16,4,128]{4,3,1,0,2:T(4,128)(2,1)}), bf16[1,4,16,4,128]{4,3,1,0,2:T(4,128)(2,1)S(1)}, u32[]{:S(2)}, u32[]{:S(2)}) async-start(bf16[1,4,16,4,128]{4,3,1,0,2:T(4,128)(2,1)} %copy.64), calls=%async_computation | async-start | bytes 131072 | tf_op jit(solution)/shard_map/all_to_all | solution.py:243
  41.0 80.6 %all-gather.7.cloned.1.call-start = ((), (), s32[]{:S(2)}) async-start(), calls=%async_computation.3 | async-start | bytes 4456448 | tf_op jit(solution)/shard_map/all_gather | solution.py:284
  50.3 7.8 %collective-permute-start.2 = (bf16[2,32,128]{2,1,0:T(8,128)(2,1)S(1)}, bf16[2,32,128]{2,1,0:T(8,128)(2,1)S(1)}, u32[]{:S(2)}, u32[]{:S(2)}) collective-permute-start(bf16[2,32,128]{2,1,0:T(8,128)(2,1)S(1)} %get-tuple-element.118), channel_id=1, source_target_pairs={{16,32},{32,16},{48,64},{64,48},{80,96},{96,80},{112,128},{128,112... | collective-permute-start | bytes 49160 | tf_op jit(solution)/shard_map/ppermute | solution.py:277
  52.3 5.9 %collective-permute-start.3 = (bf16[2,32,128]{2,1,0:T(8,128)(2,1)S(1)}, bf16[2,32,128]{2,1,0:T(8,128)(2,1)S(1)}, u32[]{:S(2)}, u32[]{:S(2)}) collective-permute-start(bf16[2,32,128]{2,1,0:T(8,128)(2,1)S(1)} %get-tuple-element.117), channel_id=1, source_target_pairs={{0,16},{16,0},{32,48},{48,32},{64,80},{80,64},{96,112},{112,96},{1... | collective-permute-start | bytes 49160 | tf_op jit(solution)/shard_map/ppermute | solution.py:278
  77.5 12.1 %collective-permute-start.4 = (bf16[32,128]{1,0:T(8,128)(2,1)S(1)}, bf16[32,128]{1,0:T(8,128)(2,1)S(1)}, u32[]{:S(2)}, u32[]{:S(2)}) collective-permute-start(bf16[32,128]{1,0:T(8,128)(2,1)S(1)} %shard_map.68.own.solved.rest_1_), channel_id=1, source_target_pairs={{16,32},{32,16},{48,64},{64,48},{80,96},{96,80},{112,128},{128,112... | collective-permute-start | bytes 24584 | tf_op jit(solution)/shard_map/ppermute | solution.py:287
  85.2 4.4 %collective-permute-start.5 = (bf16[32,128]{1,0:T(8,128)(2,1)S(1)}, bf16[32,128]{1,0:T(8,128)(2,1)S(1)}, u32[]{:S(2)}, u32[]{:S(2)}) collective-permute-start(bf16[32,128]{1,0:T(8,128)(2,1)S(1)} %shard_map.68.own.solved.rest_1_), channel_id=1, source_target_pairs={{0,16},{16,0},{32,48},{48,32},{64,80},{80,64},{96,112},{112,96},{1... | collective-permute-start | bytes 24584 | tf_op jit(solution)/shard_map/ppermute | solution.py:287
  90.2 7.7 %collective-permute-start.6 = (bf16[32,128]{1,0:T(8,128)(2,1)S(1)}, bf16[32,128]{1,0:T(8,128)(2,1)S(1)}, u32[]{:S(2)}, u32[]{:S(2)}) collective-permute-start(bf16[32,128]{1,0:T(8,128)(2,1)S(1)} %shard_map.70.own.solved.rest_2_), channel_id=1, source_target_pairs={{16,32},{32,16},{48,64},{64,48},{80,96},{96,80},{112,128},{128,112... | collective-permute-start | bytes 24584 | tf_op jit(solution)/shard_map/ppermute | solution.py:287
  94.1 4.8 %collective-permute-start.7 = (bf16[32,128]{1,0:T(8,128)(2,1)S(1)}, bf16[32,128]{1,0:T(8,128)(2,1)S(1)}, u32[]{:S(2)}, u32[]{:S(2)}) collective-permute-start(bf16[32,128]{1,0:T(8,128)(2,1)S(1)} %shard_map.70.own.solved.rest_2_), channel_id=1, source_target_pairs={{0,16},{16,0},{32,48},{48,32},{64,80},{80,64},{96,112},{112,96},{1... | collective-permute-start | bytes 24584 | tf_op jit(solution)/shard_map/ppermute | solution.py:287
  99.5 7.7 %collective-permute-start.8 = (bf16[32,128]{1,0:T(8,128)(2,1)S(1)}, bf16[32,128]{1,0:T(8,128)(2,1)S(1)}, u32[]{:S(2)}, u32[]{:S(2)}) collective-permute-start(bf16[32,128]{1,0:T(8,128)(2,1)S(1)} %shard_map.71.own.solved.rest_3_), channel_id=1, source_target_pairs={{16,32},{32,16},{48,64},{64,48},{80,96},{96,80},{112,128},{128,112... | collective-permute-start | bytes 24584 | tf_op jit(solution)/shard_map/ppermute | solution.py:287
  104.2 4.8 %collective-permute-start.9 = (bf16[32,128]{1,0:T(8,128)(2,1)S(1)}, bf16[32,128]{1,0:T(8,128)(2,1)S(1)}, u32[]{:S(2)}, u32[]{:S(2)}) collective-permute-start(bf16[32,128]{1,0:T(8,128)(2,1)S(1)} %shard_map.71.own.solved.rest_3_), channel_id=1, source_target_pairs={{0,16},{16,0},{32,48},{48,32},{64,80},{80,64},{96,112},{112,96},{1... | collective-permute-start | bytes 24584 | tf_op jit(solution)/shard_map/ppermute | solution.py:287
  109.5 7.7 %collective-permute-start.10 = (bf16[32,128]{1,0:T(8,128)(2,1)S(1)}, bf16[32,128]{1,0:T(8,128)(2,1)S(1)}, u32[]{:S(2)}, u32[]{:S(2)}) collective-permute-start(bf16[32,128]{1,0:T(8,128)(2,1)S(1)} %shard_map.72.own.solved.rest_4_), channel_id=1, source_target_pairs={{16,32},{32,16},{48,64},{64,48},{80,96},{96,80},{112,128},{128,112... | collective-permute-start | bytes 24584 | tf_op jit(solution)/shard_map/ppermute | solution.py:287
  113.3 4.8 %collective-permute-start.11 = (bf16[32,128]{1,0:T(8,128)(2,1)S(1)}, bf16[32,128]{1,0:T(8,128)(2,1)S(1)}, u32[]{:S(2)}, u32[]{:S(2)}) collective-permute-start(bf16[32,128]{1,0:T(8,128)(2,1)S(1)} %shard_map.72.own.solved.rest_4_), channel_id=1, source_target_pairs={{0,16},{16,0},{32,48},{48,32},{64,80},{80,64},{96,112},{112,96},{1... | collective-permute-start | bytes 24584 | tf_op jit(solution)/shard_map/ppermute | solution.py:287
  118.6 5.1 %collective-permute-start.12 = (bf16[32,128]{1,0:T(8,128)(2,1)S(1)}, bf16[32,128]{1,0:T(8,128)(2,1)S(1)}, u32[]{:S(2)}, u32[]{:S(2)}) collective-permute-start(bf16[32,128]{1,0:T(8,128)(2,1)S(1)} %shard_map.73.own.solved.rest_5_), channel_id=1, source_target_pairs={{0,16},{16,0},{32,48},{48,32},{64,80},{80,64},{96,112},{112,96},{1... | collective-permute-start | bytes 24584 | tf_op jit(solution)/shard_map/ppermute | solution.py:287
  124.3 8.6 %collective-permute-start.13 = (bf16[64,128]{1,0:T(8,128)(2,1)S(1)}, bf16[64,128]{1,0:T(8,128)(2,1)S(1)}, u32[]{:S(2)}, u32[]{:S(2)}) collective-permute-start(bf16[64,128]{1,0:T(8,128)(2,1)S(1)} %get-tuple-element.65), channel_id=1, source_target_pairs={{16,32},{32,16},{48,64},{64,48},{80,96},{96,80},{112,128},{128,112... | collective-permute-start | bytes 49160 | tf_op jit(solution)/shard_map/ppermute | solution.py:287
  133.6 4.5 %collective-permute-start.14 = (bf16[64,128]{1,0:T(8,128)(2,1)S(1)}, bf16[64,128]{1,0:T(8,128)(2,1)S(1)}, u32[]{:S(2)}, u32[]{:S(2)}) collective-permute-start(bf16[64,128]{1,0:T(8,128)(2,1)S(1)} %get-tuple-element.66), channel_id=1, source_target_pairs={{0,16},{16,0},{32,48},{48,32},{64,80},{80,64},{96,112},{112,96},{1... | collective-permute-start | bytes 49160 | tf_op jit(solution)/shard_map/ppermute | solution.py:287
  139.0 7.8 %collective-permute-start.15 = (bf16[64,128]{1,0:T(8,128)(2,1)S(1)}, bf16[64,128]{1,0:T(8,128)(2,1)S(1)}, u32[]{:S(2)}, u32[]{:S(2)}) collective-permute-start(bf16[64,128]{1,0:T(8,128)(2,1)S(1)} %get-tuple-element.69), channel_id=1, source_target_pairs={{16,32},{32,16},{48,64},{64,48},{80,96},{96,80},{112,128},{128,112... | collective-permute-start | bytes 49160 | tf_op jit(solution)/shard_map/ppermute | solution.py:287
  147.3 5.8 %collective-permute-start.16 = (bf16[64,128]{1,0:T(8,128)(2,1)S(1)}, bf16[64,128]{1,0:T(8,128)(2,1)S(1)}, u32[]{:S(2)}, u32[]{:S(2)}) collective-permute-start(bf16[64,128]{1,0:T(8,128)(2,1)S(1)} %get-tuple-element.74), channel_id=1, source_target_pairs={{0,16},{16,0},{32,48},{48,32},{64,80},{80,64},{96,112},{112,96},{1... | collective-permute-start | bytes 49160 | tf_op jit(solution)/shard_map/ppermute | solution.py:287
  153.7 7.8 %collective-permute-start.17 = (bf16[64,128]{1,0:T(8,128)(2,1)S(1)}, bf16[64,128]{1,0:T(8,128)(2,1)S(1)}, u32[]{:S(2)}, u32[]{:S(2)}) collective-permute-start(bf16[64,128]{1,0:T(8,128)(2,1)S(1)} %get-tuple-element.77), channel_id=1, source_target_pairs={{16,32},{32,16},{48,64},{64,48},{80,96},{96,80},{112,128},{128,112... | collective-permute-start | bytes 49160 | tf_op jit(solution)/shard_map/ppermute | solution.py:287
  162.1 4.5 %collective-permute-start.18 = (bf16[64,128]{1,0:T(8,128)(2,1)S(1)}, bf16[64,128]{1,0:T(8,128)(2,1)S(1)}, u32[]{:S(2)}, u32[]{:S(2)}) collective-permute-start(bf16[64,128]{1,0:T(8,128)(2,1)S(1)} %get-tuple-element.80), channel_id=1, source_target_pairs={{0,16},{16,0},{32,48},{48,32},{64,80},{80,64},{96,112},{112,96},{1... | collective-permute-start | bytes 49160 | tf_op jit(solution)/shard_map/ppermute | solution.py:287
  167.1 8.1 %collective-permute-start.19 = (bf16[64,128]{1,0:T(8,128)(2,1)S(1)}, bf16[64,128]{1,0:T(8,128)(2,1)S(1)}, u32[]{:S(2)}, u32[]{:S(2)}) collective-permute-start(bf16[64,128]{1,0:T(8,128)(2,1)S(1)} %get-tuple-element.83), channel_id=1, source_target_pairs={{16,32},{32,16},{48,64},{64,48},{80,96},{96,80},{112,128},{128,112... | collective-permute-start | bytes 49160 | tf_op jit(solution)/shard_map/ppermute | solution.py:287
  175.8 4.5 %collective-permute-start.20 = (bf16[64,128]{1,0:T(8,128)(2,1)S(1)}, bf16[64,128]{1,0:T(8,128)(2,1)S(1)}, u32[]{:S(2)}, u32[]{:S(2)}) collective-permute-start(bf16[64,128]{1,0:T(8,128)(2,1)S(1)} %get-tuple-element.86), channel_id=1, source_target_pairs={{0,16},{16,0},{32,48},{48,32},{64,80},{80,64},{96,112},{112,96},{1... | collective-permute-start | bytes 49160 | tf_op jit(solution)/shard_map/ppermute | solution.py:287
  180.8 7.8 %collective-permute-start.21 = (bf16[64,128]{1,0:T(8,128)(2,1)S(1)}, bf16[64,128]{1,0:T(8,128)(2,1)S(1)}, u32[]{:S(2)}, u32[]{:S(2)}) collective-permute-start(bf16[64,128]{1,0:T(8,128)(2,1)S(1)} %get-tuple-element.90), channel_id=1, source_target_pairs={{16,32},{32,16},{48,64},{64,48},{80,96},{96,80},{112,128},{128,112... | collective-permute-start | bytes 49160 | tf_op jit(solution)/shard_map/ppermute | solution.py:287
Sparse Core Ops, SparseCore 0:
  10.1 65.5 all-gather.4
  77.8 43.8 all-gather.6
